TPU v7x, 32 devices: a whole 2x2x4 slice. The times are simulated.
32 devices in a mesh: half: 2 (over x), expert: 8 (over z, core), group: 2 (over y).
Axes of the slice: x: 2, y: 2, z: 4, core: 2. Of those that a mesh axis runs over, the one named last changes fastest.
Arguments:
- inputs: bfloat16 [2, 10240, 1024], P('half', ('expert', 'group')), may hold values from -6 to 6
- cotangent: bfloat16 [2, 10240, 1024], P('half', ('expert', 'group')), may hold values from -6 to 6
- enc_lengths: int32 [80], P(('expert', 'group')), may hold values from 32 to 512, as said below
- routes: int32 [2, 10240, 2], P('half', ('expert', 'group')), may hold values from 0 to 7, all different within a row; in each aligned block of 640 rows (0 to 639, 640 to 1279, ..., all dimensions but the last counted through in order) at most 200 rows name the same one
- norm_gains: float32 [2, 3, 1024], P('half'), may hold values from 0.25 to 1.75
- rel_bias: float32 [2, 16, 32], P('half'), may hold values from -4 to 4
- self_qkv: bfloat16 [2, 1024, 3072], P('half'), may hold values from -0.1875 to 0.1875
- self_out: bfloat16 [2, 1024, 1024], P('half'), may hold values from -1 to 1
- cross_proj: bfloat16 [2, 1024, 1024], P('half'), may hold values from -0.1875 to 0.1875
- cross_value: bfloat16 [2, 1024, 1024], P('half'), may hold values from -0.75 to 0.75
- router: float32 [2, 1024, 8], P('half'), may hold values from -0.125 to 0.125
- expert_in: bfloat16 [2, 8, 1024, 5632], P('half', 'expert'), may hold values from -0.1875 to 0.1875
- expert_out: bfloat16 [2, 8, 2816, 1024], P('half', 'expert'), may hold values from -0.15625 to 0.15625
Outputs:
- outputs: bfloat16 [2, 10240, 1024], P('half', ('expert', 'group'))
- grad_inputs: bfloat16 [2, 10240, 1024], P('half', ('expert', 'group'))
- grad_gains: float32 [2, 3, 1024], P('half', None, 'group')
- grad_bias: float32 [2, 16, 32], P('half', 'group')
- grad_qkv: float32 [2, 1024, 3072], P('half', 'group')
- grad_out: float32 [2, 1024, 1024], P('half', 'group')
- grad_cross_proj: float32 [2, 1024, 1024], P('half', 'group')
- grad_cross_value: float32 [2, 1024, 1024], P('half', 'group')
- grad_router: float32 [2, 1024, 8], P('half', 'group')
- grad_expert_in: float32 [2, 8, 1024, 5632], P('half', 'expert', None, 'group')
- grad_expert_out: float32 [2, 8, 2816, 1024], P('half', 'expert', 'group')
Inputs may be any that keep to these rules, and one draw needn't show every extreme that they name: `enc_lengths`: each device's 5 encoder items, in order, fill its 640 rows exactly, and one item of each device is exactly 512 long. `routes`: each row names two different experts; among the rows of one device no expert is named more than 200 times.
All inputs are finite; a program needn't handle non-finite values.
Results may differ from a plain program's by a relative error of at most 0.025.
Values may be sent and summed in bfloat16 or wider, within the bound.
No kernel may reach another device: no remote copies, remote signals or barrier semaphores. Data moves between devices by JAX's collectives and lax.ppermute only.
A program may use at most 448 MiB of HBM per device.

v0:
```python
from functools import reduce

import jax
import jax.numpy as jnp
from jax import lax
from jax.sharding import PartitionSpec as P

D = 1024
H = 16
HD = 64
FF = 2816
NBKT = 32
DEC_SLOT = 128
DEC_LEN = 114


EPSILON = 1e-06
MASKED = -1e30
HIGHEST = lax.Precision.HIGHEST
score_rows = 512


def for_sending(value):

    def short(part):
        return part.astype(jnp.bfloat16) if part.dtype == jnp.float32 else part

    return jax.tree.map(short, value)


def shifted(block, axis, distance):
    devices = range(lax.axis_size(axis))
    route = [(i - distance, i) for i in devices if i - distance in devices]
    return lax.ppermute(block, axis, route)


def bucket_limits(exact_range, growth, divisions):
    limits = []
    for number in range(1, divisions):
        candidate = exact_range
        while candidate**divisions < exact_range**divisions * growth**number:
            candidate = candidate + 1
        limits.append(candidate)
    return limits


def rel_buckets(offset, causal):
    behind = jnp.maximum(-offset, 0)
    one_way = jnp.minimum(behind, 16) + reduce(
        jnp.add, [(behind >= threshold).astype(jnp.int32) for threshold in bucket_limits(16, 8, 16)]
    )
    distance = jnp.abs(offset)
    two_way = (
        (offset > 0).astype(jnp.int32) * 16
        + jnp.minimum(distance, 8)
        + reduce(
            jnp.add,
            [(distance >= threshold).astype(jnp.int32) for threshold in bucket_limits(8, 16, 8)],
        )
    )
    return jnp.where(causal, one_way, two_way)


def rms_norm(values, gain_vec):
    return (
        values * lax.rsqrt(jnp.mean(values * values, axis=-1, keepdims=True) + EPSILON) * gain_vec
    )


def segment_ids(lengths, places):
    item_ends = jnp.cumsum(lengths)
    return jnp.sum((places[:, None] >= item_ends[None, :]).astype(jnp.int32), axis=1)


def gate_values(normed, router_weight, routing):
    logits = jnp.dot(normed, router_weight, precision=HIGHEST)
    probabilities = jax.nn.softmax(logits, axis=-1)
    picked = jnp.take_along_axis(probabilities, routing, axis=1)
    return picked / jnp.sum(picked, axis=1, keepdims=True)


def slot_targets(routing, experts, capacity):
    ordered = routing.T.reshape(-1)
    expert_hits = (ordered[:, None] == jnp.arange(experts, dtype=jnp.int32)[None, :]).astype(
        jnp.int32
    )
    earlier = jnp.cumsum(expert_hits, axis=0) - expert_hits
    slot_rank = jnp.sum(earlier * expert_hits, axis=1)
    return (ordered * capacity + slot_rank).reshape(2, -1).T


def block_spans(row_count):
    step_rows = min(score_rows, row_count)
    return [
        (first_row, min(step_rows, row_count - first_row))
        for first_row in range(0, row_count, step_rows)
    ]


def diagonal_sums(grad_scores):
    heads, block_size, key_count = grad_scores.shape
    flipped = grad_scores[:, :, ::-1]
    padded = jnp.pad(flipped, ((0, 0), (0, 0), (0, block_size)))
    width = key_count + block_size - 1
    skewed = padded.reshape(heads, block_size * (key_count + block_size))[
        :, : block_size * width
    ].reshape(heads, block_size, width)
    return jnp.sum(skewed, axis=1)


def diagonal_spread(diag_values, block_size, key_count):
    heads, width = diag_values.shape
    padded = jnp.pad(diag_values, ((0, 0), (0, 1)))
    repeated = jnp.broadcast_to(padded[:, None, :], (heads, block_size + 1, width + 1)).reshape(
        heads, (block_size + 1) * (width + 1)
    )
    skewed = repeated[:, : block_size * (width + 2)].reshape(heads, block_size, width + 2)
    return skewed[:, :, :key_count][:, :, ::-1]


def block_scores(query_block, key_rows, scaling, allowed, bias_part):
    scores = (
        jnp.einsum("qhd,khd->hqk", query_block, key_rows, preferred_element_type=jnp.float32)
        * scaling
    )
    if bias_part is not None:
        scores = scores + bias_part
    return jnp.where(allowed[None], scores, MASKED)


def attend(queries, key_rows, value_rows, layout_fn):
    scaling = queries.shape[-1] ** (-0.5)
    contexts = []
    log_sums = []
    for first_row, block_size in block_spans(queries.shape[0]):
        allowed, bias_part, offset_hits = layout_fn(first_row, block_size)
        scores = block_scores(
            queries[first_row : first_row + block_size], key_rows, scaling, allowed, bias_part
        )
        highest = jnp.max(scores, axis=-1, keepdims=True)
        exponent = jnp.exp(scores - highest)
        totals = jnp.sum(exponent, axis=-1, keepdims=True)
        weights = (exponent / totals).astype(jnp.bfloat16)
        contexts.append(
            jnp.einsum("hqk,khd->qhd", weights, value_rows, preferred_element_type=jnp.float32)
        )
        log_sums.append(highest + jnp.log(totals))
    return (jnp.concatenate(contexts, axis=0), log_sums)


def attend_back(queries, key_rows, value_rows, grad_context, log_sums, layout_fn):
    scaling = queries.shape[-1] ** (-0.5)
    grad_queries = []
    grad_keys = jnp.zeros(key_rows.shape, jnp.float32)
    grad_values = jnp.zeros(value_rows.shape, jnp.float32)
    grad_table = None
    for position, (first_row, block_size) in enumerate(block_spans(queries.shape[0])):
        allowed, bias_part, offset_hits = layout_fn(first_row, block_size)
        query_block = queries[first_row : first_row + block_size]
        grad_block = grad_context[first_row : first_row + block_size]
        scores = block_scores(query_block, key_rows, scaling, allowed, bias_part)
        weights = jnp.exp(scores - log_sums[position])
        grad_weights = jnp.einsum(
            "qhd,khd->hqk", grad_block, value_rows, preferred_element_type=jnp.float32
        )
        grad_scores = weights * (
            grad_weights - jnp.sum(weights * grad_weights, axis=-1, keepdims=True)
        )
        if offset_hits is not None:
            table_part = jnp.dot(diagonal_sums(grad_scores), offset_hits, precision=HIGHEST)
            grad_table = table_part if grad_table is None else grad_table + table_part
        rounded = grad_scores.astype(jnp.bfloat16)
        grad_queries.append(
            jnp.einsum("hqk,khd->qhd", rounded, key_rows, preferred_element_type=jnp.float32)
            * scaling
        )
        grad_keys = (
            grad_keys
            + jnp.einsum("hqk,qhd->khd", rounded, query_block, preferred_element_type=jnp.float32)
            * scaling
        )
        grad_values = grad_values + jnp.einsum(
            "hqk,qhd->khd",
            weights.astype(jnp.bfloat16),
            grad_block,
            preferred_element_type=jnp.float32,
        )
    return (jnp.concatenate(grad_queries, axis=0), grad_keys, grad_values, grad_table)


def self_forward(starts, gain_vec, qkv_weight, out_weight, layout_fn):
    row_count = starts.shape[0]
    normed = rms_norm(starts, gain_vec).astype(jnp.bfloat16)
    project = (
        jnp.dot(normed, qkv_weight, preferred_element_type=jnp.float32)
        .astype(jnp.bfloat16)
        .reshape(row_count, 3, H, HD)
    )
    context, log_sums = attend(project[:, 0], project[:, 1], project[:, 2], layout_fn)
    context = context.astype(jnp.bfloat16).reshape(row_count, D)
    output = starts + jnp.dot(context, out_weight, preferred_element_type=jnp.float32)
    return (output, (normed, project, log_sums, context))


def self_backward(grad_out, starts, gain_vec, qkv_weight, out_weight, layout_fn, stored):
    normed, project, log_sums, context = stored
    row_count = starts.shape[0]
    grad_rounded = grad_out.astype(jnp.bfloat16)
    grad_out_weight = jnp.einsum(
        "rc,re->ce", context, grad_rounded, preferred_element_type=jnp.float32
    )
    grad_context = (
        jnp.einsum("re,ce->rc", grad_rounded, out_weight, preferred_element_type=jnp.float32)
        .astype(jnp.bfloat16)
        .reshape(row_count, H, HD)
    )
    grad_query, grad_key, grad_value, grad_table = attend_back(
        project[:, 0], project[:, 1], project[:, 2], grad_context, log_sums, layout_fn
    )
    grad_project = (
        jnp.stack([grad_query, grad_key, grad_value], axis=1)
        .astype(jnp.bfloat16)
        .reshape(row_count, 3 * D)
    )
    grad_qkv_weight = jnp.einsum(
        "rc,re->ce", normed, grad_project, preferred_element_type=jnp.float32
    )
    grad_normed = jnp.einsum(
        "re,ce->rc", grad_project, qkv_weight, preferred_element_type=jnp.float32
    )
    unused, norm_pull = jax.vjp(rms_norm, starts, gain_vec)
    grad_starts, grad_gain = norm_pull(grad_normed)
    return (grad_out + grad_starts, grad_gain, grad_qkv_weight, grad_out_weight, grad_table)


def memory_forward(encoded, gain_vec, proj_weight, value_weight):
    memory = rms_norm(encoded, gain_vec).astype(jnp.bfloat16)
    key_rows = jnp.dot(memory, proj_weight, preferred_element_type=jnp.float32).astype(jnp.bfloat16)
    value_rows = jnp.dot(memory, value_weight, preferred_element_type=jnp.float32).astype(
        jnp.bfloat16
    )
    return jnp.stack([key_rows, value_rows])


def memory_backward(grad_memory, encoded, gain_vec, proj_weight, value_weight):
    memory = rms_norm(encoded, gain_vec).astype(jnp.bfloat16)
    grad_proj_weight = jnp.einsum(
        "rc,re->ce", memory, grad_memory[0], preferred_element_type=jnp.float32
    )
    grad_value_weight = jnp.einsum(
        "rc,re->ce", memory, grad_memory[1], preferred_element_type=jnp.float32
    )
    grad_normed = jnp.einsum(
        "re,ce->rc", grad_memory[0], proj_weight, preferred_element_type=jnp.float32
    ) + jnp.einsum("re,ce->rc", grad_memory[1], value_weight, preferred_element_type=jnp.float32)
    unused, norm_pull = jax.vjp(rms_norm, encoded, gain_vec)
    grad_encoded, grad_gain = norm_pull(grad_normed)
    return (grad_encoded, grad_gain, grad_proj_weight, grad_value_weight)


def cross_forward(decoded, gain_vec, proj_weight, value_weight, memory_kv, layout_fn):
    row_count = decoded.shape[0]
    key_count = memory_kv.shape[1]
    normed = rms_norm(decoded, gain_vec).astype(jnp.bfloat16)
    queries = (
        jnp.dot(normed, proj_weight, preferred_element_type=jnp.float32)
        .astype(jnp.bfloat16)
        .reshape(row_count, H, HD)
    )
    context, log_sums = attend(
        queries,
        memory_kv[0].reshape(key_count, H, HD),
        memory_kv[1].reshape(key_count, H, HD),
        layout_fn,
    )
    context = context.astype(jnp.bfloat16).reshape(row_count, D)
    output = decoded + jnp.dot(context, value_weight, preferred_element_type=jnp.float32)
    return (output, (normed, queries, log_sums, context))


def cross_backward(
    grad_out, decoded, gain_vec, proj_weight, value_weight, memory_kv, layout_fn, stored
):
    normed, queries, log_sums, context = stored
    row_count = decoded.shape[0]
    key_count = memory_kv.shape[1]
    grad_rounded = grad_out.astype(jnp.bfloat16)
    grad_value_weight = jnp.einsum(
        "rc,re->ce", context, grad_rounded, preferred_element_type=jnp.float32
    )
    grad_context = (
        jnp.einsum("re,ce->rc", grad_rounded, value_weight, preferred_element_type=jnp.float32)
        .astype(jnp.bfloat16)
        .reshape(row_count, H, HD)
    )
    grad_query, grad_key, grad_value, unused = attend_back(
        queries,
        memory_kv[0].reshape(key_count, H, HD),
        memory_kv[1].reshape(key_count, H, HD),
        grad_context,
        log_sums,
        layout_fn,
    )
    grad_memory = jnp.stack([grad_key, grad_value]).astype(jnp.bfloat16).reshape(2, key_count, D)
    grad_query = grad_query.astype(jnp.bfloat16).reshape(row_count, D)
    grad_proj_weight = jnp.einsum(
        "rc,re->ce", normed, grad_query, preferred_element_type=jnp.float32
    )
    grad_normed = jnp.einsum(
        "re,ce->rc", grad_query, proj_weight, preferred_element_type=jnp.float32
    )
    unused, norm_pull = jax.vjp(rms_norm, decoded, gain_vec)
    grad_decoded, grad_gain = norm_pull(grad_normed)
    return (grad_out + grad_decoded, grad_gain, grad_proj_weight, grad_value_weight, grad_memory)


def moe_forward(inputs_f, gain_vec, router_weight, routing, expert_first, expert_second, active):
    row_count = inputs_f.shape[0]
    experts = router_weight.shape[1]
    capacity = 5 * row_count // (2 * experts)
    local_experts = expert_first.shape[0]
    normed = rms_norm(inputs_f, gain_vec)
    gate_rows = gate_values(normed, router_weight, routing)
    targets = slot_targets(routing, experts, capacity)
    rounded = normed.astype(jnp.bfloat16)
    buffer = (
        jnp.zeros((experts * capacity, D), jnp.bfloat16)
        .at[targets[:, 0]]
        .set(rounded)
        .at[targets[:, 1]]
        .set(rounded)
    )
    arrived = lax.all_to_all(
        buffer.reshape(experts, capacity, D), "expert", split_axis=0, concat_axis=0, tiled=True
    )
    arrived = arrived.reshape(-1, local_experts, capacity, D)

    def compute(arrived_in):
        hidden = jnp.einsum(
            "secd,edf->secf", arrived_in, expert_first, preferred_element_type=jnp.float32
        )
        active_rows = (jax.nn.gelu(hidden[..., :FF]) * hidden[..., FF:]).astype(jnp.bfloat16)
        return jnp.einsum(
            "secf,efd->secd", active_rows, expert_second, preferred_element_type=jnp.float32
        ).astype(jnp.bfloat16)

    def skip_work(arrived_in):
        return jnp.zeros(arrived_in.shape, jnp.bfloat16)

    produced = lax.cond(active, compute, skip_work, arrived)
    returned = lax.all_to_all(
        for_sending(produced.reshape(-1, capacity, D)),
        "expert",
        split_axis=0,
        concat_axis=0,
        tiled=True,
    ).reshape(experts * capacity, D)
    first_rows = returned[targets[:, 0]].astype(jnp.float32)
    second_rows = returned[targets[:, 1]].astype(jnp.float32)
    output = inputs_f + gate_rows[:, 0:1] * first_rows + gate_rows[:, 1:2] * second_rows
    return (output, (normed, gate_rows, targets, arrived, first_rows, second_rows))


def moe_backward(
    grad_out,
    inputs_f,
    gain_vec,
    router_weight,
    routing,
    expert_first,
    expert_second,
    active,
    stored,
):
    normed, gate_rows, targets, arrived, first_rows, second_rows = stored
    experts = router_weight.shape[1]
    capacity = arrived.shape[2]
    local_experts = expert_first.shape[0]
    grad_gates = jnp.stack(
        [jnp.sum(grad_out * first_rows, axis=1), jnp.sum(grad_out * second_rows, axis=1)], axis=1
    )
    grad_first = (gate_rows[:, 0:1] * grad_out).astype(jnp.bfloat16)
    grad_second = (gate_rows[:, 1:2] * grad_out).astype(jnp.bfloat16)
    grad_buffer = (
        jnp.zeros((experts * capacity, D), jnp.bfloat16)
        .at[targets[:, 0]]
        .set(grad_first)
        .at[targets[:, 1]]
        .set(grad_second)
    )
    grad_arrived = lax.all_to_all(
        grad_buffer.reshape(experts, capacity, D), "expert", split_axis=0, concat_axis=0, tiled=True
    )
    grad_arrived = grad_arrived.reshape(-1, local_experts, capacity, D)

    def compute(arrived_in, grad_in):
        hidden = jnp.einsum(
            "secd,edf->secf", arrived_in, expert_first, preferred_element_type=jnp.float32
        )
        active_full, geglu_pull = jax.vjp(
            lambda gate_in, up_in: jax.nn.gelu(gate_in) * up_in, hidden[..., :FF], hidden[..., FF:]
        )
        active_rows = active_full.astype(jnp.bfloat16)
        grad_second_weight = jnp.einsum(
            "secf,secd->efd", active_rows, grad_in, preferred_element_type=jnp.float32
        )
        grad_active = jnp.einsum(
            "secd,efd->secf", grad_in, expert_second, preferred_element_type=jnp.float32
        )
        grad_gate, grad_up = geglu_pull(grad_active)
        grad_hidden = jnp.concatenate([grad_gate, grad_up], axis=-1).astype(jnp.bfloat16)
        grad_first_weight = jnp.einsum(
            "secd,secf->edf", arrived_in, grad_hidden, preferred_element_type=jnp.float32
        )
        grad_rows = jnp.einsum(
            "secf,edf->secd", grad_hidden, expert_first, preferred_element_type=jnp.float32
        ).astype(jnp.bfloat16)
        return (grad_rows, grad_first_weight, grad_second_weight)

    def skip_work(arrived_in, grad_in):
        return (
            jnp.zeros(arrived_in.shape, jnp.bfloat16),
            jnp.zeros(expert_first.shape, jnp.float32),
            jnp.zeros(expert_second.shape, jnp.float32),
        )

    grad_rows, grad_first_weight, grad_second_weight = lax.cond(
        active, compute, skip_work, arrived, grad_arrived
    )
    grad_sent = lax.all_to_all(
        for_sending(grad_rows.reshape(-1, capacity, D)),
        "expert",
        split_axis=0,
        concat_axis=0,
        tiled=True,
    ).reshape(experts * capacity, D)
    grad_normed = grad_sent[targets[:, 0]].astype(jnp.float32) + grad_sent[targets[:, 1]].astype(
        jnp.float32
    )
    unused, gate_pull = jax.vjp(
        lambda normed_in, router_in: gate_values(normed_in, router_in, routing),
        normed,
        router_weight,
    )
    grad_from_gates, grad_router = gate_pull(grad_gates)
    unused, norm_pull = jax.vjp(rms_norm, inputs_f, gain_vec)
    grad_inputs, grad_gain = norm_pull(grad_normed + grad_from_gates)
    return (grad_out + grad_inputs, grad_gain, grad_router, grad_first_weight, grad_second_weight)


def per_device(
    inputs,
    cotangent,
    enc_lengths,
    routes,
    norm_gains,
    rel_bias,
    self_qkv,
    self_out,
    cross_proj,
    cross_value,
    router,
    expert_in,
    expert_out,
):
    decoder = lax.axis_index("half") == 1
    encoder_side = jnp.logical_not(decoder)
    starts = inputs[0].astype(jnp.float32)
    row_count = starts.shape[0]
    gain_rows = norm_gains[0]
    bias_table = rel_bias[0]
    qkv_weight = self_qkv[0]
    out_weight = self_out[0]
    proj_weight = cross_proj[0]
    value_weight = cross_value[0]
    router_weight = router[0]
    expert_first = expert_in[0]
    expert_second = expert_out[0]
    routing = routes[0]
    places = jnp.arange(row_count, dtype=jnp.int32)
    segment = segment_ids(enc_lengths, places)
    item_ids = places // DEC_SLOT
    block_list = block_spans(row_count)

    def self_layout(first_row, block_size):
        query_places = places[first_row : first_row + block_size]
        offset = places[None, :] - query_places[:, None]
        same_item = item_ids[None, :] == item_ids[first_row : first_row + block_size][:, None]
        dec_allowed = same_item & (offset <= 0) & (places[None, :] % DEC_SLOT < DEC_LEN)
        enc_allowed = segment[None, :] == segment[first_row : first_row + block_size][:, None]
        allowed = jnp.where(decoder, dec_allowed, enc_allowed)
        diagonal_offsets = (
            row_count - 1 - first_row - jnp.arange(row_count + block_size - 1, dtype=jnp.int32)
        )
        offset_hits = (
            rel_buckets(diagonal_offsets, decoder)[:, None]
            == jnp.arange(NBKT, dtype=jnp.int32)[None, :]
        ).astype(jnp.float32)
        diagonal_bias = jnp.dot(bias_table, offset_hits.T, precision=HIGHEST)
        bias_part = diagonal_spread(diagonal_bias, block_size, row_count)
        return (allowed, bias_part, offset_hits)

    def cross_layout(first_row, block_size):
        allowed = item_ids[first_row : first_row + block_size][:, None] == segment[None, :]
        return (allowed, None, None)

    first_half, self_stored = self_forward(
        starts, gain_rows[0], qkv_weight, out_weight, self_layout
    )
    encoded, enc_stored = moe_forward(
        first_half, gain_rows[1], router_weight, routing, expert_first, expert_second, encoder_side
    )

    def make_memory(encoded_in):
        return memory_forward(encoded_in, gain_rows[2], proj_weight, value_weight)

    def no_memory(encoded_in):
        return jnp.zeros((2, row_count, D), jnp.bfloat16)

    memory_kv = lax.cond(decoder, no_memory, make_memory, encoded)
    arrived_kv = jax.tree.map(
        lambda part, own: part.astype(own.dtype),
        shifted(for_sending(memory_kv), "half", 1),
        memory_kv,
    )

    def cross_run(decoded_in, memory_in):
        return cross_forward(
            decoded_in, gain_rows[1], proj_weight, value_weight, memory_in, cross_layout
        )

    def cross_skip(decoded_in, memory_in):
        log_sums = [
            jnp.zeros((H, block_size, 1), jnp.float32) for first_row, block_size in block_list
        ]
        return (
            decoded_in,
            (
                jnp.zeros((row_count, D), jnp.bfloat16),
                jnp.zeros((row_count, H, HD), jnp.bfloat16),
                log_sums,
                jnp.zeros((row_count, D), jnp.bfloat16),
            ),
        )

    cross_out, cross_stored = lax.cond(decoder, cross_run, cross_skip, first_half, arrived_kv)
    decoded, dec_stored = moe_forward(
        cross_out, gain_rows[2], router_weight, routing, expert_first, expert_second, decoder
    )
    result = jnp.where(decoder, decoded, encoded)
    grad_result = cotangent[0].astype(jnp.float32)
    zero_rows = jnp.zeros_like(grad_result)
    grad_cross_out, gain_dec_moe, router_dec, first_dec, second_dec = moe_backward(
        jnp.where(decoder, grad_result, zero_rows),
        cross_out,
        gain_rows[2],
        router_weight,
        routing,
        expert_first,
        expert_second,
        decoder,
        dec_stored,
    )

    def cross_back_run(grad_in, decoded_in, memory_in, stored_in):
        return cross_backward(
            grad_in,
            decoded_in,
            gain_rows[1],
            proj_weight,
            value_weight,
            memory_in,
            cross_layout,
            stored_in,
        )

    def cross_back_skip(grad_in, decoded_in, memory_in, stored_in):
        square = jnp.zeros((D, D), jnp.float32)
        return (
            zero_rows,
            jnp.zeros((D,), jnp.float32),
            square,
            square,
            jnp.zeros((2, row_count, D), jnp.bfloat16),
        )

    grad_first_dec, gain_cross, proj_dec, value_dec, grad_memory = lax.cond(
        decoder,
        cross_back_run,
        cross_back_skip,
        grad_cross_out,
        first_half,
        arrived_kv,
        cross_stored,
    )
    memory_grad = jax.tree.map(
        lambda part, own: part.astype(own.dtype),
        shifted(for_sending(grad_memory), "half", -1),
        grad_memory,
    )

    def memory_back_run(grad_in, encoded_in):
        return memory_backward(grad_in, encoded_in, gain_rows[2], proj_weight, value_weight)

    def memory_back_skip(grad_in, encoded_in):
        square = jnp.zeros((D, D), jnp.float32)
        return (zero_rows, jnp.zeros((D,), jnp.float32), square, square)

    grad_extra, gain_final, proj_enc, value_enc = lax.cond(
        decoder, memory_back_skip, memory_back_run, memory_grad, encoded
    )
    grad_encoded = jnp.where(decoder, zero_rows, grad_result + grad_extra)
    grad_first_enc, gain_enc_moe, router_enc, first_enc, second_enc = moe_backward(
        grad_encoded,
        first_half,
        gain_rows[1],
        router_weight,
        routing,
        expert_first,
        expert_second,
        encoder_side,
        enc_stored,
    )
    grad_first = jnp.where(decoder, grad_first_dec, grad_first_enc)
    grad_starts, gain_self, grad_qkv, grad_out, grad_table = self_backward(
        grad_first, starts, gain_rows[0], qkv_weight, out_weight, self_layout, self_stored
    )
    gain_grads = jnp.stack(
        [
            gain_self,
            jnp.where(decoder, gain_cross, gain_enc_moe),
            jnp.where(decoder, gain_dec_moe, gain_final),
        ]
    )
    gain_moved = jnp.transpose(gain_grads)
    grad_router = router_dec + router_enc
    grad_proj = proj_dec + proj_enc
    grad_value = value_dec + value_enc
    grad_first_w = first_dec + first_enc
    grad_second_w = second_dec + second_enc
    summed = (
        lax.psum_scatter(
            gain_moved.astype(jnp.bfloat16), "group", scatter_dimension=0, tiled=True
        ).astype(jnp.float32),
        lax.psum_scatter(
            grad_table.astype(jnp.bfloat16), "group", scatter_dimension=0, tiled=True
        ).astype(jnp.float32),
        lax.psum_scatter(
            grad_qkv.astype(jnp.bfloat16), "group", scatter_dimension=0, tiled=True
        ).astype(jnp.float32),
        lax.psum_scatter(
            grad_out.astype(jnp.bfloat16), "group", scatter_dimension=0, tiled=True
        ).astype(jnp.float32),
        lax.psum_scatter(
            grad_proj.astype(jnp.bfloat16), "group", scatter_dimension=0, tiled=True
        ).astype(jnp.float32),
        lax.psum_scatter(
            grad_value.astype(jnp.bfloat16), "group", scatter_dimension=0, tiled=True
        ).astype(jnp.float32),
        lax.psum_scatter(
            grad_router.astype(jnp.bfloat16), "group", scatter_dimension=0, tiled=True
        ).astype(jnp.float32),
        lax.psum_scatter(
            grad_first_w.astype(jnp.bfloat16), "group", scatter_dimension=2, tiled=True
        ).astype(jnp.float32),
        lax.psum_scatter(
            grad_second_w.astype(jnp.bfloat16), "group", scatter_dimension=1, tiled=True
        ).astype(jnp.float32),
    )
    reduced = (
        lax.psum(summed[0].astype(jnp.bfloat16), "expert").astype(jnp.float32),
        lax.psum(summed[1].astype(jnp.bfloat16), "expert").astype(jnp.float32),
        lax.psum(summed[2].astype(jnp.bfloat16), "expert").astype(jnp.float32),
        lax.psum(summed[3].astype(jnp.bfloat16), "expert").astype(jnp.float32),
        lax.psum(summed[4].astype(jnp.bfloat16), "expert").astype(jnp.float32),
        lax.psum(summed[5].astype(jnp.bfloat16), "expert").astype(jnp.float32),
        lax.psum(summed[6].astype(jnp.bfloat16), "expert").astype(jnp.float32),
    )
    expert_parts = (summed[7], summed[8])
    return (
        result.astype(jnp.bfloat16)[None],
        grad_starts.astype(jnp.bfloat16)[None],
        jnp.transpose(reduced[0])[None],
        reduced[1][None],
        reduced[2][None],
        reduced[3][None],
        reduced[4][None],
        reduced[5][None],
        reduced[6][None],
        expert_parts[0][None],
        expert_parts[1][None],
    )


def solution(mesh):
    in_specs = (
        P("half", ("expert", "group"), None),
        P("half", ("expert", "group"), None),
        P(("expert", "group")),
        P("half", ("expert", "group"), None),
        P("half", None, None),
        P("half", None, None),
        P("half", None, None),
        P("half", None, None),
        P("half", None, None),
        P("half", None, None),
        P("half", None, None),
        P("half", "expert", None, None),
        P("half", "expert", None, None),
    )
    out_specs = (
        P("half", ("expert", "group"), None),
        P("half", ("expert", "group"), None),
        P("half", None, "group"),
        P("half", "group", None),
        P("half", "group", None),
        P("half", "group", None),
        P("half", "group", None),
        P("half", "group", None),
        P("half", "group", None),
        P("half", "expert", None, "group"),
        P("half", "expert", "group", None),
    )
    return jax.shard_map(
        per_device, mesh=mesh, in_specs=in_specs, out_specs=out_specs, check_vma=False
    )
```

profile of v0, /device:TPU:0, one launch (start us, length us, event | category | flops | bytes accessed | tf_op | source)
XLA Modules:
  0.0 2675.9 jit_solution(3982503936334620852)
XLA Ops:
  55.9 42.5 %rev.15 = f32[16,128,640]{2,1,0:T(8,128)} reverse(f32[16,128,640]{2,1,0:T(8,128)} %slice.333), dimensions={2} | reverse | bytes 10485760 | tf_op jit(solution)/shard_map/rev | solution.py:118
  108.5 12.7 broadcast_in_dim.194
  121.2 19.3 copy.222
  140.5 12.5 slice.329
  153.0 70.0 %reshape.1069 = f32[16,512,1153]{2,1,0:T(8,128)} reshape(f32[16,590336]{1,0:T(8,128)} %slice.329) | data formatting | bytes 75563008 | tf_op jit(solution)/shard_map/reshape | solution.py:117
  223.0 16.0 slice.330
  239.0 167.8 %rev.14 = f32[16,512,640]{2,1,0:T(8,128)} reverse(f32[16,512,640]{2,1,0:T(8,128)} %slice.330), dimensions={2} | reverse | bytes 41943040 | tf_op jit(solution)/shard_map/rev | solution.py:118
  407.4 14.5 fusion.412
  444.6 12.1 scatter_custom_fusion
  456.7 13.8 scatter_custom_fusion.1
  476.9 74.5 %all-to-all-done = bf16[8,200,1024]{2,1,0:T(8,128)(2,1)} async-done(((bf16[8,200,1024]{2,1,0:T(8,128)(2,1)}), bf16[8,200,1024]{2,1,0:T(8,128)(2,1)}, u32[]{:S(2)}, u32[]{:S(2)}) %all-to-all-start) | async-done | bytes 3276832 | tf_op jit(solution)/shard_map/all_to_all | solution.py:333
  551.4 48.4 %conditional.8 = (bf16[8,1,200,1024]{3,2,0,1:T(8,128)(2,1)}) conditional(s32[]{:T(128)} %convert_element_type.747, () %tuple.74, (bf16[1,1024,5632]{2,1,0:T(8,128)(2,1)}, bf16[8,1,200,1024]{3,2,0,1:T(8,128)(2,1)}, bf16[1,2816,1024]{2,1,0:T(8,128)(2,1)}) %tuple.219), branch_computations={%region_16.18_spmd, %region_17.19_spmd} | conditional | flops 27729100800 | bytes 95944712 | solution.py:350
  551.4 27.4 %convolution_bitcast_fusion = f32[8,1,200,5632]{3,2,0,1:T(8,128)} fusion(bf16[1,1024,5632]{2,1,0:T(8,128)(2,1)} %get-tuple-element.213, bf16[8,1,200,1024]{3,2,0,1:T(8,128)(2,1)} %get-tuple-element.214), kind=kOutput, calls=%fused_computation.32 | convolution fusion | flops 18454937600 | bytes 50855936 | tf_op jit(solution)/shard_map/cond/branch_1_fun/secd,edf->secf/dot_general | solution.py:339
  578.7 20.6 convert_bitcast_fusion
  618.9 59.8 %all-to-all-done.1 = bf16[8,200,1024]{2,1,0:T(8,128)(2,1)} async-done(((bf16[8,200,1024]{2,1,0:T(8,128)(2,1)}), bf16[8,200,1024]{2,1,0:T(8,128)(2,1)}, u32[]{:S(2)}, u32[]{:S(2)}) %all-to-all-start.1) | async-done | bytes 3276832 | tf_op jit(solution)/shard_map/all_to_all | solution.py:351
  714.2 55.0 %collective-permute-done = bf16[2,640,1024]{1,2,0:T(8,128)(2,1)} collective-permute-done((bf16[2,640,1024]{1,2,0:T(8,128)(2,1)}, bf16[2,640,1024]{1,2,0:T(8,128)(2,1)}, u32[]{:S(2)}, u32[]{:S(2)}) %collective-permute-start) | collective-permute-done | bytes 2621472 | tf_op jit(solution)/shard_map/ppermute | solution.py:34
  769.2 15.9 conditional.10
  787.8 11.9 scatter_custom_fusion.2
  799.7 13.8 scatter_custom_fusion.3
  818.0 74.3 %all-to-all-done.2 = bf16[8,200,1024]{2,1,0:T(8,128)(2,1)} async-done(((bf16[8,200,1024]{2,1,0:T(8,128)(2,1)}), bf16[8,200,1024]{2,1,0:T(8,128)(2,1)}, u32[]{:S(2)}, u32[]{:S(2)}) %all-to-all-start.2) | async-done | bytes 3276832 | tf_op jit(solution)/shard_map/all_to_all | solution.py:333
  932.3 41.8 %all-to-all-done.3 = bf16[8,200,1024]{2,1,0:T(8,128)(2,1)} async-done(((bf16[8,200,1024]{2,1,0:T(8,128)(2,1)}), bf16[8,200,1024]{2,1,0:T(8,128)(2,1)}, u32[]{:S(2)}, u32[]{:S(2)}) %all-to-all-start.3) | async-done | bytes 3276832 | tf_op jit(solution)/shard_map/all_to_all | solution.py:351
  1016.9 74.3 %all-to-all-done.4 = bf16[8,200,1024]{2,1,0:T(8,128)(2,1)} async-done(((bf16[8,200,1024]{2,1,0:T(8,128)(2,1)}), bf16[8,200,1024]{2,1,0:T(8,128)(2,1)}, u32[]{:S(2)}, u32[]{:S(2)}) %all-to-all-start.4) | async-done | bytes 3276832 | tf_op jit(solution)/shard_map/all_to_all | solution.py:391
  1091.3 27.2 %conditional.12 = (bf16[8,1,200,1024]{3,2,0,1:T(8,128)(2,1)}, f32[1,2816,1024]{2,1,0:T(8,128)}, f32[1,1024,5632]{2,1,0:T(8,128)}) conditional(s32[]{:T(128)} %convert_element_type.693, () %tuple.82, (bf16[1,2816,1024]{2,1,0:T(8,128)(2,1)}, bf16[8,200,1024]{2,1,0:T(8,128)(2,1)}, bf16[1,1024,5632]{2,1,0:T(8,128)(2,1)}, ...), branch_computations={%region_38.40_spmd, %region_39.41_spmd} | conditional | flops 74046668800 | bytes 288161824 | solution.py:427
  1131.7 65.7 %all-to-all-done.5 = bf16[8,200,1024]{2,1,0:T(8,128)(2,1)} async-done(((bf16[8,200,1024]{2,1,0:T(8,128)(2,1)}), bf16[8,200,1024]{2,1,0:T(8,128)(2,1)}, u32[]{:S(2)}, u32[]{:S(2)}) %all-to-all-start.5) | async-done | bytes 3276832 | tf_op jit(solution)/shard_map/all_to_all | solution.py:430
  1216.3 15.5 conditional.13
  1237.6 385.2 %collective-permute-done.1 = bf16[2,640,1024]{2,1,0:T(8,128)(2,1)S(1)} collective-permute-done((bf16[2,640,1024]{2,1,0:T(8,128)(2,1)}, bf16[2,640,1024]{2,1,0:T(8,128)(2,1)S(1)}, u32[]{:S(2)}, u32[]{:S(2)}) %collective-permute-start.1) | collective-permute-done | bytes 2621472 | tf_op jit(solution)/shard_map/ppermute | solution.py:34
  1622.8 25.1 conditional.14
  1665.0 13.8 scatter_custom_fusion.7
  1683.3 74.3 %all-to-all-done.6 = bf16[8,200,1024]{2,1,0:T(8,128)(2,1)} async-done(((bf16[8,200,1024]{2,1,0:T(8,128)(2,1)}), bf16[8,200,1024]{2,1,0:T(8,128)(2,1)}, u32[]{:S(2)}, u32[]{:S(2)}) %all-to-all-start.6) | async-done | bytes 3276832 | tf_op jit(solution)/shard_map/all_to_all | solution.py:391
  1757.6 169.2 %conditional.15 = (bf16[8,1,200,1024]{3,2,0,1:T(8,128)(2,1)}, f32[1,2816,1024]{2,1,0:T(8,128)}, f32[1,1024,5632]{2,1,0:T(8,128)}) conditional(s32[]{:T(128)} %convert_element_type.747, () %tuple.87, (bf16[1,2816,1024]{2,1,0:T(8,128)(2,1)}, bf16[8,200,1024]{2,1,0:T(8,128)(2,1)}, bf16[1,1024,5632]{2,1,0:T(8,128)(2,1)}, ...), branch_computations={%region_61.64_spmd, %region_62.65_spmd} | conditional | flops 74046668800 | bytes 288161824 | solution.py:427
  1765.7 27.4 %convolution_bitcast_fusion.6 = f32[8,1,200,5632]{3,2,0,1:T(8,128)} fusion(bf16[1,1024,5632]{2,1,0:T(8,128)(2,1)} %get-tuple-element.263, bf16[8,1,200,1024]{3,2,0,1:T(8,128)(2,1)} %get-tuple-element.264), kind=kOutput, calls=%fused_computation.226 | convolution fusion | flops 18454937600 | bytes 50855936 | tf_op jit(solution)/shard_map/cond/branch_1_fun/secd,edf->secf/dot_general | solution.py:397
  1793.1 24.4 fusion.152
  1817.5 30.4 %fusion.151 = (bf16[8,200,2816]{2,1,0:T(8,128)(2,1)}, bf16[8,200,2816]{2,1,0:T(8,128)(2,1)}) fusion(f32[8,1,200,5632]{3,2,0,1:T(8,128)} %convolution_bitcast_fusion.6, bf16[8,200,1024]{2,1,0:T(8,128)(2,1)} %get-tuple-element.262, bf16[1,2816,1024]{2,1,0:T(8,128)(2,1)} %get-tuple-element.261), kind=kOutput, calls=%fused_computation.234 | convolution fusion | flops 9335603200 | bytes 63111168 | tf_op jit(solution)/shard_map/cond/branch_1_fun/secd,efd->secf/dot_general | solution.py:407
  1847.9 26.0 convert_bitcast_fusion.3
  1873.9 29.1 %convolution_bitcast_fusion.7 = f32[1,1024,5632]{1,2,0:T(8,128)} fusion(bf16[8,200,2816]{2,1,0:T(8,128)(2,1)} %get-tuple-element.613, bf16[8,200,2816]{2,1,0:T(8,128)(2,1)} %get-tuple-element.612, bf16[8,1,200,1024]{3,2,0,1:T(8,128)(2,1)} %get-tuple-element.264), kind=kOutput, calls=%fused_computation.227 | convolution fusion | flops 18490982400 | bytes 44367872 | tf_op jit(solution)/shard_map/cond/branch_1_fun/secd,secf->edf/dot_general | solution.py:412
  1903.0 23.6 copy.220
  1952.2 53.5 %all-to-all-done.7 = bf16[8,200,1024]{2,1,0:T(8,128)(2,1)} async-done(((bf16[8,200,1024]{2,1,0:T(8,128)(2,1)}), bf16[8,200,1024]{2,1,0:T(8,128)(2,1)}, u32[]{:S(2)}, u32[]{:S(2)}) %all-to-all-start.7) | async-done | bytes 3276832 | tf_op jit(solution)/shard_map/all_to_all | solution.py:430
  2038.1 16.3 multiply_reduce_fusion.11
  2054.4 21.9 subtract_multiply_fusion
  2160.6 43.3 %reduce-scatter.11.cloned.1.call-done = bf16[512,3072]{1,0:T(8,128)(2,1)} async-done(((bf16[1024,3072]{1,0:T(8,128)(2,1)}), bf16[512,3072]{1,0:T(8,128)(2,1)}) %reduce-scatter.11.cloned.1.call-update) | async-done | bytes 3145744 | tf_op jit(solution)/shard_map/reduce_scatter | solution.py:648
  2204.3 19.5 add_convert_fusion.1
  2230.5 42.5 %rev.17 = f32[16,128,640]{2,1,0:T(8,128)} reverse(f32[16,128,640]{2,1,0:T(8,128)} %copy-done.12), dimensions={2} | reverse | bytes 10485760 | tf_op jit(solution)/shard_map/rev | solution.py:102
  2272.9 168.0 %rev.16 = f32[16,512,640]{2,1,0:T(8,128)} reverse(f32[16,512,640]{2,1,0:T(8,128)} %subtract_multiply_fusion), dimensions={2} | reverse | bytes 41943040 | tf_op jit(solution)/shard_map/rev | solution.py:102
  2474.0 24.1 copy.225
  2498.1 27.1 %slice.343 = f32[16,589312]{1,0:T(8,128)} slice(f32[16,589824]{1,0:T(8,128)} %bitcast.561), slice={[0:16], [0:589312]} | slice | bytes 75431936 | tf_op jit(solution)/shard_map/slice | solution.py:105
  2525.1 66.7 %reshape.1089 = f32[16,512,1151]{2,1,0:T(8,128)} reshape(f32[16,589312]{1,0:T(8,128)} %slice.343) | data formatting | bytes 75431936 | tf_op jit(solution)/shard_map/reshape | solution.py:107
  2591.9 13.7 reduce_sum.514
  2617.3 27.4 %all-reduce.5 = (bf16[1,3,512]{2,1,0:T(4,128)(2,1)S(1)}, bf16[1,8,32]{2,1,0:T(8,128)(2,1)S(1)}, bf16[1,512,8]{1,2,0:T(8,128)(2,1)S(1)}) all-reduce(bf16[1,3,512]{2,1,0:T(4,128)(2,1)S(1)} %bitcast.651, bf16[1,8,32]{2,1,0:T(8,128)(2,1)S(1)} %dynamic-slice_bitcast_fusion, ...), channel_id=1, replica_groups=mesh['half'=2,'expert'=8,'group'=2] {'expert'}, use_global_device_ids=true, to_apply=%region_77.80 | all-reduce | flops 5888 | bytes 23552 | tf_op jit(solution)/shard_map/psum | solution.py:671
  (590 shorter events, 580.3 us)
Async XLA Ops:
  7.2 433.7 %copy-start = (bf16[1,1024,1024]{2,1,0:T(8,128)(2,1)S(1)}, bf16[1,1024,1024]{2,1,0:T(8,128)(2,1)}, u32[]{:S(2)}) copy-start(bf16[1,1024,1024]{2,1,0:T(8,128)(2,1)} %param.40) | copy-start | bytes 6291460
  8.3 90.1 %copy-start.80 = (s32[640]{0:T(1024)}, s32[640]{0:T(1024)S(1)}, u32[]{:S(2)}) copy-start(s32[640]{0:T(1024)S(1)} %convert_reduce_fusion) | copy-start | bytes 7684
  8.3 90.1 %copy-start.119 = (s32[640]{0:T(1024)}, s32[640]{0:T(1024)S(1)}, u32[]{:S(2)}) copy-start(s32[640]{0:T(1024)S(1)} %add_select_fusion.3) | copy-start | bytes 7684
  8.4 20.4 copy-start.177
  239.0 167.8 %copy-start.81 = (s32[640]{0:T(1024)S(1)}, s32[640]{0:T(1024)}, u32[]{:S(2)}) copy-start(s32[640]{0:T(1024)} %copy-done.80) | copy-start | bytes 7684
  239.0 167.8 %slice-start.2 = ((s32[640]{0:T(1024)}), s32[512]{0:T(512)S(1)}, s32[]{:S(2)}) async-start(s32[640]{0:T(1024)} %copy-done.80), calls=%async_computation.27 | async-start | bytes 4096 | tf_op jit(solution)/shard_map/slice | solution.py:490
  239.0 167.8 %copy-start.120 = (s32[640]{0:T(1024)S(1)}, s32[640]{0:T(1024)}, u32[]{:S(2)}) copy-start(s32[640]{0:T(1024)} %copy-done.119) | copy-start | bytes 7684
  239.0 167.8 %slice-start.3 = ((s32[640]{0:T(1024)}), s32[512]{0:T(512)S(1)}, s32[]{:S(2)}) async-start(s32[640]{0:T(1024)} %copy-done.119), calls=%async_computation.28 | async-start | bytes 4096 | tf_op jit(solution)/shard_map/slice | solution.py:488
  239.0 167.8 %slice-start.4 = ((s32[640]{0:T(1024)}), s32[512]{0:T(512)S(1)}, s32[]{:S(2)}) async-start(s32[640]{0:T(1024)} %copy-done.173), calls=%async_computation.29 | async-start | bytes 4096 | tf_op jit(solution)/shard_map/slice | solution.py:486
  444.6 160.8 %copy-start.88 = (f32[640]{0:T(1024)}, f32[640]{0:T(1024)S(1)}, u32[]{:S(2)}) copy-start(f32[640]{0:T(1024)S(1)} %fusion.388) | copy-start | bytes 7684
  470.6 80.8 %all-to-all-start = ((bf16[8,200,1024]{2,1,0:T(8,128)(2,1)}), bf16[8,200,1024]{2,1,0:T(8,128)(2,1)}, u32[]{:S(2)}, u32[]{:S(2)}) async-start(bf16[8,200,1024]{2,1,0:T(8,128)(2,1)} %bitcast.583), calls=%async_computation | async-start | bytes 6553600 | tf_op jit(solution)/shard_map/all_to_all | solution.py:333
  599.8 79.0 %all-to-all-start.1 = ((bf16[8,200,1024]{2,1,0:T(8,128)(2,1)}), bf16[8,200,1024]{2,1,0:T(8,128)(2,1)}, u32[]{:S(2)}, u32[]{:S(2)}) async-start(bf16[8,200,1024]{2,1,0:T(8,128)(2,1)} %bitcast.584), calls=%async_computation.1 | async-start | bytes 6553600 | tf_op jit(solution)/shard_map/all_to_all | solution.py:351
  604.4 164.8 %copy-start.124 = (f32[1,3,1024]{2,1,0:T(4,128)}, f32[1,3,1024]{2,1,0:T(4,128)S(1)}, u32[]{:S(2)}) copy-start(f32[1,3,1024]{2,1,0:T(4,128)S(1)} %copy.229) | copy-start | bytes 36868
  618.8 66.2 %copy-start.109 = (s32[1024]{0:T(1024)}, s32[1024]{0:T(1024)S(1)}, u32[]{:S(2)}) copy-start(s32[1024]{0:T(1024)S(1)} %get-tuple-element.642) | copy-start | bytes 12292
  618.8 66.2 %copy-start.105 = (s32[1024]{0:T(1024)}, s32[1024]{0:T(1024)S(1)}, u32[]{:S(2)}) copy-start(s32[1024]{0:T(1024)S(1)} %get-tuple-element.643) | copy-start | bytes 12292
  618.9 59.9 %copy-start.125 = (pred[640,2]{0,1:T(4,128)(4,1)}, pred[640,2]{0,1:T(4,128)(4,1)S(1)}, u32[]{:S(2)}) copy-start(pred[640,2]{0,1:T(4,128)(4,1)S(1)} %get-tuple-element.593) | copy-start | bytes 3844
  618.9 73.4 %copy-start.135 = (f32[640]{0:T(1024)}, f32[640]{0:T(1024)S(1)}, u32[]{:S(2)}) copy-start(f32[640]{0:T(1024)S(1)} %get-tuple-element.578) | copy-start | bytes 7684
  618.9 73.4 %copy-start.148 = (f32[640]{0:T(1024)}, f32[640]{0:T(1024)S(1)}, u32[]{:S(2)}) copy-start(f32[640]{0:T(1024)S(1)} %get-tuple-element.577) | copy-start | bytes 7684
  707.1 62.2 %copy-start.82 = (s32[640]{0:T(1024)S(1)}, s32[640]{0:T(1024)}, u32[]{:S(2)}) copy-start(s32[640]{0:T(1024)} %copy-done.80) | copy-start | bytes 7684
  707.1 62.2 %copy-start.121 = (s32[640]{0:T(1024)S(1)}, s32[640]{0:T(1024)}, u32[]{:S(2)}) copy-start(s32[640]{0:T(1024)} %copy-done.119) | copy-start | bytes 7684
  711.4 57.8 %collective-permute-start = (bf16[2,640,1024]{1,2,0:T(8,128)(2,1)}, bf16[2,640,1024]{1,2,0:T(8,128)(2,1)}, u32[]{:S(2)}, u32[]{:S(2)}) collective-permute-start(bf16[2,640,1024]{1,2,0:T(8,128)(2,1)} %copy.188), channel_id=1, source_target_pairs={{0,16},{1,17},{2,18},{3,19},{4,20},{5,21},{6,22},{7,23},{8,24},{9,... | collective-permute-start | bytes 7864328 | tf_op jit(solution)/shard_map/ppermute | solution.py:34
  813.6 78.8 %all-to-all-start.2 = ((bf16[8,200,1024]{2,1,0:T(8,128)(2,1)}), bf16[8,200,1024]{2,1,0:T(8,128)(2,1)}, u32[]{:S(2)}, u32[]{:S(2)}) async-start(bf16[8,200,1024]{2,1,0:T(8,128)(2,1)} %bitcast.587), calls=%async_computation.2 | async-start | bytes 6553600 | tf_op jit(solution)/shard_map/all_to_all | solution.py:333
  894.9 79.1 %all-to-all-start.3 = ((bf16[8,200,1024]{2,1,0:T(8,128)(2,1)}), bf16[8,200,1024]{2,1,0:T(8,128)(2,1)}, u32[]{:S(2)}, u32[]{:S(2)}) async-start(bf16[8,200,1024]{2,1,0:T(8,128)(2,1)} %bitcast.585), calls=%async_computation.3 | async-start | bytes 6553600 | tf_op jit(solution)/shard_map/all_to_all | solution.py:351
  923.4 50.7 %copy-start.110 = (s32[1024]{0:T(1024)S(1)}, s32[1024]{0:T(1024)}, u32[]{:S(2)}) copy-start(s32[1024]{0:T(1024)} %copy-done.109) | copy-start | bytes 12292
  932.3 41.8 %copy-start.144 = (f32[640]{0:T(1024)}, f32[640]{0:T(1024)S(1)}, u32[]{:S(2)}) copy-start(f32[640]{0:T(1024)S(1)} %get-tuple-element.582) | copy-start | bytes 7684
  1012.4 78.8 %all-to-all-start.4 = ((bf16[8,200,1024]{2,1,0:T(8,128)(2,1)}), bf16[8,200,1024]{2,1,0:T(8,128)(2,1)}, u32[]{:S(2)}, u32[]{:S(2)}) async-start(bf16[8,200,1024]{2,1,0:T(8,128)(2,1)} %bitcast.586), calls=%async_computation.4 | async-start | bytes 6553600 | tf_op jit(solution)/shard_map/all_to_all | solution.py:391
  1118.6 78.8 %copy-start.111 = (s32[1024]{0:T(1024)S(1)}, s32[1024]{0:T(1024)}, u32[]{:S(2)}) copy-start(s32[1024]{0:T(1024)} %copy-done.109) | copy-start | bytes 12292
  1118.6 78.8 %all-to-all-start.5 = ((bf16[8,200,1024]{2,1,0:T(8,128)(2,1)}), bf16[8,200,1024]{2,1,0:T(8,128)(2,1)}, u32[]{:S(2)}, u32[]{:S(2)}) async-start(bf16[8,200,1024]{2,1,0:T(8,128)(2,1)} %bitcast.147), calls=%async_computation.5 | async-start | bytes 6553600 | tf_op jit(solution)/shard_map/all_to_all | solution.py:430
  1131.6 78.9 %copy-start.66 = (f32[8,640]{1,0:T(8,128)}, f32[8,640]{1,0:T(8,128)S(1)}, u32[]{:S(2)}) copy-start(f32[8,640]{1,0:T(8,128)S(1)} %reshape.1094) | copy-start | bytes 61444
  1131.7 78.8 %copy-start.137 = (f32[640]{0:T(1024)}, f32[640]{0:T(1024)S(1)}, u32[]{:S(2)}) copy-start(f32[640]{0:T(1024)S(1)} %neg.43) | copy-start | bytes 7684
  1236.3 386.5 %collective-permute-start.1 = (bf16[2,640,1024]{2,1,0:T(8,128)(2,1)}, bf16[2,640,1024]{2,1,0:T(8,128)(2,1)S(1)}, u32[]{:S(2)}, u32[]{:S(2)}) collective-permute-start(bf16[2,640,1024]{2,1,0:T(8,128)(2,1)} %copy.197), channel_id=1, source_target_pairs={{16,0},{17,1},{18,2},{19,3},{20,4},{21,5},{22,6},{23,7},{24,8},{25... | collective-permute-start | bytes 7864328 | tf_op jit(solution)/shard_map/ppermute | solution.py:34
  1622.8 25.1 copy-start.19
  1678.8 78.8 %all-to-all-start.6 = ((bf16[8,200,1024]{2,1,0:T(8,128)(2,1)}), bf16[8,200,1024]{2,1,0:T(8,128)(2,1)}, u32[]{:S(2)}, u32[]{:S(2)}) async-start(bf16[8,200,1024]{2,1,0:T(8,128)(2,1)} %bitcast.588), calls=%async_computation.6 | async-start | bytes 6553600 | tf_op jit(solution)/shard_map/all_to_all | solution.py:391
  1926.8 78.8 %all-to-all-start.7 = ((bf16[8,200,1024]{2,1,0:T(8,128)(2,1)}), bf16[8,200,1024]{2,1,0:T(8,128)(2,1)}, u32[]{:S(2)}, u32[]{:S(2)}) async-start(bf16[8,200,1024]{2,1,0:T(8,128)(2,1)} %bitcast.154), calls=%async_computation.7 | async-start | bytes 6553600 | tf_op jit(solution)/shard_map/all_to_all | solution.py:430
  1931.3 229.3 %reduce-scatter.15.cloned.1.call-start = ((), (), s32[]{:S(2)}) async-start(), calls=%async_computation.18 | async-start | bytes 3145728 | tf_op jit(solution)/shard_map/reduce_scatter | solution.py:654
  1937.0 223.6 %reduce-scatter.17.cloned.1.call-start = ((), (), s32[]{:S(2)}) async-start(), calls=%async_computation.19 | async-start | bytes 3145728 | tf_op jit(solution)/shard_map/reduce_scatter | solution.py:657
  1946.3 72.5 %copy-start.68 = (f32[8,640]{1,0:T(8,128)}, f32[8,640]{1,0:T(8,128)S(1)}, u32[]{:S(2)}) copy-start(f32[8,640]{1,0:T(8,128)S(1)} %reshape.1098) | copy-start | bytes 61444
  1946.3 72.4 %copy-start.139 = (f32[640]{0:T(1024)}, f32[640]{0:T(1024)S(1)}, u32[]{:S(2)}) copy-start(f32[640]{0:T(1024)S(1)} %neg.45) | copy-start | bytes 7684
  1946.3 59.3 %copy-start.112 = (s32[1024]{0:T(1024)S(1)}, s32[1024]{0:T(1024)}, u32[]{:S(2)}) copy-start(s32[1024]{0:T(1024)} %copy-done.109) | copy-start | bytes 12292
  1951.9 208.7 %reduce-scatter.13.cloned.1.call-start = ((), (), s32[]{:S(2)}) async-start(), calls=%async_computation.17 | async-start | bytes 3145728 | tf_op jit(solution)/shard_map/reduce_scatter | solution.py:651
  2087.1 116.8 %reduce-scatter.11.cloned.1.call-start = ((), (), s32[]{:S(2)}) async-start(), calls=%async_computation.16 | async-start | bytes 9437184 | tf_op jit(solution)/shard_map/reduce_scatter | solution.py:648
  2128.4 487.9 %reduce-scatter.25.cloned.1.call-start = ((), (), s32[]{:S(2)}) async-start(), calls=%async_computation.23 | async-start | bytes 393216
  2144.8 472.5 %reduce-scatter.19.cloned.1.call-start = ((), (), s32[]{:S(2)}) async-start(), calls=%async_computation.20 | async-start | bytes 24576 | tf_op jit(solution)/shard_map/reduce_scatter | solution.py:660
  2149.1 497.5 %reduce-scatter.23.cloned.1.call-start = ((), (), s32[]{:S(2)}) async-start(), calls=%async_computation.22 | async-start | bytes 8650752 | tf_op jit(solution)/shard_map/reduce_scatter | solution.py:666
  2160.5 491.1 %all-reduce.9.cloned.1.call-start = ((), (), s32[]{:S(2)}) async-start(), calls=%async_computation.24 | async-start | bytes 12582912 | tf_op jit(solution)/shard_map/psum | solution.py:673
  2203.9 457.3 %reduce-scatter.21.cloned.1.call-start = ((), (), s32[]{:S(2)}) async-start(), calls=%async_computation.21 | async-start | bytes 17301504 | tf_op jit(solution)/shard_map/reduce_scatter | solution.py:663
  2591.8 20.2 copy-start.142
  2591.9 20.2 copy-start.35
  (137 other events, 895.3 us)
Sparse Core Ops, SparseCore 0:
  1937.1 32.2 reduce-scatter.14
  1972.3 31.8 reduce-scatter.16
  2087.2 29.7 reduce-scatter.12
  2128.5 75.3 reduce-scatter.10
  2205.9 11.6 reduce-scatter.24
  2220.3 9.7 reduce-scatter.18
  2233.1 71.4 reduce-scatter.22
  2307.2 137.1 all-reduce.8
  2447.3 133.1 reduce-scatter.20
where the time goes:
time: 2720 us; the launch traced here: 2680 us
  waiting for transfers between devices  1000 us (37%)
  local copies, waits for them, and re-layouts  905 us (33%)
  matrix products  365 us (13%)
  other arithmetic  276 us (10%)
  starting transfers between devices  45.2 us (2%)
  loops' own time  32.4 us (1%)
  blocking collectives  32.3 us (1%)
    ppermute x2, waiting for transfers between devices, shifted(): return lax.ppermute(block, axis, route)  440 us
    rev x2, local copies, waits for them, and re-layouts, diagonal_sums(): flipped = grad_scores[:, :, ::-1]  210 us
    rev x2, local copies, waits for them, and re-layouts, diagonal_spread(): return skewed[:, :, :key_count][:, :, ::-1]  210 us
    all_to_all x2, waiting for transfers between devices, moe_forward(): lax.all_to_all(buffer.reshape(experts, capacity, D), 'expert', split_axis...  149 us
    all_to_all x2, waiting for transfers between devices, moe_backward(): lax.all_to_all(grad_buffer.reshape(experts, capacity, D), 'expert', split...  149 us
    all_to_all x2, waiting for transfers between devices, moe_backward(): lax.all_to_all(for_sending(grad_rows.reshape(-1, capacity, D)), 'expert',...  119 us
    all_to_all x2, waiting for transfers between devices, moe_forward(): lax.all_to_all(for_sending(produced.reshape(-1, capacity, D)), 'expert',...  102 us
    reshape x2, local copies, waits for them, and re-layouts, diagonal_spread(): repeated[:, :block_size * (width + 2)].reshape(heads, block_size, width + 2)  80.2 us
  transfers between devices with their start and end apart: 19, of which 11 were waited for; matrix products, arithmetic and copies ran while one was open for 24% of the time, Pallas kernels for 0%

commit v1 on v0

v1 whole, which is shorter than its diff:
```python
from functools import partial

import jax
import jax.numpy as jnp
import numpy as np
from jax import lax
from jax.experimental import pallas as pl
from jax.experimental.pallas import tpu as pltpu
from jax.sharding import PartitionSpec as P

D = 1024
H = 16
HD = 64
FF = 2816
NBKT = 32
DEC_SLOT = 128
DEC_LEN = 114
ENC_MOST = 512
ENC_MIN = 32
ITEMS = 5

EPSILON = 1e-06
MASKED = -1e30
HIGHEST = lax.Precision.HIGHEST
BLOCK = 128
PAIRS = H // 2
DIAGONAL = ENC_MOST // BLOCK - 1
LINE = 2 * ENC_MOST
FF_TILE = 256
F32 = jnp.float32
BF16 = jnp.bfloat16
GELU_SCALE = float(np.sqrt(2.0 / np.pi))
GELU_CUBE = 0.044715
SWAP = ((0, 1), (1, 0))
VMEM_LIMIT = 60 * 1024 * 1024


def bucket_limits(exact_range, growth, divisions):
    limits = []
    for number in range(1, divisions):
        candidate = exact_range
        while candidate**divisions < exact_range**divisions * growth**number:
            candidate = candidate + 1
        limits.append(candidate)
    return limits


def rel_buckets(offset, causal):
    if causal:
        behind = np.maximum(-offset, 0)
        return np.minimum(behind, 16) + sum(
            (behind >= threshold).astype(np.int32) for threshold in bucket_limits(16, 8, 16)
        )
    distance = np.abs(offset)
    return (
        (offset > 0).astype(np.int32) * 16
        + np.minimum(distance, 8)
        + sum((distance >= threshold).astype(np.int32) for threshold in bucket_limits(8, 16, 8))
    )


def bucket_hits(offset, causal):
    return (rel_buckets(offset, causal)[:, None] == np.arange(NBKT)[None, :]).astype(np.float32)


def inverse_rms(values):
    return lax.rsqrt(jnp.mean(values * values, axis=-1, keepdims=True) + EPSILON)


def rms_norm(values, gain_vec):
    return values * inverse_rms(values) * gain_vec


def rms_back(grad_normed, values, gain_vec):
    scale = inverse_rms(values)
    unit = values * scale
    pulled = grad_normed * gain_vec
    grad_values = scale * (pulled - unit * jnp.mean(pulled * unit, axis=-1, keepdims=True))
    return grad_values, jnp.sum(grad_normed * unit, axis=0)


def dot(a, b):
    return jnp.dot(a, b, preferred_element_type=F32)


def dot_nt(a, b):
    return lax.dot_general(a, b, (((1,), (1,)), ((), ())), preferred_element_type=F32)


def dot_tn(a, b):
    return lax.dot_general(a, b, (((0,), (0,)), ((), ())), preferred_element_type=F32)


def skew(line, rows):
    width = line.shape[1]
    tile = jnp.broadcast_to(line, (8, width))
    row = lax.broadcasted_iota(jnp.int32, (8, width), 0)
    for step in (1, 2, 4):
        tile = jnp.where((row & step) != 0, pltpu.roll(tile, step, 1), tile)
    return jnp.concatenate(
        [pltpu.roll(tile, width - rows + first, 1) for first in range(0, rows, 8)], axis=0
    )


def unskew(total):
    rows, width = total.shape
    summed = None
    for first in range(0, rows, 8):
        moved = pltpu.roll(total[first : first + 8], rows - first, 1)
        summed = moved if summed is None else summed + moved
    row = lax.broadcasted_iota(jnp.int32, (8, width), 0)
    for step in (1, 2, 4):
        summed = jnp.where((row & step) != 0, pltpu.roll(summed, width - step, 1), summed)
    return jnp.sum(summed, axis=0, keepdims=True)


def own_lanes(head):
    return (lax.broadcasted_iota(jnp.int32, (1, 2 * HD), 1) // HD) == head


def head_lanes(head, value):
    return jnp.where(own_lanes(head), value, 0.0).astype(BF16)


def tile_places(keys, queries):
    key = lax.broadcasted_iota(jnp.int32, (keys, queries), 0)
    query = lax.broadcasted_iota(jnp.int32, (keys, queries), 1)
    return key, query


def causal_tile():
    key, query = tile_places(BLOCK, BLOCK)
    return (key <= query) & (key < DEC_LEN)


def short_tile():
    key, query = tile_places(BLOCK, BLOCK)
    return (key // ENC_MIN) == (query // ENC_MIN)


def bias_tiles(rows, queries, shares):
    return [
        (
            slice(block * BLOCK, (block + 1) * BLOCK),
            slice((DIAGONAL - block % (rows // BLOCK // shares)) * BLOCK, None),
            queries,
        )
        for block in range(rows // BLOCK)
    ]


def add_bias(scores, bias_ref, head, shares):
    rows, queries = scores.shape
    return joined(
        [
            scores[here] + bias_ref[head, :, lanes.start : lanes.start + queries]
            for here, lanes, queries in bias_tiles(rows, queries, shares)
        ]
    )


def add_bias_grad(dbias_ref, head, grad_scores, shares):
    rows, queries = grad_scores.shape
    sums = {}
    for here, lanes, queries in bias_tiles(rows, queries, shares):
        part = grad_scores[here]
        sums[lanes.start] = sums[lanes.start] + part if lanes.start in sums else part
    for first, part in sums.items():
        dbias_ref[head, :, first : first + queries] += part


def masked(scores, mask):
    return scores if mask is None else jnp.where(mask, scores, MASKED)


def key_parts(rows, shares):
    step = rows.shape[0] // shares
    return [rows[first : first + step] for first in range(0, rows.shape[0], step)]


def spread_max(values, shares):
    return [jnp.max(part, axis=0, keepdims=True) for part in key_parts(values, shares)]


def joined(parts):
    return parts[0] if len(parts) == 1 else jnp.concatenate(parts, axis=0)


def per_share(lines, rows):
    step = rows // len(lines)
    if len(lines) == 1:
        return lines[0]
    return jnp.concatenate(
        [jnp.broadcast_to(line, (step, line.shape[1])) for line in lines], axis=0
    )


def attend_groups(groups, bias_ref):
    units = [(group, head) for group in groups for head in range(2)]
    scores = []
    for (queries, keys, values, mask), head in units:
        scale = head_lanes(head, HD**-0.5)
        part = joined([dot_nt(key, query * scale) for query, key in zip(queries, keys)])
        scores.append(part)
    contexts = []
    log_sums = []
    for ((queries, keys, values, mask), head), part in zip(units, scores):
        shares = len(queries)
        if bias_ref is not None:
            part = add_bias(part, bias_ref, head, shares)
        part = masked(part, mask)
        highest = spread_max(part, shares)
        exponent = jnp.exp(part - per_share(highest, part.shape[0]))
        totals = [jnp.sum(rows, axis=0, keepdims=True) for rows in key_parts(exponent, shares)]
        log_sums.append([top + jnp.log(total) for top, total in zip(highest, totals)])
        rounded = key_parts(exponent.astype(BF16), shares)
        contexts.append(
            [
                dot_tn(rows, jnp.where(own_lanes(head), value, jnp.ones_like(value)))
                for rows, value in zip(rounded, values)
            ]
        )
    results = []
    for number in range(len(groups)):
        rows = []
        lines = []
        for share in range(len(groups[number][0])):
            first, second = contexts[2 * number][share], contexts[2 * number + 1][share]
            sums = jnp.where(own_lanes(0), second, first)
            context = jnp.where(own_lanes(0), first, second) / pltpu.roll(sums, HD, 1)
            rows.append(context.astype(BF16))
            lines.append(
                jnp.concatenate(
                    [log_sums[2 * number][share], log_sums[2 * number + 1][share]], axis=0
                )
            )
        results.append((rows, lines))
    return results


def attend_groups_back(groups, bias_ref, dbias_ref):
    units = [(group, head) for group in groups for head in range(2)]
    scores = []
    pulls = []
    for (queries, keys, values, mask, grads, lines), head in units:
        scale = head_lanes(head, HD**-0.5)
        own = head_lanes(head, 1.0)
        scores.append(joined([dot_nt(key, query * scale) for query, key in zip(queries, keys)]))
        pulls.append(joined([dot_nt(value, grad * own) for value, grad in zip(values, grads)]))
    totals = []
    for ((queries, keys, values, mask, grads, lines), head), part, pull in zip(units, scores, pulls):
        shares = len(queries)
        scale = head_lanes(head, HD**-0.5)
        own = head_lanes(head, 1.0)
        if bias_ref is not None:
            part = add_bias(part, bias_ref, head, shares)
        part = masked(part, mask)
        weights = jnp.exp(part - per_share([line[head : head + 1] for line in lines], part.shape[0]))
        product = weights * pull
        inner = [jnp.sum(rows, axis=0, keepdims=True) for rows in key_parts(product, shares)]
        grad_scores = product - weights * per_share(inner, part.shape[0])
        if dbias_ref is not None:
            add_bias_grad(dbias_ref, head, grad_scores, shares)
        rounded = key_parts(grad_scores.astype(BF16), shares)
        weights = key_parts(weights.astype(BF16), shares)
        totals.append(
            [
                [dot_tn(rows, key * scale) for rows, key in zip(rounded, keys)],
                [dot(rows, query * scale) for rows, query in zip(rounded, queries)],
                [dot(rows, grad * own) for rows, grad in zip(weights, grads)],
            ]
        )
    results = []
    for number in range(len(groups)):
        results.append(
            [
                [(one + two).astype(BF16) for one, two in zip(first, second)]
                for first, second in zip(totals[2 * number], totals[2 * number + 1])
            ]
        )
    return results


def short_places(place, item):
    later = (item >= place).astype(jnp.int32)
    return pl.multiple_of(item * ENC_MIN + later * ENC_MOST, ENC_MIN), item + later


def gather_short(ref, place):
    return jnp.concatenate(
        [ref[pl.ds(short_places(place, item)[0], ENC_MIN), :] for item in range(ITEMS - 1)], axis=0
    )


def scatter_short(ref, place, rows):
    for item in range(ITEMS - 1):
        ref[pl.ds(short_places(place, item)[0], ENC_MIN), :] = rows[
            item * ENC_MIN : (item + 1) * ENC_MIN
        ]


def block_rows(block):
    return slice(block * BLOCK, (block + 1) * BLOCK)


def self_attend_kernel(place_ref, q_ref, k_ref, v_ref, line_ref, out_ref, lse_ref, bias_ref):
    for head in range(2):
        bias_ref[head] = skew(line_ref[0, head : head + 1, :], BLOCK)
    place = place_ref[0]
    decoder = place_ref[1] == 1

    @pl.when(decoder)
    def _():
        blocks = [block_rows(block) for block in range(ITEMS)]
        shares = tuple([ref[here, :] for here in blocks] for ref in (q_ref, k_ref, v_ref))
        ((rows, lines),) = attend_groups([shares + (joined([causal_tile()] * ITEMS),)], bias_ref)
        for here, part, line in zip(blocks, rows, lines):
            out_ref[here, :] = part
            lse_ref[0, :, here] = line

    @pl.when(jnp.logical_not(decoder))
    def _():
        here = pl.ds(pl.multiple_of(place * ENC_MIN, ENC_MIN), ENC_MOST)
        groups = [
            ([q_ref[here, :]], [k_ref[here, :]], [v_ref[here, :]], None),
            tuple([gather_short(ref, place)] for ref in (q_ref, k_ref, v_ref)) + (short_tile(),),
        ]
        ((rows, lines),) = attend_groups(groups[:1], bias_ref)
        out_ref[here, :] = rows[0]
        lse_ref[0, :, :ENC_MOST] = lines[0]
        ((short_rows, short_lines),) = attend_groups(groups[1:], bias_ref)
        scatter_short(out_ref, place, short_rows[0])
        lse_ref[0, :, ENC_MOST:] = short_lines[0]


def self_attend_back_kernel(
    place_ref, q_ref, k_ref, v_ref, dc_ref, lse_ref, line_ref,
    dq_ref, dk_ref, dv_ref, dline_ref, bias_ref, dbias_ref,
):
    for head in range(2):
        bias_ref[head] = skew(line_ref[0, head : head + 1, :], BLOCK)
    dbias_ref[...] = jnp.zeros(dbias_ref.shape, F32)
    place = place_ref[0]
    decoder = place_ref[1] == 1
    outs = (dq_ref, dk_ref, dv_ref)

    @pl.when(decoder)
    def _():
        blocks = [block_rows(block) for block in range(ITEMS)]
        shares = tuple([ref[here, :] for here in blocks] for ref in (q_ref, k_ref, v_ref))
        shares += (
            joined([causal_tile()] * ITEMS),
            [dc_ref[here, :] for here in blocks],
            [lse_ref[0, :, here] for here in blocks],
        )
        (grads,) = attend_groups_back([shares], bias_ref, dbias_ref)
        for ref, rows in zip(outs, grads):
            for here, part in zip(blocks, rows):
                ref[here, :] = part

    @pl.when(jnp.logical_not(decoder))
    def _():
        here = pl.ds(pl.multiple_of(place * ENC_MIN, ENC_MIN), ENC_MOST)
        groups = [
            (
                [q_ref[here, :]],
                [k_ref[here, :]],
                [v_ref[here, :]],
                None,
                [dc_ref[here, :]],
                [lse_ref[0, :, :ENC_MOST]],
            ),
            (
                [gather_short(q_ref, place)],
                [gather_short(k_ref, place)],
                [gather_short(v_ref, place)],
                short_tile(),
                [gather_short(dc_ref, place)],
                [lse_ref[0, :, ENC_MOST:]],
            ),
        ]
        grads, short_grads = attend_groups_back(groups, bias_ref, dbias_ref)
        for ref, rows, short_rows in zip(outs, grads, short_grads):
            ref[here, :] = rows[0]
            scatter_short(ref, place, short_rows[0])

    for head in range(2):
        dline_ref[0, head : head + 1, :] = unskew(dbias_ref[head])


def cross_places(place):
    long_pair = (
        pl.ds(pl.multiple_of(place * BLOCK, BLOCK), BLOCK),
        pl.ds(pl.multiple_of(place * ENC_MIN, ENC_MIN), ENC_MOST),
    )
    pairs = []
    for item in range(ITEMS - 1):
        start, number = short_places(place, item)
        pairs.append(
            (pl.ds(pl.multiple_of(number * BLOCK, BLOCK), BLOCK), pl.ds(start, ENC_MIN))
        )
    return [[long_pair], pairs]


def cross_attend_kernel(place_ref, q_ref, k_ref, v_ref, out_ref, lse_ref):
    places = cross_places(place_ref[0])
    groups = [
        (
            [q_ref[here, :] for here, there in pairs],
            [k_ref[there, :] for here, there in pairs],
            [v_ref[there, :] for here, there in pairs],
            None,
        )
        for pairs in places
    ]
    number = 0
    for pairs, (rows, lines) in zip(places, attend_groups(groups, None)):
        for (here, there), part, line in zip(pairs, rows, lines):
            out_ref[here, :] = part
            lse_ref[0, :, block_rows(number)] = line
            number += 1


def cross_attend_back_kernel(
    place_ref, q_ref, k_ref, v_ref, dc_ref, lse_ref, dq_ref, dk_ref, dv_ref
):
    places = cross_places(place_ref[0])
    lines = [lse_ref[0, :, block_rows(number)] for number in range(ITEMS)]
    groups = [
        (
            [q_ref[here, :] for here, there in pairs],
            [k_ref[there, :] for here, there in pairs],
            [v_ref[there, :] for here, there in pairs],
            None,
            [dc_ref[here, :] for here, there in pairs],
            part,
        )
        for pairs, part in zip(places, (lines[:1], lines[1:]))
    ]
    for pairs, grads in zip(places, attend_groups_back(groups, None, None)):
        for number, (here, there) in enumerate(pairs):
            dq_ref[here, :] = grads[0][number]
            dk_ref[there, :] = grads[1][number]
            dv_ref[there, :] = grads[2][number]


def pair_spec(rows, first):
    return pl.BlockSpec((rows, 2 * HD), lambda pair, places: (0, first + pair))


def flat_spec(*shape):
    return pl.BlockSpec((1,) + shape, lambda pair, places: (pair, 0, 0))


def pair_call(kernel, places, operands, specs, out_specs, out_shape, scratch, work):
    rows = ITEMS * BLOCK
    return pl.pallas_call(
        kernel,
        grid_spec=pltpu.PrefetchScalarGridSpec(
            num_scalar_prefetch=1,
            grid=(PAIRS,),
            in_specs=specs,
            out_specs=out_specs,
            scratch_shapes=scratch,
        ),
        out_shape=out_shape,
        compiler_params=pltpu.CompilerParams(vmem_limit_bytes=VMEM_LIMIT),
        cost_estimate=pl.CostEstimate(
            flops=work * rows * rows * D, bytes_accessed=16 * rows * D, transcendentals=rows * rows * H
        ),
        name=kernel.__name__,
    )(places, *operands)


def attend(query, keys, values, places, lines):
    rows = query[0].shape[0]
    operands = [part[0] for part in (query, keys, values)]
    specs = [pair_spec(rows, part[1]) for part in (query, keys, values)]
    scratch = []
    if lines is not None:
        operands.append(lines)
        specs.append(flat_spec(2, LINE))
        scratch.append(pltpu.VMEM((2, BLOCK, LINE), F32))
    return pair_call(
        cross_attend_kernel if lines is None else self_attend_kernel,
        places,
        operands,
        specs,
        [pair_spec(rows, 0), flat_spec(2, rows)],
        [
            jax.ShapeDtypeStruct((rows, D), BF16),
            jax.ShapeDtypeStruct((PAIRS, 2, rows), F32),
        ],
        scratch,
        4,
    )


def attend_back(query, keys, values, grad_context, lse, places, lines):
    rows = query[0].shape[0]
    operands = [part[0] for part in (query, keys, values)] + [grad_context, lse]
    specs = [pair_spec(rows, part[1]) for part in (query, keys, values)]
    specs += [pair_spec(rows, 0), flat_spec(2, rows)]
    out_specs = [pair_spec(rows, 0)] * 3
    out_shape = [jax.ShapeDtypeStruct((rows, D), BF16)] * 3
    scratch = []
    if lines is not None:
        operands.append(lines)
        specs.append(flat_spec(2, LINE))
        out_specs.append(flat_spec(2, LINE))
        out_shape.append(jax.ShapeDtypeStruct((PAIRS, 2, LINE), F32))
        scratch += [pltpu.VMEM((2, BLOCK, LINE), F32)] * 2
    return pair_call(
        cross_attend_back_kernel if lines is None else self_attend_back_kernel,
        places,
        operands,
        specs,
        out_specs,
        out_shape,
        scratch,
        10,
    )


def exchange(rows, experts):
    parts = rows.reshape(experts, -1, rows.shape[-1])
    return lax.all_to_all(parts, "expert", split_axis=0, concat_axis=0, tiled=True).reshape(
        rows.shape
    )


def gelu_parts(value):
    square = value * value
    bend = jnp.tanh(value * (GELU_SCALE + GELU_SCALE * GELU_CUBE * square))
    half = 0.5 + 0.5 * bend
    slope = half + value * (half * (1.0 - bend)) * (
        GELU_SCALE + 3.0 * GELU_SCALE * GELU_CUBE * square
    )
    return value * half, slope


def row_blocks(rows):
    step = rows // 2
    return [slice(first, first + step) for first in range(0, rows, step)]


def expert_forward_kernel(x_ref, gate_ref, up_ref, down_ref, out_ref, total_ref):
    @pl.when(pl.program_id(0) == 0)
    def _():
        total_ref[...] = jnp.zeros(total_ref.shape, F32)

    for here in row_blocks(x_ref.shape[0]):
        rows = x_ref[here, :]
        value, _ = gelu_parts(dot(rows, gate_ref[...]))
        active = (value * dot(rows, up_ref[...])).astype(BF16)
        total_ref[here, :] += dot(active, down_ref[...])

    @pl.when(pl.program_id(0) == pl.num_programs(0) - 1)
    def _():
        out_ref[...] = total_ref[...].astype(BF16)


def hidden_grads(rows, grad_rows, gate_ref, up_ref, down_ref):
    gate = dot(rows, gate_ref[...])
    up = dot(rows, up_ref[...])
    grad_active = dot_nt(grad_rows, down_ref[...])
    value, slope = gelu_parts(gate)
    grad_gate = (grad_active * (up * slope)).astype(BF16)
    grad_up = (grad_active * value).astype(BF16)
    return value * up, grad_active, grad_gate, grad_up


def expert_both_kernel(
    x_ref, g_ref, gate_ref, up_ref, down_ref,
    dx_ref, out_ref, line_ref, dx_total, out_total, line_total,
):
    @pl.when(pl.program_id(0) == 0)
    def _():
        dx_total[...] = jnp.zeros(dx_total.shape, F32)
        out_total[...] = jnp.zeros(out_total.shape, F32)
        line_total[...] = jnp.zeros(line_total.shape, F32)

    for here in row_blocks(x_ref.shape[0]):
        active, grad_active, grad_gate, grad_up = hidden_grads(
            x_ref[here, :], g_ref[here, :], gate_ref, up_ref, down_ref
        )
        dx_total[here, :] += dot_nt(grad_gate, gate_ref[...]) + dot_nt(grad_up, up_ref[...])
        out_total[here, :] += dot(active.astype(BF16), down_ref[...])
        product = active * grad_active
        line_total[here, :] += sum(
            product[:, first : first + 128] for first in range(0, product.shape[1], 128)
        )

    @pl.when(pl.program_id(0) == pl.num_programs(0) - 1)
    def _():
        dx_ref[...] = dx_total[...].astype(BF16)
        out_ref[...] = out_total[...].astype(BF16)
        line_ref[...] = jnp.sum(line_total[...], axis=1, keepdims=True)


def expert_back_kernel(flags_ref, *refs, count):
    one_ref, two_ref, three_ref, scale_ref, gate_ref, up_ref, down_ref = refs[:7]
    dx_ref, x_ref, g_ref, active_ref, keep_ref, send_ref, dx_total, sems = refs[-8:]
    decoder = flags_ref[0] == 1
    first_group = flags_ref[1] == 0
    most = x_ref.shape[1]
    spare = slice(count, most)

    def load(rows, grads):
        copies = [
            pltpu.make_async_copy(rows, x_ref.at[0, pl.ds(0, count)], sems.at[0]),
            pltpu.make_async_copy(grads, g_ref.at[0, pl.ds(0, count)], sems.at[1]),
        ]
        for copy in copies:
            copy.start()
        for copy in copies:
            copy.wait()

    @pl.when(pl.program_id(0) == 0)
    def _():
        dx_total[...] = jnp.zeros(dx_total.shape, F32)

        @pl.when(decoder)
        def _():
            load(two_ref, one_ref)

        @pl.when(jnp.logical_not(decoder))
        def _():
            load(one_ref, three_ref)

        grads = g_ref[0, :count, :].astype(F32) * scale_ref[...]
        g_ref[0, :count, :] = grads.astype(BF16)
        if count < most:
            x_ref[0, spare, :] = jnp.zeros((most - count, D), BF16)
            g_ref[0, spare, :] = jnp.zeros((most - count, D), BF16)

    for here in row_blocks(count):
        active, _, grad_gate, grad_up = hidden_grads(
            x_ref[0, here, :], g_ref[0, here, :], gate_ref, up_ref, down_ref
        )
        dx_total[here, :] += dot_nt(grad_gate, gate_ref[...]) + dot_nt(grad_up, up_ref[...])
        active_ref[0, here, :] = active.astype(BF16)
        keep_ref[0, here, :] = jnp.where(first_group, grad_gate, grad_up)
        send_ref[0, here, :] = jnp.where(first_group, grad_up, grad_gate)
    if count < most:
        for ref in (active_ref, keep_ref, send_ref):
            ref[0, spare, :] = jnp.zeros((most - count, FF_TILE), BF16)

    @pl.when(pl.program_id(0) == pl.num_programs(0) - 1)
    def _():
        dx_ref[...] = dx_total[...].astype(BF16)


def expert_specs(rows):
    tiles = FF // FF_TILE
    whole = pl.BlockSpec((rows, D), lambda tile, *_: (0, 0))
    weight_specs = [
        pl.BlockSpec((D, FF_TILE), lambda tile, *_: (0, tile)),
        pl.BlockSpec((D, FF_TILE), lambda tile, *_: (0, tiles + tile)),
        pl.BlockSpec((FF_TILE, D), lambda tile, *_: (tile, 0)),
    ]
    return whole, weight_specs, tiles


def expert_cost(rows, products):
    return pl.CostEstimate(
        flops=2 * products * rows * D * FF, bytes_accessed=6 * D * FF, transcendentals=rows * FF
    )


def expert_forward(arrived, expert_first, expert_second):
    rows = arrived.shape[0]
    whole, weight_specs, tiles = expert_specs(rows)
    return pl.pallas_call(
        expert_forward_kernel,
        grid=(tiles,),
        in_specs=[whole] + weight_specs,
        out_specs=whole,
        out_shape=jax.ShapeDtypeStruct((rows, D), BF16),
        scratch_shapes=[pltpu.VMEM((rows, D), F32)],
        compiler_params=pltpu.CompilerParams(vmem_limit_bytes=VMEM_LIMIT),
        cost_estimate=expert_cost(rows, 3),
        name="expert_forward",
    )(arrived, expert_first, expert_first, expert_second)


def expert_both(arrived, grad_rows, expert_first, expert_second):
    rows = arrived.shape[0]
    whole, weight_specs, tiles = expert_specs(rows)
    row_shape = jax.ShapeDtypeStruct((rows, D), BF16)
    total = pltpu.VMEM((rows, D), F32)
    return pl.pallas_call(
        expert_both_kernel,
        grid=(tiles,),
        in_specs=[whole, whole] + weight_specs,
        out_specs=[whole, whole, pl.BlockSpec((rows, 1), lambda tile: (0, 0))],
        out_shape=[row_shape, row_shape, jax.ShapeDtypeStruct((rows, 1), F32)],
        scratch_shapes=[total, total, pltpu.VMEM((rows, 128), F32)],
        compiler_params=pltpu.CompilerParams(vmem_limit_bytes=VMEM_LIMIT),
        cost_estimate=expert_cost(rows, 6),
        name="expert_both",
    )(arrived, grad_rows, expert_first, expert_first, expert_second)


def expert_back(flags, one, two, three, scale, expert_first, expert_second, kept, number, most):
    rows = one.shape[0]
    whole, weight_specs, tiles = expert_specs(rows)
    part = pl.BlockSpec((1, most, D), lambda tile, *_: (number, 0, 0))
    strip = pl.BlockSpec((1, most, FF_TILE), lambda tile, *_: (number, 0, tile))
    kept_shapes = [jax.ShapeDtypeStruct((2, most, D), BF16)] * 2
    kept_shapes += [jax.ShapeDtypeStruct((2, most, FF), BF16)] * 3
    anywhere = pl.BlockSpec(memory_space=pl.ANY)
    in_specs = [anywhere] * 3 + [pl.BlockSpec((rows, 1), lambda tile, *_: (0, 0))] + weight_specs
    operands = [one, two, three, scale, expert_first, expert_first, expert_second]
    aliases = {}
    if kept is not None:
        aliases = {1 + len(operands) + place: 1 + place for place in range(len(kept))}
        in_specs += [anywhere] * len(kept)
        operands += kept
    dx, *kept = pl.pallas_call(
        partial(expert_back_kernel, count=rows),
        grid_spec=pltpu.PrefetchScalarGridSpec(
            num_scalar_prefetch=1,
            grid=(tiles,),
            in_specs=in_specs,
            out_specs=[whole, part, part, strip, strip, strip],
            scratch_shapes=[pltpu.VMEM((rows, D), F32), pltpu.SemaphoreType.DMA((2,))],
        ),
        out_shape=[jax.ShapeDtypeStruct((rows, D), BF16)] + kept_shapes,
        input_output_aliases=aliases,
        compiler_params=pltpu.CompilerParams(vmem_limit_bytes=VMEM_LIMIT),
        cost_estimate=expert_cost(rows, 5),
        name="expert_back",
    )(flags, *operands)
    return dx, list(kept)


def gate_pair(normed, router_weight, picked_first, picked_second):
    logits = jnp.dot(normed, router_weight, precision=HIGHEST)
    first = jnp.sum(logits * picked_first, axis=1, keepdims=True)
    second = jnp.sum(logits * picked_second, axis=1, keepdims=True)
    return jax.nn.sigmoid(first - second), jax.nn.sigmoid(second - first)


def group_swap(rows, group):
    half = rows.shape[0] // 2
    sent = lax.dynamic_slice_in_dim(rows, (1 - group) * half, half, 0)
    kept = lax.dynamic_slice_in_dim(rows, group * half, half, 0)
    return kept + lax.ppermute(sent, "group", SWAP)


def shard_rows(grad):
    rows, columns = grad.shape
    parts = grad.astype(BF16).reshape(2, lax.axis_size("expert"), -1, columns)
    return jnp.swapaxes(parts, 0, 1).reshape(rows, columns)


def expert_scatter(rows):
    return lax.psum_scatter(rows, "expert", scatter_dimension=0, tiled=True)


def expert_gather(rows):
    return lax.all_gather(rows, "expert", axis=0, tiled=True)


def together(*values):
    return lax.optimization_barrier(values)


def per_device(
    inputs,
    cotangent,
    enc_lengths,
    routes,
    norm_gains,
    rel_bias,
    self_qkv,
    self_out,
    cross_proj,
    cross_value,
    router,
    expert_in,
    expert_out,
):
    decoder = lax.axis_index("half") == 1
    group = lax.axis_index("group")
    start_rows = inputs[0].astype(F32)
    row_count = start_rows.shape[0]
    gain_rows = norm_gains[0]
    bias_table = rel_bias[0]
    qkv_weight = self_qkv[0]
    out_weight = self_out[0]
    proj_weight = cross_proj[0]
    value_weight = cross_value[0]
    router_weight = router[0]
    expert_first = expert_in[0, 0]
    expert_second = expert_out[0, 0]
    routing = routes[0]
    experts = router_weight.shape[1]
    cot = cotangent[0]
    cot_f = cot.astype(F32)

    forward = [(0, 1)]
    backward = [(1, 0)]
    half_rows = D // 2
    both_weights = jnp.concatenate([proj_weight, value_weight])
    pieces = [both_weights[first:last] for first, last in ((0, 384), (384, 960), (960, 1536), (1536, 2048))]

    long_place = jnp.sum(jnp.arange(ITEMS) * (enc_lengths == ENC_MOST)).astype(jnp.int32)
    places = jnp.stack([long_place, decoder.astype(jnp.int32)])
    offsets = ENC_MOST - np.arange(LINE)
    hits = jnp.where(decoder, bucket_hits(offsets, True), bucket_hits(offsets, False))
    lines = jnp.dot(bias_table, hits.T, precision=HIGHEST).reshape(PAIRS, 2, LINE)

    capacity = 5 * row_count // (2 * experts)
    padded = -(-capacity // 8) * 8
    first_chunk = padded // 16 * 8
    chunk_sizes = (first_chunk, padded - first_chunk)
    picked = [
        (routing[:, k : k + 1] == jnp.arange(experts, dtype=jnp.int32)[None, :]).astype(F32)
        for k in range(2)
    ]
    before = jnp.asarray(np.tril(np.ones((row_count, row_count)), -1), BF16)
    counts = dot(before, jnp.concatenate(picked, axis=1).astype(BF16))
    totals = jnp.sum(picked[0], axis=0, keepdims=True)
    slot_first = jnp.sum(picked[0] * counts[:, :experts], axis=1)
    slot_second = jnp.sum(picked[1] * (counts[:, experts:] + totals), axis=1)
    code_first = routing[:, 0] * padded + slot_first.astype(jnp.int32)
    code_second = routing[:, 1] * padded + slot_second.astype(jnp.int32)
    chunk_codes = []
    offset = 0
    for size in chunk_sizes:
        chunk_codes.append(
            (np.arange(experts)[:, None] * padded + offset + np.arange(size)[None, :])
            .reshape(-1)
            .astype(np.int32)
        )
        offset += size

    def spread(first_values, second_values):
        buffers = []
        for codes in chunk_codes:
            hit_first = (codes[:, None] == code_first[None, :]).astype(BF16)
            hit_second = (codes[:, None] == code_second[None, :]).astype(BF16)
            if first_values is second_values:
                buffers.append(dot(hit_first + hit_second, first_values).astype(BF16))
            else:
                buffers.append(
                    (dot(hit_first, first_values) + dot(hit_second, second_values)).astype(BF16)
                )
        return buffers

    def collect(buffers, code):
        total = None
        for codes, buffer in zip(chunk_codes, buffers):
            part = dot((code[:, None] == codes[None, :]).astype(BF16), buffer)
            total = part if total is None else total + part
        return total

    normed_in = rms_norm(start_rows, gain_rows[0]).astype(BF16)
    project = dot(normed_in, qkv_weight).astype(BF16)
    project, pieces[0] = together(project, pieces[0])
    query, keys, values = (project, 0), (project, PAIRS), (project, 2 * PAIRS)
    context, lse = attend(query, keys, values, places, lines)
    context, pieces[0] = together(context, lax.ppermute(pieces[0], "half", forward))
    first_half = start_rows + dot(context, out_weight)
    normed_half = rms_norm(first_half, gain_rows[1])
    rounded_half = normed_half.astype(BF16)

    first_rows = jnp.where(decoder, cot, rounded_half)
    sent = spread(first_rows, first_rows)
    arrived_one = [exchange(part, experts) for part in sent]
    returned_one = []
    for k in range(2):
        part, piece = together(arrived_one[k], pieces[1 + k])
        part = expert_forward(part, expert_first, expert_second)
        part, pieces[1 + k] = together(part, lax.ppermute(piece, "half", forward))
        if k == 1:
            part, pieces[3] = together(part, pieces[3])
        returned_one.append(exchange(part, experts))
    returned_one[1], pieces[3] = together(
        returned_one[1], lax.ppermute(pieces[3], "half", forward)
    )
    both_weights = jnp.concatenate(pieces)
    memory_proj, memory_value = both_weights[:D], both_weights[D:]
    enc_gates = gate_pair(normed_half, router_weight, *picked)
    enc_first = collect(returned_one, code_first)
    enc_second = collect(returned_one, code_second)
    encoded = first_half + enc_gates[0] * enc_first + enc_gates[1] * enc_second
    memory = rms_norm(encoded, gain_rows[2]).astype(BF16)
    memory_in = lax.ppermute(memory, "half", forward)

    cross_query = dot(rounded_half, proj_weight).astype(BF16)
    memory_keys = dot(memory_in, memory_proj).astype(BF16)
    memory_values = dot(memory_in, memory_value).astype(BF16)
    cross_context, cross_lse = attend(
        (cross_query, 0), (memory_keys, 0), (memory_values, 0), places, None
    )
    second_half = first_half + dot(cross_context, value_weight)
    normed_second = rms_norm(second_half, gain_rows[2])
    dec_gates = gate_pair(normed_second, router_weight, *picked)

    rounded_second = normed_second.astype(BF16)
    arrived_two = [exchange(part, experts) for part in spread(rounded_second, rounded_second)]
    all_codes = np.concatenate(chunk_codes)
    gate_rows = jnp.sum(
        jnp.where(all_codes[:, None] == code_first[None, :], dec_gates[0][:, 0][None, :], 0.0)
        + jnp.where(all_codes[:, None] == code_second[None, :], dec_gates[1][:, 0][None, :], 0.0),
        axis=1,
    )
    edge = experts * chunk_sizes[0]

    def exchange_line(line):
        parts = jnp.concatenate(
            [line[:edge].reshape(experts, -1), line[edge:].reshape(experts, -1)], axis=1
        )
        moved = lax.all_to_all(parts, "expert", split_axis=0, concat_axis=0, tiled=True)
        return jnp.concatenate(
            [moved[:, : chunk_sizes[0]].reshape(-1), moved[:, chunk_sizes[0] :].reshape(-1)]
        )

    produced_two = []
    returned_two = []
    gate_grads = []
    for part, grad_part in zip(arrived_two, arrived_one):
        grad_arrived, produced, line = expert_both(part, grad_part, expert_first, expert_second)
        gate_grads.append(line[:, 0])
        produced_two.append(produced)
        returned_two.append(exchange(grad_arrived, experts))
    returned_two[0], line_grads = together(returned_two[0], jnp.concatenate(gate_grads))
    line_grads = exchange_line(line_grads)

    def collect_line(line, code):
        return jnp.sum(
            jnp.where(code[:, None] == all_codes[None, :], line[None, :], 0.0), axis=1, keepdims=True
        )

    def router_back(gates, grad_first, grad_second):
        pulled = gates[0] * gates[1] * (grad_first - grad_second)
        grad_logits = pulled * (picked[0] - picked[1])
        return grad_logits, jnp.dot(grad_logits, router_weight.T, precision=HIGHEST)

    dec_logits, dec_normed = router_back(
        dec_gates, collect_line(line_grads, code_first), collect_line(line_grads, code_second)
    )
    dec_normed = (
        dec_normed
        + dec_gates[0] * collect(returned_two, code_first)
        + dec_gates[1] * collect(returned_two, code_second)
    )
    pulled_rows, gain_dec_moe = rms_back(dec_normed, second_half, gain_rows[2])
    grad_second_half = cot_f + pulled_rows

    rounded_grad = grad_second_half.astype(BF16)
    grad_cross_context = dot_nt(rounded_grad, value_weight).astype(BF16)
    grad_cross_query, grad_memory_keys, grad_memory_values = attend_back(
        (cross_query, 0),
        (memory_keys, 0),
        (memory_values, 0),
        grad_cross_context,
        cross_lse,
        places,
        None,
    )
    key_part = dot_nt(grad_memory_keys, memory_proj)
    value_part, key_part = together(dot_nt(grad_memory_values, memory_value), key_part)
    grad_memory, gate_rows = together((key_part + value_part).astype(BF16), gate_rows)
    arrived_gates = exchange_line(gate_rows)
    grad_memory, grad_memory_keys, grad_memory_values, arrived_gates = together(
        lax.ppermute(grad_memory, "half", backward),
        grad_memory_keys,
        grad_memory_values,
        arrived_gates,
    )
    back_keys = lax.ppermute(grad_memory_keys, "half", backward)
    back_values = lax.ppermute(grad_memory_values, "half", backward)
    grad_memory = grad_memory.astype(F32)
    pulled_rows, gain_cross = rms_back(
        dot_nt(grad_cross_query, proj_weight), first_half, gain_rows[1]
    )
    grad_first_dec = grad_second_half + pulled_rows

    pulled_rows, gain_memory = rms_back(grad_memory, encoded, gain_rows[2])
    grad_encoded = cot_f + pulled_rows
    grad_gate_first = jnp.sum(grad_encoded * enc_first, axis=1, keepdims=True)
    grad_gate_second = jnp.sum(grad_encoded * enc_second, axis=1, keepdims=True)
    sent = spread(
        (enc_gates[0] * grad_encoded).astype(BF16), (enc_gates[1] * grad_encoded).astype(BF16)
    )
    arrived_three = [
        exchange(jnp.where(decoder, produced, part), experts)
        for produced, part in zip(produced_two, sent)
    ]
    flags = jnp.stack([decoder.astype(jnp.int32), group])
    scales = jnp.where(decoder, arrived_gates, 1.0)[:, None]
    most = max(part.shape[0] for part in arrived_one)
    kept = None
    returned_three = []
    for k, scale in enumerate((scales[:edge], scales[edge:])):
        grad_arrived, kept = expert_back(
            flags,
            arrived_one[k],
            arrived_two[k],
            arrived_three[k],
            scale,
            expert_first,
            expert_second,
            kept,
            k,
            most,
        )
        if k == 0:
            grad_arrived, back_keys, back_values = together(grad_arrived, back_keys, back_values)
            grad_value = dot_tn(
                jnp.where(decoder, cross_context, memory),
                jnp.where(decoder, rounded_grad, back_values),
            )
            grad_proj = dot_tn(
                jnp.where(decoder, rounded_half, memory),
                jnp.where(decoder, grad_cross_query, back_keys),
            )
            early = group_swap(jnp.concatenate([grad_proj, grad_value], axis=1).astype(BF16), group)
            normed_sharded = jnp.swapaxes(
                normed_in.reshape(row_count, 2, lax.axis_size("expert"), -1), 1, 2
            ).reshape(row_count, D)
        else:
            grad_arrived, early, normed_sharded, kept, returned_three[0], arrived_three = together(
                grad_arrived, early, normed_sharded, kept, returned_three[0], arrived_three
            )
        returned_three.append(exchange(grad_arrived, experts))

    decoded = (
        second_half
        + dec_gates[0] * collect(arrived_three, code_first)
        + dec_gates[1] * collect(arrived_three, code_second)
    )
    result = jnp.where(decoder, decoded, encoded)

    expert_rows, expert_grad_rows, actives, keep_halves, send_halves = [
        part.reshape(2 * most, -1) for part in kept
    ]
    first_group = group == 0
    half_ff = FF // 2
    send_in = dot_tn(expert_rows, send_halves).astype(BF16)
    in_cuts = (0, 208, 496, 656, 816, D)
    out_cut = 320
    sends = [(send_in[first:last],) for first, last in zip(in_cuts[:-1], in_cuts[1:])]

    def swapped(parts):
        return [lax.ppermute(part, "group", SWAP) for part in parts]

    gots = [swapped(sends[0])]
    returned_three[1], sends, gots, early, result = together(
        returned_three[1], sends, gots, early, result.astype(BF16)
    )
    early = expert_scatter(early)

    enc_logits, enc_normed = router_back(enc_gates, grad_gate_first, grad_gate_second)
    enc_normed = enc_normed + collect(returned_three, code_first) + collect(returned_three, code_second)
    pulled_rows, gain_enc_moe = rms_back(enc_normed, first_half, gain_rows[1])
    grad_first = jnp.where(decoder, grad_first_dec, grad_encoded + pulled_rows)

    rounded_grad = grad_first.astype(BF16)
    grad_context = dot_nt(rounded_grad, out_weight).astype(BF16)
    middle = expert_scatter(shard_rows(dot_tn(context, rounded_grad)))
    grad_context, early, sends[1] = together(grad_context, early, sends[1])
    gots.append(swapped(sends[1]))
    early = expert_gather(early)
    grad_query, grad_keys, grad_values, grad_lines = attend_back(
        query, keys, values, grad_context, lse, places, lines
    )
    (grad_query, grad_keys, grad_values), gots, sends[2], middle, early, kept = together(
        (grad_query, grad_keys, grad_values),
        gots,
        sends[2],
        middle,
        early,
        (actives, expert_grad_rows),
    )
    late_first = dot_tn(normed_sharded, jnp.concatenate([grad_keys, grad_values], axis=1))
    late_first, (grad_query, grad_keys, grad_values), sends[2], kept = together(
        late_first.astype(BF16), (grad_query, grad_keys, grad_values), sends[2], kept
    )
    late_first = expert_scatter(late_first)
    actives, expert_grad_rows = kept
    send_out = dot_tn(
        jnp.where(first_group, actives[:, half_ff:], actives[:, :half_ff]), expert_grad_rows
    ).astype(BF16)
    gots.append(swapped(sends[2]))

    grad_table = jnp.dot(grad_lines.reshape(H, LINE), hits, precision=HIGHEST)
    grad_router = lax.dot_general(
        jnp.where(decoder, normed_second, normed_half),
        jnp.where(decoder, dec_logits, enc_logits),
        (((0,), (0,)), ((), ())),
        precision=HIGHEST,
    )
    grad_normed = dot_nt(jnp.concatenate([grad_query, grad_keys, grad_values], axis=1), qkv_weight)
    grad_normed, gots, sends[3] = together(grad_normed, gots, sends[3])
    gots.append(swapped(sends[3]))
    pulled_rows, gain_self = rms_back(grad_normed, start_rows, gain_rows[0])
    grad_starts = grad_first + pulled_rows
    gain_grads = jnp.stack(
        [
            gain_self,
            jnp.where(decoder, gain_cross, gain_enc_moe),
            jnp.where(decoder, gain_dec_moe, gain_memory),
        ]
    )
    table_rows = jnp.pad(grad_table.reshape(2, -1), ((0, 0), (0, (D - H * NBKT) // 2)))
    small = jnp.concatenate([grad_router, gain_grads.T, table_rows.reshape(D, 1)], axis=1)
    small = jnp.pad(small, ((0, 0), (0, 128 - small.shape[1])))
    late_second = jnp.concatenate(
        [dot_tn(normed_sharded, grad_query).astype(BF16), shard_rows(small)], axis=1
    )
    keep_in = dot_tn(expert_rows, keep_halves)
    late_second, late_first, gots, sends[4], keep_in = together(
        late_second, late_first, gots, sends[4] + (send_out[:out_cut],), keep_in
    )
    gots.append(swapped(sends[4]))
    late_second = expert_scatter(late_second)
    keep_out = dot_tn(
        jnp.where(first_group, actives[:, :half_ff], actives[:, half_ff:]), expert_grad_rows
    )
    late_first, late_second, keep_out, gots, send_out = together(
        late_first, late_second, keep_out, gots, send_out
    )
    late = group_swap(jnp.concatenate([late_first, late_second, middle], axis=1), group)
    late, send_out = together(late, send_out)
    late = expert_gather(late)
    gots.append(swapped([send_out[out_cut:]]))
    grad_expert_in = keep_in + jnp.concatenate([part[0] for part in gots[:5]]).astype(F32)
    grad_expert_out = keep_out + jnp.concatenate([gots[4][1], gots[5][0]]).astype(F32)
    grad_qkv = jnp.concatenate([late[:, 2 * D : 3 * D], late[:, : 2 * D]], axis=1).astype(F32)
    small = late[:, 3 * D : 3 * D + 128].astype(F32)
    small_table = small[: H * NBKT // 2, experts + 3].reshape(H // 2, NBKT)
    return (
        result[None],
        grad_starts.astype(BF16)[None],
        small[:, experts : experts + 3].T[None],
        small_table[None],
        grad_qkv[None],
        late[:, 3 * D + 128 :].astype(F32)[None],
        early[:, :D].astype(F32)[None],
        early[:, D:].astype(F32)[None],
        small[:, :experts][None],
        grad_expert_in[None, None],
        grad_expert_out[None, None],
    )


def solution(mesh):
    in_specs = (
        P("half", ("expert", "group"), None),
        P("half", ("expert", "group"), None),
        P(("expert", "group")),
        P("half", ("expert", "group"), None),
        P("half", None, None),
        P("half", None, None),
        P("half", None, None),
        P("half", None, None),
        P("half", None, None),
        P("half", None, None),
        P("half", None, None),
        P("half", "expert", None, None),
        P("half", "expert", None, None),
    )
    out_specs = (
        P("half", ("expert", "group"), None),
        P("half", ("expert", "group"), None),
        P("half", None, "group"),
        P("half", "group", None),
        P("half", "group", None),
        P("half", "group", None),
        P("half", "group", None),
        P("half", "group", None),
        P("half", "group", None),
        P("half", "expert", None, "group"),
        P("half", "expert", "group", None),
    )
    return jax.shard_map(
        per_device, mesh=mesh, in_specs=in_specs, out_specs=out_specs, check_vma=False
    )
```

time: 2720 us -> 1110 us (0.41); the launches traced: 2680 us -> 1100 us
  local copies, waits for them, and re-layouts: 905 us -> 54.7 us
  waiting for transfers between devices: 1000 us -> 348 us
  Pallas kernels: 0 us -> 282 us
  other arithmetic: 276 us -> 69.8 us
  matrix products: 365 us -> 225 us
  starting transfers between devices: 45.2 us -> 87.7 us
  loops' own time: 32.4 us -> 0 us
    rev x4 -> x0, local copies, waits for them, and re-layouts: 421 us -> none  [the longest x2 210 us: diagonal_sums(): flipped = grad_scores[:, :, ::-1]]
    all_to_all x8 -> x12, waiting for transfers between devices: 518 us -> 147 us  [exchange(): lax.all_to_all(parts, 'expert', split_axis=0, concat_axis=0, tiled=True)]
    pallas_call x0 -> x10, Pallas kernels: none -> 282 us  [the longest x2 85 us: expert_both(): pl.pallas_call(expert_both_kernel, grid=(tiles,), in_specs=[whole, whole]...]
    ppermute x2 -> x17, waiting for transfers between devices: 440 us -> 161 us  [the longest x7 81.9 us: swapped(): return [lax.ppermute(part, 'group', SWAP) for part in parts]]
    reshape x6 -> x11, local copies, waits for them, and re-layouts: 157 us -> 1.37 us  [the longest x1 0.66 us: per_device(): jnp.dot(bias_table, hits.T, precision=HIGHEST).reshape(PAIRS, 2, LINE)]
    dot_general x41 -> x53, matrix products: 365 us -> 225 us  [the longest x31 110 us: dot(): return jnp.dot(a, b, preferred_element_type=F32)]
    scatter x8 -> x0, other arithmetic: 97.5 us -> none  [the longest x4 51.7 us: moe_forward(): buffer = jnp.zeros((experts * capacity, D), jnp.bfloat16).at[targets[:, 0...]
    gather x24 -> x0, local copies, waits for them, and re-layouts: 85.9 us -> none  [the longest x16 32.6 us: gate_values(): picked = jnp.take_along_axis(probabilities, routing, axis=1)]
  transfers between devices with their start and end apart: 19 -> 35, of which waited for: 11 -> 22; matrix products, arithmetic and copies ran while one was open for 24% -> 21% of each run, Pallas kernels for 0% -> 24%
where the time goes in v1:
time: 1110 us; the launch traced here: 1100 us
  waiting for transfers between devices  348 us (31%)
  Pallas kernels  282 us (25%)
  matrix products  225 us (20%)
  starting transfers between devices  87.7 us (8%)
  other arithmetic  69.8 us (6%)
  local copies, waits for them, and re-layouts  54.7 us (5%)
  blocking collectives  18.5 us (2%)
  between operations  15.8 us (1%)
    all_to_all x12, waiting for transfers between devices, exchange(): lax.all_to_all(parts, 'expert', split_axis=0, concat_axis=0, tiled=True)  147 us
    dot_general x31, matrix products, dot(): return jnp.dot(a, b, preferred_element_type=F32)  110 us
    pallas_call x2, Pallas kernels, expert_both(): pl.pallas_call(expert_both_kernel, grid=(tiles,), in_specs=[whole, whole]...  85 us
    ppermute x7, waiting for transfers between devices, swapped(): return [lax.ppermute(part, 'group', SWAP) for part in parts]  81.9 us
    pallas_call x2, Pallas kernels, expert_back(): pl.pallas_call(partial(expert_back_kernel, count=rows), grid_spec=pltpu.P...  80.6 us
    dot_general x9, matrix products, dot_tn(): lax.dot_general(a, b, (((0,), (0,)), ((), ())), preferred_element_type=F32)  74.6 us
    pallas_call x4, Pallas kernels, pair_call(): pl.pallas_call(kernel, grid_spec=pltpu.PrefetchScalarGridSpec(num_scalar_...  73.3 us
    all_to_all x12, starting transfers between devices, exchange(): lax.all_to_all(parts, 'expert', split_axis=0, concat_axis=0, tiled=True)  54.8 us
  transfers between devices with their start and end apart: 35, of which 22 were waited for; matrix products, arithmetic and copies ran while one was open for 21% of the time, Pallas kernels for 24%

profile of v1, /device:TPU:0, one launch (start us, length us, event | category | flops | bytes accessed | tf_op | source)
XLA Modules:
  0.0 1101.8 jit_solution(10136426012674367902)
XLA Ops:
  12.4 8.7 fusion.4.q_ref.k_ref.v_ref
  21.1 5.7 collective-permute-start
  31.3 18.3 %self_attend_kernel.1 = (bf16[640,1024]{1,0:T(8,128)(2,1)}, f32[8,2,640]{2,1,0:T(2,128)}) custom-call(s32[2]{0:T(128)} %pad_add_fusion.1.place_ref, bf16[640,3072]{1,0:T(8,128)(2,1)} %fusion.4.q_ref.k_ref.v_ref, bf16[640,3072]{1,0:T(8,128)(2,1)} %fusion.4.q_ref.k_ref.v_ref, bf16[640,3072]{1,0:T(8,128)(2,1)} %fusion.4.q_ref.k_ref.v_ref, ...), custom_call_target="tpu_custom_call" | custom-call | flops 1677721600 | bytes 10485760 | tf_op jit(solution)/shard_map/self_attend_kernel/pallas_call | solution.py:457
  60.0 5.2 all-to-all-start.1
  69.3 33.9 %all-to-all-done.1 = bf16[8,96,1024]{2,1,0:T(8,128)(2,1)} async-done(((bf16[8,96,1024]{2,1,0:T(8,128)(2,1)}), bf16[8,96,1024]{2,1,0:T(8,128)(2,1)}, u32[]{:S(2)}, u32[]{:S(2)}) %all-to-all-start.1) | async-done | bytes 1572896 | tf_op jit(solution)/shard_map/all_to_all | solution.py:527
  112.6 21.4 %expert_forward.2 = bf16[768,1024]{1,0:T(8,128)(2,1)} custom-call(bf16[768,1024]{1,0:T(8,128)(2,1)} %bitcast.19.x_ref.g_ref.refs_0_, bf16[1024,5632]{1,0:T(8,128)(2,1)} %bitcast.269, bf16[1024,5632]{1,0:T(8,128)(2,1)} %bitcast.270, bf16[2816,1024]{1,0:T(8,128)(2,1)} %bitcast.283), custom_call_target="tpu_custom_call" | custom-call | flops 13287555072 | bytes 17301504 | tf_op jit(solution)/shard_map/expert_forward/pallas_call | solution.py:674
  137.5 10.6 all-to-all-done
  158.3 22.0 %expert_forward.3 = bf16[832,1024]{1,0:T(8,128)(2,1)} custom-call(bf16[832,1024]{1,0:T(8,128)(2,1)} %bitcast.15.x_ref.g_ref.refs_0_, bf16[1024,5632]{1,0:T(8,128)(2,1)} %bitcast.271, bf16[1024,5632]{1,0:T(8,128)(2,1)} %bitcast.272, bf16[2816,1024]{1,0:T(8,128)(2,1)} %bitcast.284), custom_call_target="tpu_custom_call" | custom-call | flops 14394851328 | bytes 17301504 | tf_op jit(solution)/shard_map/expert_forward/pallas_call | solution.py:674
  183.6 6.6 all-to-all-done.2
  205.2 14.2 %collective-permute-done.3 = bf16[512,1024]{1,0:T(8,128)(2,1)} collective-permute-done((bf16[512,1024]{1,0:T(8,128)(2,1)}, bf16[512,1024]{1,0:T(8,128)(2,1)}, u32[]{:S(2)}, u32[]{:S(2)}) %collective-permute-start.3) | collective-permute-done | bytes 1048608 | tf_op jit(solution)/shard_map/ppermute | solution.py:882
  219.4 15.8 %all-to-all-done.3 = bf16[8,104,1024]{2,1,0:T(8,128)(2,1)} async-done(((bf16[8,104,1024]{2,1,0:T(8,128)(2,1)}), bf16[8,104,1024]{2,1,0:T(8,128)(2,1)}, u32[]{:S(2)}, u32[]{:S(2)}) %all-to-all-start.3) | async-done | bytes 1703968 | tf_op jit(solution)/shard_map/all_to_all | solution.py:527
  239.2 5.7 multiply_reduce_fusion.9
  250.9 24.0 %collective-permute-done.4 = bf16[640,1024]{1,0:T(8,128)(2,1)S(1)} collective-permute-done((bf16[640,1024]{1,0:T(8,128)(2,1)S(1)}, bf16[640,1024]{1,0:T(8,128)(2,1)S(1)}, u32[]{:S(2)}, u32[]{:S(2)}) %collective-permute-start.4) | collective-permute-done | bytes 1310752 | tf_op jit(solution)/shard_map/ppermute | solution.py:891
  283.3 9.8 cross_attend_kernel.1
  304.5 4.5 convolution_convert_fusion.5
  309.0 33.3 %all-to-all-done.5 = bf16[8,96,1024]{2,1,0:T(8,128)(2,1)} async-done(((bf16[8,96,1024]{2,1,0:T(8,128)(2,1)}), bf16[8,96,1024]{2,1,0:T(8,128)(2,1)}, u32[]{:S(2)}, u32[]{:S(2)}) %all-to-all-start.5) | async-done | bytes 1572896 | tf_op jit(solution)/shard_map/all_to_all | solution.py:527
  342.3 4.5 all-to-all-start.4
  346.8 41.1 %expert_both.3 = (bf16[768,1024]{1,0:T(8,128)(2,1)}, bf16[768,1024]{1,0:T(8,128)(2,1)}, f32[768,1]{1,0:T(8,128)}) custom-call(bf16[768,1024]{1,0:T(8,128)(2,1)} %bitcast.33.x_ref.refs_1_, bf16[768,1024]{1,0:T(8,128)(2,1)} %bitcast.19.x_ref.g_ref.refs_0_, bf16[1024,5632]{1,0:T(8,128)(2,1)} %bitcast.273, bf16[1024,5632]{1,0:T(8,128)(2,1)} %bitcast.274, ...), custom_call_target="tpu_custom_call" | custom-call | flops 26575110144 | bytes 17301504 | tf_op jit(solution)/shard_map/expert_both/pallas_call | solution.py:692
  389.1 5.1 all-to-all-start.6
  394.2 43.9 %expert_both.2 = (bf16[832,1024]{1,0:T(8,128)(2,1)}, bf16[832,1024]{1,0:T(8,128)(2,1)}, f32[832,1]{1,0:T(8,128)}) custom-call(bf16[832,1024]{1,0:T(8,128)(2,1)} %bitcast.31.x_ref.refs_1_, bf16[832,1024]{1,0:T(8,128)(2,1)} %bitcast.15.x_ref.g_ref.refs_0_, bf16[1024,5632]{1,0:T(8,128)(2,1)} %bitcast.275, bf16[1024,5632]{1,0:T(8,128)(2,1)} %bitcast.276, ...), custom_call_target="tpu_custom_call" | custom-call | flops 28789702656 | bytes 17301504 | tf_op jit(solution)/shard_map/expert_both/pallas_call | solution.py:692
  439.6 10.5 all_to_all.84
  469.6 25.4 %all-to-all-done.8 = bf16[8,104,1024]{2,1,0:T(8,128)(2,1)} async-done(((bf16[8,104,1024]{2,1,0:T(8,128)(2,1)}), bf16[8,104,1024]{2,1,0:T(8,128)(2,1)}, u32[]{:S(2)}, u32[]{:S(2)}) %all-to-all-start.8) | async-done | bytes 1703968 | tf_op jit(solution)/shard_map/all_to_all | solution.py:527
  510.4 12.1 %cross_attend_back_kernel.1 = (bf16[640,1024]{1,0:T(8,128)(2,1)}, bf16[640,1024]{1,0:T(8,128)(2,1)}, bf16[640,1024]{1,0:T(8,128)(2,1)}) custom-call(s32[2]{0:T(128)} %pad_add_fusion.1.place_ref, bf16[640,1024]{1,0:T(8,128)(2,1)} %convolution_convert_fusion.12.q_ref, bf16[640,1024]{1,0:T(8,128)(2,1)} %convolution_convert_fusion.11.k_ref, ...), custom_call_target="tpu_custom_call" | custom-call | flops 4194304000 | bytes 10485760 | tf_op jit(solution)/shard_map/cross_attend_back_kernel/pallas_call | solution.py:457
  532.5 8.0 all_to_all.85
  540.7 22.9 %collective-permute-done.5 = bf16[640,1024]{1,0:T(8,128)(2,1)} collective-permute-done((bf16[640,1024]{1,0:T(8,128)(2,1)}, bf16[640,1024]{1,0:T(8,128)(2,1)}, u32[]{:S(2)}, u32[]{:S(2)}) %collective-permute-start.5) | collective-permute-done | bytes 1310752 | tf_op jit(solution)/shard_map/ppermute | solution.py:970
  597.1 21.1 %all-to-all-done.11 = bf16[8,96,1024]{2,1,0:T(8,128)(2,1)} async-done(((bf16[8,96,1024]{2,1,0:T(8,128)(2,1)}), bf16[8,96,1024]{2,1,0:T(8,128)(2,1)}, u32[]{:S(2)}, u32[]{:S(2)}) %all-to-all-start.11) | async-done | bytes 1572896 | tf_op jit(solution)/shard_map/all_to_all | solution.py:527
  622.5 39.2 %expert_back.2 = (bf16[768,1024]{1,0:T(8,128)(2,1)}, bf16[2,832,1024]{2,1,0:T(8,128)(2,1)}, bf16[2,832,1024]{2,1,0:T(8,128)(2,1)}, bf16[2,832,2816]{2,1,0:T(8,12...) custom-call(s32[2]{0:T(128)} %pad_add_fusion.flags_ref, ...), custom_call_target="tpu_custom_call" | custom-call | flops 22145925120 | bytes 17301504 | tf_op jit(solution)/shard_map/expert_back/pallas_call | solution.py:720
  672.9 5.0 all-to-all-start.12
  677.9 41.4 %expert_back.3 = (bf16[832,1024]{1,0:T(8,128)(2,1)}, bf16[2,832,1024]{2,1,0:T(8,128)(2,1)}, bf16[2,832,1024]{2,1,0:T(8,128)(2,1)}, bf16[2,832,2816]{2,1,0:T(8,12...) custom-call(s32[2]{0:T(128)} %pad_add_fusion.flags_ref, ...), custom_call_target="tpu_custom_call", output_to_operand_aliasing={{1}: (8, {}), {2}: (9, {}), {3}: (10, {}), {4}: (11, {}), {... | custom-call | flops 23991418880 | bytes 17301504 | tf_op jit(solution)/shard_map/expert_back/pallas_call | solution.py:720
  723.8 4.7 all-to-all-start.13
  729.1 15.1 %bitcast_convert_fusion = bf16[1024,2816]{1,0:T(8,128)(2,1)S(1)} fusion(bf16[2,832,1024]{2,1,0:T(8,128)(2,1)} %get-tuple-element.188, bf16[2,832,2816]{2,1,0:T(8,128)(2,1)} %get-tuple-element.189), kind=kOutput, calls=%fused_computation | convolution fusion | flops 9599451136 | bytes 18546688 | tf_op jit(solution)/shard_map/dot_general | solution.py:91
  758.3 4.5 select_convert_fusion
  762.8 10.9 collective-permute-done.9
  804.2 9.4 reduce-scatter.13.cloned.1.call-done
  817.4 33.0 %self_attend_back_kernel.1 = (bf16[640,1024]{1,0:T(8,128)(2,1)}, bf16[640,1024]{1,0:T(8,128)(2,1)}, bf16[640,1024]{1,0:T(8,128)(2,1)}, f32[8,2,1024]{2,1,0:T(2,128)}) custom-call(s32[2]{0:T(128)} %pad_add_fusion.1.place_ref, bf16[640,3072]{1,0:T(8,128)(2,1)} %fusion.4.q_ref.k_ref.v_ref, bf16[640,3072]{1,0:T(8,128)(2,1)} %fusion.4.q_ref.k_ref.v_ref, ...), custom_call_target="tpu_custom_call" | custom-call | flops 4194304000 | bytes 10485760 | tf_op jit(solution)/shard_map/self_attend_back_kernel/pallas_call | solution.py:457
  850.9 30.2 %all-gather.3.cloned.1.call-done = bf16[512,2048]{1,0:T(8,128)(2,1)} async-done(((bf16[64,2048]{1,0:T(8,128)(2,1)}), bf16[512,2048]{1,0:T(8,128)(2,1)}) %all-gather.3.cloned.1.call-update) | async-done | bytes 2097168 | tf_op jit(solution)/shard_map/all_gather | solution.py:763
  881.1 6.6 convolution_convert_fusion
  888.5 4.7 fusion.165
  893.1 17.0 %convolution_bitcast_fusion = f32[1024,2816]{1,0:T(8,128)} fusion(bf16[2,832,1024]{2,1,0:T(8,128)(2,1)S(1)} %copy-done.79, bf16[2,832,2816]{2,1,0:T(8,128)(2,1)} %get-tuple-element.233), kind=kOutput, calls=%fused_computation.2 | convolution fusion | flops 9596567552 | bytes 24313856 | tf_op jit(solution)/shard_map/dot_general | solution.py:91
  912.5 11.3 %fusion.38 = bf16[1408,1024]{1,0:T(8,128)(2,1)S(1)} fusion(bf16[1664,1024]{1,0:T(8,128)(2,1)} %bitcast.291, pred[]{:T(512)S(6)} %eq.600, bf16[1664,2816]{1,0:T(8,128)(2,1)} %bitcast.289), kind=kOutput, calls=%fused_computation.47 | convolution fusion | flops 4802068480 | bytes 15663105 | tf_op jit(solution)/shard_map/dot_general | solution.py:91
  928.2 5.1 collective-permute-done.11
  944.8 10.2 collective-permute-done.12
  957.2 11.8 %fusion.7 = f32[1408,1024]{1,0:T(8,128)} fusion(bf16[1664,1024]{1,0:T(8,128)(2,1)} %bitcast.292, pred[]{:T(512)S(6)} %eq.600, bf16[1664,2816]{1,0:T(8,128)(2,1)} %bitcast.290), kind=kOutput, calls=%fused_computation.13 | convolution fusion | flops 4800626688 | bytes 18546688 | tf_op jit(solution)/shard_map/dot_general | solution.py:91
  969.1 26.8 %collective-permute-done.14 = bf16[320,1024]{1,0:T(8,128)(2,1)} collective-permute-done((bf16[320,1024]{1,0:T(8,128)(2,1)}, bf16[320,1024]{1,0:T(8,128)(2,1)}, u32[]{:S(2)}, u32[]{:S(2)}) %collective-permute-start.14) | collective-permute-done | bytes 655392 | tf_op jit(solution)/shard_map/ppermute | solution.py:1050
  1002.2 10.8 collective-permute-done.15
  1035.0 11.6 %add_bitcast_fusion = f32[1,1,1024,2816]{3,2,1,0:T(8,128)} fusion(f32[1024,2816]{1,0:T(8,128)} %convolution_bitcast_fusion, bf16[1024,2816]{1,0:T(8,128)(2,1)} %constant_dynamic-update-slice_fusion.3), kind=kLoop, calls=%fused_computation.1 | loop fusion | flops 5767168 | bytes 28835840 | tf_op jit(solution)/shard_map/broadcast_in_dim | solution.py:1147
  1046.6 28.9 %collective-permute-done.16 = bf16[1088,1024]{1,0:T(8,128)(2,1)} collective-permute-done((bf16[1088,1024]{1,0:T(8,128)(2,1)}, bf16[1088,1024]{1,0:T(8,128)(2,1)}, u32[]{:S(2)}, u32[]{:S(2)}) %collective-permute-start.16) | collective-permute-done | bytes 2228256 | tf_op jit(solution)/shard_map/ppermute | solution.py:1050
  1075.4 7.4 add_bitcast_fusion.1
  (384 shorter events, 305.8 us)
Async XLA Ops:
  7.2 43.9 %copy-start = (bf16[1,1024,1024]{2,1,0:T(8,128)(2,1)S(1)}, bf16[1,1024,1024]{2,1,0:T(8,128)(2,1)}, u32[]{:S(2)}) copy-start(bf16[1,1024,1024]{2,1,0:T(8,128)(2,1)} %param.55) | copy-start | bytes 6291460
  8.7 45.7 %copy-start.53 = (f32[1,1,1024]{2,0,1:T(1,128)}, f32[1,1,1024]{2,0,1:T(1,128)S(1)}, u32[]{:S(2)}) copy-start(f32[1,1,1024]{2,0,1:T(1,128)S(1)} %get-tuple-element.346) | copy-start | bytes 12292
  12.4 14.4 %copy-start.72 = (s32[5]{0:T(128)S(1)}, s32[5]{0:T(128)}, u32[]{:S(2)}) copy-start(s32[5]{0:T(128)} %param.50) | copy-start | bytes 64
  12.4 15.1 %copy-start.67 = (s32[1,640,2]{1,2,0:T(2,128)S(1)}, s32[1,640,2]{1,2,0:T(2,128)}, u32[]{:S(2)}) copy-start(s32[1,640,2]{1,2,0:T(2,128)} %param.51) | copy-start | bytes 15364
  12.4 15.1 %copy-start.70 = (f32[1,16,32]{2,1,0:T(8,128)S(1)}, f32[1,16,32]{2,1,0:T(8,128)}, u32[]{:S(2)}) copy-start(f32[1,16,32]{2,1,0:T(8,128)} %param.53) | copy-start | bytes 6148
  21.1 30.0 %collective-permute-start = (bf16[384,1024]{1,0:T(8,128)(2,1)}, bf16[384,1024]{1,0:T(8,128)(2,1)}, u32[]{:S(2)}, u32[]{:S(2)}) collective-permute-start(bf16[384,1024]{1,0:T(8,128)(2,1)} %slice_bitcast_fusion.5), channel_id=1, source_target_pairs={{0,16},{1,17},{2,18},{3,19},{4,20},{5,21},{6,22},{7,23},{8,24},{9,... | collective-permute-start | bytes 2359304 | tf_op jit(solution)/shard_map/ppermute | solution.py:865
  60.0 43.2 %all-to-all-start.1 = ((bf16[8,96,1024]{2,1,0:T(8,128)(2,1)}), bf16[8,96,1024]{2,1,0:T(8,128)(2,1)}, u32[]{:S(2)}, u32[]{:S(2)}) async-start(bf16[8,96,1024]{2,1,0:T(8,128)(2,1)} %bitcast.238), calls=%async_computation.1 | async-start | bytes 3145728 | tf_op jit(solution)/shard_map/all_to_all | solution.py:527
  103.2 45.0 %all-to-all-start = ((bf16[8,104,1024]{2,1,0:T(8,128)(2,1)}), bf16[8,104,1024]{2,1,0:T(8,128)(2,1)}, u32[]{:S(2)}, u32[]{:S(2)}) async-start(bf16[8,104,1024]{2,1,0:T(8,128)(2,1)} %bitcast.233), calls=%async_computation | async-start | bytes 3407872 | tf_op jit(solution)/shard_map/all_to_all | solution.py:527
  109.9 27.6 %collective-permute-start.1 = (bf16[576,1024]{1,0:T(8,128)(2,1)}, bf16[576,1024]{1,0:T(8,128)(2,1)}, u32[]{:S(2)}, u32[]{:S(2)}) collective-permute-start(bf16[576,1024]{1,0:T(8,128)(2,1)} %slice_bitcast_fusion.1), channel_id=1, source_target_pairs={{0,16},{1,17},{2,18},{3,19},{4,20},{5,21},{6,22},{7,23},{8,24},{9,... | collective-permute-start | bytes 3538952 | tf_op jit(solution)/shard_map/ppermute | solution.py:877
  148.1 42.1 %all-to-all-start.2 = ((bf16[8,96,1024]{2,1,0:T(8,128)(2,1)}), bf16[8,96,1024]{2,1,0:T(8,128)(2,1)}, u32[]{:S(2)}, u32[]{:S(2)}) async-start(bf16[8,96,1024]{2,1,0:T(8,128)(2,1)} %bitcast.236), calls=%async_computation.2 | async-start | bytes 3145728 | tf_op jit(solution)/shard_map/all_to_all | solution.py:527
  156.0 27.6 %collective-permute-start.2 = (bf16[576,1024]{1,0:T(8,128)(2,1)}, bf16[576,1024]{1,0:T(8,128)(2,1)}, u32[]{:S(2)}, u32[]{:S(2)}) collective-permute-start(bf16[576,1024]{1,0:T(8,128)(2,1)} %pad_maximum_fusion.6), channel_id=1, source_target_pairs={{0,16},{1,17},{2,18},{3,19},{4,20},{5,21},{6,22},{7,23},{8,24},{9,... | collective-permute-start | bytes 3538952 | tf_op jit(solution)/shard_map/ppermute | solution.py:877
  190.3 45.0 %all-to-all-start.3 = ((bf16[8,104,1024]{2,1,0:T(8,128)(2,1)}), bf16[8,104,1024]{2,1,0:T(8,128)(2,1)}, u32[]{:S(2)}, u32[]{:S(2)}) async-start(bf16[8,104,1024]{2,1,0:T(8,128)(2,1)} %bitcast.232), calls=%async_computation.3 | async-start | bytes 3407872 | tf_op jit(solution)/shard_map/all_to_all | solution.py:527
  194.6 24.8 %collective-permute-start.3 = (bf16[512,1024]{1,0:T(8,128)(2,1)}, bf16[512,1024]{1,0:T(8,128)(2,1)}, u32[]{:S(2)}, u32[]{:S(2)}) collective-permute-start(bf16[512,1024]{1,0:T(8,128)(2,1)} %slice_bitcast_fusion.4), channel_id=1, source_target_pairs={{0,16},{1,17},{2,18},{3,19},{4,20},{5,21},{6,22},{7,23},{8,24},{9,... | collective-permute-start | bytes 3145736 | tf_op jit(solution)/shard_map/ppermute | solution.py:882
  245.3 29.7 %collective-permute-start.4 = (bf16[640,1024]{1,0:T(8,128)(2,1)S(1)}, bf16[640,1024]{1,0:T(8,128)(2,1)S(1)}, u32[]{:S(2)}, u32[]{:S(2)}) collective-permute-start(bf16[640,1024]{1,0:T(8,128)(2,1)S(1)} %multiply_convert_fusion.3), channel_id=1, source_target_pairs={{0,16},{1,17},{2,18},{3,19},{4,20},{5,21},{6,22},{7,23},{8,24},{9,... | collective-permute-start | bytes 3932168 | tf_op jit(solution)/shard_map/ppermute | solution.py:891
  297.5 208.7 %copy-start.51 = (f32[640]{0:T(1024)}, f32[640]{0:T(1024)S(1)}, u32[]{:S(2)}) copy-start(f32[640]{0:T(1024)S(1)} %add_rsqrt_fusion) | copy-start | bytes 7684
  300.2 42.1 %all-to-all-start.5 = ((bf16[8,96,1024]{2,1,0:T(8,128)(2,1)}), bf16[8,96,1024]{2,1,0:T(8,128)(2,1)}, u32[]{:S(2)}, u32[]{:S(2)}) async-start(bf16[8,96,1024]{2,1,0:T(8,128)(2,1)} %bitcast.239), calls=%async_computation.5 | async-start | bytes 3145728 | tf_op jit(solution)/shard_map/all_to_all | solution.py:527
  342.3 46.8 %all-to-all-start.4 = ((bf16[8,104,1024]{2,1,0:T(8,128)(2,1)}), bf16[8,104,1024]{2,1,0:T(8,128)(2,1)}, u32[]{:S(2)}, u32[]{:S(2)}) async-start(bf16[8,104,1024]{2,1,0:T(8,128)(2,1)} %bitcast.234), calls=%async_computation.4 | async-start | bytes 3407872 | tf_op jit(solution)/shard_map/all_to_all | solution.py:527
  389.1 50.2 %all-to-all-start.6 = ((bf16[8,96,1024]{2,1,0:T(8,128)(2,1)}), bf16[8,96,1024]{2,1,0:T(8,128)(2,1)}, u32[]{:S(2)}, u32[]{:S(2)}) async-start(bf16[8,96,1024]{2,1,0:T(8,128)(2,1)} %bitcast.237), calls=%async_computation.6 | async-start | bytes 3145728 | tf_op jit(solution)/shard_map/all_to_all | solution.py:527
  450.1 45.0 %all-to-all-start.8 = ((bf16[8,104,1024]{2,1,0:T(8,128)(2,1)}), bf16[8,104,1024]{2,1,0:T(8,128)(2,1)}, u32[]{:S(2)}, u32[]{:S(2)}) async-start(bf16[8,104,1024]{2,1,0:T(8,128)(2,1)} %bitcast.230), calls=%async_computation.8 | async-start | bytes 3407872 | tf_op jit(solution)/shard_map/all_to_all | solution.py:527
  468.7 32.6 %copy-start.64 = (f32[640]{0:T(1024)}, f32[640]{0:T(1024)S(1)}, u32[]{:S(2)}) copy-start(f32[640]{0:T(1024)S(1)} %get-tuple-element.330) | copy-start | bytes 7684
  530.9 32.6 %collective-permute-start.5 = (bf16[640,1024]{1,0:T(8,128)(2,1)}, bf16[640,1024]{1,0:T(8,128)(2,1)}, u32[]{:S(2)}, u32[]{:S(2)}) collective-permute-start(bf16[640,1024]{1,0:T(8,128)(2,1)} %add_convert_fusion.2), channel_id=1, source_target_pairs={{16,0},{17,1},{18,2},{19,3},{20,4},{21,5},{22,6},{23,7},{24,8},{25... | collective-permute-start | bytes 3932168 | tf_op jit(solution)/shard_map/ppermute | solution.py:970
  540.6 25.9 %copy-start.2 = (f32[640,1024]{1,0:T(8,128)S(1)}, f32[640,1024]{1,0:T(8,128)}, u32[]{:S(2)}) copy-start(f32[640,1024]{1,0:T(8,128)} %copy-done.1) | copy-start | bytes 7864324
  575.9 42.3 %all-to-all-start.11 = ((bf16[8,96,1024]{2,1,0:T(8,128)(2,1)}), bf16[8,96,1024]{2,1,0:T(8,128)(2,1)}, u32[]{:S(2)}, u32[]{:S(2)}) async-start(bf16[8,96,1024]{2,1,0:T(8,128)(2,1)} %bitcast.227), calls=%async_computation.11 | async-start | bytes 3145728 | tf_op jit(solution)/shard_map/all_to_all | solution.py:527
  587.0 74.7 %collective-permute-start.6 = (bf16[640,1024]{1,0:T(8,128)(2,1)}, bf16[640,1024]{1,0:T(8,128)(2,1)}, u32[]{:S(2)}, u32[]{:S(2)}) collective-permute-start(bf16[640,1024]{1,0:T(8,128)(2,1)} %get-tuple-element.177), channel_id=1, source_target_pairs={{16,0},{17,1},{18,2},{19,3},{20,4},{21,5},{22,6},{23,7},{24,8},{25... | collective-permute-start | bytes 3932168 | tf_op jit(solution)/shard_map/ppermute | solution.py:975
  588.3 73.4 %collective-permute-start.7 = (bf16[640,1024]{1,0:T(8,128)(2,1)}, bf16[640,1024]{1,0:T(8,128)(2,1)}, u32[]{:S(2)}, u32[]{:S(2)}) collective-permute-start(bf16[640,1024]{1,0:T(8,128)(2,1)} %get-tuple-element.178), channel_id=1, source_target_pairs={{16,0},{17,1},{18,2},{19,3},{20,4},{21,5},{22,6},{23,7},{24,8},{25... | collective-permute-start | bytes 3932168 | tf_op jit(solution)/shard_map/ppermute | solution.py:976
  618.2 54.7 %all-to-all-start.10 = ((bf16[8,104,1024]{2,1,0:T(8,128)(2,1)}), bf16[8,104,1024]{2,1,0:T(8,128)(2,1)}, u32[]{:S(2)}, u32[]{:S(2)}) async-start(bf16[8,104,1024]{2,1,0:T(8,128)(2,1)} %bitcast.226), calls=%async_computation.10 | async-start | bytes 3407872 | tf_op jit(solution)/shard_map/all_to_all | solution.py:527
  622.5 39.2 %copy-start.45 = (bf16[640,1024]{1,0:T(8,128)(2,1)S(1)}, bf16[640,1024]{1,0:T(8,128)(2,1)}, u32[]{:S(2)}) copy-start(bf16[640,1024]{1,0:T(8,128)(2,1)} %copy-done.43) | copy-start | bytes 3932164
  671.5 48.2 %collective-permute-start.8 = (bf16[512,2048]{0,1:T(8,128)(2,1)}, bf16[512,2048]{0,1:T(8,128)(2,1)}, u32[]{:S(2)}, u32[]{:S(2)}) collective-permute-start(bf16[512,2048]{0,1:T(8,128)(2,1)} %fusion.93), channel_id=1, source_target_pairs={{0,1},{1,0},{2,3},{3,2},{4,5},{5,4},{6,7},{7,6},{8,9},{9,8},{10,11... | collective-permute-start | bytes 6291464 | tf_op jit(solution)/shard_map/ppermute | solution.py:749
  672.9 50.9 %all-to-all-start.12 = ((bf16[8,96,1024]{2,1,0:T(8,128)(2,1)}), bf16[8,96,1024]{2,1,0:T(8,128)(2,1)}, u32[]{:S(2)}, u32[]{:S(2)}) async-start(bf16[8,96,1024]{2,1,0:T(8,128)(2,1)} %bitcast.235), calls=%async_computation.12 | async-start | bytes 3145728 | tf_op jit(solution)/shard_map/all_to_all | solution.py:527
  723.8 49.8 %all-to-all-start.13 = ((bf16[8,104,1024]{2,1,0:T(8,128)(2,1)}), bf16[8,104,1024]{2,1,0:T(8,128)(2,1)}, u32[]{:S(2)}, u32[]{:S(2)}) async-start(bf16[8,104,1024]{2,1,0:T(8,128)(2,1)} %bitcast.231), calls=%async_computation.13 | async-start | bytes 3407872 | tf_op jit(solution)/shard_map/all_to_all | solution.py:527
  728.5 85.1 %reduce-scatter.13.cloned.1.call-start = ((), (), s32[]{:S(2)}) async-start(), calls=%async_computation.23 | async-start | bytes 2359296
  745.4 28.3 %collective-permute-start.9 = (bf16[208,2816]{1,0:T(8,128)(2,1)S(1)}, bf16[208,2816]{1,0:T(8,128)(2,1)}, u32[]{:S(2)}, u32[]{:S(2)}) collective-permute-start(bf16[208,2816]{1,0:T(8,128)(2,1)S(1)} %get-tuple-element.336), channel_id=1, source_target_pairs={{0,1},{1,0},{2,3},{3,2},{4,5},{5,4},{6,7},{7,6},{8,9},{9,8},{10,11... | collective-permute-start | bytes 3514376 | tf_op jit(solution)/shard_map/ppermute | solution.py:1050
  777.6 73.3 %reduce-scatter.7.cloned.1.call-start = ((), (), s32[]{:S(2)}) async-start(), calls=%async_computation.18 | async-start | bytes 2359296 | tf_op jit(solution)/shard_map/reduce_scatter | solution.py:759
  799.5 81.6 %all-gather.3.cloned.1.call-start = ((), (), s32[]{:S(2)}) async-start(), calls=%async_computation.19 | async-start | bytes 2359296 | tf_op jit(solution)/shard_map/all_gather | solution.py:763
  815.8 139.3 %reduce-scatter.9.cloned.1.call-start = ((), (), s32[]{:S(2)}) async-start(), calls=%async_computation.20 | async-start | bytes 4718592 | tf_op jit(solution)/shard_map/reduce_scatter | solution.py:759
  815.8 35.1 %collective-permute-start.10 = (bf16[288,2816]{1,0:T(8,128)(2,1)}, bf16[288,2816]{1,0:T(8,128)(2,1)}, u32[]{:S(2)}, u32[]{:S(2)}) collective-permute-start(bf16[288,2816]{1,0:T(8,128)(2,1)} %slice.212), channel_id=1, source_target_pairs={{0,1},{1,0},{2,3},{3,2},{4,5},{5,4},{6,7},{7,6},{8,9},{9,8},{10,11... | collective-permute-start | bytes 4866056 | tf_op jit(solution)/shard_map/ppermute | solution.py:1050
  817.4 63.7 %copy-start.41 = (bf16[640,8,2,64]{0,3,2,1:T(8,128)(2,1)S(1)}, bf16[640,8,2,64]{0,3,2,1:T(8,128)(2,1)}, u32[]{:S(2)}) copy-start(bf16[640,8,2,64]{0,3,2,1:T(8,128)(2,1)} %copy.97) | copy-start | bytes 3932164
  887.8 108.1 %reduce-scatter.11.cloned.1.call-start = ((), (), s32[]{:S(2)}) async-start(), calls=%async_computation.21 | async-start | bytes 2654208 | tf_op jit(solution)/shard_map/reduce_scatter | solution.py:759
  893.1 17.1 %copy-start.57 = (f32[8,2,1024]{2,1,0:T(2,128)S(1)}, f32[8,2,1024]{2,1,0:T(2,128)}, u32[]{:S(2)}) copy-start(f32[8,2,1024]{2,1,0:T(2,128)} %get-tuple-element.224) | copy-start | bytes 196612
  893.1 17.2 %copy-start.37 = (f32[1024,32]{1,0:T(8,128)S(1)}, f32[1024,32]{1,0:T(8,128)}, u32[]{:S(2)}) copy-start(f32[1024,32]{1,0:T(8,128)} %constant.69.clone) | copy-start | bytes 393220
  893.1 17.2 %copy-start.38 = (f32[1024,32]{1,0:T(8,128)S(1)}, f32[1024,32]{1,0:T(8,128)}, u32[]{:S(2)}) copy-start(f32[1024,32]{1,0:T(8,128)} %constant.70.clone) | copy-start | bytes 393220
  910.8 22.4 %collective-permute-start.11 = (bf16[160,2816]{1,0:T(8,128)(2,1)}, bf16[160,2816]{1,0:T(8,128)(2,1)S(1)}, u32[]{:S(2)}, u32[]{:S(2)}) collective-permute-start(bf16[160,2816]{1,0:T(8,128)(2,1)} %get-tuple-element.221), channel_id=1, source_target_pairs={{0,1},{1,0},{2,3},{3,2},{4,5},{5,4},{6,7},{7,6},{8,9},{9,8},{10,11... | collective-permute-start | bytes 2703368 | tf_op jit(solution)/shard_map/ppermute | solution.py:1050
  933.3 21.8 %collective-permute-start.12 = (bf16[160,2816]{1,0:T(8,128)(2,1)}, bf16[160,2816]{1,0:T(8,128)(2,1)}, u32[]{:S(2)}, u32[]{:S(2)}) collective-permute-start(bf16[160,2816]{1,0:T(8,128)(2,1)} %get-tuple-element.229), channel_id=1, source_target_pairs={{0,1},{1,0},{2,3},{3,2},{4,5},{5,4},{6,7},{7,6},{8,9},{9,8},{10,11... | collective-permute-start | bytes 2703368 | tf_op jit(solution)/shard_map/ppermute | solution.py:1050
  955.1 127.8 %all-gather.5.cloned.1.call-start = ((), (), s32[]{:S(2)}) async-start(), calls=%async_computation.22 | async-start | bytes 4866048 | tf_op jit(solution)/shard_map/all_gather | solution.py:763
  955.1 40.8 %collective-permute-start.13 = (bf16[208,2816]{1,0:T(8,128)(2,1)}, bf16[208,2816]{1,0:T(8,128)(2,1)}, u32[]{:S(2)}, u32[]{:S(2)}) collective-permute-start(bf16[208,2816]{1,0:T(8,128)(2,1)} %get-tuple-element.240), channel_id=1, source_target_pairs={{0,1},{1,0},{2,3},{3,2},{4,5},{5,4},{6,7},{7,6},{8,9},{9,8},{10,11... | collective-permute-start | bytes 3514376 | tf_op jit(solution)/shard_map/ppermute | solution.py:1050
  956.7 39.2 %collective-permute-start.14 = (bf16[320,1024]{1,0:T(8,128)(2,1)}, bf16[320,1024]{1,0:T(8,128)(2,1)}, u32[]{:S(2)}, u32[]{:S(2)}) collective-permute-start(bf16[320,1024]{1,0:T(8,128)(2,1)} %slice.216), channel_id=1, source_target_pairs={{0,1},{1,0},{2,3},{3,2},{4,5},{5,4},{6,7},{7,6},{8,9},{9,8},{10,11... | collective-permute-start | bytes 1966088 | tf_op jit(solution)/shard_map/ppermute | solution.py:1050
  1000.8 12.2 %collective-permute-start.15 = (bf16[64,4224]{1,0:T(8,128)(2,1)}, bf16[64,4224]{1,0:T(8,128)(2,1)}, u32[]{:S(2)}, u32[]{:S(2)}) collective-permute-start(bf16[64,4224]{1,0:T(8,128)(2,1)} %constant_dynamic-slice_fusion), channel_id=1, source_target_pairs={{0,1},{1,0},{2,3},{3,2},{4,5},{5,4},{6,7},{7,6},{8,9},{9,8},{10,11... | collective-permute-start | bytes 1622024 | tf_op jit(solution)/shard_map/ppermute | solution.py:749
  1028.0 47.4 %collective-permute-start.16 = (bf16[1088,1024]{1,0:T(8,128)(2,1)}, bf16[1088,1024]{1,0:T(8,128)(2,1)}, u32[]{:S(2)}, u32[]{:S(2)}) collective-permute-start(bf16[1088,1024]{1,0:T(8,128)(2,1)} %slice.198), channel_id=1, source_target_pairs={{0,1},{1,0},{2,3},{3,2},{4,5},{5,4},{6,7},{7,6},{8,9},{9,8},{10,11... | collective-permute-start | bytes 6684680 | tf_op jit(solution)/shard_map/ppermute | solution.py:1050
  (69 other events, 336.8 us)
Sparse Core Ops, SparseCore 0:
  777.7 35.8 reduce-scatter.12
  816.5 34.3 reduce-scatter.6
  853.1 27.9 all-gather.2
  887.9 49.4 reduce-scatter.8
  955.2 36.0 reduce-scatter.10
  1015.3 48.1 all-gather.4

commit v2 on v1

--- a/solution.py
+++ b/solution.py
@@ -5,6 +5,7 @@
 import numpy as np
 from jax import lax
 from jax.experimental import pallas as pl
+from jax.experimental.layout import Layout, with_layout_constraint
 from jax.experimental.pallas import tpu as pltpu
 from jax.sharding import PartitionSpec as P
 
@@ -448,17 +449,18 @@
     return pl.BlockSpec((rows, 2 * HD), lambda pair, places: (0, first + pair))
 
 
-def flat_spec(*shape):
-    return pl.BlockSpec((1,) + shape, lambda pair, places: (pair, 0, 0))
-
-
-def pair_call(kernel, places, operands, specs, out_specs, out_shape, scratch, work):
+def flat_spec(first, *shape):
+    return pl.BlockSpec((1,) + shape, lambda pair, places: (first + pair, 0, 0))
+
+
+def pair_call(kernel, places, operands, specs, out_specs, out_shape, scratch, work, pairs=PAIRS):
     rows = ITEMS * BLOCK
+    share = rows * rows * D * pairs // PAIRS
     return pl.pallas_call(
         kernel,
         grid_spec=pltpu.PrefetchScalarGridSpec(
             num_scalar_prefetch=1,
-            grid=(PAIRS,),
+            grid=(pairs,),
             in_specs=specs,
             out_specs=out_specs,
             scratch_shapes=scratch,
@@ -466,7 +468,7 @@
         out_shape=out_shape,
         compiler_params=pltpu.CompilerParams(vmem_limit_bytes=VMEM_LIMIT),
         cost_estimate=pl.CostEstimate(
-            flops=work * rows * rows * D, bytes_accessed=16 * rows * D, transcendentals=rows * rows * H
+            flops=work * share, bytes_accessed=16 * rows * D, transcendentals=share // HD
         ),
         name=kernel.__name__,
     )(places, *operands)
@@ -479,14 +481,14 @@
     scratch = []
     if lines is not None:
         operands.append(lines)
-        specs.append(flat_spec(2, LINE))
+        specs.append(flat_spec(0, 2, LINE))
         scratch.append(pltpu.VMEM((2, BLOCK, LINE), F32))
     return pair_call(
         cross_attend_kernel if lines is None else self_attend_kernel,
         places,
         operands,
         specs,
-        [pair_spec(rows, 0), flat_spec(2, rows)],
+        [pair_spec(rows, 0), flat_spec(0, 2, rows)],
         [
             jax.ShapeDtypeStruct((rows, D), BF16),
             jax.ShapeDtypeStruct((PAIRS, 2, rows), F32),
@@ -496,19 +498,19 @@
     )
 
 
-def attend_back(query, keys, values, grad_context, lse, places, lines):
+def attend_back(query, keys, values, grad_context, lse, places, lines, first=0, pairs=PAIRS):
     rows = query[0].shape[0]
     operands = [part[0] for part in (query, keys, values)] + [grad_context, lse]
-    specs = [pair_spec(rows, part[1]) for part in (query, keys, values)]
-    specs += [pair_spec(rows, 0), flat_spec(2, rows)]
+    specs = [pair_spec(rows, part[1] + first) for part in (query, keys, values)]
+    specs += [pair_spec(rows, first), flat_spec(first, 2, rows)]
     out_specs = [pair_spec(rows, 0)] * 3
-    out_shape = [jax.ShapeDtypeStruct((rows, D), BF16)] * 3
+    out_shape = [jax.ShapeDtypeStruct((rows, pairs * 2 * HD), BF16)] * 3
     scratch = []
     if lines is not None:
         operands.append(lines)
-        specs.append(flat_spec(2, LINE))
-        out_specs.append(flat_spec(2, LINE))
-        out_shape.append(jax.ShapeDtypeStruct((PAIRS, 2, LINE), F32))
+        specs.append(flat_spec(first, 2, LINE))
+        out_specs.append(flat_spec(0, 2, LINE))
+        out_shape.append(jax.ShapeDtypeStruct((pairs, 2, LINE), F32))
         scratch += [pltpu.VMEM((2, BLOCK, LINE), F32)] * 2
     return pair_call(
         cross_attend_back_kernel if lines is None else self_attend_back_kernel,
@@ -519,6 +521,7 @@
         out_shape,
         scratch,
         10,
+        pairs,
     )
 
 
@@ -571,13 +574,11 @@
 
 
 def expert_both_kernel(
-    x_ref, g_ref, gate_ref, up_ref, down_ref,
-    dx_ref, out_ref, line_ref, dx_total, out_total, line_total,
+    x_ref, g_ref, gate_ref, up_ref, down_ref, dx_ref, active_ref, line_ref, dx_total, line_total
 ):
     @pl.when(pl.program_id(0) == 0)
     def _():
         dx_total[...] = jnp.zeros(dx_total.shape, F32)
-        out_total[...] = jnp.zeros(out_total.shape, F32)
         line_total[...] = jnp.zeros(line_total.shape, F32)
 
     for here in row_blocks(x_ref.shape[0]):
@@ -585,7 +586,7 @@
             x_ref[here, :], g_ref[here, :], gate_ref, up_ref, down_ref
         )
         dx_total[here, :] += dot_nt(grad_gate, gate_ref[...]) + dot_nt(grad_up, up_ref[...])
-        out_total[here, :] += dot(active.astype(BF16), down_ref[...])
+        active_ref[here, :] = active.astype(BF16)
         product = active * grad_active
         line_total[here, :] += sum(
             product[:, first : first + 128] for first in range(0, product.shape[1], 128)
@@ -594,7 +595,6 @@
     @pl.when(pl.program_id(0) == pl.num_programs(0) - 1)
     def _():
         dx_ref[...] = dx_total[...].astype(BF16)
-        out_ref[...] = out_total[...].astype(BF16)
         line_ref[...] = jnp.sum(line_total[...], axis=1, keepdims=True)
 
 
@@ -693,11 +693,19 @@
         expert_both_kernel,
         grid=(tiles,),
         in_specs=[whole, whole] + weight_specs,
-        out_specs=[whole, whole, pl.BlockSpec((rows, 1), lambda tile: (0, 0))],
-        out_shape=[row_shape, row_shape, jax.ShapeDtypeStruct((rows, 1), F32)],
-        scratch_shapes=[total, total, pltpu.VMEM((rows, 128), F32)],
+        out_specs=[
+            whole,
+            pl.BlockSpec((rows, FF_TILE), lambda tile: (0, tile)),
+            pl.BlockSpec((rows, 1), lambda tile: (0, 0)),
+        ],
+        out_shape=[
+            row_shape,
+            jax.ShapeDtypeStruct((rows, FF), BF16),
+            jax.ShapeDtypeStruct((rows, 1), F32),
+        ],
+        scratch_shapes=[total, pltpu.VMEM((rows, 128), F32)],
         compiler_params=pltpu.CompilerParams(vmem_limit_bytes=VMEM_LIMIT),
-        cost_estimate=expert_cost(rows, 6),
+        cost_estimate=expert_cost(rows, 5),
         name="expert_both",
     )(arrived, grad_rows, expert_first, expert_first, expert_second)
 
@@ -742,11 +750,16 @@
     return jax.nn.sigmoid(first - second), jax.nn.sigmoid(second - first)
 
 
-def group_swap(rows, group):
+def group_parts(rows, group):
     half = rows.shape[0] // 2
     sent = lax.dynamic_slice_in_dim(rows, (1 - group) * half, half, 0)
     kept = lax.dynamic_slice_in_dim(rows, group * half, half, 0)
-    return kept + lax.ppermute(sent, "group", SWAP)
+    return kept, lax.ppermute(sent, "group", SWAP)
+
+
+def group_swap(rows, group):
+    kept, got = group_parts(rows, group)
+    return kept + got
 
 
 def shard_rows(grad):
@@ -803,8 +816,8 @@
     forward = [(0, 1)]
     backward = [(1, 0)]
     half_rows = D // 2
-    both_weights = jnp.concatenate([proj_weight, value_weight])
-    pieces = [both_weights[first:last] for first, last in ((0, 384), (384, 960), (960, 1536), (1536, 2048))]
+    both_weights = jnp.concatenate([proj_weight, value_weight], axis=1)
+    pieces = [both_weights[first:last] for first, last in ((0, 352), (352, 704), (704, D))]
 
     long_place = jnp.sum(jnp.arange(ITEMS) * (enc_lengths == ENC_MOST)).astype(jnp.int32)
     places = jnp.stack([long_place, decoder.astype(jnp.int32)])
@@ -850,19 +863,17 @@
                 )
         return buffers
 
-    def collect(buffers, code):
+    def collect(buffers, code, first=0):
         total = None
-        for codes, buffer in zip(chunk_codes, buffers):
+        for codes, buffer in zip(chunk_codes[first:], buffers):
             part = dot((code[:, None] == codes[None, :]).astype(BF16), buffer)
             total = part if total is None else total + part
         return total
 
     normed_in = rms_norm(start_rows, gain_rows[0]).astype(BF16)
     project = dot(normed_in, qkv_weight).astype(BF16)
-    project, pieces[0] = together(project, pieces[0])
     query, keys, values = (project, 0), (project, PAIRS), (project, 2 * PAIRS)
     context, lse = attend(query, keys, values, places, lines)
-    context, pieces[0] = together(context, lax.ppermute(pieces[0], "half", forward))
     first_half = start_rows + dot(context, out_weight)
     normed_half = rms_norm(first_half, gain_rows[1])
     rounded_half = normed_half.astype(BF16)
@@ -872,17 +883,17 @@
     arrived_one = [exchange(part, experts) for part in sent]
     returned_one = []
     for k in range(2):
-        part, piece = together(arrived_one[k], pieces[1 + k])
+        part, piece = together(arrived_one[k], pieces[k])
         part = expert_forward(part, expert_first, expert_second)
-        part, pieces[1 + k] = together(part, lax.ppermute(piece, "half", forward))
+        part, pieces[k] = together(part, lax.ppermute(piece, "half", forward))
         if k == 1:
-            part, pieces[3] = together(part, pieces[3])
+            part, pieces[2] = together(part, pieces[2])
         returned_one.append(exchange(part, experts))
-    returned_one[1], pieces[3] = together(
-        returned_one[1], lax.ppermute(pieces[3], "half", forward)
+    returned_one[1], pieces[2] = together(
+        returned_one[1], lax.ppermute(pieces[2], "half", forward)
     )
     both_weights = jnp.concatenate(pieces)
-    memory_proj, memory_value = both_weights[:D], both_weights[D:]
+    memory_proj, memory_value = both_weights[:, :D], both_weights[:, D:]
     enc_gates = gate_pair(normed_half, router_weight, *picked)
     enc_first = collect(returned_one, code_first)
     enc_second = collect(returned_one, code_second)
@@ -891,10 +902,10 @@
     memory_in = lax.ppermute(memory, "half", forward)
 
     cross_query = dot(rounded_half, proj_weight).astype(BF16)
-    memory_keys = dot(memory_in, memory_proj).astype(BF16)
-    memory_values = dot(memory_in, memory_value).astype(BF16)
+    memory_both = dot(memory_in, both_weights).astype(BF16)
+    memory_keys, memory_values = (memory_both, 0), (memory_both, PAIRS)
     cross_context, cross_lse = attend(
-        (cross_query, 0), (memory_keys, 0), (memory_values, 0), places, None
+        (cross_query, 0), memory_keys, memory_values, places, None
     )
     second_half = first_half + dot(cross_context, value_weight)
     normed_second = rms_norm(second_half, gain_rows[2])
@@ -910,25 +921,35 @@
     )
     edge = experts * chunk_sizes[0]
 
-    def exchange_line(line):
-        parts = jnp.concatenate(
-            [line[:edge].reshape(experts, -1), line[edge:].reshape(experts, -1)], axis=1
-        )
-        moved = lax.all_to_all(parts, "expert", split_axis=0, concat_axis=0, tiled=True)
-        return jnp.concatenate(
-            [moved[:, : chunk_sizes[0]].reshape(-1), moved[:, chunk_sizes[0] :].reshape(-1)]
-        )
-
-    produced_two = []
+    def exchange_lines(lines):
+        parts = []
+        for line in lines:
+            parts += [line[:edge].reshape(experts, -1), line[edge:].reshape(experts, -1)]
+        moved = lax.all_gather(jnp.concatenate(parts, axis=1), "expert", axis=0)
+        moved = lax.dynamic_index_in_dim(moved, lax.axis_index("expert"), 1, keepdims=False)
+        results = []
+        first = 0
+        for _ in lines:
+            halves = []
+            for size in chunk_sizes:
+                halves.append(moved[:, first : first + size].reshape(-1))
+                first += size
+            results.append(jnp.concatenate(halves))
+        return results
+
+    actives_two = []
     returned_two = []
     gate_grads = []
     for part, grad_part in zip(arrived_two, arrived_one):
-        grad_arrived, produced, line = expert_both(part, grad_part, expert_first, expert_second)
+        grad_arrived, active, line = expert_both(part, grad_part, expert_first, expert_second)
         gate_grads.append(line[:, 0])
-        produced_two.append(produced)
+        actives_two.append(active)
         returned_two.append(exchange(grad_arrived, experts))
-    returned_two[0], line_grads = together(returned_two[0], jnp.concatenate(gate_grads))
-    line_grads = exchange_line(line_grads)
+    first_parts, line_grads = together(
+        [collect(returned_two[:1], code) for code in (code_first, code_second)],
+        jnp.concatenate(gate_grads),
+    )
+    line_grads, arrived_gates = exchange_lines([line_grads, gate_rows])
 
     def collect_line(line, code):
         return jnp.sum(
@@ -945,8 +966,8 @@
     )
     dec_normed = (
         dec_normed
-        + dec_gates[0] * collect(returned_two, code_first)
-        + dec_gates[1] * collect(returned_two, code_second)
+        + dec_gates[0] * (first_parts[0] + collect(returned_two[1:], code_first, 1))
+        + dec_gates[1] * (first_parts[1] + collect(returned_two[1:], code_second, 1))
     )
     pulled_rows, gain_dec_moe = rms_back(dec_normed, second_half, gain_rows[2])
     grad_second_half = cot_f + pulled_rows
@@ -955,8 +976,8 @@
     grad_cross_context = dot_nt(rounded_grad, value_weight).astype(BF16)
     grad_cross_query, grad_memory_keys, grad_memory_values = attend_back(
         (cross_query, 0),
-        (memory_keys, 0),
-        (memory_values, 0),
+        memory_keys,
+        memory_values,
         grad_cross_context,
         cross_lse,
         places,
@@ -964,16 +985,15 @@
     )
     key_part = dot_nt(grad_memory_keys, memory_proj)
     value_part, key_part = together(dot_nt(grad_memory_values, memory_value), key_part)
-    grad_memory, gate_rows = together((key_part + value_part).astype(BF16), gate_rows)
-    arrived_gates = exchange_line(gate_rows)
-    grad_memory, grad_memory_keys, grad_memory_values, arrived_gates = together(
+    grad_memory, actives_two = together((key_part + value_part).astype(BF16), actives_two)
+    produced_two = [dot(active, expert_second).astype(BF16) for active in actives_two]
+    grad_memory, grad_memory_keys, grad_memory_values, produced_two = together(
         lax.ppermute(grad_memory, "half", backward),
         grad_memory_keys,
         grad_memory_values,
-        arrived_gates,
+        produced_two,
     )
     back_keys = lax.ppermute(grad_memory_keys, "half", backward)
-    back_values = lax.ppermute(grad_memory_values, "half", backward)
     grad_memory = grad_memory.astype(F32)
     pulled_rows, gain_cross = rms_back(
         dot_nt(grad_cross_query, proj_weight), first_half, gain_rows[1]
@@ -991,6 +1011,17 @@
         exchange(jnp.where(decoder, produced, part), experts)
         for produced, part in zip(produced_two, sent)
     ]
+    normed_sharded = jnp.swapaxes(
+        normed_in.reshape(row_count, 2, lax.axis_size("expert"), -1), 1, 2
+    ).reshape(row_count, D)
+    back_keys, grad_memory_values = together(back_keys, grad_memory_values)
+    back_values = lax.ppermute(grad_memory_values, "half", backward)
+    grad_proj = dot_tn(
+        jnp.where(decoder, rounded_half, memory), jnp.where(decoder, grad_cross_query, back_keys)
+    ).astype(BF16)
+    arrived_three[0], normed_sharded, grad_proj = together(
+        arrived_three[0], normed_sharded, grad_proj
+    )
     flags = jnp.stack([decoder.astype(jnp.int32), group])
     scales = jnp.where(decoder, arrived_gates, 1.0)[:, None]
     most = max(part.shape[0] for part in arrived_one)
@@ -1010,49 +1041,41 @@
             most,
         )
         if k == 0:
-            grad_arrived, back_keys, back_values = together(grad_arrived, back_keys, back_values)
+            grad_arrived, back_values = together(grad_arrived, back_values)
+            arrived_three[1], back_values = together(arrived_three[1], back_values)
             grad_value = dot_tn(
                 jnp.where(decoder, cross_context, memory),
                 jnp.where(decoder, rounded_grad, back_values),
             )
-            grad_proj = dot_tn(
-                jnp.where(decoder, rounded_half, memory),
-                jnp.where(decoder, grad_cross_query, back_keys),
-            )
-            early = group_swap(jnp.concatenate([grad_proj, grad_value], axis=1).astype(BF16), group)
-            normed_sharded = jnp.swapaxes(
-                normed_in.reshape(row_count, 2, lax.axis_size("expert"), -1), 1, 2
-            ).reshape(row_count, D)
+            early = jnp.concatenate([grad_proj, grad_value.astype(BF16)], axis=1)
+            early = group_parts(early, group)
         else:
-            grad_arrived, early, normed_sharded, kept, returned_three[0], arrived_three = together(
-                grad_arrived, early, normed_sharded, kept, returned_three[0], arrived_three
+            grad_arrived, early, kept, returned_three[0], arrived_three = together(
+                grad_arrived, early, kept, returned_three[0], arrived_three
             )
         returned_three.append(exchange(grad_arrived, experts))
-
-    decoded = (
-        second_half
-        + dec_gates[0] * collect(arrived_three, code_first)
-        + dec_gates[1] * collect(arrived_three, code_second)
-    )
-    result = jnp.where(decoder, decoded, encoded)
 
     expert_rows, expert_grad_rows, actives, keep_halves, send_halves = [
         part.reshape(2 * most, -1) for part in kept
     ]
     first_group = group == 0
     half_ff = FF // 2
-    send_in = dot_tn(expert_rows, send_halves).astype(BF16)
-    in_cuts = (0, 208, 496, 656, 816, D)
-    out_cut = 320
-    sends = [(send_in[first:last],) for first, last in zip(in_cuts[:-1], in_cuts[1:])]
+    in_cuts = (0, 256, 512, 656, 832, 960, D)
+    out_cuts = (0, 352, 736, half_ff)
+
+    def cut(values, cuts):
+        return [[values[first:last]] for first, last in zip(cuts[:-1], cuts[1:])]
+
+    first_in = dot_tn(expert_rows[:, : in_cuts[1]], send_halves).astype(BF16)
+    rest_in = dot_tn(expert_rows[:, in_cuts[1] :], send_halves).astype(BF16)
+    sends = [[first_in]] + cut(rest_in, [place - in_cuts[1] for place in in_cuts[1:]])
 
     def swapped(parts):
         return [lax.ppermute(part, "group", SWAP) for part in parts]
 
     gots = [swapped(sends[0])]
-    returned_three[1], sends, gots, early, result = together(
-        returned_three[1], sends, gots, early, result.astype(BF16)
-    )
+    early = with_layout_constraint(early[0] + early[1], Layout((0, 1)))
+    returned_three[1], sends, gots, early = together(returned_three[1], sends, gots, early)
     early = expert_scatter(early)
 
     enc_logits, enc_normed = router_back(enc_gates, grad_gate_first, grad_gate_second)
@@ -1062,31 +1085,31 @@
 
     rounded_grad = grad_first.astype(BF16)
     grad_context = dot_nt(rounded_grad, out_weight).astype(BF16)
-    middle = expert_scatter(shard_rows(dot_tn(context, rounded_grad)))
-    grad_context, early, sends[1] = together(grad_context, early, sends[1])
     gots.append(swapped(sends[1]))
+    halves = [
+        attend_back(query, keys, values, grad_context, lse, places, lines, 0, PAIRS // 2)
+    ]
+    halves[0], gots, sends[2], early, grad_context = together(
+        halves[0], gots, sends[2], early, grad_context
+    )
     early = expert_gather(early)
-    grad_query, grad_keys, grad_values, grad_lines = attend_back(
-        query, keys, values, grad_context, lse, places, lines
-    )
-    (grad_query, grad_keys, grad_values), gots, sends[2], middle, early, kept = together(
-        (grad_query, grad_keys, grad_values),
-        gots,
-        sends[2],
-        middle,
-        early,
-        (actives, expert_grad_rows),
-    )
-    late_first = dot_tn(normed_sharded, jnp.concatenate([grad_keys, grad_values], axis=1))
-    late_first, (grad_query, grad_keys, grad_values), sends[2], kept = together(
-        late_first.astype(BF16), (grad_query, grad_keys, grad_values), sends[2], kept
+    gots.append(swapped(sends[2]))
+    halves.append(
+        attend_back(query, keys, values, grad_context, lse, places, lines, PAIRS // 2, PAIRS // 2)
+    )
+    halves, gots, kept, arrived_three = together(
+        halves, gots, (actives, expert_grad_rows), arrived_three
+    )
+    late_first = dot_tn(normed_sharded, jnp.concatenate(halves[0][:3], axis=1))
+    late_first, halves, sends[3], kept, rounded_grad, early = together(
+        late_first.astype(BF16), halves, sends[3], kept, rounded_grad, early
     )
     late_first = expert_scatter(late_first)
-    actives, expert_grad_rows = kept
-    send_out = dot_tn(
-        jnp.where(first_group, actives[:, half_ff:], actives[:, :half_ff]), expert_grad_rows
-    ).astype(BF16)
-    gots.append(swapped(sends[2]))
+    gots.append(swapped(sends[3]))
+    grad_project = jnp.concatenate(
+        [half[part] for part in range(3) for half in halves], axis=1
+    )
+    grad_lines = jnp.concatenate([half[3] for half in halves])
 
     grad_table = jnp.dot(grad_lines.reshape(H, LINE), hits, precision=HIGHEST)
     grad_router = lax.dot_general(
@@ -1095,9 +1118,9 @@
         (((0,), (0,)), ((), ())),
         precision=HIGHEST,
     )
-    grad_normed = dot_nt(jnp.concatenate([grad_query, grad_keys, grad_values], axis=1), qkv_weight)
-    grad_normed, gots, sends[3] = together(grad_normed, gots, sends[3])
-    gots.append(swapped(sends[3]))
+    grad_normed = dot_nt(grad_project, qkv_weight)
+    grad_normed, gots, sends[4] = together(grad_normed, gots, sends[4])
+    gots.append(swapped(sends[4]))
     pulled_rows, gain_self = rms_back(grad_normed, start_rows, gain_rows[0])
     grad_starts = grad_first + pulled_rows
     gain_grads = jnp.stack(
@@ -1111,27 +1134,57 @@
     small = jnp.concatenate([grad_router, gain_grads.T, table_rows.reshape(D, 1)], axis=1)
     small = jnp.pad(small, ((0, 0), (0, 128 - small.shape[1])))
     late_second = jnp.concatenate(
-        [dot_tn(normed_sharded, grad_query).astype(BF16), shard_rows(small)], axis=1
-    )
+        [
+            dot_tn(normed_sharded, jnp.concatenate(halves[1][:3], axis=1)).astype(BF16),
+            shard_rows(small),
+            shard_rows(dot_tn(context, rounded_grad)),
+        ],
+        axis=1,
+    )
+    late_second = expert_scatter(late_second)
     keep_in = dot_tn(expert_rows, keep_halves)
-    late_second, late_first, gots, sends[4], keep_in = together(
-        late_second, late_first, gots, sends[4] + (send_out[:out_cut],), keep_in
-    )
-    gots.append(swapped(sends[4]))
-    late_second = expert_scatter(late_second)
+    keep_in, gots, sends[5], kept, arrived_three = together(
+        keep_in, gots, sends[5], kept, arrived_three
+    )
+    actives, expert_grad_rows = kept
+    send_out = dot_tn(
+        jnp.where(first_group, actives[:, half_ff:], actives[:, :half_ff]), expert_grad_rows
+    ).astype(BF16)
+    out_sends = cut(send_out, out_cuts)
+    sends[5], out_sends[0] = together(sends[5], out_sends[0])
+    gots.append(swapped(sends[5] + out_sends[0]))
+    decoded = (
+        second_half
+        + dec_gates[0] * collect(arrived_three, code_first)
+        + dec_gates[1] * collect(arrived_three, code_second)
+    )
+    result = jnp.where(decoder, decoded, encoded)
+
+    result, gots, out_sends, kept = together(result.astype(BF16), gots, out_sends, kept)
+    gots.append(swapped(out_sends[1]))
+    actives, expert_grad_rows = kept
     keep_out = dot_tn(
         jnp.where(first_group, actives[:, :half_ff], actives[:, half_ff:]), expert_grad_rows
     )
-    late_first, late_second, keep_out, gots, send_out = together(
-        late_first, late_second, keep_out, gots, send_out
-    )
-    late = group_swap(jnp.concatenate([late_first, late_second, middle], axis=1), group)
-    late, send_out = together(late, send_out)
+    late_first, keep_out, gots = together(late_first, keep_out, gots)
+    late_first, late_second, gots, out_sends = together(late_first, late_second, gots, out_sends)
+    late = group_swap(jnp.concatenate([late_first, late_second], axis=1), group)
+    late, out_sends = together(late, out_sends)
     late = expert_gather(late)
-    gots.append(swapped([send_out[out_cut:]]))
-    grad_expert_in = keep_in + jnp.concatenate([part[0] for part in gots[:5]]).astype(F32)
-    grad_expert_out = keep_out + jnp.concatenate([gots[4][1], gots[5][0]]).astype(F32)
-    grad_qkv = jnp.concatenate([late[:, 2 * D : 3 * D], late[:, : 2 * D]], axis=1).astype(F32)
+    gots.append(swapped(out_sends[2]))
+    got_in = [part[0] for part in gots[: len(sends)]]
+    got_out = [gots[5][1], gots[6][0], gots[7][0]]
+    grad_expert_in = keep_in + jnp.concatenate(got_in).astype(F32)
+    grad_expert_out = keep_out + jnp.concatenate(got_out).astype(F32)
+    half_columns = D // 2
+    grad_qkv = jnp.concatenate(
+        [
+            late[:, first + half * part : first + half * part + half_columns]
+            for part in range(3)
+            for first, half in ((0, half_columns), (3 * half_columns, half_columns))
+        ],
+        axis=1,
+    ).astype(F32)
     small = late[:, 3 * D : 3 * D + 128].astype(F32)
     small_table = small[: H * NBKT // 2, experts + 3].reshape(H // 2, NBKT)
     return (

time: 1110 us -> 1040 us (0.937)
  waiting for transfers between devices: 348 us -> 270 us
  blocking collectives: 18.5 us -> 30.7 us
    all_gather x0 -> x1, blocking collectives: none -> 30.7 us  [exchange_lines(): moved = lax.all_gather(jnp.concatenate(parts, axis=1), 'expert', axis=0)]
    all_to_all x12, waiting for transfers between devices: 147 us -> 118 us  [exchange(): lax.all_to_all(parts, 'expert', split_axis=0, concat_axis=0, tiled=True)]
    all_gather x2, waiting for transfers between devices: 30.2 us -> 3.1 us  [expert_gather(): return lax.all_gather(rows, 'expert', axis=0, tiled=True)]
    ppermute x7 -> x9, waiting for transfers between devices: 81.9 us -> 57.3 us  [swapped(): return [lax.ppermute(part, 'group', SWAP) for part in parts]]
    ppermute x6 -> x5, waiting for transfers between devices: 32.3 us -> 51.5 us  [the longest x1 19.7 us: per_device(): lax.ppermute(pieces[2], 'half', forward)]
    all_to_all x2 -> x0, blocking collectives: 18.5 us -> none  [exchange_line(): lax.all_to_all(parts, 'expert', split_axis=0, concat_axis=0, tiled=True)]
    unnamed x178 -> x264, local copies, waits for them, and re-layouts: 23.2 us -> 29.9 us
    dot_general x31 -> x32, matrix products: 110 us -> 114 us  [dot(): return jnp.dot(a, b, preferred_element_type=F32)]
  transfers between devices with their start and end apart: 35 -> 35, of which waited for: 22 -> 21; matrix products, arithmetic and copies ran while one was open for 21% -> 24% of each run, Pallas kernels for 24% -> 23%
where the time goes in v2:
time: 1040 us; the launch traced here: 1030 us
  Pallas kernels  274 us (26%)
  waiting for transfers between devices  270 us (26%)
  matrix products  226 us (22%)
  starting transfers between devices  85 us (8%)
  other arithmetic  74.9 us (7%)
  local copies, waits for them, and re-layouts  51.8 us (5%)
  blocking collectives  30.7 us (3%)
  between operations  16.3 us (2%)
    all_to_all x12, waiting for transfers between devices, exchange(): lax.all_to_all(parts, 'expert', split_axis=0, concat_axis=0, tiled=True)  118 us
    dot_general x32, matrix products, dot(): return jnp.dot(a, b, preferred_element_type=F32)  114 us
    pallas_call x2, Pallas kernels, expert_back(): pl.pallas_call(partial(expert_back_kernel, count=rows), grid_spec=pltpu.P...  80.4 us
    pallas_call x5, Pallas kernels, pair_call(): pl.pallas_call(kernel, grid_spec=pltpu.PrefetchScalarGridSpec(num_scalar_...  75.9 us
    pallas_call x2, Pallas kernels, expert_both(): pl.pallas_call(expert_both_kernel, grid=(tiles,), in_specs=[whole, whole]...  74.3 us
    dot_general x10, matrix products, dot_tn(): lax.dot_general(a, b, (((0,), (0,)), ((), ())), preferred_element_type=F32)  73.7 us
    ppermute x9, waiting for transfers between devices, swapped(): return [lax.ppermute(part, 'group', SWAP) for part in parts]  57.3 us
    all_to_all x12, starting transfers between devices, exchange(): lax.all_to_all(parts, 'expert', split_axis=0, concat_axis=0, tiled=True)  56.5 us
  transfers between devices with their start and end apart: 35, of which 21 were waited for; matrix products, arithmetic and copies ran while one was open for 24% of the time, Pallas kernels for 23%

profile of v2, /device:TPU:0, one launch (start us, length us, event | category | flops | bytes accessed | tf_op | source)
XLA Modules:
  0.0 1028.5 jit_solution(11086645754825170273)
XLA Ops:
  15.2 8.8 fusion.4.q_ref.k_ref.v_ref
  24.0 18.5 %self_attend_kernel.1 = (bf16[640,1024]{1,0:T(8,128)(2,1)}, f32[8,2,640]{2,1,0:T(2,128)}) custom-call(s32[2]{0:T(128)} %pad_add_fusion.place_ref, bf16[640,3072]{1,0:T(8,128)(2,1)} %fusion.4.q_ref.k_ref.v_ref, bf16[640,3072]{1,0:T(8,128)(2,1)} %fusion.4.q_ref.k_ref.v_ref, bf16[640,3072]{1,0:T(8,128)(2,1)} %fusion.4.q_ref.k_ref.v_ref, ...), custom_call_target="tpu_custom_call" | custom-call | flops 1677721600 | bytes 10485760 | tf_op jit(solution)/shard_map/self_attend_kernel/pallas_call | solution.py:459
  51.7 6.3 all-to-all-start
  62.0 33.9 %all-to-all-done = bf16[8,96,1024]{2,1,0:T(8,128)(2,1)} async-done(((bf16[8,96,1024]{2,1,0:T(8,128)(2,1)}), bf16[8,96,1024]{2,1,0:T(8,128)(2,1)}, u32[]{:S(2)}, u32[]{:S(2)}) %all-to-all-start) | async-done | bytes 1572896 | tf_op jit(solution)/shard_map/all_to_all | solution.py:530
  106.4 21.4 %expert_forward.2 = bf16[768,1024]{1,0:T(8,128)(2,1)} custom-call(bf16[768,1024]{1,0:T(8,128)(2,1)} %bitcast.15.x_ref.g_ref.refs_0_, bf16[1024,5632]{1,0:T(8,128)(2,1)} %bitcast.295, bf16[1024,5632]{1,0:T(8,128)(2,1)} %bitcast.296, bf16[2816,1024]{1,0:T(8,128)(2,1)} %bitcast.309), custom_call_target="tpu_custom_call" | custom-call | flops 13287555072 | bytes 17301504 | tf_op jit(solution)/shard_map/expert_forward/pallas_call | solution.py:674
  127.8 9.3 collective-permute-done
  150.0 22.0 %expert_forward.3 = bf16[832,1024]{1,0:T(8,128)(2,1)} custom-call(bf16[832,1024]{1,0:T(8,128)(2,1)} %bitcast.22.x_ref.g_ref.refs_0_, bf16[1024,5632]{1,0:T(8,128)(2,1)} %bitcast.297, bf16[1024,5632]{1,0:T(8,128)(2,1)} %bitcast.298, bf16[2816,1024]{1,0:T(8,128)(2,1)} %bitcast.310), custom_call_target="tpu_custom_call" | custom-call | flops 14394851328 | bytes 17301504 | tf_op jit(solution)/shard_map/expert_forward/pallas_call | solution.py:674
  172.0 6.4 collective-permute-done.1
  198.0 19.7 %collective-permute-done.2 = bf16[320,2048]{1,0:T(8,128)(2,1)} collective-permute-done((bf16[320,2048]{1,0:T(8,128)(2,1)}, bf16[320,2048]{1,0:T(8,128)(2,1)}, u32[]{:S(2)}, u32[]{:S(2)}) %collective-permute-start.2) | collective-permute-done | bytes 1310752 | tf_op jit(solution)/shard_map/ppermute | solution.py:893
  217.7 10.2 all-to-all-done.3
  231.9 5.7 multiply_reduce_fusion.9
  248.1 19.5 %collective-permute-done.3 = bf16[640,1024]{1,0:T(8,128)(2,1)S(1)} collective-permute-done((bf16[640,1024]{1,0:T(8,128)(2,1)S(1)}, bf16[640,1024]{1,0:T(8,128)(2,1)S(1)}, u32[]{:S(2)}, u32[]{:S(2)}) %collective-permute-start.3) | collective-permute-done | bytes 1310752 | tf_op jit(solution)/shard_map/ppermute | solution.py:902
  271.8 9.9 cross_attend_kernel.1
  297.6 33.3 %all-to-all-done.5 = bf16[8,96,1024]{2,1,0:T(8,128)(2,1)} async-done(((bf16[8,96,1024]{2,1,0:T(8,128)(2,1)}), bf16[8,96,1024]{2,1,0:T(8,128)(2,1)}, u32[]{:S(2)}, u32[]{:S(2)}) %all-to-all-start.5) | async-done | bytes 1572896 | tf_op jit(solution)/shard_map/all_to_all | solution.py:530
  335.2 36.0 %expert_both.2 = (bf16[768,1024]{1,0:T(8,128)(2,1)}, bf16[768,2816]{1,0:T(8,128)(2,1)}, f32[768,1]{1,0:T(8,128)}) custom-call(bf16[768,1024]{1,0:T(8,128)(2,1)} %bitcast.30.x_ref.refs_1_, bf16[768,1024]{1,0:T(8,128)(2,1)} %bitcast.15.x_ref.g_ref.refs_0_, bf16[1024,5632]{1,0:T(8,128)(2,1)} %bitcast.299, bf16[1024,5632]{1,0:T(8,128)(2,1)} %bitcast.300, ...), custom_call_target="tpu_custom_call" | custom-call | flops 22145925120 | bytes 17301504 | tf_op jit(solution)/shard_map/expert_both/pallas_call | solution.py:692
  371.2 4.7 all-to-all-done.4
  375.9 4.7 all-to-all-start.6
  380.6 38.4 %expert_both.3 = (bf16[832,1024]{1,0:T(8,128)(2,1)}, bf16[832,2816]{1,0:T(8,128)(2,1)}, f32[832,1]{1,0:T(8,128)}) custom-call(bf16[832,1024]{1,0:T(8,128)(2,1)} %bitcast.28.x_ref.refs_1_, bf16[832,1024]{1,0:T(8,128)(2,1)} %bitcast.22.x_ref.g_ref.refs_0_, bf16[1024,5632]{1,0:T(8,128)(2,1)} %bitcast.301, bf16[1024,5632]{1,0:T(8,128)(2,1)} %bitcast.302, ...), custom_call_target="tpu_custom_call" | custom-call | flops 23991418880 | bytes 17301504 | tf_op jit(solution)/shard_map/expert_both/pallas_call | solution.py:692
  419.0 5.0 all-to-all-start.7
  440.3 30.7 %all-gather = f32[64,400]{1,0:T(8,128)S(1)} all-gather(f32[8,400]{1,0:T(8,128)S(1)} %pad_maximum_fusion.6), channel_id=2, replica_groups=mesh['half'=2,'expert'=8,'group'=2] {'expert'}, dimensions={0}, use_global_device_ids=true | all-gather | bytes 115200 | tf_op jit(solution)/shard_map/all_gather | solution.py:928
  487.7 11.9 %cross_attend_back_kernel.1 = (bf16[640,1024]{1,0:T(8,128)(2,1)}, bf16[640,1024]{1,0:T(8,128)(2,1)}, bf16[640,1024]{1,0:T(8,128)(2,1)}) custom-call(s32[2]{0:T(128)} %pad_add_fusion.place_ref, bf16[640,1024]{1,0:T(8,128)(2,1)} %convolution_convert_fusion.15.q_ref, bf16[640,2048]{1,0:T(8,128)(2,1)} %convolution_convert_fusion.4.k_ref.v_ref, ...), custom_call_target="tpu_custom_call" | custom-call | flops 4194304000 | bytes 10485760 | tf_op jit(solution)/shard_map/cross_attend_back_kernel/pallas_call | solution.py:459
  507.3 6.3 convolution_convert_fusion.8
  518.3 20.7 %collective-permute-done.4 = bf16[640,1024]{1,0:T(8,128)(2,1)S(1)} collective-permute-done((bf16[640,1024]{1,0:T(8,128)(2,1)S(1)}, bf16[640,1024]{1,0:T(8,128)(2,1)S(1)}, u32[]{:S(2)}, u32[]{:S(2)}) %collective-permute-start.4) | collective-permute-done | bytes 1310752 | tf_op jit(solution)/shard_map/ppermute | solution.py:991
  560.8 27.6 %all-to-all-done.9 = bf16[8,96,1024]{2,1,0:T(8,128)(2,1)} async-done(((bf16[8,96,1024]{2,1,0:T(8,128)(2,1)}), bf16[8,96,1024]{2,1,0:T(8,128)(2,1)}, u32[]{:S(2)}, u32[]{:S(2)}) %all-to-all-start.9) | async-done | bytes 1572896 | tf_op jit(solution)/shard_map/all_to_all | solution.py:530
  600.0 4.9 convolution_convert_fusion.7
  604.9 39.0 %expert_back.2 = (bf16[768,1024]{1,0:T(8,128)(2,1)}, bf16[2,832,1024]{2,1,0:T(8,128)(2,1)}, bf16[2,832,1024]{2,1,0:T(8,128)(2,1)}, bf16[2,832,2816]{2,1,0:T(8,12...) custom-call(s32[2]{0:T(128)} %pad_add_fusion.1.flags_ref, ...), custom_call_target="tpu_custom_call" | custom-call | flops 22145925120 | bytes 17301504 | tf_op jit(solution)/shard_map/expert_back/pallas_call | solution.py:728
  643.9 5.4 all-to-all-start.10
  657.5 41.4 %expert_back.3 = (bf16[832,1024]{1,0:T(8,128)(2,1)}, bf16[2,832,1024]{2,1,0:T(8,128)(2,1)}, bf16[2,832,1024]{2,1,0:T(8,128)(2,1)}, bf16[2,832,2816]{2,1,0:T(8,12...) custom-call(s32[2]{0:T(128)} %pad_add_fusion.1.flags_ref, ...), custom_call_target="tpu_custom_call", output_to_operand_aliasing={{1}: (8, {}), {2}: (9, {}), {3}: (10, {}), {4}: (11, {}), {... | custom-call | flops 23991418880 | bytes 17301504 | tf_op jit(solution)/shard_map/expert_back/pallas_call | solution.py:728
  698.8 5.4 collective-permute-done.7
  704.2 4.9 all-to-all-start.11
  709.4 8.0 convolution_convert_fusion.1
  719.1 8.4 convolution_convert_fusion
  735.0 16.7 %collective-permute-done.8 = bf16[256,2816]{1,0:T(8,128)(2,1)} collective-permute-done((bf16[256,2816]{1,0:T(8,128)(2,1)}, bf16[256,2816]{1,0:T(8,128)(2,1)}, u32[]{:S(2)}, u32[]{:S(2)}) %collective-permute-start.8) | collective-permute-done | bytes 1441824 | tf_op jit(solution)/shard_map/ppermute | solution.py:1074
  777.2 17.7 %self_attend_back_kernel.2 = (bf16[640,512]{1,0:T(8,128)(2,1)}, bf16[640,512]{1,0:T(8,128)(2,1)}, bf16[640,512]{1,0:T(8,128)(2,1)}, f32[4,2,1024]{2,1,0:T(2,128)}) custom-call(s32[2]{0:T(128)} %pad_add_fusion.place_ref, bf16[640,3072]{1,0:T(8,128)(2,1)} %fusion.4.q_ref.k_ref.v_ref, bf16[640,3072]{1,0:T(8,128)(2,1)} %fusion.4.q_ref.k_ref.v_ref, ...), custom_call_target="tpu_custom_call" | custom-call | flops 2097152000 | bytes 10485760 | tf_op jit(solution)/shard_map/self_attend_back_kernel/pallas_call | solution.py:459
  795.4 17.9 %self_attend_back_kernel.3 = (bf16[640,512]{1,0:T(8,128)(2,1)}, bf16[640,512]{1,0:T(8,128)(2,1)}, bf16[640,512]{1,0:T(8,128)(2,1)}, f32[4,2,1024]{2,1,0:T(2,128)}) custom-call(s32[2]{0:T(128)} %pad_add_fusion.place_ref, bf16[640,3072]{1,0:T(8,128)(2,1)} %fusion.4.q_ref.k_ref.v_ref, bf16[640,3072]{1,0:T(8,128)(2,1)} %fusion.4.q_ref.k_ref.v_ref, ...), custom_call_target="tpu_custom_call" | custom-call | flops 2097152000 | bytes 10485760 | tf_op jit(solution)/shard_map/self_attend_back_kernel/pallas_call | solution.py:459
  814.7 5.5 convolution_convert_fusion.3
  846.4 6.3 collective-permute-done.11
  855.6 5.8 pad_maximum_fusion
  863.1 17.7 %convolution_bitcast_fusion = f32[1024,2816]{1,0:T(8,128)} fusion(bf16[2,832,1024]{2,1,0:T(8,128)(2,1)} %get-tuple-element.246, bf16[2,832,2816]{2,1,0:T(8,128)(2,1)} %get-tuple-element.247), kind=kOutput, calls=%fused_computation.1 | convolution fusion | flops 9596567552 | bytes 24313856 | tf_op jit(solution)/shard_map/dot_general | solution.py:92
  880.9 9.6 fusion.33
  901.7 4.9 select_convert_fusion
  907.8 7.6 collective-permute-done.13
  916.5 7.3 fusion.7
  923.8 9.4 collective-permute-done.15
  938.3 10.8 %collective-permute-done.16 = bf16[64,4224]{1,0:T(8,128)(2,1)} collective-permute-done((bf16[64,4224]{1,0:T(8,128)(2,1)}, bf16[64,4224]{1,0:T(8,128)(2,1)}, u32[]{:S(2)}, u32[]{:S(2)}) %collective-permute-start.16) | collective-permute-done | bytes 540704 | tf_op jit(solution)/shard_map/ppermute | solution.py:757
  970.6 11.6 %add_bitcast_fusion = f32[1,1,1024,2816]{3,2,1,0:T(8,128)} fusion(f32[1024,2816]{1,0:T(8,128)} %convolution_bitcast_fusion, bf16[1024,2816]{1,0:T(8,128)(2,1)} %constant_dynamic-update-slice_fusion.11), kind=kLoop, calls=%fused_computation | loop fusion | flops 5767168 | bytes 28835840 | tf_op jit(solution)/shard_map/broadcast_in_dim | solution.py:1200
  982.3 15.9 %collective-permute-done.17 = bf16[672,1024]{1,0:T(8,128)(2,1)S(1)} collective-permute-done((bf16[672,1024]{1,0:T(8,128)(2,1)}, bf16[672,1024]{1,0:T(8,128)(2,1)S(1)}, u32[]{:S(2)}, u32[]{:S(2)}) %collective-permute-start.17) | collective-permute-done | bytes 1376288 | tf_op jit(solution)/shard_map/ppermute | solution.py:1074
  998.1 7.1 add_bitcast_fusion.1
  (476 shorter events, 312.3 us)
Async XLA Ops:
  7.2 35.3 %copy-start = (bf16[1,1024,1024]{2,1,0:T(8,128)(2,1)S(1)}, bf16[1,1024,1024]{2,1,0:T(8,128)(2,1)}, u32[]{:S(2)}) copy-start(bf16[1,1024,1024]{2,1,0:T(8,128)(2,1)} %param.55) | copy-start | bytes 6291460
  12.3 34.1 %copy-start.64 = (f32[1,1,1024]{2,0,1:T(1,128)}, f32[1,1,1024]{2,0,1:T(1,128)S(1)}, u32[]{:S(2)}) copy-start(f32[1,1,1024]{2,0,1:T(1,128)S(1)} %get-tuple-element.446) | copy-start | bytes 12292
  51.7 44.2 %all-to-all-start = ((bf16[8,96,1024]{2,1,0:T(8,128)(2,1)}), bf16[8,96,1024]{2,1,0:T(8,128)(2,1)}, u32[]{:S(2)}, u32[]{:S(2)}) async-start(bf16[8,96,1024]{2,1,0:T(8,128)(2,1)} %bitcast.263), calls=%async_computation | async-start | bytes 3145728 | tf_op jit(solution)/shard_map/all_to_all | solution.py:530
  95.8 45.0 %all-to-all-start.2 = ((bf16[8,104,1024]{2,1,0:T(8,128)(2,1)}), bf16[8,104,1024]{2,1,0:T(8,128)(2,1)}, u32[]{:S(2)}, u32[]{:S(2)}) async-start(bf16[8,104,1024]{2,1,0:T(8,128)(2,1)} %bitcast.258), calls=%async_computation.2 | async-start | bytes 3407872 | tf_op jit(solution)/shard_map/all_to_all | solution.py:530
  103.8 33.2 %collective-permute-start = (bf16[352,2048]{1,0:T(8,128)(2,1)}, bf16[352,2048]{1,0:T(8,128)(2,1)}, u32[]{:S(2)}, u32[]{:S(2)}) collective-permute-start(bf16[352,2048]{1,0:T(8,128)(2,1)} %get-tuple-element.191), channel_id=1, source_target_pairs={{0,16},{1,17},{2,18},{3,19},{4,20},{5,21},{6,22},{7,23},{8,24},{9,... | collective-permute-start | bytes 4325384 | tf_op jit(solution)/shard_map/ppermute | solution.py:888
  140.8 42.1 %all-to-all-start.1 = ((bf16[8,96,1024]{2,1,0:T(8,128)(2,1)}), bf16[8,96,1024]{2,1,0:T(8,128)(2,1)}, u32[]{:S(2)}, u32[]{:S(2)}) async-start(bf16[8,96,1024]{2,1,0:T(8,128)(2,1)} %bitcast.261), calls=%async_computation.1 | async-start | bytes 3145728 | tf_op jit(solution)/shard_map/all_to_all | solution.py:530
  145.1 33.3 %collective-permute-start.1 = (bf16[352,2048]{1,0:T(8,128)(2,1)}, bf16[352,2048]{1,0:T(8,128)(2,1)}, u32[]{:S(2)}, u32[]{:S(2)}) collective-permute-start(bf16[352,2048]{1,0:T(8,128)(2,1)} %get-tuple-element.194), channel_id=1, source_target_pairs={{0,16},{1,17},{2,18},{3,19},{4,20},{5,21},{6,22},{7,23},{8,24},{9,... | collective-permute-start | bytes 4325384 | tf_op jit(solution)/shard_map/ppermute | solution.py:888
  182.9 45.0 %all-to-all-start.3 = ((bf16[8,104,1024]{2,1,0:T(8,128)(2,1)}), bf16[8,104,1024]{2,1,0:T(8,128)(2,1)}, u32[]{:S(2)}, u32[]{:S(2)}) async-start(bf16[8,104,1024]{2,1,0:T(8,128)(2,1)} %bitcast.257), calls=%async_computation.3 | async-start | bytes 3407872 | tf_op jit(solution)/shard_map/all_to_all | solution.py:530
  187.3 30.4 %collective-permute-start.2 = (bf16[320,2048]{1,0:T(8,128)(2,1)}, bf16[320,2048]{1,0:T(8,128)(2,1)}, u32[]{:S(2)}, u32[]{:S(2)}) collective-permute-start(bf16[320,2048]{1,0:T(8,128)(2,1)} %pad_maximum_fusion.1), channel_id=1, source_target_pairs={{0,16},{1,17},{2,18},{3,19},{4,20},{5,21},{6,22},{7,23},{8,24},{9,... | collective-permute-start | bytes 3932168 | tf_op jit(solution)/shard_map/ppermute | solution.py:893
  189.7 282.6 %copy-start.88 = (s32[640]{0:T(1024)}, s32[640]{0:T(1024)S(1)}, u32[]{:S(2)}) copy-start(s32[640]{0:T(1024)S(1)} %get-tuple-element.424) | copy-start | bytes 7684
  189.7 285.7 %copy-start.62 = (s32[640]{0:T(1024)}, s32[640]{0:T(1024)S(1)}, u32[]{:S(2)}) copy-start(s32[640]{0:T(1024)S(1)} %get-tuple-element.425) | copy-start | bytes 7684
  237.9 29.7 %collective-permute-start.3 = (bf16[640,1024]{1,0:T(8,128)(2,1)S(1)}, bf16[640,1024]{1,0:T(8,128)(2,1)S(1)}, u32[]{:S(2)}, u32[]{:S(2)}) collective-permute-start(bf16[640,1024]{1,0:T(8,128)(2,1)S(1)} %multiply_convert_fusion.3), channel_id=1, source_target_pairs={{0,16},{1,17},{2,18},{3,19},{4,20},{5,21},{6,22},{7,23},{8,24},{9,... | collective-permute-start | bytes 3932168 | tf_op jit(solution)/shard_map/ppermute | solution.py:902
  286.1 197.4 %copy-start.60 = (f32[640]{0:T(1024)}, f32[640]{0:T(1024)S(1)}, u32[]{:S(2)}) copy-start(f32[640]{0:T(1024)S(1)} %add_rsqrt_fusion) | copy-start | bytes 7684
  288.8 42.1 %all-to-all-start.5 = ((bf16[8,96,1024]{2,1,0:T(8,128)(2,1)}), bf16[8,96,1024]{2,1,0:T(8,128)(2,1)}, u32[]{:S(2)}, u32[]{:S(2)}) async-start(bf16[8,96,1024]{2,1,0:T(8,128)(2,1)} %bitcast.264), calls=%async_computation.5 | async-start | bytes 3145728 | tf_op jit(solution)/shard_map/all_to_all | solution.py:530
  330.9 45.0 %all-to-all-start.4 = ((bf16[8,104,1024]{2,1,0:T(8,128)(2,1)}), bf16[8,104,1024]{2,1,0:T(8,128)(2,1)}, u32[]{:S(2)}, u32[]{:S(2)}) async-start(bf16[8,104,1024]{2,1,0:T(8,128)(2,1)} %bitcast.259), calls=%async_computation.4 | async-start | bytes 3407872 | tf_op jit(solution)/shard_map/all_to_all | solution.py:530
  375.9 43.1 %all-to-all-start.6 = ((bf16[8,96,1024]{2,1,0:T(8,128)(2,1)}), bf16[8,96,1024]{2,1,0:T(8,128)(2,1)}, u32[]{:S(2)}, u32[]{:S(2)}) async-start(bf16[8,96,1024]{2,1,0:T(8,128)(2,1)} %bitcast.262), calls=%async_computation.6 | async-start | bytes 3145728 | tf_op jit(solution)/shard_map/all_to_all | solution.py:530
  419.0 53.4 %all-to-all-start.7 = ((bf16[8,104,1024]{2,1,0:T(8,128)(2,1)}), bf16[8,104,1024]{2,1,0:T(8,128)(2,1)}, u32[]{:S(2)}, u32[]{:S(2)}) async-start(bf16[8,104,1024]{2,1,0:T(8,128)(2,1)} %bitcast.255), calls=%async_computation.7 | async-start | bytes 3407872 | tf_op jit(solution)/shard_map/all_to_all | solution.py:530
  428.2 50.4 %copy-start.70 = (f32[640]{0:T(1024)}, f32[640]{0:T(1024)S(1)}, u32[]{:S(2)}) copy-start(f32[640]{0:T(1024)S(1)} %get-tuple-element.447) | copy-start | bytes 7684
  428.3 50.4 %copy-start.72 = (f32[640]{0:T(1024)}, f32[640]{0:T(1024)S(1)}, u32[]{:S(2)}) copy-start(f32[640]{0:T(1024)S(1)} %get-tuple-element.448) | copy-start | bytes 7684
  505.7 33.3 %collective-permute-start.4 = (bf16[640,1024]{1,0:T(8,128)(2,1)S(1)}, bf16[640,1024]{1,0:T(8,128)(2,1)S(1)}, u32[]{:S(2)}, u32[]{:S(2)}) collective-permute-start(bf16[640,1024]{1,0:T(8,128)(2,1)S(1)} %add_convert_fusion.2), channel_id=1, source_target_pairs={{16,0},{17,1},{18,2},{19,3},{20,4},{21,5},{22,6},{23,7},{24,8},{25... | collective-permute-start | bytes 3932168 | tf_op jit(solution)/shard_map/ppermute | solution.py:991
  513.6 25.3 %copy-start.2 = (f32[640,1024]{1,0:T(8,128)S(1)}, f32[640,1024]{1,0:T(8,128)}, u32[]{:S(2)}) copy-start(f32[640,1024]{1,0:T(8,128)} %copy-done.1) | copy-start | bytes 7864324
  513.6 26.8 %copy-start.15 = (f32[640,1024]{1,0:T(8,128)S(1)}, f32[640,1024]{1,0:T(8,128)}, u32[]{:S(2)}) copy-start(f32[640,1024]{1,0:T(8,128)} %get-tuple-element.453) | copy-start | bytes 7864324
  518.3 22.1 %copy-start.14 = (f32[640,1024]{1,0:T(8,128)S(1)}, f32[640,1024]{1,0:T(8,128)}, u32[]{:S(2)}) copy-start(f32[640,1024]{1,0:T(8,128)} %copy-done.13) | copy-start | bytes 7864324
  546.2 42.3 %all-to-all-start.9 = ((bf16[8,96,1024]{2,1,0:T(8,128)(2,1)}), bf16[8,96,1024]{2,1,0:T(8,128)(2,1)}, u32[]{:S(2)}, u32[]{:S(2)}) async-start(bf16[8,96,1024]{2,1,0:T(8,128)(2,1)} %bitcast.253), calls=%async_computation.9 | async-start | bytes 3145728 | tf_op jit(solution)/shard_map/all_to_all | solution.py:530
  552.5 46.1 %collective-permute-start.5 = (bf16[640,1024]{1,0:T(8,128)(2,1)}, bf16[640,1024]{1,0:T(8,128)(2,1)}, u32[]{:S(2)}, u32[]{:S(2)}) collective-permute-start(bf16[640,1024]{1,0:T(8,128)(2,1)} %get-tuple-element.224), channel_id=1, source_target_pairs={{16,0},{17,1},{18,2},{19,3},{20,4},{21,5},{22,6},{23,7},{24,8},{25... | collective-permute-start | bytes 3932168 | tf_op jit(solution)/shard_map/ppermute | solution.py:996
  560.8 31.9 %copy-start.75 = (f32[640]{0:T(1024)S(1)}, f32[640]{0:T(1024)}, u32[]{:S(2)}) copy-start(f32[640]{0:T(1024)} %copy-done.74) | copy-start | bytes 7684
  588.4 55.5 %all-to-all-start.8 = ((bf16[8,104,1024]{2,1,0:T(8,128)(2,1)}), bf16[8,104,1024]{2,1,0:T(8,128)(2,1)}, u32[]{:S(2)}, u32[]{:S(2)}) async-start(bf16[8,104,1024]{2,1,0:T(8,128)(2,1)} %bitcast.252), calls=%async_computation.8 | async-start | bytes 3407872 | tf_op jit(solution)/shard_map/all_to_all | solution.py:530
  598.7 45.3 %collective-permute-start.6 = (bf16[640,1024]{1,0:T(8,128)(2,1)}, bf16[640,1024]{1,0:T(8,128)(2,1)}, u32[]{:S(2)}, u32[]{:S(2)}) collective-permute-start(bf16[640,1024]{1,0:T(8,128)(2,1)} %get-tuple-element.229), channel_id=1, source_target_pairs={{16,0},{17,1},{18,2},{19,3},{20,4},{21,5},{22,6},{23,7},{24,8},{25... | collective-permute-start | bytes 3932168 | tf_op jit(solution)/shard_map/ppermute | solution.py:1018
  643.9 60.3 %all-to-all-start.10 = ((bf16[8,96,1024]{2,1,0:T(8,128)(2,1)}), bf16[8,96,1024]{2,1,0:T(8,128)(2,1)}, u32[]{:S(2)}, u32[]{:S(2)}) async-start(bf16[8,96,1024]{2,1,0:T(8,128)(2,1)} %bitcast.260), calls=%async_computation.10 | async-start | bytes 3145728 | tf_op jit(solution)/shard_map/all_to_all | solution.py:530
  655.8 48.4 %collective-permute-start.7 = (bf16[512,2048]{1,0:T(8,128)(2,1)}, bf16[512,2048]{1,0:T(8,128)(2,1)}, u32[]{:S(2)}, u32[]{:S(2)}) collective-permute-start(bf16[512,2048]{1,0:T(8,128)(2,1)} %get-tuple-element.433), channel_id=1, source_target_pairs={{0,1},{1,0},{2,3},{3,2},{4,5},{5,4},{6,7},{7,6},{8,9},{9,8},{10,11... | collective-permute-start | bytes 6291464 | tf_op jit(solution)/shard_map/ppermute | solution.py:757
  704.2 47.5 %all-to-all-start.11 = ((bf16[8,104,1024]{2,1,0:T(8,128)(2,1)}), bf16[8,104,1024]{2,1,0:T(8,128)(2,1)}, u32[]{:S(2)}, u32[]{:S(2)}) async-start(bf16[8,104,1024]{2,1,0:T(8,128)(2,1)} %bitcast.256), calls=%async_computation.11 | async-start | bytes 3407872 | tf_op jit(solution)/shard_map/all_to_all | solution.py:530
  709.1 85.9 %reduce-scatter.4.cloned.1.call-start = ((), (), s32[]{:S(2)}) async-start(), calls=%async_computation.15 | async-start | bytes 2359296 | tf_op jit(solution)/shard_map/reduce_scatter | solution.py:772
  709.4 42.7 %copy-start.79 = (f32[640]{0:T(1024)}, f32[640]{0:T(1024)S(1)}, u32[]{:S(2)}) copy-start(f32[640]{0:T(1024)S(1)} %subtract_multiply_fusion) | copy-start | bytes 7684
  717.4 34.3 %collective-permute-start.8 = (bf16[256,2816]{1,0:T(8,128)(2,1)}, bf16[256,2816]{1,0:T(8,128)(2,1)}, u32[]{:S(2)}, u32[]{:S(2)}) collective-permute-start(bf16[256,2816]{1,0:T(8,128)(2,1)} %convolution_convert_fusion.1), channel_id=1, source_target_pairs={{0,1},{1,0},{2,3},{3,2},{4,5},{5,4},{6,7},{7,6},{8,9},{9,8},{10,11... | collective-permute-start | bytes 4325384 | tf_op jit(solution)/shard_map/ppermute | solution.py:1074
  751.7 71.5 %all-gather.4.cloned.1.call-start = ((), (), s32[]{:S(2)}) async-start(), calls=%async_computation.16 | async-start | bytes 2359296 | tf_op jit(solution)/shard_map/all_gather | solution.py:776
  757.8 37.1 %collective-permute-start.9 = (bf16[256,2816]{1,0:T(8,128)(2,1)S(1)}, bf16[256,2816]{1,0:T(8,128)(2,1)}, u32[]{:S(2)}, u32[]{:S(2)}) collective-permute-start(bf16[256,2816]{1,0:T(8,128)(2,1)S(1)} %slice.237), channel_id=1, source_target_pairs={{0,1},{1,0},{2,3},{3,2},{4,5},{5,4},{6,7},{7,6},{8,9},{9,8},{10,11... | collective-permute-start | bytes 4325384 | tf_op jit(solution)/shard_map/ppermute | solution.py:1074
  795.0 19.7 %copy-start.38 = (bf16[640,8,2,64]{0,3,2,1:T(8,128)(2,1)S(1)}, bf16[640,8,2,64]{0,3,2,1:T(8,128)(2,1)}, u32[]{:S(2)}) copy-start(bf16[640,8,2,64]{0,3,2,1:T(8,128)(2,1)} %copy.80) | copy-start | bytes 3932164
  795.0 138.2 %reduce-scatter.6.cloned.1.call-start = ((), (), s32[]{:S(2)}) async-start(), calls=%async_computation.17 | async-start | bytes 3538944 | tf_op jit(solution)/shard_map/reduce_scatter | solution.py:772
  795.0 19.6 %collective-permute-start.10 = (bf16[144,2816]{1,0:T(8,128)(2,1)}, bf16[144,2816]{1,0:T(8,128)(2,1)}, u32[]{:S(2)}, u32[]{:S(2)}) collective-permute-start(bf16[144,2816]{1,0:T(8,128)(2,1)} %slice.238), channel_id=1, source_target_pairs={{0,1},{1,0},{2,3},{3,2},{4,5},{5,4},{6,7},{7,6},{8,9},{9,8},{10,11... | collective-permute-start | bytes 2433032 | tf_op jit(solution)/shard_map/ppermute | solution.py:1074
  823.3 109.9 %reduce-scatter.8.cloned.1.call-start = ((), (), s32[]{:S(2)}) async-start(), calls=%async_computation.18 | async-start | bytes 6193152 | tf_op jit(solution)/shard_map/reduce_scatter | solution.py:772
  828.3 24.4 %collective-permute-start.11 = (bf16[176,2816]{1,0:T(8,128)(2,1)}, bf16[176,2816]{1,0:T(8,128)(2,1)}, u32[]{:S(2)}, u32[]{:S(2)}) collective-permute-start(bf16[176,2816]{1,0:T(8,128)(2,1)} %slice.239), channel_id=1, source_target_pairs={{0,1},{1,0},{2,3},{3,2},{4,5},{5,4},{6,7},{7,6},{8,9},{9,8},{10,11... | collective-permute-start | bytes 2973704 | tf_op jit(solution)/shard_map/ppermute | solution.py:1074
  861.4 143.7 %all-gather.6.cloned.1.call-start = ((), (), s32[]{:S(2)}) async-start(), calls=%async_computation.19 | async-start | bytes 4866048 | tf_op jit(solution)/shard_map/all_gather | solution.py:776
  861.7 19.1 %collective-permute-start.12 = (bf16[128,2816]{1,0:T(8,128)(2,1)}, bf16[128,2816]{1,0:T(8,128)(2,1)}, u32[]{:S(2)}, u32[]{:S(2)}) collective-permute-start(bf16[128,2816]{1,0:T(8,128)(2,1)} %slice.240), channel_id=1, source_target_pairs={{0,1},{1,0},{2,3},{3,2},{4,5},{5,4},{6,7},{7,6},{8,9},{9,8},{10,11... | collective-permute-start | bytes 2162696 | tf_op jit(solution)/shard_map/ppermute | solution.py:1074
  890.6 24.8 %collective-permute-start.14 = (bf16[352,1024]{1,0:T(8,128)(2,1)S(1)}, bf16[352,1024]{1,0:T(8,128)(2,1)S(1)}, u32[]{:S(2)}, u32[]{:S(2)}) collective-permute-start(bf16[352,1024]{1,0:T(8,128)(2,1)S(1)} %slice.242), channel_id=1, source_target_pairs={{0,1},{1,0},{2,3},{3,2},{4,5},{5,4},{6,7},{7,6},{8,9},{9,8},{10,11... | collective-permute-start | bytes 2162696 | tf_op jit(solution)/shard_map/ppermute | solution.py:1074
  891.6 23.8 %collective-permute-start.13 = (bf16[64,2816]{1,0:T(8,128)(2,1)S(1)}, bf16[64,2816]{1,0:T(8,128)(2,1)S(1)}, u32[]{:S(2)}, u32[]{:S(2)}) collective-permute-start(bf16[64,2816]{1,0:T(8,128)(2,1)S(1)} %copy-done.57), channel_id=1, source_target_pairs={{0,1},{1,0},{2,3},{3,2},{4,5},{5,4},{6,7},{7,6},{8,9},{9,8},{10,11... | collective-permute-start | bytes 1081352 | tf_op jit(solution)/shard_map/ppermute | solution.py:1074
  915.4 17.8 %collective-permute-start.15 = (bf16[384,1024]{1,0:T(8,128)(2,1)S(1)}, bf16[384,1024]{1,0:T(8,128)(2,1)}, u32[]{:S(2)}, u32[]{:S(2)}) collective-permute-start(bf16[384,1024]{1,0:T(8,128)(2,1)S(1)} %slice.243), channel_id=1, source_target_pairs={{0,1},{1,0},{2,3},{3,2},{4,5},{5,4},{6,7},{7,6},{8,9},{9,8},{10,11... | collective-permute-start | bytes 2359304 | tf_op jit(solution)/shard_map/ppermute | solution.py:1074
  937.3 11.8 %collective-permute-start.16 = (bf16[64,4224]{1,0:T(8,128)(2,1)}, bf16[64,4224]{1,0:T(8,128)(2,1)}, u32[]{:S(2)}, u32[]{:S(2)}) collective-permute-start(bf16[64,4224]{1,0:T(8,128)(2,1)} %constant_dynamic-slice_fusion), channel_id=1, source_target_pairs={{0,1},{1,0},{2,3},{3,2},{4,5},{5,4},{6,7},{7,6},{8,9},{9,8},{10,11... | collective-permute-start | bytes 1622024 | tf_op jit(solution)/shard_map/ppermute | solution.py:757
  969.6 28.5 %collective-permute-start.17 = (bf16[672,1024]{1,0:T(8,128)(2,1)}, bf16[672,1024]{1,0:T(8,128)(2,1)S(1)}, u32[]{:S(2)}, u32[]{:S(2)}) collective-permute-start(bf16[672,1024]{1,0:T(8,128)(2,1)} %slice.244), channel_id=1, source_target_pairs={{0,1},{1,0},{2,3},{3,2},{4,5},{5,4},{6,7},{7,6},{8,9},{9,8},{10,11... | collective-permute-start | bytes 4128776 | tf_op jit(solution)/shard_map/ppermute | solution.py:1074
  (107 other events, 594.3 us)
Sparse Core Ops, SparseCore 0:
  751.8 38.5 reduce-scatter.3
  795.1 28.1 all-gather.3
  825.6 39.8 reduce-scatter.5
  868.2 61.4 reduce-scatter.7
  951.3 47.9 all-gather.5

commit v3 on v2

--- a/solution.py
+++ b/solution.py
@@ -774,6 +774,30 @@
 
 def expert_gather(rows):
     return lax.all_gather(rows, "expert", axis=0, tiled=True)
+
+
+def widen_kernel(part_ref, *refs):
+    refs[-1][...] = part_ref[...].astype(F32)
+
+
+def interleave(part, place, whole=None):
+    rows = part.shape[0]
+    half = D // 2
+    operands = [part] if whole is None else [part, whole]
+    specs = [pl.BlockSpec((rows, half), lambda step: (0, step))]
+    if whole is not None:
+        specs.append(pl.BlockSpec(memory_space=pl.ANY))
+    return pl.pallas_call(
+        widen_kernel,
+        grid=(3,),
+        in_specs=specs,
+        out_specs=pl.BlockSpec((rows, half), lambda step: (0, 2 * step + place)),
+        out_shape=jax.ShapeDtypeStruct((rows, 3 * D), F32),
+        input_output_aliases={} if whole is None else {1: 0},
+        compiler_params=pltpu.CompilerParams(vmem_limit_bytes=VMEM_LIMIT),
+        cost_estimate=pl.CostEstimate(flops=0, bytes_accessed=9 * rows * D, transcendentals=0),
+        name="interleave",
+    )(*operands)
 
 
 def together(*values):
@@ -1007,10 +1031,6 @@
     sent = spread(
         (enc_gates[0] * grad_encoded).astype(BF16), (enc_gates[1] * grad_encoded).astype(BF16)
     )
-    arrived_three = [
-        exchange(jnp.where(decoder, produced, part), experts)
-        for produced, part in zip(produced_two, sent)
-    ]
     normed_sharded = jnp.swapaxes(
         normed_in.reshape(row_count, 2, lax.axis_size("expert"), -1), 1, 2
     ).reshape(row_count, D)
@@ -1019,9 +1039,9 @@
     grad_proj = dot_tn(
         jnp.where(decoder, rounded_half, memory), jnp.where(decoder, grad_cross_query, back_keys)
     ).astype(BF16)
-    arrived_three[0], normed_sharded, grad_proj = together(
-        arrived_three[0], normed_sharded, grad_proj
-    )
+    sent = [jnp.where(decoder, produced, part) for produced, part in zip(produced_two, sent)]
+    sent[1], normed_sharded, grad_proj = together(sent[1], normed_sharded, grad_proj)
+    arrived_three = [exchange(part, experts) for part in sent]
     flags = jnp.stack([decoder.astype(jnp.int32), group])
     scales = jnp.where(decoder, arrived_gates, 1.0)[:, None]
     most = max(part.shape[0] for part in arrived_one)
@@ -1060,8 +1080,8 @@
     ]
     first_group = group == 0
     half_ff = FF // 2
-    in_cuts = (0, 256, 512, 656, 832, 960, D)
-    out_cuts = (0, 352, 736, half_ff)
+    in_cuts = (0, 208, 464, 608, 784, 928, D)
+    out_cuts = (0, 256, 608, half_ff)
 
     def cut(values, cuts):
         return [[values[first:last]] for first, last in zip(cuts[:-1], cuts[1:])]
@@ -1143,15 +1163,17 @@
     )
     late_second = expert_scatter(late_second)
     keep_in = dot_tn(expert_rows, keep_halves)
-    keep_in, gots, sends[5], kept, arrived_three = together(
-        keep_in, gots, sends[5], kept, arrived_three
-    )
+    keep_in, gots, late_first, sends[5], kept, arrived_three = together(
+        keep_in, gots, late_first, sends[5], kept, arrived_three
+    )
+    late_first = group_swap(late_first, group)
     actives, expert_grad_rows = kept
     send_out = dot_tn(
         jnp.where(first_group, actives[:, half_ff:], actives[:, :half_ff]), expert_grad_rows
     ).astype(BF16)
     out_sends = cut(send_out, out_cuts)
-    sends[5], out_sends[0] = together(sends[5], out_sends[0])
+    sends[5], out_sends[0], late_first = together(sends[5], out_sends[0], late_first)
+    late_first = expert_gather(late_first)
     gots.append(swapped(sends[5] + out_sends[0]))
     decoded = (
         second_half
@@ -1166,34 +1188,24 @@
     keep_out = dot_tn(
         jnp.where(first_group, actives[:, :half_ff], actives[:, half_ff:]), expert_grad_rows
     )
-    late_first, keep_out, gots = together(late_first, keep_out, gots)
-    late_first, late_second, gots, out_sends = together(late_first, late_second, gots, out_sends)
-    late = group_swap(jnp.concatenate([late_first, late_second], axis=1), group)
-    late, out_sends = together(late, out_sends)
-    late = expert_gather(late)
+    late_second, keep_out, gots, out_sends = together(late_second, keep_out, gots, out_sends)
+    late_second = group_swap(late_second, group)
+    late_second, out_sends = together(late_second, out_sends)
+    late_second = expert_gather(late_second)
     gots.append(swapped(out_sends[2]))
     got_in = [part[0] for part in gots[: len(sends)]]
     got_out = [gots[5][1], gots[6][0], gots[7][0]]
     grad_expert_in = keep_in + jnp.concatenate(got_in).astype(F32)
     grad_expert_out = keep_out + jnp.concatenate(got_out).astype(F32)
-    half_columns = D // 2
-    grad_qkv = jnp.concatenate(
-        [
-            late[:, first + half * part : first + half * part + half_columns]
-            for part in range(3)
-            for first, half in ((0, half_columns), (3 * half_columns, half_columns))
-        ],
-        axis=1,
-    ).astype(F32)
-    small = late[:, 3 * D : 3 * D + 128].astype(F32)
+    small = late_second[:, 3 * D // 2 : 3 * D // 2 + 128].astype(F32)
     small_table = small[: H * NBKT // 2, experts + 3].reshape(H // 2, NBKT)
     return (
         result[None],
         grad_starts.astype(BF16)[None],
         small[:, experts : experts + 3].T[None],
         small_table[None],
-        grad_qkv[None],
-        late[:, 3 * D + 128 :].astype(F32)[None],
+        interleave(late_second, 1, interleave(late_first, 0))[None],
+        late_second[:, 3 * D // 2 + 128 :].astype(F32)[None],
         early[:, :D].astype(F32)[None],
         early[:, D:].astype(F32)[None],
         small[:, :experts][None],

time: 1040 us -> 1040 us (level)
  waiting for transfers between devices: 270 us -> 256 us
    ppermute x1, waiting for transfers between devices: 0.01 us -> 23.6 us  [per_device(): back_keys = lax.ppermute(grad_memory_keys, 'half', backward)]
    all_to_all x12, waiting for transfers between devices: 118 us -> 94.9 us  [exchange(): lax.all_to_all(parts, 'expert', split_axis=0, concat_axis=0, tiled=True)]
    unnamed x264 -> x240, local copies, waits for them, and re-layouts: 29.9 us -> 23 us
  transfers between devices with their start and end apart: 35 -> 37, of which waited for: 21 -> 23; matrix products, arithmetic and copies ran while one was open for 24% -> 26% of each run, Pallas kernels for 23% -> 23%
where the time goes in v3:
time: 1040 us; the launch traced here: 1020 us
  Pallas kernels  281 us (27%)
  waiting for transfers between devices  256 us (25%)
  matrix products  234 us (22%)
  starting transfers between devices  85.7 us (8%)
  other arithmetic  73.8 us (7%)
  local copies, waits for them, and re-layouts  46.5 us (4%)
  blocking collectives  30.6 us (3%)
  between operations  16.2 us (2%)
    dot_general x32, matrix products, dot(): return jnp.dot(a, b, preferred_element_type=F32)  119 us
    all_to_all x12, waiting for transfers between devices, exchange(): lax.all_to_all(parts, 'expert', split_axis=0, concat_axis=0, tiled=True)  94.9 us
    pallas_call x2, Pallas kernels, expert_back(): pl.pallas_call(partial(expert_back_kernel, count=rows), grid_spec=pltpu.P...  80.5 us
    dot_general x10, matrix products, dot_tn(): lax.dot_general(a, b, (((0,), (0,)), ((), ())), preferred_element_type=F32)  76.8 us
    pallas_call x5, Pallas kernels, pair_call(): pl.pallas_call(kernel, grid_spec=pltpu.PrefetchScalarGridSpec(num_scalar_...  75.8 us
    pallas_call x2, Pallas kernels, expert_both(): pl.pallas_call(expert_both_kernel, grid=(tiles,), in_specs=[whole, whole]...  74.3 us
    all_to_all x12, starting transfers between devices, exchange(): lax.all_to_all(parts, 'expert', split_axis=0, concat_axis=0, tiled=True)  56.5 us
    ppermute x9, waiting for transfers between devices, swapped(): return [lax.ppermute(part, 'group', SWAP) for part in parts]  52.4 us
  transfers between devices with their start and end apart: 37, of which 23 were waited for; matrix products, arithmetic and copies ran while one was open for 26% of the time, Pallas kernels for 23%

profile of v3, /device:TPU:0, one launch (start us, length us, event | category | flops | bytes accessed | tf_op | source)
XLA Modules:
  0.0 1024.3 jit_solution(10963176706610857324)
XLA Ops:
  15.3 8.7 fusion.4.q_ref.k_ref.v_ref
  24.0 18.5 %self_attend_kernel.1 = (bf16[640,1024]{1,0:T(8,128)(2,1)}, f32[8,2,640]{2,1,0:T(2,128)}) custom-call(s32[2]{0:T(128)} %pad_add_fusion.place_ref, bf16[640,3072]{1,0:T(8,128)(2,1)} %fusion.4.q_ref.k_ref.v_ref, bf16[640,3072]{1,0:T(8,128)(2,1)} %fusion.4.q_ref.k_ref.v_ref, bf16[640,3072]{1,0:T(8,128)(2,1)} %fusion.4.q_ref.k_ref.v_ref, ...), custom_call_target="tpu_custom_call" | custom-call | flops 1677721600 | bytes 10485760 | tf_op jit(solution)/shard_map/self_attend_kernel/pallas_call | solution.py:459
  51.6 6.3 all-to-all-start
  61.9 33.9 %all-to-all-done = bf16[8,96,1024]{2,1,0:T(8,128)(2,1)} async-done(((bf16[8,96,1024]{2,1,0:T(8,128)(2,1)}), bf16[8,96,1024]{2,1,0:T(8,128)(2,1)}, u32[]{:S(2)}, u32[]{:S(2)}) %all-to-all-start) | async-done | bytes 1572896 | tf_op jit(solution)/shard_map/all_to_all | solution.py:530
  106.4 21.3 %expert_forward.2 = bf16[768,1024]{1,0:T(8,128)(2,1)} custom-call(bf16[768,1024]{1,0:T(8,128)(2,1)} %bitcast.15.x_ref.g_ref.refs_0_, bf16[1024,5632]{1,0:T(8,128)(2,1)} %bitcast.273, bf16[1024,5632]{1,0:T(8,128)(2,1)} %bitcast.274, bf16[2816,1024]{1,0:T(8,128)(2,1)} %bitcast.287), custom_call_target="tpu_custom_call" | custom-call | flops 13287555072 | bytes 17301504 | tf_op jit(solution)/shard_map/expert_forward/pallas_call | solution.py:674
  127.7 9.3 collective-permute-done
  150.0 22.0 %expert_forward.3 = bf16[832,1024]{1,0:T(8,128)(2,1)} custom-call(bf16[832,1024]{1,0:T(8,128)(2,1)} %bitcast.22.x_ref.g_ref.refs_0_, bf16[1024,5632]{1,0:T(8,128)(2,1)} %bitcast.275, bf16[1024,5632]{1,0:T(8,128)(2,1)} %bitcast.276, bf16[2816,1024]{1,0:T(8,128)(2,1)} %bitcast.288), custom_call_target="tpu_custom_call" | custom-call | flops 14394851328 | bytes 17301504 | tf_op jit(solution)/shard_map/expert_forward/pallas_call | solution.py:674
  171.9 6.4 collective-permute-done.1
  198.0 19.7 %collective-permute-done.2 = bf16[320,2048]{1,0:T(8,128)(2,1)} collective-permute-done((bf16[320,2048]{1,0:T(8,128)(2,1)}, bf16[320,2048]{1,0:T(8,128)(2,1)}, u32[]{:S(2)}, u32[]{:S(2)}) %collective-permute-start.2) | collective-permute-done | bytes 1310752 | tf_op jit(solution)/shard_map/ppermute | solution.py:917
  217.7 10.2 all-to-all-done.3
  231.9 5.7 multiply_reduce_fusion.9
  248.1 19.5 %collective-permute-done.3 = bf16[640,1024]{1,0:T(8,128)(2,1)S(1)} collective-permute-done((bf16[640,1024]{1,0:T(8,128)(2,1)S(1)}, bf16[640,1024]{1,0:T(8,128)(2,1)S(1)}, u32[]{:S(2)}, u32[]{:S(2)}) %collective-permute-start.3) | collective-permute-done | bytes 1310752 | tf_op jit(solution)/shard_map/ppermute | solution.py:926
  271.8 9.9 cross_attend_kernel.1
  297.5 33.3 %all-to-all-done.5 = bf16[8,96,1024]{2,1,0:T(8,128)(2,1)} async-done(((bf16[8,96,1024]{2,1,0:T(8,128)(2,1)}), bf16[8,96,1024]{2,1,0:T(8,128)(2,1)}, u32[]{:S(2)}, u32[]{:S(2)}) %all-to-all-start.5) | async-done | bytes 1572896 | tf_op jit(solution)/shard_map/all_to_all | solution.py:530
  335.2 36.0 %expert_both.2 = (bf16[768,1024]{1,0:T(8,128)(2,1)}, bf16[768,2816]{1,0:T(8,128)(2,1)}, f32[768,1]{1,0:T(8,128)}) custom-call(bf16[768,1024]{1,0:T(8,128)(2,1)} %bitcast.30.x_ref.refs_1_, bf16[768,1024]{1,0:T(8,128)(2,1)} %bitcast.15.x_ref.g_ref.refs_0_, bf16[1024,5632]{1,0:T(8,128)(2,1)} %bitcast.277, bf16[1024,5632]{1,0:T(8,128)(2,1)} %bitcast.278, ...), custom_call_target="tpu_custom_call" | custom-call | flops 22145925120 | bytes 17301504 | tf_op jit(solution)/shard_map/expert_both/pallas_call | solution.py:692
  371.1 4.7 all-to-all-done.4
  380.3 38.4 %expert_both.3 = (bf16[832,1024]{1,0:T(8,128)(2,1)}, bf16[832,2816]{1,0:T(8,128)(2,1)}, f32[832,1]{1,0:T(8,128)}) custom-call(bf16[832,1024]{1,0:T(8,128)(2,1)} %bitcast.28.x_ref.refs_1_, bf16[832,1024]{1,0:T(8,128)(2,1)} %bitcast.22.x_ref.g_ref.refs_0_, bf16[1024,5632]{1,0:T(8,128)(2,1)} %bitcast.279, bf16[1024,5632]{1,0:T(8,128)(2,1)} %bitcast.280, ...), custom_call_target="tpu_custom_call" | custom-call | flops 23991418880 | bytes 17301504 | tf_op jit(solution)/shard_map/expert_both/pallas_call | solution.py:692
  418.7 5.0 all-to-all-start.7
  440.1 30.6 %all-gather = f32[64,400]{1,0:T(8,128)S(1)} all-gather(f32[8,400]{1,0:T(8,128)S(1)} %pad_maximum_fusion.6), channel_id=2, replica_groups=mesh['half'=2,'expert'=8,'group'=2] {'expert'}, dimensions={0}, use_global_device_ids=true | all-gather | bytes 115200 | tf_op jit(solution)/shard_map/all_gather | solution.py:952
  487.4 11.9 %cross_attend_back_kernel.1 = (bf16[640,1024]{1,0:T(8,128)(2,1)}, bf16[640,1024]{1,0:T(8,128)(2,1)}, bf16[640,1024]{1,0:T(8,128)(2,1)}) custom-call(s32[2]{0:T(128)} %pad_add_fusion.place_ref, bf16[640,1024]{1,0:T(8,128)(2,1)} %convolution_convert_fusion.15.q_ref, bf16[640,2048]{1,0:T(8,128)(2,1)} %convolution_convert_fusion.4.k_ref.v_ref, ...), custom_call_target="tpu_custom_call" | custom-call | flops 4194304000 | bytes 10485760 | tf_op jit(solution)/shard_map/cross_attend_back_kernel/pallas_call | solution.py:459
  507.0 6.6 convolution_convert_fusion.8
  513.6 4.6 convolution_convert_fusion.13
  518.2 20.4 %collective-permute-done.4 = bf16[640,1024]{1,0:T(8,128)(2,1)S(1)} collective-permute-done((bf16[640,1024]{1,0:T(8,128)(2,1)S(1)}, bf16[640,1024]{1,0:T(8,128)(2,1)S(1)}, u32[]{:S(2)}, u32[]{:S(2)}) %collective-permute-start.4) | collective-permute-done | bytes 1310752 | tf_op jit(solution)/shard_map/ppermute | solution.py:1015
  561.7 23.6 %collective-permute-done.5 = bf16[640,1024]{1,0:T(8,128)(2,1)S(1)} collective-permute-done((bf16[640,1024]{1,0:T(8,128)(2,1)}, bf16[640,1024]{1,0:T(8,128)(2,1)S(1)}, u32[]{:S(2)}, u32[]{:S(2)}) %collective-permute-start.5) | collective-permute-done | bytes 1310752 | tf_op jit(solution)/shard_map/ppermute | solution.py:1020
  588.5 4.8 all-to-all-start.8
  597.3 39.1 %expert_back.2 = (bf16[768,1024]{1,0:T(8,128)(2,1)}, bf16[2,832,1024]{2,1,0:T(8,128)(2,1)}, bf16[2,832,1024]{2,1,0:T(8,128)(2,1)}, bf16[2,832,2816]{2,1,0:T(8,12...) custom-call(s32[2]{0:T(128)} %pad_add_fusion.1.flags_ref, ...), custom_call_target="tpu_custom_call" | custom-call | flops 22145925120 | bytes 17301504 | tf_op jit(solution)/shard_map/expert_back/pallas_call | solution.py:728
  636.4 5.1 all-to-all-start.10
  649.5 41.4 %expert_back.3 = (bf16[832,1024]{1,0:T(8,128)(2,1)}, bf16[2,832,1024]{2,1,0:T(8,128)(2,1)}, bf16[2,832,1024]{2,1,0:T(8,128)(2,1)}, bf16[2,832,2816]{2,1,0:T(8,12...) custom-call(s32[2]{0:T(128)} %pad_add_fusion.1.flags_ref, ...), custom_call_target="tpu_custom_call", output_to_operand_aliasing={{1}: (8, {}), {2}: (9, {}), {3}: (10, {}), {4}: (11, {}), {... | custom-call | flops 23991418880 | bytes 17301504 | tf_op jit(solution)/shard_map/expert_back/pallas_call | solution.py:728
  690.9 5.4 collective-permute-done.7
  696.3 4.9 all-to-all-start.11
  701.5 7.4 convolution_convert_fusion.1
  710.5 9.0 convolution_convert_fusion
  729.3 8.1 collective-permute-done.8
  766.7 17.8 %self_attend_back_kernel.2 = (bf16[640,512]{1,0:T(8,128)(2,1)}, bf16[640,512]{1,0:T(8,128)(2,1)}, bf16[640,512]{1,0:T(8,128)(2,1)}, f32[4,2,1024]{2,1,0:T(2,128)}) custom-call(s32[2]{0:T(128)} %pad_add_fusion.place_ref, bf16[640,3072]{1,0:T(8,128)(2,1)} %fusion.4.q_ref.k_ref.v_ref, bf16[640,3072]{1,0:T(8,128)(2,1)} %fusion.4.q_ref.k_ref.v_ref, ...), custom_call_target="tpu_custom_call" | custom-call | flops 2097152000 | bytes 10485760 | tf_op jit(solution)/shard_map/self_attend_back_kernel/pallas_call | solution.py:459
  785.3 17.8 %self_attend_back_kernel.3 = (bf16[640,512]{1,0:T(8,128)(2,1)}, bf16[640,512]{1,0:T(8,128)(2,1)}, bf16[640,512]{1,0:T(8,128)(2,1)}, f32[4,2,1024]{2,1,0:T(2,128)}) custom-call(s32[2]{0:T(128)} %pad_add_fusion.place_ref, bf16[640,3072]{1,0:T(8,128)(2,1)} %fusion.4.q_ref.k_ref.v_ref, bf16[640,3072]{1,0:T(8,128)(2,1)} %fusion.4.q_ref.k_ref.v_ref, ...), custom_call_target="tpu_custom_call" | custom-call | flops 2097152000 | bytes 10485760 | tf_op jit(solution)/shard_map/self_attend_back_kernel/pallas_call | solution.py:459
  804.3 5.5 convolution_convert_fusion.3
  812.2 4.6 fusion.168
  835.0 6.3 collective-permute-done.11
  844.1 5.8 pad_maximum_fusion
  852.0 17.7 %convolution_bitcast_fusion = f32[1024,2816]{1,0:T(8,128)} fusion(bf16[2,832,1024]{2,1,0:T(8,128)(2,1)} %get-tuple-element.238, bf16[2,832,2816]{2,1,0:T(8,128)(2,1)} %get-tuple-element.239), kind=kOutput, calls=%fused_computation.1 | convolution fusion | flops 9596567552 | bytes 24313856 | tf_op jit(solution)/shard_map/dot_general | solution.py:92
  870.2 10.0 fusion.33
  884.8 4.6 fusion.25
  900.9 7.4 select_convert_fusion
  908.4 14.3 %collective-permute-done.15 = bf16[256,1024]{1,0:T(8,128)(2,1)} collective-permute-done((bf16[256,1024]{1,0:T(8,128)(2,1)}, bf16[256,1024]{1,0:T(8,128)(2,1)}, u32[]{:S(2)}, u32[]{:S(2)}) %collective-permute-start.15) | collective-permute-done | bytes 524320 | tf_op jit(solution)/shard_map/ppermute | solution.py:1094
  923.4 11.8 %fusion.7 = f32[1408,1024]{1,0:T(8,128)} fusion(bf16[1664,1024]{1,0:T(8,128)(2,1)} %bitcast.298, bf16[1664,2816]{1,0:T(8,128)(2,1)} %bitcast.296, pred[]{:T(512)S(6)} %eq.603), kind=kOutput, calls=%fused_computation.18 | convolution fusion | flops 4800626688 | bytes 18546688 | tf_op jit(solution)/shard_map/dot_general | solution.py:92
  969.5 11.6 %add_bitcast_fusion = f32[1,1,1024,2816]{3,2,1,0:T(8,128)} fusion(f32[1024,2816]{1,0:T(8,128)} %convolution_bitcast_fusion, bf16[1024,2816]{1,0:T(8,128)(2,1)} %constant_dynamic-update-slice_fusion.9), kind=kLoop, calls=%fused_computation | loop fusion | flops 5767168 | bytes 28835840 | tf_op jit(solution)/shard_map/broadcast_in_dim | solution.py:1212
  981.1 18.9 %collective-permute-done.18 = bf16[800,1024]{1,0:T(8,128)(2,1)} collective-permute-done((bf16[800,1024]{1,0:T(8,128)(2,1)}, bf16[800,1024]{1,0:T(8,128)(2,1)}, u32[]{:S(2)}, u32[]{:S(2)}) %collective-permute-start.18) | collective-permute-done | bytes 1638432 | tf_op jit(solution)/shard_map/ppermute | solution.py:1094
  1000.0 7.4 add_bitcast_fusion.1
  (456 shorter events, 314.9 us)
Async XLA Ops:
  7.2 35.3 %copy-start = (bf16[1,1024,1024]{2,1,0:T(8,128)(2,1)S(1)}, bf16[1,1024,1024]{2,1,0:T(8,128)(2,1)}, u32[]{:S(2)}) copy-start(bf16[1,1024,1024]{2,1,0:T(8,128)(2,1)} %param.55) | copy-start | bytes 6291460
  12.3 34.1 %copy-start.58 = (f32[1,1,1024]{2,0,1:T(1,128)}, f32[1,1,1024]{2,0,1:T(1,128)S(1)}, u32[]{:S(2)}) copy-start(f32[1,1,1024]{2,0,1:T(1,128)S(1)} %get-tuple-element.432) | copy-start | bytes 12292
  51.6 44.2 %all-to-all-start = ((bf16[8,96,1024]{2,1,0:T(8,128)(2,1)}), bf16[8,96,1024]{2,1,0:T(8,128)(2,1)}, u32[]{:S(2)}, u32[]{:S(2)}) async-start(bf16[8,96,1024]{2,1,0:T(8,128)(2,1)} %bitcast.241), calls=%async_computation | async-start | bytes 3145728 | tf_op jit(solution)/shard_map/all_to_all | solution.py:530
  95.8 45.0 %all-to-all-start.2 = ((bf16[8,104,1024]{2,1,0:T(8,128)(2,1)}), bf16[8,104,1024]{2,1,0:T(8,128)(2,1)}, u32[]{:S(2)}, u32[]{:S(2)}) async-start(bf16[8,104,1024]{2,1,0:T(8,128)(2,1)} %bitcast.236), calls=%async_computation.2 | async-start | bytes 3407872 | tf_op jit(solution)/shard_map/all_to_all | solution.py:530
  103.8 33.2 %collective-permute-start = (bf16[352,2048]{1,0:T(8,128)(2,1)}, bf16[352,2048]{1,0:T(8,128)(2,1)}, u32[]{:S(2)}, u32[]{:S(2)}) collective-permute-start(bf16[352,2048]{1,0:T(8,128)(2,1)} %get-tuple-element.183), channel_id=1, source_target_pairs={{0,16},{1,17},{2,18},{3,19},{4,20},{5,21},{6,22},{7,23},{8,24},{9,... | collective-permute-start | bytes 4325384 | tf_op jit(solution)/shard_map/ppermute | solution.py:912
  140.8 42.1 %all-to-all-start.1 = ((bf16[8,96,1024]{2,1,0:T(8,128)(2,1)}), bf16[8,96,1024]{2,1,0:T(8,128)(2,1)}, u32[]{:S(2)}, u32[]{:S(2)}) async-start(bf16[8,96,1024]{2,1,0:T(8,128)(2,1)} %bitcast.239), calls=%async_computation.1 | async-start | bytes 3145728 | tf_op jit(solution)/shard_map/all_to_all | solution.py:530
  145.1 33.3 %collective-permute-start.1 = (bf16[352,2048]{1,0:T(8,128)(2,1)}, bf16[352,2048]{1,0:T(8,128)(2,1)}, u32[]{:S(2)}, u32[]{:S(2)}) collective-permute-start(bf16[352,2048]{1,0:T(8,128)(2,1)} %get-tuple-element.186), channel_id=1, source_target_pairs={{0,16},{1,17},{2,18},{3,19},{4,20},{5,21},{6,22},{7,23},{8,24},{9,... | collective-permute-start | bytes 4325384 | tf_op jit(solution)/shard_map/ppermute | solution.py:912
  182.9 45.0 %all-to-all-start.3 = ((bf16[8,104,1024]{2,1,0:T(8,128)(2,1)}), bf16[8,104,1024]{2,1,0:T(8,128)(2,1)}, u32[]{:S(2)}, u32[]{:S(2)}) async-start(bf16[8,104,1024]{2,1,0:T(8,128)(2,1)} %bitcast.235), calls=%async_computation.3 | async-start | bytes 3407872 | tf_op jit(solution)/shard_map/all_to_all | solution.py:530
  187.3 30.4 %collective-permute-start.2 = (bf16[320,2048]{1,0:T(8,128)(2,1)}, bf16[320,2048]{1,0:T(8,128)(2,1)}, u32[]{:S(2)}, u32[]{:S(2)}) collective-permute-start(bf16[320,2048]{1,0:T(8,128)(2,1)} %pad_maximum_fusion.1), channel_id=1, source_target_pairs={{0,16},{1,17},{2,18},{3,19},{4,20},{5,21},{6,22},{7,23},{8,24},{9,... | collective-permute-start | bytes 3932168 | tf_op jit(solution)/shard_map/ppermute | solution.py:917
  189.7 282.4 %copy-start.82 = (s32[640]{0:T(1024)}, s32[640]{0:T(1024)S(1)}, u32[]{:S(2)}) copy-start(s32[640]{0:T(1024)S(1)} %get-tuple-element.408) | copy-start | bytes 7684
  189.7 285.4 %copy-start.56 = (s32[640]{0:T(1024)}, s32[640]{0:T(1024)S(1)}, u32[]{:S(2)}) copy-start(s32[640]{0:T(1024)S(1)} %get-tuple-element.409) | copy-start | bytes 7684
  237.9 29.7 %collective-permute-start.3 = (bf16[640,1024]{1,0:T(8,128)(2,1)S(1)}, bf16[640,1024]{1,0:T(8,128)(2,1)S(1)}, u32[]{:S(2)}, u32[]{:S(2)}) collective-permute-start(bf16[640,1024]{1,0:T(8,128)(2,1)S(1)} %multiply_convert_fusion.3), channel_id=1, source_target_pairs={{0,16},{1,17},{2,18},{3,19},{4,20},{5,21},{6,22},{7,23},{8,24},{9,... | collective-permute-start | bytes 3932168 | tf_op jit(solution)/shard_map/ppermute | solution.py:926
  286.0 197.1 %copy-start.54 = (f32[640]{0:T(1024)}, f32[640]{0:T(1024)S(1)}, u32[]{:S(2)}) copy-start(f32[640]{0:T(1024)S(1)} %add_rsqrt_fusion) | copy-start | bytes 7684
  288.7 42.1 %all-to-all-start.5 = ((bf16[8,96,1024]{2,1,0:T(8,128)(2,1)}), bf16[8,96,1024]{2,1,0:T(8,128)(2,1)}, u32[]{:S(2)}, u32[]{:S(2)}) async-start(bf16[8,96,1024]{2,1,0:T(8,128)(2,1)} %bitcast.242), calls=%async_computation.5 | async-start | bytes 3145728 | tf_op jit(solution)/shard_map/all_to_all | solution.py:530
  330.8 45.0 %all-to-all-start.4 = ((bf16[8,104,1024]{2,1,0:T(8,128)(2,1)}), bf16[8,104,1024]{2,1,0:T(8,128)(2,1)}, u32[]{:S(2)}, u32[]{:S(2)}) async-start(bf16[8,104,1024]{2,1,0:T(8,128)(2,1)} %bitcast.237), calls=%async_computation.4 | async-start | bytes 3407872 | tf_op jit(solution)/shard_map/all_to_all | solution.py:530
  375.8 42.9 %all-to-all-start.6 = ((bf16[8,96,1024]{2,1,0:T(8,128)(2,1)}), bf16[8,96,1024]{2,1,0:T(8,128)(2,1)}, u32[]{:S(2)}, u32[]{:S(2)}) async-start(bf16[8,96,1024]{2,1,0:T(8,128)(2,1)} %bitcast.240), calls=%async_computation.6 | async-start | bytes 3145728 | tf_op jit(solution)/shard_map/all_to_all | solution.py:530
  418.7 53.4 %all-to-all-start.7 = ((bf16[8,104,1024]{2,1,0:T(8,128)(2,1)}), bf16[8,104,1024]{2,1,0:T(8,128)(2,1)}, u32[]{:S(2)}, u32[]{:S(2)}) async-start(bf16[8,104,1024]{2,1,0:T(8,128)(2,1)} %bitcast.233), calls=%async_computation.7 | async-start | bytes 3407872 | tf_op jit(solution)/shard_map/all_to_all | solution.py:530
  428.0 50.4 %copy-start.64 = (f32[640]{0:T(1024)}, f32[640]{0:T(1024)S(1)}, u32[]{:S(2)}) copy-start(f32[640]{0:T(1024)S(1)} %get-tuple-element.433) | copy-start | bytes 7684
  428.0 50.4 %copy-start.66 = (f32[640]{0:T(1024)}, f32[640]{0:T(1024)S(1)}, u32[]{:S(2)}) copy-start(f32[640]{0:T(1024)S(1)} %get-tuple-element.434) | copy-start | bytes 7684
  505.4 33.3 %collective-permute-start.4 = (bf16[640,1024]{1,0:T(8,128)(2,1)S(1)}, bf16[640,1024]{1,0:T(8,128)(2,1)S(1)}, u32[]{:S(2)}, u32[]{:S(2)}) collective-permute-start(bf16[640,1024]{1,0:T(8,128)(2,1)S(1)} %add_convert_fusion.2), channel_id=1, source_target_pairs={{16,0},{17,1},{18,2},{19,3},{20,4},{21,5},{22,6},{23,7},{24,8},{25... | collective-permute-start | bytes 3932168 | tf_op jit(solution)/shard_map/ppermute | solution.py:1015
  513.6 25.1 %copy-start.2 = (f32[640,1024]{1,0:T(8,128)S(1)}, f32[640,1024]{1,0:T(8,128)}, u32[]{:S(2)}) copy-start(f32[640,1024]{1,0:T(8,128)} %copy-done.1) | copy-start | bytes 7864324
  513.6 26.5 %copy-start.13 = (f32[640,1024]{1,0:T(8,128)S(1)}, f32[640,1024]{1,0:T(8,128)}, u32[]{:S(2)}) copy-start(f32[640,1024]{1,0:T(8,128)} %get-tuple-element.439) | copy-start | bytes 7864324
  545.8 42.7 %all-to-all-start.9 = ((bf16[8,96,1024]{2,1,0:T(8,128)(2,1)}), bf16[8,96,1024]{2,1,0:T(8,128)(2,1)}, u32[]{:S(2)}, u32[]{:S(2)}) async-start(bf16[8,96,1024]{2,1,0:T(8,128)(2,1)} %bitcast.231), calls=%async_computation.9 | async-start | bytes 3145728 | tf_op jit(solution)/shard_map/all_to_all | solution.py:530
  552.2 33.1 %collective-permute-start.5 = (bf16[640,1024]{1,0:T(8,128)(2,1)}, bf16[640,1024]{1,0:T(8,128)(2,1)S(1)}, u32[]{:S(2)}, u32[]{:S(2)}) collective-permute-start(bf16[640,1024]{1,0:T(8,128)(2,1)} %get-tuple-element.215), channel_id=1, source_target_pairs={{16,0},{17,1},{18,2},{19,3},{20,4},{21,5},{22,6},{23,7},{24,8},{25... | collective-permute-start | bytes 3932168 | tf_op jit(solution)/shard_map/ppermute | solution.py:1020
  560.4 25.0 %copy-start.38 = (bf16[640,1024]{1,0:T(8,128)(2,1)S(1)}, bf16[640,1024]{1,0:T(8,128)(2,1)}, u32[]{:S(2)}) copy-start(bf16[640,1024]{1,0:T(8,128)(2,1)} %copy-done.36) | copy-start | bytes 3932164
  588.5 47.8 %all-to-all-start.8 = ((bf16[8,104,1024]{2,1,0:T(8,128)(2,1)}), bf16[8,104,1024]{2,1,0:T(8,128)(2,1)}, u32[]{:S(2)}, u32[]{:S(2)}) async-start(bf16[8,104,1024]{2,1,0:T(8,128)(2,1)} %bitcast.230), calls=%async_computation.8 | async-start | bytes 3407872 | tf_op jit(solution)/shard_map/all_to_all | solution.py:530
  596.0 146.0 %copy-start.73 = (f32[640]{0:T(1024)}, f32[640]{0:T(1024)S(1)}, u32[]{:S(2)}) copy-start(f32[640]{0:T(1024)S(1)} %subtract_multiply_fusion) | copy-start | bytes 7684
  596.0 40.4 %collective-permute-start.6 = (bf16[640,1024]{1,0:T(8,128)(2,1)}, bf16[640,1024]{1,0:T(8,128)(2,1)}, u32[]{:S(2)}, u32[]{:S(2)}) collective-permute-start(bf16[640,1024]{1,0:T(8,128)(2,1)} %get-tuple-element.221), channel_id=1, source_target_pairs={{16,0},{17,1},{18,2},{19,3},{20,4},{21,5},{22,6},{23,7},{24,8},{25... | collective-permute-start | bytes 3932168 | tf_op jit(solution)/shard_map/ppermute | solution.py:1038
  636.4 54.6 %all-to-all-start.10 = ((bf16[8,96,1024]{2,1,0:T(8,128)(2,1)}), bf16[8,96,1024]{2,1,0:T(8,128)(2,1)}, u32[]{:S(2)}, u32[]{:S(2)}) async-start(bf16[8,96,1024]{2,1,0:T(8,128)(2,1)} %bitcast.238), calls=%async_computation.10 | async-start | bytes 3145728 | tf_op jit(solution)/shard_map/all_to_all | solution.py:530
  648.0 48.3 %collective-permute-start.7 = (bf16[512,2048]{1,0:T(8,128)(2,1)}, bf16[512,2048]{1,0:T(8,128)(2,1)}, u32[]{:S(2)}, u32[]{:S(2)}) collective-permute-start(bf16[512,2048]{1,0:T(8,128)(2,1)} %get-tuple-element.419), channel_id=1, source_target_pairs={{0,1},{1,0},{2,3},{3,2},{4,5},{5,4},{6,7},{7,6},{8,9},{9,8},{10,11... | collective-permute-start | bytes 6291464 | tf_op jit(solution)/shard_map/ppermute | solution.py:757
  696.3 45.6 %all-to-all-start.11 = ((bf16[8,104,1024]{2,1,0:T(8,128)(2,1)}), bf16[8,104,1024]{2,1,0:T(8,128)(2,1)}, u32[]{:S(2)}, u32[]{:S(2)}) async-start(bf16[8,104,1024]{2,1,0:T(8,128)(2,1)} %bitcast.234), calls=%async_computation.11 | async-start | bytes 3407872 | tf_op jit(solution)/shard_map/all_to_all | solution.py:530
  701.2 83.3 %reduce-scatter.4.cloned.1.call-start = ((), (), s32[]{:S(2)}) async-start(), calls=%async_computation.15 | async-start | bytes 2359296 | tf_op jit(solution)/shard_map/reduce_scatter | solution.py:772
  708.9 28.5 %collective-permute-start.8 = (bf16[208,2816]{1,0:T(8,128)(2,1)}, bf16[208,2816]{1,0:T(8,128)(2,1)}, u32[]{:S(2)}, u32[]{:S(2)}) collective-permute-start(bf16[208,2816]{1,0:T(8,128)(2,1)} %convolution_convert_fusion.1), channel_id=1, source_target_pairs={{0,1},{1,0},{2,3},{3,2},{4,5},{5,4},{6,7},{7,6},{8,9},{9,8},{10,11... | collective-permute-start | bytes 3514376 | tf_op jit(solution)/shard_map/ppermute | solution.py:1094
  742.0 69.8 %all-gather.5.cloned.1.call-start = ((), (), s32[]{:S(2)}) async-start(), calls=%async_computation.16 | async-start | bytes 2359296 | tf_op jit(solution)/shard_map/all_gather | solution.py:776
  747.8 36.7 %collective-permute-start.9 = (bf16[256,2816]{1,0:T(8,128)(2,1)S(1)}, bf16[256,2816]{1,0:T(8,128)(2,1)}, u32[]{:S(2)}, u32[]{:S(2)}) collective-permute-start(bf16[256,2816]{1,0:T(8,128)(2,1)S(1)} %slice.213), channel_id=1, source_target_pairs={{0,1},{1,0},{2,3},{3,2},{4,5},{5,4},{6,7},{7,6},{8,9},{9,8},{10,11... | collective-permute-start | bytes 4325384 | tf_op jit(solution)/shard_map/ppermute | solution.py:1094
  784.6 85.6 %reduce-scatter.6.cloned.1.call-start = ((), (), s32[]{:S(2)}) async-start(), calls=%async_computation.17 | async-start | bytes 3538944 | tf_op jit(solution)/shard_map/reduce_scatter | solution.py:772
  784.6 19.7 %collective-permute-start.10 = (bf16[144,2816]{1,0:T(8,128)(2,1)}, bf16[144,2816]{1,0:T(8,128)(2,1)}, u32[]{:S(2)}, u32[]{:S(2)}) collective-permute-start(bf16[144,2816]{1,0:T(8,128)(2,1)} %get-tuple-element.267), channel_id=1, source_target_pairs={{0,1},{1,0},{2,3},{3,2},{4,5},{5,4},{6,7},{7,6},{8,9},{9,8},{10,11... | collective-permute-start | bytes 2433032 | tf_op jit(solution)/shard_map/ppermute | solution.py:1094
  811.8 126.5 %reduce-scatter.8.cloned.1.call-start = ((), (), s32[]{:S(2)}) async-start(), calls=%async_computation.18 | async-start | bytes 6193152 | tf_op jit(solution)/shard_map/reduce_scatter | solution.py:772
  816.9 24.4 %collective-permute-start.11 = (bf16[176,2816]{1,0:T(8,128)(2,1)}, bf16[176,2816]{1,0:T(8,128)(2,1)}, u32[]{:S(2)}, u32[]{:S(2)}) collective-permute-start(bf16[176,2816]{1,0:T(8,128)(2,1)} %slice.215), channel_id=1, source_target_pairs={{0,1},{1,0},{2,3},{3,2},{4,5},{5,4},{6,7},{7,6},{8,9},{9,8},{10,11... | collective-permute-start | bytes 2973704 | tf_op jit(solution)/shard_map/ppermute | solution.py:1094
  850.0 101.9 %all-gather.9.cloned.1.call-start = ((), (), s32[]{:S(2)}) async-start(), calls=%async_computation.20 | async-start | bytes 1769472 | tf_op jit(solution)/shard_map/all_gather | solution.py:776
  850.4 19.8 %collective-permute-start.12 = (bf16[144,2816]{1,0:T(8,128)(2,1)}, bf16[144,2816]{1,0:T(8,128)(2,1)}, u32[]{:S(2)}, u32[]{:S(2)}) collective-permute-start(bf16[144,2816]{1,0:T(8,128)(2,1)} %get-tuple-element.299), channel_id=1, source_target_pairs={{0,1},{1,0},{2,3},{3,2},{4,5},{5,4},{6,7},{7,6},{8,9},{9,8},{10,11... | collective-permute-start | bytes 2433032 | tf_op jit(solution)/shard_map/ppermute | solution.py:1094
  883.2 14.8 %collective-permute-start.13 = (bf16[64,1536]{1,0:T(8,128)(2,1)S(1)}, bf16[64,1536]{1,0:T(8,128)(2,1)S(1)}, u32[]{:S(2)}, u32[]{:S(2)}) collective-permute-start(bf16[64,1536]{1,0:T(8,128)(2,1)S(1)} %constant_dynamic-slice_fusion.1), channel_id=1, source_target_pairs={{0,1},{1,0},{2,3},{3,2},{4,5},{5,4},{6,7},{7,6},{8,9},{9,8},{10,11... | collective-permute-start | bytes 589832 | tf_op jit(solution)/shard_map/ppermute | solution.py:757
  898.8 23.9 %collective-permute-start.14 = (bf16[96,2816]{1,0:T(8,128)(2,1)}, bf16[96,2816]{1,0:T(8,128)(2,1)}, u32[]{:S(2)}, u32[]{:S(2)}) collective-permute-start(bf16[96,2816]{1,0:T(8,128)(2,1)} %slice.217), channel_id=1, source_target_pairs={{0,1},{1,0},{2,3},{3,2},{4,5},{5,4},{6,7},{7,6},{8,9},{9,8},{10,11... | collective-permute-start | bytes 1622024 | tf_op jit(solution)/shard_map/ppermute | solution.py:1094
  899.4 23.3 %collective-permute-start.15 = (bf16[256,1024]{1,0:T(8,128)(2,1)}, bf16[256,1024]{1,0:T(8,128)(2,1)}, u32[]{:S(2)}, u32[]{:S(2)}) collective-permute-start(bf16[256,1024]{1,0:T(8,128)(2,1)} %slice.218), channel_id=1, source_target_pairs={{0,1},{1,0},{2,3},{3,2},{4,5},{5,4},{6,7},{7,6},{8,9},{9,8},{10,11... | collective-permute-start | bytes 1572872 | tf_op jit(solution)/shard_map/ppermute | solution.py:1094
  908.3 99.1 %all-gather.7.cloned.1.call-start = ((), (), s32[]{:S(2)}) async-start(), calls=%async_computation.19 | async-start | bytes 3096576 | tf_op jit(solution)/shard_map/all_gather | solution.py:776
  922.7 15.6 %collective-permute-start.16 = (bf16[352,1024]{1,0:T(8,128)(2,1)}, bf16[352,1024]{1,0:T(8,128)(2,1)}, u32[]{:S(2)}, u32[]{:S(2)}) collective-permute-start(bf16[352,1024]{1,0:T(8,128)(2,1)} %slice.219), channel_id=1, source_target_pairs={{0,1},{1,0},{2,3},{3,2},{4,5},{5,4},{6,7},{7,6},{8,9},{9,8},{10,11... | collective-permute-start | bytes 2162696 | tf_op jit(solution)/shard_map/ppermute | solution.py:1094
  939.4 7.3 collective-permute-start.17
  966.8 33.2 %collective-permute-start.18 = (bf16[800,1024]{1,0:T(8,128)(2,1)}, bf16[800,1024]{1,0:T(8,128)(2,1)}, u32[]{:S(2)}, u32[]{:S(2)}) collective-permute-start(bf16[800,1024]{1,0:T(8,128)(2,1)} %slice.220), channel_id=1, source_target_pairs={{0,1},{1,0},{2,3},{3,2},{4,5},{5,4},{6,7},{7,6},{8,9},{9,8},{10,11... | collective-permute-start | bytes 4915208 | tf_op jit(solution)/shard_map/ppermute | solution.py:1094
  (100 other events, 553.0 us)
Sparse Core Ops, SparseCore 0:
  742.1 36.6 reduce-scatter.3
  784.7 27.0 all-gather.4
  814.1 39.7 reduce-scatter.5
  856.7 61.4 reduce-scatter.7
  919.7 23.3 all-gather.8
  947.7 34.0 all-gather.6

commit v4 on v3

--- a/solution.py
+++ b/solution.py
@@ -798,6 +798,42 @@
         cost_estimate=pl.CostEstimate(flops=0, bytes_accessed=9 * rows * D, transcendentals=0),
         name="interleave",
     )(*operands)
+
+
+def add_pieces_kernel(kept_ref, *refs, spans):
+    step = pl.program_id(0)
+    for piece_ref, (first, last) in zip(refs[:-1], spans):
+
+        @pl.when((step >= first) & (step < last))
+        def _():
+            refs[-1][...] = kept_ref[...] + piece_ref[...].astype(F32)
+
+
+def add_pieces(kept, pieces):
+    rows, columns = kept.shape
+    spans = []
+    specs = [pl.BlockSpec((BLOCK, columns), lambda step: (step, 0))]
+    for piece in pieces:
+        first = spans[-1][1] if spans else 0
+        last = first + piece.shape[0] // BLOCK
+        spans.append((first, last))
+
+        def place(step, first=first, last=last):
+            return jnp.clip(step - first, 0, last - first - 1), 0
+
+        specs.append(pl.BlockSpec((BLOCK, columns), place))
+    return pl.pallas_call(
+        partial(add_pieces_kernel, spans=spans),
+        grid=(rows // BLOCK,),
+        in_specs=specs,
+        out_specs=specs[0],
+        out_shape=jax.ShapeDtypeStruct((rows, columns), F32),
+        compiler_params=pltpu.CompilerParams(vmem_limit_bytes=VMEM_LIMIT),
+        cost_estimate=pl.CostEstimate(
+            flops=rows * columns, bytes_accessed=10 * rows * columns, transcendentals=0
+        ),
+        name="add_pieces",
+    )(kept, *pieces)
 
 
 def together(*values):
@@ -1041,6 +1077,7 @@
     ).astype(BF16)
     sent = [jnp.where(decoder, produced, part) for produced, part in zip(produced_two, sent)]
     sent[1], normed_sharded, grad_proj = together(sent[1], normed_sharded, grad_proj)
+    early = [group_parts(grad_proj, group)]
     arrived_three = [exchange(part, experts) for part in sent]
     flags = jnp.stack([decoder.astype(jnp.int32), group])
     scales = jnp.where(decoder, arrived_gates, 1.0)[:, None]
@@ -1061,14 +1098,13 @@
             most,
         )
         if k == 0:
-            grad_arrived, back_values = together(grad_arrived, back_values)
+            grad_arrived, back_values, early = together(grad_arrived, back_values, early)
             arrived_three[1], back_values = together(arrived_three[1], back_values)
             grad_value = dot_tn(
                 jnp.where(decoder, cross_context, memory),
                 jnp.where(decoder, rounded_grad, back_values),
             )
-            early = jnp.concatenate([grad_proj, grad_value.astype(BF16)], axis=1)
-            early = group_parts(early, group)
+            early.append(group_parts(grad_value.astype(BF16), group))
         else:
             grad_arrived, early, kept, returned_three[0], arrived_three = together(
                 grad_arrived, early, kept, returned_three[0], arrived_three
@@ -1080,8 +1116,8 @@
     ]
     first_group = group == 0
     half_ff = FF // 2
-    in_cuts = (0, 208, 464, 608, 784, 928, D)
-    out_cuts = (0, 256, 608, half_ff)
+    in_cuts = (0, 256, 512, 640, 768, 896, D)
+    out_cuts = (0, 256, 512, half_ff)
 
     def cut(values, cuts):
         return [[values[first:last]] for first, last in zip(cuts[:-1], cuts[1:])]
@@ -1094,7 +1130,8 @@
         return [lax.ppermute(part, "group", SWAP) for part in parts]
 
     gots = [swapped(sends[0])]
-    early = with_layout_constraint(early[0] + early[1], Layout((0, 1)))
+    early = jnp.concatenate([mine + other for mine, other in early], axis=1)
+    early = with_layout_constraint(early, Layout((0, 1)))
     returned_three[1], sends, gots, early = together(returned_three[1], sends, gots, early)
     early = expert_scatter(early)
 
@@ -1163,18 +1200,34 @@
     )
     late_second = expert_scatter(late_second)
     keep_in = dot_tn(expert_rows, keep_halves)
-    keep_in, gots, late_first, sends[5], kept, arrived_three = together(
-        keep_in, gots, late_first, sends[5], kept, arrived_three
-    )
-    late_first = group_swap(late_first, group)
+    keep_in, gots, late_first, sends[5], kept = together(keep_in, gots, late_first, sends[5], kept)
+    gots.append(swapped(sends[5]))
     actives, expert_grad_rows = kept
     send_out = dot_tn(
         jnp.where(first_group, actives[:, half_ff:], actives[:, :half_ff]), expert_grad_rows
     ).astype(BF16)
     out_sends = cut(send_out, out_cuts)
-    sends[5], out_sends[0], late_first = together(sends[5], out_sends[0], late_first)
+    out_sends, gots, late_first, kept = together(out_sends, gots, late_first, kept)
+    late_first = group_swap(late_first, group)
+    grad_expert_in = add_pieces(keep_in, [part[0] for part in gots])
+    grad_expert_in, late_first, out_sends, kept = together(
+        grad_expert_in, late_first, out_sends, kept
+    )
     late_first = expert_gather(late_first)
-    gots.append(swapped(sends[5] + out_sends[0]))
+    out_gots = [swapped(out_sends[0])]
+    actives, expert_grad_rows = kept
+    keep_out = dot_tn(
+        jnp.where(first_group, actives[:, :half_ff], actives[:, half_ff:]), expert_grad_rows
+    )
+    keep_out, out_gots, out_sends = together(keep_out, out_gots, out_sends)
+    out_gots.append(swapped(out_sends[1]))
+    late_second, out_gots, out_sends, arrived_three = together(
+        late_second, out_gots, out_sends, arrived_three
+    )
+    late_second = group_swap(late_second, group)
+    late_second, out_sends, arrived_three = together(late_second, out_sends, arrived_three)
+    late_second = expert_gather(late_second)
+    out_gots.append(swapped(out_sends[2]))
     decoded = (
         second_half
         + dec_gates[0] * collect(arrived_three, code_first)
@@ -1182,21 +1235,8 @@
     )
     result = jnp.where(decoder, decoded, encoded)
 
-    result, gots, out_sends, kept = together(result.astype(BF16), gots, out_sends, kept)
-    gots.append(swapped(out_sends[1]))
-    actives, expert_grad_rows = kept
-    keep_out = dot_tn(
-        jnp.where(first_group, actives[:, :half_ff], actives[:, half_ff:]), expert_grad_rows
-    )
-    late_second, keep_out, gots, out_sends = together(late_second, keep_out, gots, out_sends)
-    late_second = group_swap(late_second, group)
-    late_second, out_sends = together(late_second, out_sends)
-    late_second = expert_gather(late_second)
-    gots.append(swapped(out_sends[2]))
-    got_in = [part[0] for part in gots[: len(sends)]]
-    got_out = [gots[5][1], gots[6][0], gots[7][0]]
-    grad_expert_in = keep_in + jnp.concatenate(got_in).astype(F32)
-    grad_expert_out = keep_out + jnp.concatenate(got_out).astype(F32)
+    result = result.astype(BF16)
+    grad_expert_out = add_pieces(keep_out, [part[0] for part in out_gots])
     small = late_second[:, 3 * D // 2 : 3 * D // 2 + 128].astype(F32)
     small_table = small[: H * NBKT // 2, experts + 3].reshape(H // 2, NBKT)
     return (

time: 1040 us -> 1020 us (0.981)
  Pallas kernels: 281 us -> 303 us
  other arithmetic: 73.8 us -> 53.1 us
    pallas_call x0 -> x2, Pallas kernels: none -> 21.7 us  [add_pieces(): pl.pallas_call(partial(add_pieces_kernel, spans=spans), grid=(rows // BLO...]
    broadcast_in_dim x2 -> x0, other arithmetic: 19 us -> none  [the longest x1 11.6 us: per_device(): grad_expert_in[None, None]]
    unnamed x240 -> x243, local copies, waits for them, and re-layouts: 23 us -> 14.3 us
  transfers between devices with their start and end apart: 37 -> 38, of which waited for: 23 -> 19; matrix products, arithmetic and copies ran while one was open for 26% -> 23% of each run, Pallas kernels for 23% -> 26%
where the time goes in v4:
time: 1020 us; the launch traced here: 1010 us
  Pallas kernels  303 us (30%)
  waiting for transfers between devices  248 us (24%)
  matrix products  229 us (22%)
  starting transfers between devices  87.7 us (9%)
  other arithmetic  53.1 us (5%)
  local copies, waits for them, and re-layouts  39.1 us (4%)
  blocking collectives  30.6 us (3%)
  between operations  16.6 us (2%)
    dot_general x32, matrix products, dot(): return jnp.dot(a, b, preferred_element_type=F32)  112 us
    all_to_all x12, waiting for transfers between devices, exchange(): lax.all_to_all(parts, 'expert', split_axis=0, concat_axis=0, tiled=True)  90.4 us
    pallas_call x2, Pallas kernels, expert_back(): pl.pallas_call(partial(expert_back_kernel, count=rows), grid_spec=pltpu.P...  80.7 us
    pallas_call x5, Pallas kernels, pair_call(): pl.pallas_call(kernel, grid_spec=pltpu.PrefetchScalarGridSpec(num_scalar_...  75.4 us
    dot_general x10, matrix products, dot_tn(): lax.dot_general(a, b, (((0,), (0,)), ((), ())), preferred_element_type=F32)  74.7 us
    pallas_call x2, Pallas kernels, expert_both(): pl.pallas_call(expert_both_kernel, grid=(tiles,), in_specs=[whole, whole]...  74.4 us
    all_to_all x12, starting transfers between devices, exchange(): lax.all_to_all(parts, 'expert', split_axis=0, concat_axis=0, tiled=True)  57.6 us
    ppermute x9, waiting for transfers between devices, swapped(): return [lax.ppermute(part, 'group', SWAP) for part in parts]  45.8 us
  transfers between devices with their start and end apart: 38, of which 19 were waited for; matrix products, arithmetic and copies ran while one was open for 23% of the time, Pallas kernels for 26%

profile of v4, /device:TPU:0, one launch (start us, length us, event | category | flops | bytes accessed | tf_op | source)
XLA Modules:
  0.0 1007.0 jit_solution(14955203374237883042)
XLA Ops:
  15.2 8.7 fusion.4.q_ref.k_ref.v_ref
  23.9 18.3 %self_attend_kernel.1 = (bf16[640,1024]{1,0:T(8,128)(2,1)}, f32[8,2,640]{2,1,0:T(2,128)}) custom-call(s32[2]{0:T(128)} %pad_add_fusion.place_ref, bf16[640,3072]{1,0:T(8,128)(2,1)} %fusion.4.q_ref.k_ref.v_ref, bf16[640,3072]{1,0:T(8,128)(2,1)} %fusion.4.q_ref.k_ref.v_ref, bf16[640,3072]{1,0:T(8,128)(2,1)} %fusion.4.q_ref.k_ref.v_ref, ...), custom_call_target="tpu_custom_call" | custom-call | flops 1677721600 | bytes 10485760 | tf_op jit(solution)/shard_map/self_attend_kernel/pallas_call | solution.py:459
  51.4 6.6 all-to-all-start
  62.1 33.9 %all-to-all-done = bf16[8,96,1024]{2,1,0:T(8,128)(2,1)} async-done(((bf16[8,96,1024]{2,1,0:T(8,128)(2,1)}), bf16[8,96,1024]{2,1,0:T(8,128)(2,1)}, u32[]{:S(2)}, u32[]{:S(2)}) %all-to-all-start) | async-done | bytes 1572896 | tf_op jit(solution)/shard_map/all_to_all | solution.py:530
  106.5 21.4 %expert_forward.2 = bf16[768,1024]{1,0:T(8,128)(2,1)} custom-call(bf16[768,1024]{1,0:T(8,128)(2,1)} %bitcast.15.x_ref.g_ref.refs_0_, bf16[1024,5632]{1,0:T(8,128)(2,1)} %bitcast.273, bf16[1024,5632]{1,0:T(8,128)(2,1)} %bitcast.274, bf16[2816,1024]{1,0:T(8,128)(2,1)} %bitcast.285), custom_call_target="tpu_custom_call" | custom-call | flops 13287555072 | bytes 17301504 | tf_op jit(solution)/shard_map/expert_forward/pallas_call | solution.py:674
  127.9 9.3 collective-permute-done
  150.1 22.0 %expert_forward.3 = bf16[832,1024]{1,0:T(8,128)(2,1)} custom-call(bf16[832,1024]{1,0:T(8,128)(2,1)} %bitcast.22.x_ref.g_ref.refs_0_, bf16[1024,5632]{1,0:T(8,128)(2,1)} %bitcast.275, bf16[1024,5632]{1,0:T(8,128)(2,1)} %bitcast.276, bf16[2816,1024]{1,0:T(8,128)(2,1)} %bitcast.286), custom_call_target="tpu_custom_call" | custom-call | flops 14394851328 | bytes 17301504 | tf_op jit(solution)/shard_map/expert_forward/pallas_call | solution.py:674
  172.1 6.4 collective-permute-done.1
  178.5 4.6 all-to-all-done.1
  198.1 19.7 %collective-permute-done.2 = bf16[320,2048]{1,0:T(8,128)(2,1)} collective-permute-done((bf16[320,2048]{1,0:T(8,128)(2,1)}, bf16[320,2048]{1,0:T(8,128)(2,1)}, u32[]{:S(2)}, u32[]{:S(2)}) %collective-permute-start.2) | collective-permute-done | bytes 1310752 | tf_op jit(solution)/shard_map/ppermute | solution.py:953
  217.8 10.2 %all-to-all-done.3 = bf16[8,104,1024]{2,1,0:T(8,128)(2,1)} async-done(((bf16[8,104,1024]{2,1,0:T(8,128)(2,1)}), bf16[8,104,1024]{2,1,0:T(8,128)(2,1)}, u32[]{:S(2)}, u32[]{:S(2)}) %all-to-all-start.3) | async-done | bytes 1703968 | tf_op jit(solution)/shard_map/all_to_all | solution.py:530
  232.0 5.7 multiply_reduce_fusion.9
  248.2 19.5 %collective-permute-done.3 = bf16[640,1024]{1,0:T(8,128)(2,1)S(1)} collective-permute-done((bf16[640,1024]{1,0:T(8,128)(2,1)S(1)}, bf16[640,1024]{1,0:T(8,128)(2,1)S(1)}, u32[]{:S(2)}, u32[]{:S(2)}) %collective-permute-start.3) | collective-permute-done | bytes 1310752 | tf_op jit(solution)/shard_map/ppermute | solution.py:962
  271.9 9.8 cross_attend_kernel.1
  297.6 33.3 %all-to-all-done.4 = bf16[8,96,1024]{2,1,0:T(8,128)(2,1)} async-done(((bf16[8,96,1024]{2,1,0:T(8,128)(2,1)}), bf16[8,96,1024]{2,1,0:T(8,128)(2,1)}, u32[]{:S(2)}, u32[]{:S(2)}) %all-to-all-start.4) | async-done | bytes 1572896 | tf_op jit(solution)/shard_map/all_to_all | solution.py:530
  335.3 36.0 %expert_both.2 = (bf16[768,1024]{1,0:T(8,128)(2,1)}, bf16[768,2816]{1,0:T(8,128)(2,1)}, f32[768,1]{1,0:T(8,128)}) custom-call(bf16[768,1024]{1,0:T(8,128)(2,1)} %bitcast.27.x_ref.refs_1_, bf16[768,1024]{1,0:T(8,128)(2,1)} %bitcast.15.x_ref.g_ref.refs_0_, bf16[1024,5632]{1,0:T(8,128)(2,1)} %bitcast.277, bf16[1024,5632]{1,0:T(8,128)(2,1)} %bitcast.278, ...), custom_call_target="tpu_custom_call" | custom-call | flops 22145925120 | bytes 17301504 | tf_op jit(solution)/shard_map/expert_both/pallas_call | solution.py:692
  371.2 4.7 all-to-all-done.6
  375.9 4.7 all-to-all-start.5
  380.6 38.4 %expert_both.3 = (bf16[832,1024]{1,0:T(8,128)(2,1)}, bf16[832,2816]{1,0:T(8,128)(2,1)}, f32[832,1]{1,0:T(8,128)}) custom-call(bf16[832,1024]{1,0:T(8,128)(2,1)} %bitcast.31.x_ref.refs_1_, bf16[832,1024]{1,0:T(8,128)(2,1)} %bitcast.22.x_ref.g_ref.refs_0_, bf16[1024,5632]{1,0:T(8,128)(2,1)} %bitcast.279, bf16[1024,5632]{1,0:T(8,128)(2,1)} %bitcast.280, ...), custom_call_target="tpu_custom_call" | custom-call | flops 23991418880 | bytes 17301504 | tf_op jit(solution)/shard_map/expert_both/pallas_call | solution.py:692
  419.0 5.1 all-to-all-start.7
  440.5 30.6 %all-gather = f32[64,400]{1,0:T(8,128)S(1)} all-gather(f32[8,400]{1,0:T(8,128)S(1)} %pad_maximum_fusion.7), channel_id=2, replica_groups=mesh['half'=2,'expert'=8,'group'=2] {'expert'}, dimensions={0}, use_global_device_ids=true | all-gather | bytes 115200 | tf_op jit(solution)/shard_map/all_gather | solution.py:988
  487.8 12.0 %cross_attend_back_kernel.1 = (bf16[640,1024]{1,0:T(8,128)(2,1)}, bf16[640,1024]{1,0:T(8,128)(2,1)}, bf16[640,1024]{1,0:T(8,128)(2,1)}) custom-call(s32[2]{0:T(128)} %pad_add_fusion.place_ref, bf16[640,1024]{1,0:T(8,128)(2,1)} %convolution_convert_fusion.15.q_ref, bf16[640,2048]{1,0:T(8,128)(2,1)} %convolution_convert_fusion.4.k_ref.v_ref, ...), custom_call_target="tpu_custom_call" | custom-call | flops 4194304000 | bytes 10485760 | tf_op jit(solution)/shard_map/cross_attend_back_kernel/pallas_call | solution.py:459
  509.5 6.3 convolution_convert_fusion.8
  515.8 4.6 convolution_convert_fusion.13
  520.5 20.7 %collective-permute-done.4 = bf16[640,1024]{1,0:T(8,128)(2,1)S(1)} collective-permute-done((bf16[640,1024]{1,0:T(8,128)(2,1)S(1)}, bf16[640,1024]{1,0:T(8,128)(2,1)S(1)}, u32[]{:S(2)}, u32[]{:S(2)}) %collective-permute-start.4) | collective-permute-done | bytes 1310752 | tf_op jit(solution)/shard_map/ppermute | solution.py:1051
  564.5 23.4 %collective-permute-done.5 = bf16[640,1024]{1,0:T(8,128)(2,1)S(1)} collective-permute-done((bf16[640,1024]{1,0:T(8,128)(2,1)}, bf16[640,1024]{1,0:T(8,128)(2,1)S(1)}, u32[]{:S(2)}, u32[]{:S(2)}) %collective-permute-start.5) | collective-permute-done | bytes 1310752 | tf_op jit(solution)/shard_map/ppermute | solution.py:1056
  591.1 4.8 all-to-all-start.8
  604.2 39.2 %expert_back.2 = (bf16[768,1024]{1,0:T(8,128)(2,1)}, bf16[2,832,1024]{2,1,0:T(8,128)(2,1)}, bf16[2,832,1024]{2,1,0:T(8,128)(2,1)}, bf16[2,832,2816]{2,1,0:T(8,12...) custom-call(s32[2]{0:T(128)} %pad_add_fusion.1.flags_ref, ...), custom_call_target="tpu_custom_call" | custom-call | flops 22145925120 | bytes 17301504 | tf_op jit(solution)/shard_map/expert_back/pallas_call | solution.py:728
  643.5 5.3 all-to-all-start.10
  654.6 41.5 %expert_back.3 = (bf16[832,1024]{1,0:T(8,128)(2,1)}, bf16[2,832,1024]{2,1,0:T(8,128)(2,1)}, bf16[2,832,1024]{2,1,0:T(8,128)(2,1)}, bf16[2,832,2816]{2,1,0:T(8,12...) custom-call(s32[2]{0:T(128)} %pad_add_fusion.1.flags_ref, ...), custom_call_target="tpu_custom_call", output_to_operand_aliasing={{1}: (8, {}), {2}: (9, {}), {3}: (10, {}), {4}: (11, {}), {... | custom-call | flops 23991418880 | bytes 17301504 | tf_op jit(solution)/shard_map/expert_back/pallas_call | solution.py:728
  696.1 5.3 all-to-all-start.11
  701.6 8.0 convolution_convert_fusion.1
  711.0 8.4 convolution_convert_fusion
  729.8 14.1 %collective-permute-done.9.refs_0_ = bf16[256,2816]{1,0:T(8,128)(2,1)} collective-permute-done((bf16[256,2816]{1,0:T(8,128)(2,1)}, bf16[256,2816]{1,0:T(8,128)(2,1)}, u32[]{:S(2)}, u32[]{:S(2)}) %collective-permute-start.9) | collective-permute-done | bytes 1441824 | tf_op jit(solution)/shard_map/ppermute | solution.py:1130
  769.0 17.6 %self_attend_back_kernel.2 = (bf16[640,512]{1,0:T(8,128)(2,1)}, bf16[640,512]{1,0:T(8,128)(2,1)}, bf16[640,512]{1,0:T(8,128)(2,1)}, f32[4,2,1024]{2,1,0:T(2,128)}) custom-call(s32[2]{0:T(128)} %pad_add_fusion.place_ref, bf16[640,3072]{1,0:T(8,128)(2,1)} %fusion.4.q_ref.k_ref.v_ref, bf16[640,3072]{1,0:T(8,128)(2,1)} %fusion.4.q_ref.k_ref.v_ref, ...), custom_call_target="tpu_custom_call" | custom-call | flops 2097152000 | bytes 10485760 | tf_op jit(solution)/shard_map/self_attend_back_kernel/pallas_call | solution.py:459
  787.6 17.6 %self_attend_back_kernel.3 = (bf16[640,512]{1,0:T(8,128)(2,1)}, bf16[640,512]{1,0:T(8,128)(2,1)}, bf16[640,512]{1,0:T(8,128)(2,1)}, f32[4,2,1024]{2,1,0:T(2,128)}) custom-call(s32[2]{0:T(128)} %pad_add_fusion.place_ref, bf16[640,3072]{1,0:T(8,128)(2,1)} %fusion.4.q_ref.k_ref.v_ref, bf16[640,3072]{1,0:T(8,128)(2,1)} %fusion.4.q_ref.k_ref.v_ref, ...), custom_call_target="tpu_custom_call" | custom-call | flops 2097152000 | bytes 10485760 | tf_op jit(solution)/shard_map/self_attend_back_kernel/pallas_call | solution.py:459
  805.3 5.6 convolution_convert_fusion.3
  815.7 4.6 fusion.169
  825.5 6.8 fusion
  843.7 5.8 pad_maximum_fusion
  850.5 17.7 %convolution_bitcast_fusion.kept_ref = f32[1024,2816]{1,0:T(8,128)} fusion(bf16[2,832,1024]{2,1,0:T(8,128)(2,1)} %get-tuple-element.250, bf16[2,832,2816]{2,1,0:T(8,128)(2,1)} %get-tuple-element.309), kind=kOutput, calls=%fused_computation | convolution fusion | flops 9596567552 | bytes 24313856 | tf_op jit(solution)/shard_map/dot_general | solution.py:92
  869.5 10.0 fusion.33
  888.3 12.4 %add_pieces.2 = f32[1024,2816]{1,0:T(8,128)} custom-call(f32[1024,2816]{1,0:T(8,128)} %convolution_bitcast_fusion.kept_ref, bf16[256,2816]{1,0:T(8,128)(2,1)} %collective-permute-done.9.refs_0_, bf16[256,2816]{1,0:T(8,128)(2,1)} %collective-permute-done.10.refs_1_, bf16[128,2816]{1,0:T(8,128)(2,1)} %collective-permute-done.11.refs_2_, ...), custom_call_target="tpu_custom_call" | custom-call | flops 2883584 | bytes 28835840 | tf_op jit(solution)/shard_map/add_pieces/pallas_call | solution.py:825
  903.4 11.7 %fusion.7.kept_ref = f32[1408,1024]{1,0:T(8,128)} fusion(bf16[1664,1024]{1,0:T(8,128)(2,1)} %bitcast.296, bf16[1664,2816]{1,0:T(8,128)(2,1)} %bitcast.294, pred[]{:T(512)S(6)} %eq.594), kind=kOutput, calls=%fused_computation.12 | convolution fusion | flops 4800626688 | bytes 18546688 | tf_op jit(solution)/shard_map/dot_general | solution.py:92
  916.5 10.9 %collective-permute-done.17.refs_1_ = bf16[256,1024]{1,0:T(8,128)(2,1)} collective-permute-done((bf16[256,1024]{1,0:T(8,128)(2,1)S(1)}, bf16[256,1024]{1,0:T(8,128)(2,1)}, u32[]{:S(2)}, u32[]{:S(2)}) %collective-permute-start.17) | collective-permute-done | bytes 524320 | tf_op jit(solution)/shard_map/ppermute | solution.py:1130
  929.8 6.1 collective-permute-done.18
  964.3 16.4 %collective-permute-done.19.refs_2_ = bf16[896,1024]{1,0:T(8,128)(2,1)} collective-permute-done((bf16[896,1024]{1,0:T(8,128)(2,1)}, bf16[896,1024]{1,0:T(8,128)(2,1)}, u32[]{:S(2)}, u32[]{:S(2)}) %collective-permute-start.19) | collective-permute-done | bytes 1835040 | tf_op jit(solution)/shard_map/ppermute | solution.py:1130
  980.6 9.3 add_pieces.3
  (459 shorter events, 295.6 us)
Async XLA Ops:
  7.2 35.1 %copy-start = (bf16[1,1024,1024]{2,1,0:T(8,128)(2,1)S(1)}, bf16[1,1024,1024]{2,1,0:T(8,128)(2,1)}, u32[]{:S(2)}) copy-start(bf16[1,1024,1024]{2,1,0:T(8,128)(2,1)} %param.55) | copy-start | bytes 6291460
  12.3 33.9 %copy-start.64 = (f32[1,1,1024]{2,0,1:T(1,128)}, f32[1,1,1024]{2,0,1:T(1,128)S(1)}, u32[]{:S(2)}) copy-start(f32[1,1,1024]{2,0,1:T(1,128)S(1)} %get-tuple-element.452) | copy-start | bytes 12292
  51.4 44.6 %all-to-all-start = ((bf16[8,96,1024]{2,1,0:T(8,128)(2,1)}), bf16[8,96,1024]{2,1,0:T(8,128)(2,1)}, u32[]{:S(2)}, u32[]{:S(2)}) async-start(bf16[8,96,1024]{2,1,0:T(8,128)(2,1)} %bitcast.242), calls=%async_computation | async-start | bytes 3145728 | tf_op jit(solution)/shard_map/all_to_all | solution.py:530
  96.0 45.0 %all-to-all-start.2 = ((bf16[8,104,1024]{2,1,0:T(8,128)(2,1)}), bf16[8,104,1024]{2,1,0:T(8,128)(2,1)}, u32[]{:S(2)}, u32[]{:S(2)}) async-start(bf16[8,104,1024]{2,1,0:T(8,128)(2,1)} %bitcast.237), calls=%async_computation.2 | async-start | bytes 3407872 | tf_op jit(solution)/shard_map/all_to_all | solution.py:530
  104.0 33.2 %collective-permute-start = (bf16[352,2048]{1,0:T(8,128)(2,1)}, bf16[352,2048]{1,0:T(8,128)(2,1)}, u32[]{:S(2)}, u32[]{:S(2)}) collective-permute-start(bf16[352,2048]{1,0:T(8,128)(2,1)} %get-tuple-element.190), channel_id=1, source_target_pairs={{0,16},{1,17},{2,18},{3,19},{4,20},{5,21},{6,22},{7,23},{8,24},{9,... | collective-permute-start | bytes 4325384 | tf_op jit(solution)/shard_map/ppermute | solution.py:948
  140.9 42.1 %all-to-all-start.1 = ((bf16[8,96,1024]{2,1,0:T(8,128)(2,1)}), bf16[8,96,1024]{2,1,0:T(8,128)(2,1)}, u32[]{:S(2)}, u32[]{:S(2)}) async-start(bf16[8,96,1024]{2,1,0:T(8,128)(2,1)} %bitcast.240), calls=%async_computation.1 | async-start | bytes 3145728 | tf_op jit(solution)/shard_map/all_to_all | solution.py:530
  145.2 33.3 %collective-permute-start.1 = (bf16[352,2048]{1,0:T(8,128)(2,1)}, bf16[352,2048]{1,0:T(8,128)(2,1)}, u32[]{:S(2)}, u32[]{:S(2)}) collective-permute-start(bf16[352,2048]{1,0:T(8,128)(2,1)} %get-tuple-element.193), channel_id=1, source_target_pairs={{0,16},{1,17},{2,18},{3,19},{4,20},{5,21},{6,22},{7,23},{8,24},{9,... | collective-permute-start | bytes 4325384 | tf_op jit(solution)/shard_map/ppermute | solution.py:948
  183.1 45.0 %all-to-all-start.3 = ((bf16[8,104,1024]{2,1,0:T(8,128)(2,1)}), bf16[8,104,1024]{2,1,0:T(8,128)(2,1)}, u32[]{:S(2)}, u32[]{:S(2)}) async-start(bf16[8,104,1024]{2,1,0:T(8,128)(2,1)} %bitcast.236), calls=%async_computation.3 | async-start | bytes 3407872 | tf_op jit(solution)/shard_map/all_to_all | solution.py:530
  187.4 30.4 %collective-permute-start.2 = (bf16[320,2048]{1,0:T(8,128)(2,1)}, bf16[320,2048]{1,0:T(8,128)(2,1)}, u32[]{:S(2)}, u32[]{:S(2)}) collective-permute-start(bf16[320,2048]{1,0:T(8,128)(2,1)} %pad_maximum_fusion.2), channel_id=1, source_target_pairs={{0,16},{1,17},{2,18},{3,19},{4,20},{5,21},{6,22},{7,23},{8,24},{9,... | collective-permute-start | bytes 3932168 | tf_op jit(solution)/shard_map/ppermute | solution.py:953
  189.8 282.7 %copy-start.88 = (s32[640]{0:T(1024)}, s32[640]{0:T(1024)S(1)}, u32[]{:S(2)}) copy-start(s32[640]{0:T(1024)S(1)} %get-tuple-element.422) | copy-start | bytes 7684
  189.8 285.7 %copy-start.62 = (s32[640]{0:T(1024)}, s32[640]{0:T(1024)S(1)}, u32[]{:S(2)}) copy-start(s32[640]{0:T(1024)S(1)} %get-tuple-element.423) | copy-start | bytes 7684
  238.0 29.7 %collective-permute-start.3 = (bf16[640,1024]{1,0:T(8,128)(2,1)S(1)}, bf16[640,1024]{1,0:T(8,128)(2,1)S(1)}, u32[]{:S(2)}, u32[]{:S(2)}) collective-permute-start(bf16[640,1024]{1,0:T(8,128)(2,1)S(1)} %multiply_convert_fusion.3), channel_id=1, source_target_pairs={{0,16},{1,17},{2,18},{3,19},{4,20},{5,21},{6,22},{7,23},{8,24},{9,... | collective-permute-start | bytes 3932168 | tf_op jit(solution)/shard_map/ppermute | solution.py:962
  286.1 197.4 %copy-start.60 = (f32[640]{0:T(1024)}, f32[640]{0:T(1024)S(1)}, u32[]{:S(2)}) copy-start(f32[640]{0:T(1024)S(1)} %add_rsqrt_fusion) | copy-start | bytes 7684
  288.8 42.1 %all-to-all-start.4 = ((bf16[8,96,1024]{2,1,0:T(8,128)(2,1)}), bf16[8,96,1024]{2,1,0:T(8,128)(2,1)}, u32[]{:S(2)}, u32[]{:S(2)}) async-start(bf16[8,96,1024]{2,1,0:T(8,128)(2,1)} %bitcast.243), calls=%async_computation.4 | async-start | bytes 3145728 | tf_op jit(solution)/shard_map/all_to_all | solution.py:530
  330.9 45.0 %all-to-all-start.6 = ((bf16[8,104,1024]{2,1,0:T(8,128)(2,1)}), bf16[8,104,1024]{2,1,0:T(8,128)(2,1)}, u32[]{:S(2)}, u32[]{:S(2)}) async-start(bf16[8,104,1024]{2,1,0:T(8,128)(2,1)} %bitcast.238), calls=%async_computation.6 | async-start | bytes 3407872 | tf_op jit(solution)/shard_map/all_to_all | solution.py:530
  375.9 43.1 %all-to-all-start.5 = ((bf16[8,96,1024]{2,1,0:T(8,128)(2,1)}), bf16[8,96,1024]{2,1,0:T(8,128)(2,1)}, u32[]{:S(2)}, u32[]{:S(2)}) async-start(bf16[8,96,1024]{2,1,0:T(8,128)(2,1)} %bitcast.241), calls=%async_computation.5 | async-start | bytes 3145728 | tf_op jit(solution)/shard_map/all_to_all | solution.py:530
  419.0 53.4 %all-to-all-start.7 = ((bf16[8,104,1024]{2,1,0:T(8,128)(2,1)}), bf16[8,104,1024]{2,1,0:T(8,128)(2,1)}, u32[]{:S(2)}, u32[]{:S(2)}) async-start(bf16[8,104,1024]{2,1,0:T(8,128)(2,1)} %bitcast.234), calls=%async_computation.7 | async-start | bytes 3407872 | tf_op jit(solution)/shard_map/all_to_all | solution.py:530
  428.3 50.4 %copy-start.70 = (f32[640]{0:T(1024)}, f32[640]{0:T(1024)S(1)}, u32[]{:S(2)}) copy-start(f32[640]{0:T(1024)S(1)} %get-tuple-element.453) | copy-start | bytes 7684
  428.4 50.4 %copy-start.72 = (f32[640]{0:T(1024)}, f32[640]{0:T(1024)S(1)}, u32[]{:S(2)}) copy-start(f32[640]{0:T(1024)S(1)} %get-tuple-element.454) | copy-start | bytes 7684
  507.8 33.3 %collective-permute-start.4 = (bf16[640,1024]{1,0:T(8,128)(2,1)S(1)}, bf16[640,1024]{1,0:T(8,128)(2,1)S(1)}, u32[]{:S(2)}, u32[]{:S(2)}) collective-permute-start(bf16[640,1024]{1,0:T(8,128)(2,1)S(1)} %add_convert_fusion.2), channel_id=1, source_target_pairs={{16,0},{17,1},{18,2},{19,3},{20,4},{21,5},{22,6},{23,7},{24,8},{25... | collective-permute-start | bytes 3932168 | tf_op jit(solution)/shard_map/ppermute | solution.py:1051
  515.8 25.4 %copy-start.2 = (f32[640,1024]{1,0:T(8,128)S(1)}, f32[640,1024]{1,0:T(8,128)}, u32[]{:S(2)}) copy-start(f32[640,1024]{1,0:T(8,128)} %copy-done.1) | copy-start | bytes 7864324
  515.8 26.8 %copy-start.15 = (f32[640,1024]{1,0:T(8,128)S(1)}, f32[640,1024]{1,0:T(8,128)}, u32[]{:S(2)}) copy-start(f32[640,1024]{1,0:T(8,128)} %get-tuple-element.459) | copy-start | bytes 7864324
  548.3 42.7 %all-to-all-start.9 = ((bf16[8,96,1024]{2,1,0:T(8,128)(2,1)}), bf16[8,96,1024]{2,1,0:T(8,128)(2,1)}, u32[]{:S(2)}, u32[]{:S(2)}) async-start(bf16[8,96,1024]{2,1,0:T(8,128)(2,1)} %bitcast.231), calls=%async_computation.9 | async-start | bytes 3145728 | tf_op jit(solution)/shard_map/all_to_all | solution.py:530
  554.7 33.1 %collective-permute-start.5 = (bf16[640,1024]{1,0:T(8,128)(2,1)}, bf16[640,1024]{1,0:T(8,128)(2,1)S(1)}, u32[]{:S(2)}, u32[]{:S(2)}) collective-permute-start(bf16[640,1024]{1,0:T(8,128)(2,1)} %get-tuple-element.222), channel_id=1, source_target_pairs={{16,0},{17,1},{18,2},{19,3},{20,4},{21,5},{22,6},{23,7},{24,8},{25... | collective-permute-start | bytes 3932168 | tf_op jit(solution)/shard_map/ppermute | solution.py:1056
  591.1 52.4 %all-to-all-start.8 = ((bf16[8,104,1024]{2,1,0:T(8,128)(2,1)}), bf16[8,104,1024]{2,1,0:T(8,128)(2,1)}, u32[]{:S(2)}, u32[]{:S(2)}) async-start(bf16[8,104,1024]{2,1,0:T(8,128)(2,1)} %bitcast.230), calls=%async_computation.8 | async-start | bytes 3407872 | tf_op jit(solution)/shard_map/all_to_all | solution.py:530
  598.4 145.8 %copy-start.79 = (f32[640]{0:T(1024)}, f32[640]{0:T(1024)S(1)}, u32[]{:S(2)}) copy-start(f32[640]{0:T(1024)S(1)} %subtract_multiply_fusion) | copy-start | bytes 7684
  601.6 41.9 %collective-permute-start.7 = (bf16[512,1024]{1,0:T(8,128)(2,1)}, bf16[512,1024]{1,0:T(8,128)(2,1)}, u32[]{:S(2)}, u32[]{:S(2)}) collective-permute-start(bf16[512,1024]{1,0:T(8,128)(2,1)} %get-tuple-element.443), channel_id=1, source_target_pairs={{0,1},{1,0},{2,3},{3,2},{4,5},{5,4},{6,7},{7,6},{8,9},{9,8},{10,11... | collective-permute-start | bytes 3145736 | tf_op jit(solution)/shard_map/ppermute | solution.py:757
  602.9 40.5 %collective-permute-start.6 = (bf16[640,1024]{1,0:T(8,128)(2,1)}, bf16[640,1024]{1,0:T(8,128)(2,1)}, u32[]{:S(2)}, u32[]{:S(2)}) collective-permute-start(bf16[640,1024]{1,0:T(8,128)(2,1)} %get-tuple-element.229), channel_id=1, source_target_pairs={{16,0},{17,1},{18,2},{19,3},{20,4},{21,5},{22,6},{23,7},{24,8},{25... | collective-permute-start | bytes 3932168 | tf_op jit(solution)/shard_map/ppermute | solution.py:1074
  643.5 52.6 %all-to-all-start.10 = ((bf16[8,96,1024]{2,1,0:T(8,128)(2,1)}), bf16[8,96,1024]{2,1,0:T(8,128)(2,1)}, u32[]{:S(2)}, u32[]{:S(2)}) async-start(bf16[8,96,1024]{2,1,0:T(8,128)(2,1)} %bitcast.239), calls=%async_computation.10 | async-start | bytes 3145728 | tf_op jit(solution)/shard_map/all_to_all | solution.py:530
  653.9 42.1 %collective-permute-start.8 = (bf16[512,1024]{1,0:T(8,128)(2,1)S(1)}, bf16[512,1024]{1,0:T(8,128)(2,1)}, u32[]{:S(2)}, u32[]{:S(2)}) collective-permute-start(bf16[512,1024]{1,0:T(8,128)(2,1)S(1)} %get-tuple-element.441), channel_id=1, source_target_pairs={{0,1},{1,0},{2,3},{3,2},{4,5},{5,4},{6,7},{7,6},{8,9},{9,8},{10,11... | collective-permute-start | bytes 3145736 | tf_op jit(solution)/shard_map/ppermute | solution.py:757
  696.1 47.8 %all-to-all-start.11 = ((bf16[8,104,1024]{2,1,0:T(8,128)(2,1)}), bf16[8,104,1024]{2,1,0:T(8,128)(2,1)}, u32[]{:S(2)}, u32[]{:S(2)}) async-start(bf16[8,104,1024]{2,1,0:T(8,128)(2,1)} %bitcast.235), calls=%async_computation.11 | async-start | bytes 3407872 | tf_op jit(solution)/shard_map/all_to_all | solution.py:530
  701.4 85.3 %reduce-scatter.4.cloned.1.call-start = ((), (), s32[]{:S(2)}) async-start(), calls=%async_computation.15 | async-start | bytes 2359296 | tf_op jit(solution)/shard_map/reduce_scatter | solution.py:772
  709.6 34.3 %collective-permute-start.9 = (bf16[256,2816]{1,0:T(8,128)(2,1)}, bf16[256,2816]{1,0:T(8,128)(2,1)}, u32[]{:S(2)}, u32[]{:S(2)}) collective-permute-start(bf16[256,2816]{1,0:T(8,128)(2,1)} %convolution_convert_fusion.1), channel_id=1, source_target_pairs={{0,1},{1,0},{2,3},{3,2},{4,5},{5,4},{6,7},{7,6},{8,9},{9,8},{10,11... | collective-permute-start | bytes 4325384 | tf_op jit(solution)/shard_map/ppermute | solution.py:1130
  744.0 71.4 %all-gather.5.cloned.1.call-start = ((), (), s32[]{:S(2)}) async-start(), calls=%async_computation.16 | async-start | bytes 2359296 | tf_op jit(solution)/shard_map/all_gather | solution.py:776
  750.0 36.7 %collective-permute-start.10 = (bf16[256,2816]{1,0:T(8,128)(2,1)S(1)}, bf16[256,2816]{1,0:T(8,128)(2,1)}, u32[]{:S(2)}, u32[]{:S(2)}) collective-permute-start(bf16[256,2816]{1,0:T(8,128)(2,1)S(1)} %slice.213), channel_id=1, source_target_pairs={{0,1},{1,0},{2,3},{3,2},{4,5},{5,4},{6,7},{7,6},{8,9},{9,8},{10,11... | collective-permute-start | bytes 4325384 | tf_op jit(solution)/shard_map/ppermute | solution.py:1130
  786.7 81.4 %reduce-scatter.8.cloned.1.call-start = ((), (), s32[]{:S(2)}) async-start(), calls=%async_computation.18 | async-start | bytes 3538944 | tf_op jit(solution)/shard_map/reduce_scatter | solution.py:772
  786.8 18.5 %collective-permute-start.11 = (bf16[128,2816]{1,0:T(8,128)(2,1)}, bf16[128,2816]{1,0:T(8,128)(2,1)}, u32[]{:S(2)}, u32[]{:S(2)}) collective-permute-start(bf16[128,2816]{1,0:T(8,128)(2,1)} %get-tuple-element.277), channel_id=1, source_target_pairs={{0,1},{1,0},{2,3},{3,2},{4,5},{5,4},{6,7},{7,6},{8,9},{9,8},{10,11... | collective-permute-start | bytes 2162696 | tf_op jit(solution)/shard_map/ppermute | solution.py:1130
  815.4 112.1 %reduce-scatter.6.cloned.1.call-start = ((), (), s32[]{:S(2)}) async-start(), calls=%async_computation.17 | async-start | bytes 6193152 | tf_op jit(solution)/shard_map/reduce_scatter | solution.py:772
  820.4 20.5 %collective-permute-start.12 = (bf16[128,2816]{1,0:T(8,128)(2,1)}, bf16[128,2816]{1,0:T(8,128)(2,1)}, u32[]{:S(2)}, u32[]{:S(2)}) collective-permute-start(bf16[128,2816]{1,0:T(8,128)(2,1)} %get-tuple-element.303), channel_id=1, source_target_pairs={{0,1},{1,0},{2,3},{3,2},{4,5},{5,4},{6,7},{7,6},{8,9},{9,8},{10,11... | collective-permute-start | bytes 2162696 | tf_op jit(solution)/shard_map/ppermute | solution.py:1130
  849.5 97.8 %all-gather.9.cloned.1.call-start = ((), (), s32[]{:S(2)}) async-start(), calls=%async_computation.20 | async-start | bytes 1769472 | tf_op jit(solution)/shard_map/all_gather | solution.py:776
  849.8 18.4 %collective-permute-start.13 = (bf16[128,2816]{1,0:T(8,128)(2,1)}, bf16[128,2816]{1,0:T(8,128)(2,1)}, u32[]{:S(2)}, u32[]{:S(2)}) collective-permute-start(bf16[128,2816]{1,0:T(8,128)(2,1)} %get-tuple-element.314), channel_id=1, source_target_pairs={{0,1},{1,0},{2,3},{3,2},{4,5},{5,4},{6,7},{7,6},{8,9},{9,8},{10,11... | collective-permute-start | bytes 2162696 | tf_op jit(solution)/shard_map/ppermute | solution.py:1130
  868.2 18.1 %collective-permute-start.14 = (bf16[128,2816]{1,0:T(8,128)(2,1)}, bf16[128,2816]{1,0:T(8,128)(2,1)}, u32[]{:S(2)}, u32[]{:S(2)}) collective-permute-start(bf16[128,2816]{1,0:T(8,128)(2,1)} %get-tuple-element.327), channel_id=1, source_target_pairs={{0,1},{1,0},{2,3},{3,2},{4,5},{5,4},{6,7},{7,6},{8,9},{9,8},{10,11... | collective-permute-start | bytes 2162696 | tf_op jit(solution)/shard_map/ppermute | solution.py:1130
  887.0 13.7 %collective-permute-start.15 = (bf16[64,1536]{1,0:T(8,128)(2,1)}, bf16[64,1536]{1,0:T(8,128)(2,1)}, u32[]{:S(2)}, u32[]{:S(2)}) collective-permute-start(bf16[64,1536]{1,0:T(8,128)(2,1)} %constant_dynamic-slice_fusion.1), channel_id=1, source_target_pairs={{0,1},{1,0},{2,3},{3,2},{4,5},{5,4},{6,7},{7,6},{8,9},{9,8},{10,11... | collective-permute-start | bytes 589832 | tf_op jit(solution)/shard_map/ppermute | solution.py:757
  902.4 12.7 %collective-permute-start.16 = (bf16[256,1024]{1,0:T(8,128)(2,1)}, bf16[256,1024]{1,0:T(8,128)(2,1)}, u32[]{:S(2)}, u32[]{:S(2)}) collective-permute-start(bf16[256,1024]{1,0:T(8,128)(2,1)} %get-tuple-element.343), channel_id=1, source_target_pairs={{0,1},{1,0},{2,3},{3,2},{4,5},{5,4},{6,7},{7,6},{8,9},{9,8},{10,11... | collective-permute-start | bytes 1572872 | tf_op jit(solution)/shard_map/ppermute | solution.py:1130
  903.1 86.8 %all-gather.7.cloned.1.call-start = ((), (), s32[]{:S(2)}) async-start(), calls=%async_computation.19 | async-start | bytes 3096576 | tf_op jit(solution)/shard_map/all_gather | solution.py:776
  915.1 12.3 %collective-permute-start.17 = (bf16[256,1024]{1,0:T(8,128)(2,1)S(1)}, bf16[256,1024]{1,0:T(8,128)(2,1)}, u32[]{:S(2)}, u32[]{:S(2)}) collective-permute-start(bf16[256,1024]{1,0:T(8,128)(2,1)S(1)} %copy-done.54), channel_id=1, source_target_pairs={{0,1},{1,0},{2,3},{3,2},{4,5},{5,4},{6,7},{7,6},{8,9},{9,8},{10,11... | collective-permute-start | bytes 1572872 | tf_op jit(solution)/shard_map/ppermute | solution.py:1130
  928.5 7.4 collective-permute-start.18
  941.9 38.7 %collective-permute-start.19 = (bf16[896,1024]{1,0:T(8,128)(2,1)}, bf16[896,1024]{1,0:T(8,128)(2,1)}, u32[]{:S(2)}, u32[]{:S(2)}) collective-permute-start(bf16[896,1024]{1,0:T(8,128)(2,1)} %slice.220), channel_id=1, source_target_pairs={{0,1},{1,0},{2,3},{3,2},{4,5},{5,4},{6,7},{7,6},{8,9},{9,8},{10,11... | collective-permute-start | bytes 5505032 | tf_op jit(solution)/shard_map/ppermute | solution.py:1130
  (105 other events, 617.2 us)
Sparse Core Ops, SparseCore 0:
  744.1 38.4 reduce-scatter.3
  786.8 28.4 all-gather.4
  817.6 39.8 reduce-scatter.7
  860.3 61.4 reduce-scatter.5
  923.8 23.4 all-gather.8
  948.7 34.5 all-gather.6

commit v5 on v4

--- a/solution.py
+++ b/solution.py
@@ -28,6 +28,8 @@
 DIAGONAL = ENC_MOST // BLOCK - 1
 LINE = 2 * ENC_MOST
 FF_TILE = 256
+CROSS_WIDE = 2
+SELF_WIDE = 2
 F32 = jnp.float32
 BF16 = jnp.bfloat16
 GELU_SCALE = float(np.sqrt(2.0 / np.pi))
@@ -287,15 +289,16 @@
     return pl.multiple_of(item * ENC_MIN + later * ENC_MOST, ENC_MIN), item + later
 
 
-def gather_short(ref, place):
+def gather_short(ref, place, lanes):
     return jnp.concatenate(
-        [ref[pl.ds(short_places(place, item)[0], ENC_MIN), :] for item in range(ITEMS - 1)], axis=0
-    )
-
-
-def scatter_short(ref, place, rows):
+        [ref[pl.ds(short_places(place, item)[0], ENC_MIN), lanes] for item in range(ITEMS - 1)],
+        axis=0,
+    )
+
+
+def scatter_short(ref, place, rows, lanes):
     for item in range(ITEMS - 1):
-        ref[pl.ds(short_places(place, item)[0], ENC_MIN), :] = rows[
+        ref[pl.ds(short_places(place, item)[0], ENC_MIN), lanes] = rows[
             item * ENC_MIN : (item + 1) * ENC_MIN
         ]
 
@@ -305,88 +308,97 @@
 
 
 def self_attend_kernel(place_ref, q_ref, k_ref, v_ref, line_ref, out_ref, lse_ref, bias_ref):
-    for head in range(2):
-        bias_ref[head] = skew(line_ref[0, head : head + 1, :], BLOCK)
+    pairs = range(q_ref.shape[1] // (2 * HD))
+    for pair in pairs:
+        for head in range(2):
+            bias_ref[pair, head] = skew(line_ref[pair, head : head + 1, :], BLOCK)
     place = place_ref[0]
     decoder = place_ref[1] == 1
 
     @pl.when(decoder)
     def _():
         blocks = [block_rows(block) for block in range(ITEMS)]
-        shares = tuple([ref[here, :] for here in blocks] for ref in (q_ref, k_ref, v_ref))
-        ((rows, lines),) = attend_groups([shares + (joined([causal_tile()] * ITEMS),)], bias_ref)
-        for here, part, line in zip(blocks, rows, lines):
-            out_ref[here, :] = part
-            lse_ref[0, :, here] = line
+        for pair in pairs:
+            lanes = pair_lanes(pair)
+            shares = tuple([ref[here, lanes] for here in blocks] for ref in (q_ref, k_ref, v_ref))
+            mask = joined([causal_tile()] * ITEMS)
+            ((rows, lines),) = attend_groups([shares + (mask,)], bias_ref.at[pair])
+            for here, part, line in zip(blocks, rows, lines):
+                out_ref[here, lanes] = part
+                lse_ref[pair, :, here] = line
 
     @pl.when(jnp.logical_not(decoder))
     def _():
         here = pl.ds(pl.multiple_of(place * ENC_MIN, ENC_MIN), ENC_MOST)
-        groups = [
-            ([q_ref[here, :]], [k_ref[here, :]], [v_ref[here, :]], None),
-            tuple([gather_short(ref, place)] for ref in (q_ref, k_ref, v_ref)) + (short_tile(),),
-        ]
-        ((rows, lines),) = attend_groups(groups[:1], bias_ref)
-        out_ref[here, :] = rows[0]
-        lse_ref[0, :, :ENC_MOST] = lines[0]
-        ((short_rows, short_lines),) = attend_groups(groups[1:], bias_ref)
-        scatter_short(out_ref, place, short_rows[0])
-        lse_ref[0, :, ENC_MOST:] = short_lines[0]
+        for pair in pairs:
+            lanes = pair_lanes(pair)
+            group = tuple([ref[here, lanes]] for ref in (q_ref, k_ref, v_ref)) + (None,)
+            ((rows, lines),) = attend_groups([group], bias_ref.at[pair])
+            out_ref[here, lanes] = rows[0]
+            lse_ref[pair, :, :ENC_MOST] = lines[0]
+        for pair in pairs:
+            lanes = pair_lanes(pair)
+            group = tuple([gather_short(ref, place, lanes)] for ref in (q_ref, k_ref, v_ref))
+            ((rows, lines),) = attend_groups([group + (short_tile(),)], bias_ref.at[pair])
+            scatter_short(out_ref, place, rows[0], lanes)
+            lse_ref[pair, :, ENC_MOST:] = lines[0]
 
 
 def self_attend_back_kernel(
     place_ref, q_ref, k_ref, v_ref, dc_ref, lse_ref, line_ref,
     dq_ref, dk_ref, dv_ref, dline_ref, bias_ref, dbias_ref,
 ):
-    for head in range(2):
-        bias_ref[head] = skew(line_ref[0, head : head + 1, :], BLOCK)
+    pairs = range(q_ref.shape[1] // (2 * HD))
+    for pair in pairs:
+        for head in range(2):
+            bias_ref[pair, head] = skew(line_ref[pair, head : head + 1, :], BLOCK)
     dbias_ref[...] = jnp.zeros(dbias_ref.shape, F32)
     place = place_ref[0]
     decoder = place_ref[1] == 1
+    ins = (q_ref, k_ref, v_ref)
     outs = (dq_ref, dk_ref, dv_ref)
 
     @pl.when(decoder)
     def _():
         blocks = [block_rows(block) for block in range(ITEMS)]
-        shares = tuple([ref[here, :] for here in blocks] for ref in (q_ref, k_ref, v_ref))
-        shares += (
-            joined([causal_tile()] * ITEMS),
-            [dc_ref[here, :] for here in blocks],
-            [lse_ref[0, :, here] for here in blocks],
-        )
-        (grads,) = attend_groups_back([shares], bias_ref, dbias_ref)
-        for ref, rows in zip(outs, grads):
-            for here, part in zip(blocks, rows):
-                ref[here, :] = part
+        for pair in pairs:
+            lanes = pair_lanes(pair)
+            shares = tuple([ref[here, lanes] for here in blocks] for ref in ins)
+            shares += (
+                joined([causal_tile()] * ITEMS),
+                [dc_ref[here, lanes] for here in blocks],
+                [lse_ref[pair, :, here] for here in blocks],
+            )
+            (grads,) = attend_groups_back([shares], bias_ref.at[pair], dbias_ref.at[pair])
+            for ref, rows in zip(outs, grads):
+                for here, part in zip(blocks, rows):
+                    ref[here, lanes] = part
 
     @pl.when(jnp.logical_not(decoder))
     def _():
         here = pl.ds(pl.multiple_of(place * ENC_MIN, ENC_MIN), ENC_MOST)
-        groups = [
-            (
-                [q_ref[here, :]],
-                [k_ref[here, :]],
-                [v_ref[here, :]],
-                None,
-                [dc_ref[here, :]],
-                [lse_ref[0, :, :ENC_MOST]],
-            ),
-            (
-                [gather_short(q_ref, place)],
-                [gather_short(k_ref, place)],
-                [gather_short(v_ref, place)],
-                short_tile(),
-                [gather_short(dc_ref, place)],
-                [lse_ref[0, :, ENC_MOST:]],
-            ),
-        ]
-        grads, short_grads = attend_groups_back(groups, bias_ref, dbias_ref)
-        for ref, rows, short_rows in zip(outs, grads, short_grads):
-            ref[here, :] = rows[0]
-            scatter_short(ref, place, short_rows[0])
-
-    for head in range(2):
-        dline_ref[0, head : head + 1, :] = unskew(dbias_ref[head])
+        for pair in pairs:
+            lanes = pair_lanes(pair)
+            groups = [
+                tuple([ref[here, lanes]] for ref in ins)
+                + (None, [dc_ref[here, lanes]], [lse_ref[pair, :, :ENC_MOST]]),
+                tuple([gather_short(ref, place, lanes)] for ref in ins)
+                + (
+                    short_tile(),
+                    [gather_short(dc_ref, place, lanes)],
+                    [lse_ref[pair, :, ENC_MOST:]],
+                ),
+            ]
+            grads, short_grads = attend_groups_back(
+                groups, bias_ref.at[pair], dbias_ref.at[pair]
+            )
+            for ref, rows, short_rows in zip(outs, grads, short_grads):
+                ref[here, lanes] = rows[0]
+                scatter_short(ref, place, short_rows[0], lanes)
+
+    for pair in pairs:
+        for head in range(2):
+            dline_ref[pair, head : head + 1, :] = unskew(dbias_ref[pair, head])
 
 
 def cross_places(place):
@@ -403,22 +415,27 @@
     return [[long_pair], pairs]
 
 
+def pair_lanes(pair):
+    return slice(pair * 2 * HD, (pair + 1) * 2 * HD)
+
+
 def cross_attend_kernel(place_ref, q_ref, k_ref, v_ref, out_ref, lse_ref):
     places = cross_places(place_ref[0])
+    pairs = [(pair, spots) for pair in range(q_ref.shape[1] // (2 * HD)) for spots in places]
     groups = [
         (
-            [q_ref[here, :] for here, there in pairs],
-            [k_ref[there, :] for here, there in pairs],
-            [v_ref[there, :] for here, there in pairs],
+            [q_ref[here, pair_lanes(pair)] for here, there in spots],
+            [k_ref[there, pair_lanes(pair)] for here, there in spots],
+            [v_ref[there, pair_lanes(pair)] for here, there in spots],
             None,
         )
-        for pairs in places
+        for pair, spots in pairs
     ]
     number = 0
-    for pairs, (rows, lines) in zip(places, attend_groups(groups, None)):
-        for (here, there), part, line in zip(pairs, rows, lines):
-            out_ref[here, :] = part
-            lse_ref[0, :, block_rows(number)] = line
+    for (pair, spots), (rows, lines) in zip(pairs, attend_groups(groups, None)):
+        for (here, there), part, line in zip(spots, rows, lines):
+            out_ref[here, pair_lanes(pair)] = part
+            lse_ref[pair, :, block_rows(number % ITEMS)] = line
             number += 1
 
 
@@ -426,41 +443,48 @@
     place_ref, q_ref, k_ref, v_ref, dc_ref, lse_ref, dq_ref, dk_ref, dv_ref
 ):
     places = cross_places(place_ref[0])
-    lines = [lse_ref[0, :, block_rows(number)] for number in range(ITEMS)]
-    groups = [
-        (
-            [q_ref[here, :] for here, there in pairs],
-            [k_ref[there, :] for here, there in pairs],
-            [v_ref[there, :] for here, there in pairs],
-            None,
-            [dc_ref[here, :] for here, there in pairs],
-            part,
+    pairs = [(pair, spots) for pair in range(q_ref.shape[1] // (2 * HD)) for spots in places]
+    groups = []
+    number = 0
+    for pair, spots in pairs:
+        lanes = pair_lanes(pair)
+        lines = []
+        for _ in spots:
+            lines.append(lse_ref[pair, :, block_rows(number % ITEMS)])
+            number += 1
+        groups.append(
+            (
+                [q_ref[here, lanes] for here, there in spots],
+                [k_ref[there, lanes] for here, there in spots],
+                [v_ref[there, lanes] for here, there in spots],
+                None,
+                [dc_ref[here, lanes] for here, there in spots],
+                lines,
+            )
         )
-        for pairs, part in zip(places, (lines[:1], lines[1:]))
-    ]
-    for pairs, grads in zip(places, attend_groups_back(groups, None, None)):
-        for number, (here, there) in enumerate(pairs):
-            dq_ref[here, :] = grads[0][number]
-            dk_ref[there, :] = grads[1][number]
-            dv_ref[there, :] = grads[2][number]
-
-
-def pair_spec(rows, first):
-    return pl.BlockSpec((rows, 2 * HD), lambda pair, places: (0, first + pair))
-
-
-def flat_spec(first, *shape):
-    return pl.BlockSpec((1,) + shape, lambda pair, places: (first + pair, 0, 0))
-
-
-def pair_call(kernel, places, operands, specs, out_specs, out_shape, scratch, work, pairs=PAIRS):
+    for (pair, spots), grads in zip(pairs, attend_groups_back(groups, None, None)):
+        for number, (here, there) in enumerate(spots):
+            dq_ref[here, pair_lanes(pair)] = grads[0][number]
+            dk_ref[there, pair_lanes(pair)] = grads[1][number]
+            dv_ref[there, pair_lanes(pair)] = grads[2][number]
+
+
+def pair_spec(rows, first, wide):
+    return pl.BlockSpec((rows, wide * 2 * HD), lambda step, places: (0, first // wide + step))
+
+
+def flat_spec(first, wide, *shape):
+    return pl.BlockSpec((wide,) + shape, lambda step, places: (first // wide + step, 0, 0))
+
+
+def pair_call(kernel, places, operands, specs, out_specs, out_shape, scratch, work, pairs, wide):
     rows = ITEMS * BLOCK
     share = rows * rows * D * pairs // PAIRS
     return pl.pallas_call(
         kernel,
         grid_spec=pltpu.PrefetchScalarGridSpec(
             num_scalar_prefetch=1,
-            grid=(pairs,),
+            grid=(pairs // wide,),
             in_specs=specs,
             out_specs=out_specs,
             scratch_shapes=scratch,
@@ -476,42 +500,46 @@
 
 def attend(query, keys, values, places, lines):
     rows = query[0].shape[0]
+    wide = SELF_WIDE if lines is not None else CROSS_WIDE
     operands = [part[0] for part in (query, keys, values)]
-    specs = [pair_spec(rows, part[1]) for part in (query, keys, values)]
+    specs = [pair_spec(rows, part[1], wide) for part in (query, keys, values)]
     scratch = []
     if lines is not None:
         operands.append(lines)
-        specs.append(flat_spec(0, 2, LINE))
-        scratch.append(pltpu.VMEM((2, BLOCK, LINE), F32))
+        specs.append(flat_spec(0, wide, 2, LINE))
+        scratch.append(pltpu.VMEM((wide, 2, BLOCK, LINE), F32))
     return pair_call(
         cross_attend_kernel if lines is None else self_attend_kernel,
         places,
         operands,
         specs,
-        [pair_spec(rows, 0), flat_spec(0, 2, rows)],
+        [pair_spec(rows, 0, wide), flat_spec(0, wide, 2, rows)],
         [
             jax.ShapeDtypeStruct((rows, D), BF16),
             jax.ShapeDtypeStruct((PAIRS, 2, rows), F32),
         ],
         scratch,
         4,
+        PAIRS,
+        wide,
     )
 
 
 def attend_back(query, keys, values, grad_context, lse, places, lines, first=0, pairs=PAIRS):
     rows = query[0].shape[0]
+    wide = SELF_WIDE if lines is not None else CROSS_WIDE
     operands = [part[0] for part in (query, keys, values)] + [grad_context, lse]
-    specs = [pair_spec(rows, part[1] + first) for part in (query, keys, values)]
-    specs += [pair_spec(rows, first), flat_spec(first, 2, rows)]
-    out_specs = [pair_spec(rows, 0)] * 3
+    specs = [pair_spec(rows, part[1] + first, wide) for part in (query, keys, values)]
+    specs += [pair_spec(rows, first, wide), flat_spec(first, wide, 2, rows)]
+    out_specs = [pair_spec(rows, 0, wide)] * 3
     out_shape = [jax.ShapeDtypeStruct((rows, pairs * 2 * HD), BF16)] * 3
     scratch = []
     if lines is not None:
         operands.append(lines)
-        specs.append(flat_spec(first, 2, LINE))
-        out_specs.append(flat_spec(0, 2, LINE))
+        specs.append(flat_spec(first, wide, 2, LINE))
+        out_specs.append(flat_spec(0, wide, 2, LINE))
         out_shape.append(jax.ShapeDtypeStruct((pairs, 2, LINE), F32))
-        scratch += [pltpu.VMEM((2, BLOCK, LINE), F32)] * 2
+        scratch += [pltpu.VMEM((wide, 2, BLOCK, LINE), F32)] * 2
     return pair_call(
         cross_attend_back_kernel if lines is None else self_attend_back_kernel,
         places,
@@ -522,6 +550,7 @@
         scratch,
         10,
         pairs,
+        wide,
     )
 
 
@@ -750,10 +779,15 @@
     return jax.nn.sigmoid(first - second), jax.nn.sigmoid(second - first)
 
 
-def group_parts(rows, group):
+def group_halves(rows, group):
     half = rows.shape[0] // 2
     sent = lax.dynamic_slice_in_dim(rows, (1 - group) * half, half, 0)
     kept = lax.dynamic_slice_in_dim(rows, group * half, half, 0)
+    return kept, sent
+
+
+def group_parts(rows, group):
+    kept, sent = group_halves(rows, group)
     return kept, lax.ppermute(sent, "group", SWAP)
 
 
@@ -809,22 +843,22 @@
             refs[-1][...] = kept_ref[...] + piece_ref[...].astype(F32)
 
 
-def add_pieces(kept, pieces):
+def add_pieces(kept, pieces, block):
     rows, columns = kept.shape
     spans = []
-    specs = [pl.BlockSpec((BLOCK, columns), lambda step: (step, 0))]
+    specs = [pl.BlockSpec((block, columns), lambda step: (step, 0))]
     for piece in pieces:
         first = spans[-1][1] if spans else 0
-        last = first + piece.shape[0] // BLOCK
+        last = first + piece.shape[0] // block
         spans.append((first, last))
 
         def place(step, first=first, last=last):
             return jnp.clip(step - first, 0, last - first - 1), 0
 
-        specs.append(pl.BlockSpec((BLOCK, columns), place))
+        specs.append(pl.BlockSpec((block, columns), place))
     return pl.pallas_call(
         partial(add_pieces_kernel, spans=spans),
-        grid=(rows // BLOCK,),
+        grid=(rows // block,),
         in_specs=specs,
         out_specs=specs[0],
         out_shape=jax.ShapeDtypeStruct((rows, columns), F32),
@@ -1076,15 +1110,19 @@
         jnp.where(decoder, rounded_half, memory), jnp.where(decoder, grad_cross_query, back_keys)
     ).astype(BF16)
     sent = [jnp.where(decoder, produced, part) for produced, part in zip(produced_two, sent)]
-    sent[1], normed_sharded, grad_proj = together(sent[1], normed_sharded, grad_proj)
-    early = [group_parts(grad_proj, group)]
-    arrived_three = [exchange(part, experts) for part in sent]
     flags = jnp.stack([decoder.astype(jnp.int32), group])
     scales = jnp.where(decoder, arrived_gates, 1.0)[:, None]
+    scales = [scales[:edge], scales[edge:]]
+    proj_kept, proj_sent = group_halves(grad_proj, group)
+    sent[1], normed_sharded, proj_kept, proj_sent, flags, scales = together(
+        sent[1], normed_sharded, proj_kept, proj_sent, flags, scales
+    )
+    early = [(proj_kept, lax.ppermute(proj_sent, "group", SWAP))]
+    arrived_three = [exchange(part, experts) for part in sent]
     most = max(part.shape[0] for part in arrived_one)
     kept = None
     returned_three = []
-    for k, scale in enumerate((scales[:edge], scales[edge:])):
+    for k, scale in enumerate(scales):
         grad_arrived, kept = expert_back(
             flags,
             arrived_one[k],
@@ -1117,7 +1155,7 @@
     first_group = group == 0
     half_ff = FF // 2
     in_cuts = (0, 256, 512, 640, 768, 896, D)
-    out_cuts = (0, 256, 512, half_ff)
+    out_cuts = (0, half_ff // 4, half_ff // 2, half_ff)
 
     def cut(values, cuts):
         return [[values[first:last]] for first, last in zip(cuts[:-1], cuts[1:])]
@@ -1209,7 +1247,7 @@
     out_sends = cut(send_out, out_cuts)
     out_sends, gots, late_first, kept = together(out_sends, gots, late_first, kept)
     late_first = group_swap(late_first, group)
-    grad_expert_in = add_pieces(keep_in, [part[0] for part in gots])
+    grad_expert_in = add_pieces(keep_in, [part[0] for part in gots], BLOCK)
     grad_expert_in, late_first, out_sends, kept = together(
         grad_expert_in, late_first, out_sends, kept
     )
@@ -1236,7 +1274,7 @@
     result = jnp.where(decoder, decoded, encoded)
 
     result = result.astype(BF16)
-    grad_expert_out = add_pieces(keep_out, [part[0] for part in out_gots])
+    grad_expert_out = add_pieces(keep_out, [part[0] for part in out_gots], half_ff // 4)
     small = late_second[:, 3 * D // 2 : 3 * D // 2 + 128].astype(F32)
     small_table = small[: H * NBKT // 2, experts + 3].reshape(H // 2, NBKT)
     return (

time: 1020 us -> 1020 us (level)
  transfers between devices with their start and end apart: 38 -> 38, of which waited for: 19 -> 19; matrix products, arithmetic and copies ran while one was open for 23% -> 23% of each run, Pallas kernels for 26% -> 25%
where the time goes in v5:
time: 1020 us; the launch traced here: 1000 us
  Pallas kernels  295 us (29%)
  waiting for transfers between devices  257 us (25%)
  matrix products  228 us (22%)
  starting transfers between devices  85.3 us (8%)
  other arithmetic  52.2 us (5%)
  local copies, waits for them, and re-layouts  38.8 us (4%)
  blocking collectives  30.6 us (3%)
  between operations  16.5 us (2%)
    dot_general x32, matrix products, dot(): return jnp.dot(a, b, preferred_element_type=F32)  113 us
    all_to_all x12, waiting for transfers between devices, exchange(): lax.all_to_all(parts, 'expert', split_axis=0, concat_axis=0, tiled=True)  90.4 us
    pallas_call x2, Pallas kernels, expert_back(): pl.pallas_call(partial(expert_back_kernel, count=rows), grid_spec=pltpu.P...  80.4 us
    pallas_call x2, Pallas kernels, expert_both(): pl.pallas_call(expert_both_kernel, grid=(tiles,), in_specs=[whole, whole]...  74.4 us
    dot_general x10, matrix products, dot_tn(): lax.dot_general(a, b, (((0,), (0,)), ((), ())), preferred_element_type=F32)  73.7 us
    pallas_call x5, Pallas kernels, pair_call(): pl.pallas_call(kernel, grid_spec=pltpu.PrefetchScalarGridSpec(num_scalar_...  71.3 us
    all_to_all x12, starting transfers between devices, exchange(): lax.all_to_all(parts, 'expert', split_axis=0, concat_axis=0, tiled=True)  57.4 us
    ppermute x9, waiting for transfers between devices, swapped(): return [lax.ppermute(part, 'group', SWAP) for part in parts]  52.9 us
  transfers between devices with their start and end apart: 38, of which 19 were waited for; matrix products, arithmetic and copies ran while one was open for 23% of the time, Pallas kernels for 25%

profile of v5, /device:TPU:0, one launch (start us, length us, event | category | flops | bytes accessed | tf_op | source)
XLA Modules:
  0.0 1003.5 jit_solution(17881464358807305841)
XLA Ops:
  15.3 8.8 fusion.4.q_ref.k_ref.v_ref
  24.0 18.7 %self_attend_kernel.1 = (bf16[640,1024]{1,0:T(8,128)(2,1)}, f32[8,2,640]{2,1,0:T(2,128)}) custom-call(s32[2]{0:T(128)} %get-tuple-element.472.place_ref, bf16[640,3072]{1,0:T(8,128)(2,1)} %fusion.4.q_ref.k_ref.v_ref, bf16[640,3072]{1,0:T(8,128)(2,1)} %fusion.4.q_ref.k_ref.v_ref, bf16[640,3072]{1,0:T(8,128)(2,1)} %fusion.4.q_ref.k_ref.v_ref, ...), custom_call_target="tpu_custom_call" | custom-call | flops 1677721600 | bytes 10485760 | tf_op jit(solution)/shard_map/self_attend_kernel/pallas_call | solution.py:483
  51.9 6.4 all-to-all-start
  62.4 33.9 %all-to-all-done = bf16[8,96,1024]{2,1,0:T(8,128)(2,1)} async-done(((bf16[8,96,1024]{2,1,0:T(8,128)(2,1)}), bf16[8,96,1024]{2,1,0:T(8,128)(2,1)}, u32[]{:S(2)}, u32[]{:S(2)}) %all-to-all-start) | async-done | bytes 1572896 | tf_op jit(solution)/shard_map/all_to_all | solution.py:559
  106.7 21.4 %expert_forward.2 = bf16[768,1024]{1,0:T(8,128)(2,1)} custom-call(bf16[768,1024]{1,0:T(8,128)(2,1)} %bitcast.15.x_ref.g_ref.refs_0_, bf16[1024,5632]{1,0:T(8,128)(2,1)} %bitcast.273, bf16[1024,5632]{1,0:T(8,128)(2,1)} %bitcast.274, bf16[2816,1024]{1,0:T(8,128)(2,1)} %bitcast.285), custom_call_target="tpu_custom_call" | custom-call | flops 13287555072 | bytes 17301504 | tf_op jit(solution)/shard_map/expert_forward/pallas_call | solution.py:703
  128.0 9.5 collective-permute-done
  150.5 22.0 %expert_forward.3 = bf16[832,1024]{1,0:T(8,128)(2,1)} custom-call(bf16[832,1024]{1,0:T(8,128)(2,1)} %bitcast.22.x_ref.g_ref.refs_0_, bf16[1024,5632]{1,0:T(8,128)(2,1)} %bitcast.275, bf16[1024,5632]{1,0:T(8,128)(2,1)} %bitcast.276, bf16[2816,1024]{1,0:T(8,128)(2,1)} %bitcast.286), custom_call_target="tpu_custom_call" | custom-call | flops 14394851328 | bytes 17301504 | tf_op jit(solution)/shard_map/expert_forward/pallas_call | solution.py:703
  172.4 6.4 collective-permute-done.1
  178.8 4.6 all-to-all-done.1
  198.4 19.7 %collective-permute-done.2 = bf16[320,2048]{1,0:T(8,128)(2,1)} collective-permute-done((bf16[320,2048]{1,0:T(8,128)(2,1)}, bf16[320,2048]{1,0:T(8,128)(2,1)}, u32[]{:S(2)}, u32[]{:S(2)}) %collective-permute-start.2) | collective-permute-done | bytes 1310752 | tf_op jit(solution)/shard_map/ppermute | solution.py:987
  218.1 10.2 %all-to-all-done.3 = bf16[8,104,1024]{2,1,0:T(8,128)(2,1)} async-done(((bf16[8,104,1024]{2,1,0:T(8,128)(2,1)}), bf16[8,104,1024]{2,1,0:T(8,128)(2,1)}, u32[]{:S(2)}, u32[]{:S(2)}) %all-to-all-start.3) | async-done | bytes 1703968 | tf_op jit(solution)/shard_map/all_to_all | solution.py:559
  232.4 5.7 multiply_reduce_fusion.9
  248.5 19.5 %collective-permute-done.3 = bf16[640,1024]{1,0:T(8,128)(2,1)S(1)} collective-permute-done((bf16[640,1024]{1,0:T(8,128)(2,1)S(1)}, bf16[640,1024]{1,0:T(8,128)(2,1)S(1)}, u32[]{:S(2)}, u32[]{:S(2)}) %collective-permute-start.3) | collective-permute-done | bytes 1310752 | tf_op jit(solution)/shard_map/ppermute | solution.py:996
  272.2 7.5 cross_attend_kernel.1
  295.6 33.3 %all-to-all-done.4 = bf16[8,96,1024]{2,1,0:T(8,128)(2,1)} async-done(((bf16[8,96,1024]{2,1,0:T(8,128)(2,1)}), bf16[8,96,1024]{2,1,0:T(8,128)(2,1)}, u32[]{:S(2)}, u32[]{:S(2)}) %all-to-all-start.4) | async-done | bytes 1572896 | tf_op jit(solution)/shard_map/all_to_all | solution.py:559
  333.2 36.0 %expert_both.2 = (bf16[768,1024]{1,0:T(8,128)(2,1)}, bf16[768,2816]{1,0:T(8,128)(2,1)}, f32[768,1]{1,0:T(8,128)}) custom-call(bf16[768,1024]{1,0:T(8,128)(2,1)} %bitcast.27.x_ref.refs_1_, bf16[768,1024]{1,0:T(8,128)(2,1)} %bitcast.15.x_ref.g_ref.refs_0_, bf16[1024,5632]{1,0:T(8,128)(2,1)} %bitcast.277, bf16[1024,5632]{1,0:T(8,128)(2,1)} %bitcast.278, ...), custom_call_target="tpu_custom_call" | custom-call | flops 22145925120 | bytes 17301504 | tf_op jit(solution)/shard_map/expert_both/pallas_call | solution.py:721
  369.2 4.7 all-to-all-done.6
  378.4 38.4 %expert_both.3 = (bf16[832,1024]{1,0:T(8,128)(2,1)}, bf16[832,2816]{1,0:T(8,128)(2,1)}, f32[832,1]{1,0:T(8,128)}) custom-call(bf16[832,1024]{1,0:T(8,128)(2,1)} %bitcast.31.x_ref.refs_1_, bf16[832,1024]{1,0:T(8,128)(2,1)} %bitcast.22.x_ref.g_ref.refs_0_, bf16[1024,5632]{1,0:T(8,128)(2,1)} %bitcast.279, bf16[1024,5632]{1,0:T(8,128)(2,1)} %bitcast.280, ...), custom_call_target="tpu_custom_call" | custom-call | flops 23991418880 | bytes 17301504 | tf_op jit(solution)/shard_map/expert_both/pallas_call | solution.py:721
  416.8 5.0 all-to-all-start.7
  438.2 30.6 %all-gather = f32[64,400]{1,0:T(8,128)S(1)} all-gather(f32[8,400]{1,0:T(8,128)S(1)} %pad_maximum_fusion.7), channel_id=2, replica_groups=mesh['half'=2,'expert'=8,'group'=2] {'expert'}, dimensions={0}, use_global_device_ids=true | all-gather | bytes 115200 | tf_op jit(solution)/shard_map/all_gather | solution.py:1022
  485.5 10.7 %cross_attend_back_kernel.1 = (bf16[640,1024]{1,0:T(8,128)(2,1)}, bf16[640,1024]{1,0:T(8,128)(2,1)}, bf16[640,1024]{1,0:T(8,128)(2,1)}) custom-call(s32[2]{0:T(128)} %get-tuple-element.472.place_ref, bf16[640,1024]{1,0:T(8,128)(2,1)} %convolution_convert_fusion.15.q_ref, bf16[640,2048]{1,0:T(8,128)(2,1)} %convolution_convert_fusion.4.k_ref.v_ref, ...), custom_call_target="tpu_custom_call" | custom-call | flops 4194304000 | bytes 10485760 | tf_op jit(solution)/shard_map/cross_attend_back_kernel/pallas_call | solution.py:483
  503.8 6.3 convolution_convert_fusion.8
  510.1 4.6 convolution_convert_fusion.13
  514.8 20.8 %collective-permute-done.4 = bf16[640,1024]{1,0:T(8,128)(2,1)S(1)} collective-permute-done((bf16[640,1024]{1,0:T(8,128)(2,1)S(1)}, bf16[640,1024]{1,0:T(8,128)(2,1)S(1)}, u32[]{:S(2)}, u32[]{:S(2)}) %collective-permute-start.4) | collective-permute-done | bytes 1310752 | tf_op jit(solution)/shard_map/ppermute | solution.py:1085
  560.7 25.0 %collective-permute-done.5 = bf16[640,1024]{1,0:T(8,128)(2,1)S(1)} collective-permute-done((bf16[640,1024]{1,0:T(8,128)(2,1)}, bf16[640,1024]{1,0:T(8,128)(2,1)S(1)}, u32[]{:S(2)}, u32[]{:S(2)}) %collective-permute-start.5) | collective-permute-done | bytes 1310752 | tf_op jit(solution)/shard_map/ppermute | solution.py:1090
  589.1 4.8 all-to-all-start.8
  598.6 39.0 %expert_back.2 = (bf16[768,1024]{1,0:T(8,128)(2,1)}, bf16[2,832,1024]{2,1,0:T(8,128)(2,1)}, bf16[2,832,1024]{2,1,0:T(8,128)(2,1)}, bf16[2,832,2816]{2,1,0:T(8,12...) custom-call(s32[2]{0:T(128)} %get-tuple-element.230.flags_ref, ...), custom_call_target="tpu_custom_call" | custom-call | flops 22145925120 | bytes 17301504 | tf_op jit(solution)/shard_map/expert_back/pallas_call | solution.py:757
  637.7 5.4 all-to-all-start.10
  648.9 41.4 %expert_back.3 = (bf16[832,1024]{1,0:T(8,128)(2,1)}, bf16[2,832,1024]{2,1,0:T(8,128)(2,1)}, bf16[2,832,1024]{2,1,0:T(8,128)(2,1)}, bf16[2,832,2816]{2,1,0:T(8,12...) custom-call(s32[2]{0:T(128)} %get-tuple-element.230.flags_ref, ...), custom_call_target="tpu_custom_call", output_to_operand_aliasing={{1}: (8, {}), {2}: (9, {}), {3}: (10, {}), {4}: (11, {}), {... | custom-call | flops 23991418880 | bytes 17301504 | tf_op jit(solution)/shard_map/expert_back/pallas_call | solution.py:757
  690.3 5.2 all-to-all-start.11
  696.1 8.0 convolution_convert_fusion.1
  705.6 8.4 convolution_convert_fusion
  724.5 13.9 %collective-permute-done.9.refs_0_ = bf16[256,2816]{1,0:T(8,128)(2,1)} collective-permute-done((bf16[256,2816]{1,0:T(8,128)(2,1)}, bf16[256,2816]{1,0:T(8,128)(2,1)}, u32[]{:S(2)}, u32[]{:S(2)}) %collective-permute-start.9) | collective-permute-done | bytes 1441824 | tf_op jit(solution)/shard_map/ppermute | solution.py:1168
  763.3 17.1 %self_attend_back_kernel.2 = (bf16[640,512]{1,0:T(8,128)(2,1)}, bf16[640,512]{1,0:T(8,128)(2,1)}, bf16[640,512]{1,0:T(8,128)(2,1)}, f32[4,2,1024]{2,1,0:T(2,128)}) custom-call(s32[2]{0:T(128)} %get-tuple-element.472.place_ref, bf16[640,3072]{1,0:T(8,128)(2,1)} %fusion.4.q_ref.k_ref.v_ref, bf16[640,3072]{1,0:T(8,128)(2,1)} %fusion.4.q_ref.k_ref.v_ref, ...), custom_call_target="tpu_custom_call" | custom-call | flops 2097152000 | bytes 10485760 | tf_op jit(solution)/shard_map/self_attend_back_kernel/pallas_call | solution.py:483
  781.0 17.3 %self_attend_back_kernel.3 = (bf16[640,512]{1,0:T(8,128)(2,1)}, bf16[640,512]{1,0:T(8,128)(2,1)}, bf16[640,512]{1,0:T(8,128)(2,1)}, f32[4,2,1024]{2,1,0:T(2,128)}) custom-call(s32[2]{0:T(128)} %get-tuple-element.472.place_ref, bf16[640,3072]{1,0:T(8,128)(2,1)} %fusion.4.q_ref.k_ref.v_ref, bf16[640,3072]{1,0:T(8,128)(2,1)} %fusion.4.q_ref.k_ref.v_ref, ...), custom_call_target="tpu_custom_call" | custom-call | flops 2097152000 | bytes 10485760 | tf_op jit(solution)/shard_map/self_attend_back_kernel/pallas_call | solution.py:483
  798.3 5.6 convolution_convert_fusion.3
  803.9 5.8 all-gather.5.cloned.1.call-done
  809.9 4.6 fusion.169
  819.8 7.3 fusion
  838.6 5.8 pad_maximum_fusion
  845.0 17.9 %convolution_bitcast_fusion.kept_ref = f32[1024,2816]{1,0:T(8,128)} fusion(bf16[2,832,1024]{2,1,0:T(8,128)(2,1)} %get-tuple-element.258, bf16[2,832,2816]{2,1,0:T(8,128)(2,1)} %get-tuple-element.317), kind=kOutput, calls=%fused_computation | convolution fusion | flops 9596567552 | bytes 24313856 | tf_op jit(solution)/shard_map/dot_general | solution.py:94
  864.4 10.0 fusion.33
  883.1 12.4 %add_pieces.2 = f32[1024,2816]{1,0:T(8,128)} custom-call(f32[1024,2816]{1,0:T(8,128)} %convolution_bitcast_fusion.kept_ref, bf16[256,2816]{1,0:T(8,128)(2,1)} %collective-permute-done.9.refs_0_, bf16[256,2816]{1,0:T(8,128)(2,1)} %collective-permute-done.10.refs_1_, bf16[128,2816]{1,0:T(8,128)(2,1)} %collective-permute-done.11.refs_2_, ...), custom_call_target="tpu_custom_call" | custom-call | flops 2883584 | bytes 28835840 | tf_op jit(solution)/shard_map/add_pieces/pallas_call | solution.py:859
  897.9 11.9 %fusion.7.kept_ref = f32[1408,1024]{1,0:T(8,128)} fusion(bf16[1664,1024]{1,0:T(8,128)(2,1)} %bitcast.296, bf16[1664,2816]{1,0:T(8,128)(2,1)} %bitcast.294, pred[]{:T(512)S(6)} %eq.594), kind=kOutput, calls=%fused_computation.12 | convolution fusion | flops 4800626688 | bytes 18546688 | tf_op jit(solution)/shard_map/dot_general | solution.py:94
  914.7 15.1 %collective-permute-done.17.refs_1_ = bf16[352,1024]{1,0:T(8,128)(2,1)} collective-permute-done((bf16[352,1024]{1,0:T(8,128)(2,1)S(1)}, bf16[352,1024]{1,0:T(8,128)(2,1)}, u32[]{:S(2)}, u32[]{:S(2)}) %collective-permute-start.17) | collective-permute-done | bytes 720928 | tf_op jit(solution)/shard_map/ppermute | solution.py:1168
  931.6 6.5 collective-permute-done.18
  963.8 15.4 %collective-permute-done.19.refs_2_ = bf16[704,1024]{1,0:T(8,128)(2,1)S(1)} collective-permute-done((bf16[704,1024]{1,0:T(8,128)(2,1)}, bf16[704,1024]{1,0:T(8,128)(2,1)S(1)}, u32[]{:S(2)}, u32[]{:S(2)}) %collective-permute-start.19) | collective-permute-done | bytes 1441824 | tf_op jit(solution)/shard_map/ppermute | solution.py:1168
  980.3 6.4 add_pieces.3
  (464 shorter events, 292.5 us)
Async XLA Ops:
  7.2 35.6 %copy-start = (bf16[1,1024,1024]{2,1,0:T(8,128)(2,1)S(1)}, bf16[1,1024,1024]{2,1,0:T(8,128)(2,1)}, u32[]{:S(2)}) copy-start(bf16[1,1024,1024]{2,1,0:T(8,128)(2,1)} %param.55) | copy-start | bytes 6291460
  12.3 34.4 %copy-start.65 = (f32[1,1,1024]{2,0,1:T(1,128)}, f32[1,1,1024]{2,0,1:T(1,128)S(1)}, u32[]{:S(2)}) copy-start(f32[1,1,1024]{2,0,1:T(1,128)S(1)} %get-tuple-element.460) | copy-start | bytes 12292
  51.9 44.4 %all-to-all-start = ((bf16[8,96,1024]{2,1,0:T(8,128)(2,1)}), bf16[8,96,1024]{2,1,0:T(8,128)(2,1)}, u32[]{:S(2)}, u32[]{:S(2)}) async-start(bf16[8,96,1024]{2,1,0:T(8,128)(2,1)} %bitcast.242), calls=%async_computation | async-start | bytes 3145728 | tf_op jit(solution)/shard_map/all_to_all | solution.py:559
  96.3 45.0 %all-to-all-start.2 = ((bf16[8,104,1024]{2,1,0:T(8,128)(2,1)}), bf16[8,104,1024]{2,1,0:T(8,128)(2,1)}, u32[]{:S(2)}, u32[]{:S(2)}) async-start(bf16[8,104,1024]{2,1,0:T(8,128)(2,1)} %bitcast.237), calls=%async_computation.2 | async-start | bytes 3407872 | tf_op jit(solution)/shard_map/all_to_all | solution.py:559
  104.3 33.2 %collective-permute-start = (bf16[352,2048]{1,0:T(8,128)(2,1)}, bf16[352,2048]{1,0:T(8,128)(2,1)}, u32[]{:S(2)}, u32[]{:S(2)}) collective-permute-start(bf16[352,2048]{1,0:T(8,128)(2,1)} %get-tuple-element.194), channel_id=1, source_target_pairs={{0,16},{1,17},{2,18},{3,19},{4,20},{5,21},{6,22},{7,23},{8,24},{9,... | collective-permute-start | bytes 4325384 | tf_op jit(solution)/shard_map/ppermute | solution.py:982
  141.3 42.1 %all-to-all-start.1 = ((bf16[8,96,1024]{2,1,0:T(8,128)(2,1)}), bf16[8,96,1024]{2,1,0:T(8,128)(2,1)}, u32[]{:S(2)}, u32[]{:S(2)}) async-start(bf16[8,96,1024]{2,1,0:T(8,128)(2,1)} %bitcast.240), calls=%async_computation.1 | async-start | bytes 3145728 | tf_op jit(solution)/shard_map/all_to_all | solution.py:559
  145.6 33.3 %collective-permute-start.1 = (bf16[352,2048]{1,0:T(8,128)(2,1)}, bf16[352,2048]{1,0:T(8,128)(2,1)}, u32[]{:S(2)}, u32[]{:S(2)}) collective-permute-start(bf16[352,2048]{1,0:T(8,128)(2,1)} %get-tuple-element.197), channel_id=1, source_target_pairs={{0,16},{1,17},{2,18},{3,19},{4,20},{5,21},{6,22},{7,23},{8,24},{9,... | collective-permute-start | bytes 4325384 | tf_op jit(solution)/shard_map/ppermute | solution.py:982
  183.4 45.0 %all-to-all-start.3 = ((bf16[8,104,1024]{2,1,0:T(8,128)(2,1)}), bf16[8,104,1024]{2,1,0:T(8,128)(2,1)}, u32[]{:S(2)}, u32[]{:S(2)}) async-start(bf16[8,104,1024]{2,1,0:T(8,128)(2,1)} %bitcast.236), calls=%async_computation.3 | async-start | bytes 3407872 | tf_op jit(solution)/shard_map/all_to_all | solution.py:559
  187.7 30.4 %collective-permute-start.2 = (bf16[320,2048]{1,0:T(8,128)(2,1)}, bf16[320,2048]{1,0:T(8,128)(2,1)}, u32[]{:S(2)}, u32[]{:S(2)}) collective-permute-start(bf16[320,2048]{1,0:T(8,128)(2,1)} %pad_maximum_fusion.2), channel_id=1, source_target_pairs={{0,16},{1,17},{2,18},{3,19},{4,20},{5,21},{6,22},{7,23},{8,24},{9,... | collective-permute-start | bytes 3932168 | tf_op jit(solution)/shard_map/ppermute | solution.py:987
  190.1 280.0 %copy-start.89 = (s32[640]{0:T(1024)}, s32[640]{0:T(1024)S(1)}, u32[]{:S(2)}) copy-start(s32[640]{0:T(1024)S(1)} %get-tuple-element.430) | copy-start | bytes 7684
  190.2 283.1 %copy-start.63 = (s32[640]{0:T(1024)}, s32[640]{0:T(1024)S(1)}, u32[]{:S(2)}) copy-start(s32[640]{0:T(1024)S(1)} %get-tuple-element.431) | copy-start | bytes 7684
  238.4 29.7 %collective-permute-start.3 = (bf16[640,1024]{1,0:T(8,128)(2,1)S(1)}, bf16[640,1024]{1,0:T(8,128)(2,1)S(1)}, u32[]{:S(2)}, u32[]{:S(2)}) collective-permute-start(bf16[640,1024]{1,0:T(8,128)(2,1)S(1)} %multiply_convert_fusion.3), channel_id=1, source_target_pairs={{0,16},{1,17},{2,18},{3,19},{4,20},{5,21},{6,22},{7,23},{8,24},{9,... | collective-permute-start | bytes 3932168 | tf_op jit(solution)/shard_map/ppermute | solution.py:996
  284.1 197.2 %copy-start.61 = (f32[640]{0:T(1024)}, f32[640]{0:T(1024)S(1)}, u32[]{:S(2)}) copy-start(f32[640]{0:T(1024)S(1)} %add_rsqrt_fusion) | copy-start | bytes 7684
  286.8 42.1 %all-to-all-start.4 = ((bf16[8,96,1024]{2,1,0:T(8,128)(2,1)}), bf16[8,96,1024]{2,1,0:T(8,128)(2,1)}, u32[]{:S(2)}, u32[]{:S(2)}) async-start(bf16[8,96,1024]{2,1,0:T(8,128)(2,1)} %bitcast.243), calls=%async_computation.4 | async-start | bytes 3145728 | tf_op jit(solution)/shard_map/all_to_all | solution.py:559
  328.9 44.9 %all-to-all-start.6 = ((bf16[8,104,1024]{2,1,0:T(8,128)(2,1)}), bf16[8,104,1024]{2,1,0:T(8,128)(2,1)}, u32[]{:S(2)}, u32[]{:S(2)}) async-start(bf16[8,104,1024]{2,1,0:T(8,128)(2,1)} %bitcast.238), calls=%async_computation.6 | async-start | bytes 3407872 | tf_op jit(solution)/shard_map/all_to_all | solution.py:559
  373.8 42.9 %all-to-all-start.5 = ((bf16[8,96,1024]{2,1,0:T(8,128)(2,1)}), bf16[8,96,1024]{2,1,0:T(8,128)(2,1)}, u32[]{:S(2)}, u32[]{:S(2)}) async-start(bf16[8,96,1024]{2,1,0:T(8,128)(2,1)} %bitcast.241), calls=%async_computation.5 | async-start | bytes 3145728 | tf_op jit(solution)/shard_map/all_to_all | solution.py:559
  416.8 53.4 %all-to-all-start.7 = ((bf16[8,104,1024]{2,1,0:T(8,128)(2,1)}), bf16[8,104,1024]{2,1,0:T(8,128)(2,1)}, u32[]{:S(2)}, u32[]{:S(2)}) async-start(bf16[8,104,1024]{2,1,0:T(8,128)(2,1)} %bitcast.234), calls=%async_computation.7 | async-start | bytes 3407872 | tf_op jit(solution)/shard_map/all_to_all | solution.py:559
  426.0 50.4 %copy-start.71 = (f32[640]{0:T(1024)}, f32[640]{0:T(1024)S(1)}, u32[]{:S(2)}) copy-start(f32[640]{0:T(1024)S(1)} %get-tuple-element.461) | copy-start | bytes 7684
  426.1 50.4 %copy-start.73 = (f32[640]{0:T(1024)}, f32[640]{0:T(1024)S(1)}, u32[]{:S(2)}) copy-start(f32[640]{0:T(1024)S(1)} %get-tuple-element.462) | copy-start | bytes 7684
  433.8 36.4 %copy-start.98 = (s32[832]{0:T(1024)S(1)}, s32[832]{0:T(1024)}, u32[]{:S(2)}) copy-start(s32[832]{0:T(1024)} %constant.106) | copy-start | bytes 9988
  502.2 33.4 %collective-permute-start.4 = (bf16[640,1024]{1,0:T(8,128)(2,1)S(1)}, bf16[640,1024]{1,0:T(8,128)(2,1)S(1)}, u32[]{:S(2)}, u32[]{:S(2)}) collective-permute-start(bf16[640,1024]{1,0:T(8,128)(2,1)S(1)} %add_convert_fusion.2), channel_id=1, source_target_pairs={{16,0},{17,1},{18,2},{19,3},{20,4},{21,5},{22,6},{23,7},{24,8},{25... | collective-permute-start | bytes 3932168 | tf_op jit(solution)/shard_map/ppermute | solution.py:1085
  510.1 26.9 %copy-start.15 = (f32[640,1024]{1,0:T(8,128)S(1)}, f32[640,1024]{1,0:T(8,128)}, u32[]{:S(2)}) copy-start(f32[640,1024]{1,0:T(8,128)} %get-tuple-element.467) | copy-start | bytes 7864324
  542.8 46.4 %all-to-all-start.9 = ((bf16[8,96,1024]{2,1,0:T(8,128)(2,1)}), bf16[8,96,1024]{2,1,0:T(8,128)(2,1)}, u32[]{:S(2)}, u32[]{:S(2)}) async-start(bf16[8,96,1024]{2,1,0:T(8,128)(2,1)} %bitcast.231), calls=%async_computation.9 | async-start | bytes 3145728 | tf_op jit(solution)/shard_map/all_to_all | solution.py:559
  552.6 33.1 %collective-permute-start.5 = (bf16[640,1024]{1,0:T(8,128)(2,1)}, bf16[640,1024]{1,0:T(8,128)(2,1)S(1)}, u32[]{:S(2)}, u32[]{:S(2)}) collective-permute-start(bf16[640,1024]{1,0:T(8,128)(2,1)} %get-tuple-element.226), channel_id=1, source_target_pairs={{16,0},{17,1},{18,2},{19,3},{20,4},{21,5},{22,6},{23,7},{24,8},{25... | collective-permute-start | bytes 3932168 | tf_op jit(solution)/shard_map/ppermute | solution.py:1090
  589.1 48.6 %all-to-all-start.8 = ((bf16[8,104,1024]{2,1,0:T(8,128)(2,1)}), bf16[8,104,1024]{2,1,0:T(8,128)(2,1)}, u32[]{:S(2)}, u32[]{:S(2)}) async-start(bf16[8,104,1024]{2,1,0:T(8,128)(2,1)} %bitcast.230), calls=%async_computation.8 | async-start | bytes 3407872 | tf_op jit(solution)/shard_map/all_to_all | solution.py:559
  593.9 144.7 %copy-start.80 = (f32[640]{0:T(1024)}, f32[640]{0:T(1024)S(1)}, u32[]{:S(2)}) copy-start(f32[640]{0:T(1024)S(1)} %subtract_multiply_fusion) | copy-start | bytes 7684
  594.9 42.8 %collective-permute-start.7 = (bf16[512,1024]{1,0:T(8,128)(2,1)}, bf16[512,1024]{1,0:T(8,128)(2,1)}, u32[]{:S(2)}, u32[]{:S(2)}) collective-permute-start(bf16[512,1024]{1,0:T(8,128)(2,1)} %get-tuple-element.237), channel_id=1, source_target_pairs={{0,1},{1,0},{2,3},{3,2},{4,5},{5,4},{6,7},{7,6},{8,9},{9,8},{10,11... | collective-permute-start | bytes 3145736 | tf_op jit(solution)/shard_map/ppermute | solution.py:1120
  596.4 41.3 %collective-permute-start.6 = (bf16[640,1024]{1,0:T(8,128)(2,1)}, bf16[640,1024]{1,0:T(8,128)(2,1)}, u32[]{:S(2)}, u32[]{:S(2)}) collective-permute-start(bf16[640,1024]{1,0:T(8,128)(2,1)} %get-tuple-element.235), channel_id=1, source_target_pairs={{16,0},{17,1},{18,2},{19,3},{20,4},{21,5},{22,6},{23,7},{24,8},{25... | collective-permute-start | bytes 3932168 | tf_op jit(solution)/shard_map/ppermute | solution.py:1108
  637.7 52.6 %all-to-all-start.10 = ((bf16[8,96,1024]{2,1,0:T(8,128)(2,1)}), bf16[8,96,1024]{2,1,0:T(8,128)(2,1)}, u32[]{:S(2)}, u32[]{:S(2)}) async-start(bf16[8,96,1024]{2,1,0:T(8,128)(2,1)} %bitcast.239), calls=%async_computation.10 | async-start | bytes 3145728 | tf_op jit(solution)/shard_map/all_to_all | solution.py:559
  648.3 41.9 %collective-permute-start.8 = (bf16[512,1024]{1,0:T(8,128)(2,1)S(1)}, bf16[512,1024]{1,0:T(8,128)(2,1)}, u32[]{:S(2)}, u32[]{:S(2)}) collective-permute-start(bf16[512,1024]{1,0:T(8,128)(2,1)S(1)} %get-tuple-element.449), channel_id=1, source_target_pairs={{0,1},{1,0},{2,3},{3,2},{4,5},{5,4},{6,7},{7,6},{8,9},{9,8},{10,11... | collective-permute-start | bytes 3145736 | tf_op jit(solution)/shard_map/ppermute | solution.py:791
  690.3 48.1 %all-to-all-start.11 = ((bf16[8,104,1024]{2,1,0:T(8,128)(2,1)}), bf16[8,104,1024]{2,1,0:T(8,128)(2,1)}, u32[]{:S(2)}, u32[]{:S(2)}) async-start(bf16[8,104,1024]{2,1,0:T(8,128)(2,1)} %bitcast.235), calls=%async_computation.11 | async-start | bytes 3407872 | tf_op jit(solution)/shard_map/all_to_all | solution.py:559
  695.6 84.8 %reduce-scatter.4.cloned.1.call-start = ((), (), s32[]{:S(2)}) async-start(), calls=%async_computation.15 | async-start | bytes 2359296 | tf_op jit(solution)/shard_map/reduce_scatter | solution.py:806
  704.1 34.3 %collective-permute-start.9 = (bf16[256,2816]{1,0:T(8,128)(2,1)}, bf16[256,2816]{1,0:T(8,128)(2,1)}, u32[]{:S(2)}, u32[]{:S(2)}) collective-permute-start(bf16[256,2816]{1,0:T(8,128)(2,1)} %convolution_convert_fusion.1), channel_id=1, source_target_pairs={{0,1},{1,0},{2,3},{3,2},{4,5},{5,4},{6,7},{7,6},{8,9},{9,8},{10,11... | collective-permute-start | bytes 4325384 | tf_op jit(solution)/shard_map/ppermute | solution.py:1168
  738.4 71.3 %all-gather.5.cloned.1.call-start = ((), (), s32[]{:S(2)}) async-start(), calls=%async_computation.16 | async-start | bytes 2359296 | tf_op jit(solution)/shard_map/all_gather | solution.py:810
  744.4 36.0 %collective-permute-start.10 = (bf16[256,2816]{1,0:T(8,128)(2,1)S(1)}, bf16[256,2816]{1,0:T(8,128)(2,1)}, u32[]{:S(2)}, u32[]{:S(2)}) collective-permute-start(bf16[256,2816]{1,0:T(8,128)(2,1)S(1)} %slice.211), channel_id=1, source_target_pairs={{0,1},{1,0},{2,3},{3,2},{4,5},{5,4},{6,7},{7,6},{8,9},{9,8},{10,11... | collective-permute-start | bytes 4325384 | tf_op jit(solution)/shard_map/ppermute | solution.py:1168
  780.4 82.5 %reduce-scatter.8.cloned.1.call-start = ((), (), s32[]{:S(2)}) async-start(), calls=%async_computation.18 | async-start | bytes 3538944 | tf_op jit(solution)/shard_map/reduce_scatter | solution.py:806
  780.5 17.8 %collective-permute-start.11 = (bf16[128,2816]{1,0:T(8,128)(2,1)}, bf16[128,2816]{1,0:T(8,128)(2,1)}, u32[]{:S(2)}, u32[]{:S(2)}) collective-permute-start(bf16[128,2816]{1,0:T(8,128)(2,1)} %get-tuple-element.285), channel_id=1, source_target_pairs={{0,1},{1,0},{2,3},{3,2},{4,5},{5,4},{6,7},{7,6},{8,9},{9,8},{10,11... | collective-permute-start | bytes 2162696 | tf_op jit(solution)/shard_map/ppermute | solution.py:1168
  809.7 120.1 %reduce-scatter.6.cloned.1.call-start = ((), (), s32[]{:S(2)}) async-start(), calls=%async_computation.17 | async-start | bytes 6193152 | tf_op jit(solution)/shard_map/reduce_scatter | solution.py:806
  814.6 21.2 %collective-permute-start.12 = (bf16[128,2816]{1,0:T(8,128)(2,1)}, bf16[128,2816]{1,0:T(8,128)(2,1)}, u32[]{:S(2)}, u32[]{:S(2)}) collective-permute-start(bf16[128,2816]{1,0:T(8,128)(2,1)} %get-tuple-element.311), channel_id=1, source_target_pairs={{0,1},{1,0},{2,3},{3,2},{4,5},{5,4},{6,7},{7,6},{8,9},{9,8},{10,11... | collective-permute-start | bytes 2162696 | tf_op jit(solution)/shard_map/ppermute | solution.py:1168
  844.4 101.6 %all-gather.9.cloned.1.call-start = ((), (), s32[]{:S(2)}) async-start(), calls=%async_computation.20 | async-start | bytes 1769472 | tf_op jit(solution)/shard_map/all_gather | solution.py:810
  844.5 18.4 %collective-permute-start.13 = (bf16[128,2816]{1,0:T(8,128)(2,1)}, bf16[128,2816]{1,0:T(8,128)(2,1)}, u32[]{:S(2)}, u32[]{:S(2)}) collective-permute-start(bf16[128,2816]{1,0:T(8,128)(2,1)} %get-tuple-element.322), channel_id=1, source_target_pairs={{0,1},{1,0},{2,3},{3,2},{4,5},{5,4},{6,7},{7,6},{8,9},{9,8},{10,11... | collective-permute-start | bytes 2162696 | tf_op jit(solution)/shard_map/ppermute | solution.py:1168
  862.9 18.1 %collective-permute-start.14 = (bf16[128,2816]{1,0:T(8,128)(2,1)}, bf16[128,2816]{1,0:T(8,128)(2,1)}, u32[]{:S(2)}, u32[]{:S(2)}) collective-permute-start(bf16[128,2816]{1,0:T(8,128)(2,1)} %get-tuple-element.335), channel_id=1, source_target_pairs={{0,1},{1,0},{2,3},{3,2},{4,5},{5,4},{6,7},{7,6},{8,9},{9,8},{10,11... | collective-permute-start | bytes 2162696 | tf_op jit(solution)/shard_map/ppermute | solution.py:1168
  881.7 13.9 %collective-permute-start.15 = (bf16[64,1536]{1,0:T(8,128)(2,1)}, bf16[64,1536]{1,0:T(8,128)(2,1)}, u32[]{:S(2)}, u32[]{:S(2)}) collective-permute-start(bf16[64,1536]{1,0:T(8,128)(2,1)} %constant_dynamic-slice_fusion.1), channel_id=1, source_target_pairs={{0,1},{1,0},{2,3},{3,2},{4,5},{5,4},{6,7},{7,6},{8,9},{9,8},{10,11... | collective-permute-start | bytes 589832 | tf_op jit(solution)/shard_map/ppermute | solution.py:791
  897.2 16.8 %collective-permute-start.16 = (bf16[352,1024]{1,0:T(8,128)(2,1)}, bf16[352,1024]{1,0:T(8,128)(2,1)}, u32[]{:S(2)}, u32[]{:S(2)}) collective-permute-start(bf16[352,1024]{1,0:T(8,128)(2,1)} %get-tuple-element.351), channel_id=1, source_target_pairs={{0,1},{1,0},{2,3},{3,2},{4,5},{5,4},{6,7},{7,6},{8,9},{9,8},{10,11... | collective-permute-start | bytes 2162696 | tf_op jit(solution)/shard_map/ppermute | solution.py:1168
  897.8 88.9 %all-gather.7.cloned.1.call-start = ((), (), s32[]{:S(2)}) async-start(), calls=%async_computation.19 | async-start | bytes 3096576 | tf_op jit(solution)/shard_map/all_gather | solution.py:810
  914.1 15.7 %collective-permute-start.17 = (bf16[352,1024]{1,0:T(8,128)(2,1)S(1)}, bf16[352,1024]{1,0:T(8,128)(2,1)}, u32[]{:S(2)}, u32[]{:S(2)}) collective-permute-start(bf16[352,1024]{1,0:T(8,128)(2,1)S(1)} %copy-done.48), channel_id=1, source_target_pairs={{0,1},{1,0},{2,3},{3,2},{4,5},{5,4},{6,7},{7,6},{8,9},{9,8},{10,11... | collective-permute-start | bytes 2162696 | tf_op jit(solution)/shard_map/ppermute | solution.py:1168
  930.8 7.3 collective-permute-start.18
  949.6 29.6 %collective-permute-start.19 = (bf16[704,1024]{1,0:T(8,128)(2,1)}, bf16[704,1024]{1,0:T(8,128)(2,1)S(1)}, u32[]{:S(2)}, u32[]{:S(2)}) collective-permute-start(bf16[704,1024]{1,0:T(8,128)(2,1)} %slice.218), channel_id=1, source_target_pairs={{0,1},{1,0},{2,3},{3,2},{4,5},{5,4},{6,7},{7,6},{8,9},{9,8},{10,11... | collective-permute-start | bytes 4325384 | tf_op jit(solution)/shard_map/ppermute | solution.py:1168
  (107 other events, 647.0 us)
Sparse Core Ops, SparseCore 0:
  738.5 38.6 reduce-scatter.3
  780.5 29.1 all-gather.4
  812.0 39.8 reduce-scatter.7
  854.6 61.4 reduce-scatter.5
  918.2 23.3 all-gather.8
  943.1 34.5 all-gather.6

commit v6 on v5

--- a/solution.py
+++ b/solution.py
@@ -1236,10 +1236,11 @@
         ],
         axis=1,
     )
+    late_second, gots, sends[5] = together(late_second, gots, sends[5])
+    gots.append(swapped(sends[5]))
     late_second = expert_scatter(late_second)
     keep_in = dot_tn(expert_rows, keep_halves)
-    keep_in, gots, late_first, sends[5], kept = together(keep_in, gots, late_first, sends[5], kept)
-    gots.append(swapped(sends[5]))
+    keep_in, gots, late_first, kept = together(keep_in, gots, late_first, kept)
     actives, expert_grad_rows = kept
     send_out = dot_tn(
         jnp.where(first_group, actives[:, half_ff:], actives[:, :half_ff]), expert_grad_rows
@@ -1265,7 +1266,8 @@
     late_second = group_swap(late_second, group)
     late_second, out_sends, arrived_three = together(late_second, out_sends, arrived_three)
     late_second = expert_gather(late_second)
-    out_gots.append(swapped(out_sends[2]))
+    last_got, late_first = together(swapped(out_sends[2]), late_first)
+    out_gots.append(last_got)
     decoded = (
         second_half
         + dec_gates[0] * collect(arrived_three, code_first)

time: 1020 us -> 1020 us (level)
  no operation moved by 1% of the time
where the time goes in v6:
time: 1020 us; the launch traced here: 1010 us
  Pallas kernels  296 us (29%)
  waiting for transfers between devices  262 us (26%)
  matrix products  228 us (22%)
  starting transfers between devices  84.7 us (8%)
  other arithmetic  52.2 us (5%)
  local copies, waits for them, and re-layouts  37.7 us (4%)
  blocking collectives  30.6 us (3%)
  between operations  16.7 us (2%)
    dot_general x32, matrix products, dot(): return jnp.dot(a, b, preferred_element_type=F32)  113 us
    all_to_all x12, waiting for transfers between devices, exchange(): lax.all_to_all(parts, 'expert', split_axis=0, concat_axis=0, tiled=True)  90.4 us
    pallas_call x2, Pallas kernels, expert_back(): pl.pallas_call(partial(expert_back_kernel, count=rows), grid_spec=pltpu.P...  80.4 us
    pallas_call x2, Pallas kernels, expert_both(): pl.pallas_call(expert_both_kernel, grid=(tiles,), in_specs=[whole, whole]...  74.4 us
    dot_general x10, matrix products, dot_tn(): lax.dot_general(a, b, (((0,), (0,)), ((), ())), preferred_element_type=F32)  73.7 us
    pallas_call x5, Pallas kernels, pair_call(): pl.pallas_call(kernel, grid_spec=pltpu.PrefetchScalarGridSpec(num_scalar_...  71.4 us
    ppermute x9, waiting for transfers between devices, swapped(): return [lax.ppermute(part, 'group', SWAP) for part in parts]  58.5 us
    all_to_all x12, starting transfers between devices, exchange(): lax.all_to_all(parts, 'expert', split_axis=0, concat_axis=0, tiled=True)  57.4 us
  transfers between devices with their start and end apart: 38, of which 19 were waited for; matrix products, arithmetic and copies ran while one was open for 23% of the time, Pallas kernels for 25%

profile of v6, /device:TPU:0, one launch (start us, length us, event | category | flops | bytes accessed | tf_op | source)
XLA Modules:
  0.0 1007.6 jit_solution(6991388319051940208)
XLA Ops:
  15.3 8.8 fusion.4.q_ref.k_ref.v_ref
  24.0 18.7 %self_attend_kernel.1 = (bf16[640,1024]{1,0:T(8,128)(2,1)}, f32[8,2,640]{2,1,0:T(2,128)}) custom-call(s32[2]{0:T(128)} %get-tuple-element.490.place_ref, bf16[640,3072]{1,0:T(8,128)(2,1)} %fusion.4.q_ref.k_ref.v_ref, bf16[640,3072]{1,0:T(8,128)(2,1)} %fusion.4.q_ref.k_ref.v_ref, bf16[640,3072]{1,0:T(8,128)(2,1)} %fusion.4.q_ref.k_ref.v_ref, ...), custom_call_target="tpu_custom_call" | custom-call | flops 1677721600 | bytes 10485760 | tf_op jit(solution)/shard_map/self_attend_kernel/pallas_call | solution.py:483
  51.9 6.4 all-to-all-start
  62.4 33.9 %all-to-all-done = bf16[8,96,1024]{2,1,0:T(8,128)(2,1)} async-done(((bf16[8,96,1024]{2,1,0:T(8,128)(2,1)}), bf16[8,96,1024]{2,1,0:T(8,128)(2,1)}, u32[]{:S(2)}, u32[]{:S(2)}) %all-to-all-start) | async-done | bytes 1572896 | tf_op jit(solution)/shard_map/all_to_all | solution.py:559
  106.7 21.4 %expert_forward.2 = bf16[768,1024]{1,0:T(8,128)(2,1)} custom-call(bf16[768,1024]{1,0:T(8,128)(2,1)} %bitcast.15.x_ref.g_ref.refs_0_, bf16[1024,5632]{1,0:T(8,128)(2,1)} %bitcast.273, bf16[1024,5632]{1,0:T(8,128)(2,1)} %bitcast.274, bf16[2816,1024]{1,0:T(8,128)(2,1)} %bitcast.285), custom_call_target="tpu_custom_call" | custom-call | flops 13287555072 | bytes 17301504 | tf_op jit(solution)/shard_map/expert_forward/pallas_call | solution.py:703
  128.0 9.5 collective-permute-done
  150.5 22.0 %expert_forward.3 = bf16[832,1024]{1,0:T(8,128)(2,1)} custom-call(bf16[832,1024]{1,0:T(8,128)(2,1)} %bitcast.22.x_ref.g_ref.refs_0_, bf16[1024,5632]{1,0:T(8,128)(2,1)} %bitcast.275, bf16[1024,5632]{1,0:T(8,128)(2,1)} %bitcast.276, bf16[2816,1024]{1,0:T(8,128)(2,1)} %bitcast.286), custom_call_target="tpu_custom_call" | custom-call | flops 14394851328 | bytes 17301504 | tf_op jit(solution)/shard_map/expert_forward/pallas_call | solution.py:703
  172.4 6.4 collective-permute-done.1
  198.4 19.7 %collective-permute-done.2 = bf16[320,2048]{1,0:T(8,128)(2,1)} collective-permute-done((bf16[320,2048]{1,0:T(8,128)(2,1)}, bf16[320,2048]{1,0:T(8,128)(2,1)}, u32[]{:S(2)}, u32[]{:S(2)}) %collective-permute-start.2) | collective-permute-done | bytes 1310752 | tf_op jit(solution)/shard_map/ppermute | solution.py:987
  218.1 10.2 %all-to-all-done.3 = bf16[8,104,1024]{2,1,0:T(8,128)(2,1)} async-done(((bf16[8,104,1024]{2,1,0:T(8,128)(2,1)}), bf16[8,104,1024]{2,1,0:T(8,128)(2,1)}, u32[]{:S(2)}, u32[]{:S(2)}) %all-to-all-start.3) | async-done | bytes 1703968 | tf_op jit(solution)/shard_map/all_to_all | solution.py:559
  232.4 5.7 multiply_reduce_fusion.9
  248.5 19.5 %collective-permute-done.3 = bf16[640,1024]{1,0:T(8,128)(2,1)S(1)} collective-permute-done((bf16[640,1024]{1,0:T(8,128)(2,1)S(1)}, bf16[640,1024]{1,0:T(8,128)(2,1)S(1)}, u32[]{:S(2)}, u32[]{:S(2)}) %collective-permute-start.3) | collective-permute-done | bytes 1310752 | tf_op jit(solution)/shard_map/ppermute | solution.py:996
  272.2 7.5 cross_attend_kernel.1
  295.6 33.3 %all-to-all-done.4 = bf16[8,96,1024]{2,1,0:T(8,128)(2,1)} async-done(((bf16[8,96,1024]{2,1,0:T(8,128)(2,1)}), bf16[8,96,1024]{2,1,0:T(8,128)(2,1)}, u32[]{:S(2)}, u32[]{:S(2)}) %all-to-all-start.4) | async-done | bytes 1572896 | tf_op jit(solution)/shard_map/all_to_all | solution.py:559
  333.2 36.0 %expert_both.2 = (bf16[768,1024]{1,0:T(8,128)(2,1)}, bf16[768,2816]{1,0:T(8,128)(2,1)}, f32[768,1]{1,0:T(8,128)}) custom-call(bf16[768,1024]{1,0:T(8,128)(2,1)} %bitcast.27.x_ref.refs_1_, bf16[768,1024]{1,0:T(8,128)(2,1)} %bitcast.15.x_ref.g_ref.refs_0_, bf16[1024,5632]{1,0:T(8,128)(2,1)} %bitcast.277, bf16[1024,5632]{1,0:T(8,128)(2,1)} %bitcast.278, ...), custom_call_target="tpu_custom_call" | custom-call | flops 22145925120 | bytes 17301504 | tf_op jit(solution)/shard_map/expert_both/pallas_call | solution.py:721
  369.2 4.7 all-to-all-done.6
  378.4 38.4 %expert_both.3 = (bf16[832,1024]{1,0:T(8,128)(2,1)}, bf16[832,2816]{1,0:T(8,128)(2,1)}, f32[832,1]{1,0:T(8,128)}) custom-call(bf16[832,1024]{1,0:T(8,128)(2,1)} %bitcast.31.x_ref.refs_1_, bf16[832,1024]{1,0:T(8,128)(2,1)} %bitcast.22.x_ref.g_ref.refs_0_, bf16[1024,5632]{1,0:T(8,128)(2,1)} %bitcast.279, bf16[1024,5632]{1,0:T(8,128)(2,1)} %bitcast.280, ...), custom_call_target="tpu_custom_call" | custom-call | flops 23991418880 | bytes 17301504 | tf_op jit(solution)/shard_map/expert_both/pallas_call | solution.py:721
  416.8 5.0 all-to-all-start.7
  438.2 30.6 %all-gather = f32[64,400]{1,0:T(8,128)S(1)} all-gather(f32[8,400]{1,0:T(8,128)S(1)} %pad_maximum_fusion.7), channel_id=2, replica_groups=mesh['half'=2,'expert'=8,'group'=2] {'expert'}, dimensions={0}, use_global_device_ids=true | all-gather | bytes 115200 | tf_op jit(solution)/shard_map/all_gather | solution.py:1022
  485.5 10.7 %cross_attend_back_kernel.1 = (bf16[640,1024]{1,0:T(8,128)(2,1)}, bf16[640,1024]{1,0:T(8,128)(2,1)}, bf16[640,1024]{1,0:T(8,128)(2,1)}) custom-call(s32[2]{0:T(128)} %get-tuple-element.490.place_ref, bf16[640,1024]{1,0:T(8,128)(2,1)} %convolution_convert_fusion.15.q_ref, bf16[640,2048]{1,0:T(8,128)(2,1)} %convolution_convert_fusion.4.k_ref.v_ref, ...), custom_call_target="tpu_custom_call" | custom-call | flops 4194304000 | bytes 10485760 | tf_op jit(solution)/shard_map/cross_attend_back_kernel/pallas_call | solution.py:483
  503.8 6.3 convolution_convert_fusion.8
  510.1 4.6 convolution_convert_fusion.13
  514.8 20.8 %collective-permute-done.4 = bf16[640,1024]{1,0:T(8,128)(2,1)S(1)} collective-permute-done((bf16[640,1024]{1,0:T(8,128)(2,1)S(1)}, bf16[640,1024]{1,0:T(8,128)(2,1)S(1)}, u32[]{:S(2)}, u32[]{:S(2)}) %collective-permute-start.4) | collective-permute-done | bytes 1310752 | tf_op jit(solution)/shard_map/ppermute | solution.py:1085
  560.7 25.0 %collective-permute-done.5 = bf16[640,1024]{1,0:T(8,128)(2,1)S(1)} collective-permute-done((bf16[640,1024]{1,0:T(8,128)(2,1)}, bf16[640,1024]{1,0:T(8,128)(2,1)S(1)}, u32[]{:S(2)}, u32[]{:S(2)}) %collective-permute-start.5) | collective-permute-done | bytes 1310752 | tf_op jit(solution)/shard_map/ppermute | solution.py:1090
  589.1 4.8 all-to-all-start.8
  598.6 39.0 %expert_back.2 = (bf16[768,1024]{1,0:T(8,128)(2,1)}, bf16[2,832,1024]{2,1,0:T(8,128)(2,1)}, bf16[2,832,1024]{2,1,0:T(8,128)(2,1)}, bf16[2,832,2816]{2,1,0:T(8,12...) custom-call(s32[2]{0:T(128)} %get-tuple-element.239.flags_ref, ...), custom_call_target="tpu_custom_call" | custom-call | flops 22145925120 | bytes 17301504 | tf_op jit(solution)/shard_map/expert_back/pallas_call | solution.py:757
  637.7 5.4 all-to-all-start.10
  648.9 41.4 %expert_back.3 = (bf16[832,1024]{1,0:T(8,128)(2,1)}, bf16[2,832,1024]{2,1,0:T(8,128)(2,1)}, bf16[2,832,1024]{2,1,0:T(8,128)(2,1)}, bf16[2,832,2816]{2,1,0:T(8,12...) custom-call(s32[2]{0:T(128)} %get-tuple-element.239.flags_ref, ...), custom_call_target="tpu_custom_call", output_to_operand_aliasing={{1}: (8, {}), {2}: (9, {}), {3}: (10, {}), {4}: (11, {}), {... | custom-call | flops 23991418880 | bytes 17301504 | tf_op jit(solution)/shard_map/expert_back/pallas_call | solution.py:757
  690.3 5.2 all-to-all-start.11
  696.1 8.0 convolution_convert_fusion.1
  705.6 8.4 convolution_convert_fusion
  724.5 13.9 %collective-permute-done.9.refs_0_ = bf16[256,2816]{1,0:T(8,128)(2,1)} collective-permute-done((bf16[256,2816]{1,0:T(8,128)(2,1)}, bf16[256,2816]{1,0:T(8,128)(2,1)}, u32[]{:S(2)}, u32[]{:S(2)}) %collective-permute-start.9) | collective-permute-done | bytes 1441824 | tf_op jit(solution)/shard_map/ppermute | solution.py:1168
  763.3 17.1 %self_attend_back_kernel.2 = (bf16[640,512]{1,0:T(8,128)(2,1)}, bf16[640,512]{1,0:T(8,128)(2,1)}, bf16[640,512]{1,0:T(8,128)(2,1)}, f32[4,2,1024]{2,1,0:T(2,128)}) custom-call(s32[2]{0:T(128)} %get-tuple-element.490.place_ref, bf16[640,3072]{1,0:T(8,128)(2,1)} %fusion.4.q_ref.k_ref.v_ref, bf16[640,3072]{1,0:T(8,128)(2,1)} %fusion.4.q_ref.k_ref.v_ref, ...), custom_call_target="tpu_custom_call" | custom-call | flops 2097152000 | bytes 10485760 | tf_op jit(solution)/shard_map/self_attend_back_kernel/pallas_call | solution.py:483
  781.0 17.4 %self_attend_back_kernel.3 = (bf16[640,512]{1,0:T(8,128)(2,1)}, bf16[640,512]{1,0:T(8,128)(2,1)}, bf16[640,512]{1,0:T(8,128)(2,1)}, f32[4,2,1024]{2,1,0:T(2,128)}) custom-call(s32[2]{0:T(128)} %get-tuple-element.490.place_ref, bf16[640,3072]{1,0:T(8,128)(2,1)} %fusion.4.q_ref.k_ref.v_ref, bf16[640,3072]{1,0:T(8,128)(2,1)} %fusion.4.q_ref.k_ref.v_ref, ...), custom_call_target="tpu_custom_call" | custom-call | flops 2097152000 | bytes 10485760 | tf_op jit(solution)/shard_map/self_attend_back_kernel/pallas_call | solution.py:483
  798.5 5.6 convolution_convert_fusion.3
  804.1 5.6 all-gather.5.cloned.1.call-done
  809.9 4.6 fusion.169
  819.8 6.9 fusion
  838.7 5.8 pad_maximum_fusion
  844.5 10.0 collective-permute-done.13.refs_4_
  855.3 17.8 %convolution_bitcast_fusion.kept_ref = f32[1024,2816]{1,0:T(8,128)} fusion(bf16[2,832,1024]{2,1,0:T(8,128)(2,1)} %get-tuple-element.267, bf16[2,832,2816]{2,1,0:T(8,128)(2,1)} %get-tuple-element.333), kind=kOutput, calls=%fused_computation | convolution fusion | flops 9596567552 | bytes 24313856 | tf_op jit(solution)/shard_map/dot_general | solution.py:94
  873.1 10.0 fusion.33
  887.6 12.4 %add_pieces.2 = f32[1024,2816]{1,0:T(8,128)} custom-call(f32[1024,2816]{1,0:T(8,128)} %convolution_bitcast_fusion.kept_ref, bf16[256,2816]{1,0:T(8,128)(2,1)} %collective-permute-done.9.refs_0_, bf16[256,2816]{1,0:T(8,128)(2,1)} %collective-permute-done.10.refs_1_, bf16[128,2816]{1,0:T(8,128)(2,1)} %collective-permute-done.11.refs_2_, ...), custom_call_target="tpu_custom_call" | custom-call | flops 2883584 | bytes 28835840 | tf_op jit(solution)/shard_map/add_pieces/pallas_call | solution.py:859
  902.4 11.9 %fusion.7.kept_ref = f32[1408,1024]{1,0:T(8,128)} fusion(bf16[1664,1024]{1,0:T(8,128)(2,1)} %bitcast.296, bf16[1664,2816]{1,0:T(8,128)(2,1)} %bitcast.294, pred[]{:T(512)S(6)} %eq.594), kind=kOutput, calls=%fused_computation.12 | convolution fusion | flops 4800626688 | bytes 18546688 | tf_op jit(solution)/shard_map/dot_general | solution.py:94
  919.3 15.0 %collective-permute-done.17.refs_1_ = bf16[352,1024]{1,0:T(8,128)(2,1)} collective-permute-done((bf16[352,1024]{1,0:T(8,128)(2,1)S(1)}, bf16[352,1024]{1,0:T(8,128)(2,1)}, u32[]{:S(2)}, u32[]{:S(2)}) %collective-permute-start.17) | collective-permute-done | bytes 720928 | tf_op jit(solution)/shard_map/ppermute | solution.py:1168
  936.2 6.4 collective-permute-done.18
  964.8 15.3 %collective-permute-done.19.refs_2_ = bf16[704,1024]{1,0:T(8,128)(2,1)S(1)} collective-permute-done((bf16[704,1024]{1,0:T(8,128)(2,1)}, bf16[704,1024]{1,0:T(8,128)(2,1)S(1)}, u32[]{:S(2)}, u32[]{:S(2)}) %collective-permute-start.19) | collective-permute-done | bytes 1441824 | tf_op jit(solution)/shard_map/ppermute | solution.py:1168
  984.1 6.4 add_pieces.3
  (464 shorter events, 291.5 us)
Async XLA Ops:
  7.2 35.6 %copy-start = (bf16[1,1024,1024]{2,1,0:T(8,128)(2,1)S(1)}, bf16[1,1024,1024]{2,1,0:T(8,128)(2,1)}, u32[]{:S(2)}) copy-start(bf16[1,1024,1024]{2,1,0:T(8,128)(2,1)} %param.55) | copy-start | bytes 6291460
  12.3 34.4 %copy-start.65 = (f32[1,1,1024]{2,0,1:T(1,128)}, f32[1,1,1024]{2,0,1:T(1,128)S(1)}, u32[]{:S(2)}) copy-start(f32[1,1,1024]{2,0,1:T(1,128)S(1)} %get-tuple-element.478) | copy-start | bytes 12292
  51.9 44.4 %all-to-all-start = ((bf16[8,96,1024]{2,1,0:T(8,128)(2,1)}), bf16[8,96,1024]{2,1,0:T(8,128)(2,1)}, u32[]{:S(2)}, u32[]{:S(2)}) async-start(bf16[8,96,1024]{2,1,0:T(8,128)(2,1)} %bitcast.242), calls=%async_computation | async-start | bytes 3145728 | tf_op jit(solution)/shard_map/all_to_all | solution.py:559
  96.3 45.0 %all-to-all-start.2 = ((bf16[8,104,1024]{2,1,0:T(8,128)(2,1)}), bf16[8,104,1024]{2,1,0:T(8,128)(2,1)}, u32[]{:S(2)}, u32[]{:S(2)}) async-start(bf16[8,104,1024]{2,1,0:T(8,128)(2,1)} %bitcast.237), calls=%async_computation.2 | async-start | bytes 3407872 | tf_op jit(solution)/shard_map/all_to_all | solution.py:559
  104.3 33.2 %collective-permute-start = (bf16[352,2048]{1,0:T(8,128)(2,1)}, bf16[352,2048]{1,0:T(8,128)(2,1)}, u32[]{:S(2)}, u32[]{:S(2)}) collective-permute-start(bf16[352,2048]{1,0:T(8,128)(2,1)} %get-tuple-element.203), channel_id=1, source_target_pairs={{0,16},{1,17},{2,18},{3,19},{4,20},{5,21},{6,22},{7,23},{8,24},{9,... | collective-permute-start | bytes 4325384 | tf_op jit(solution)/shard_map/ppermute | solution.py:982
  141.3 42.1 %all-to-all-start.1 = ((bf16[8,96,1024]{2,1,0:T(8,128)(2,1)}), bf16[8,96,1024]{2,1,0:T(8,128)(2,1)}, u32[]{:S(2)}, u32[]{:S(2)}) async-start(bf16[8,96,1024]{2,1,0:T(8,128)(2,1)} %bitcast.240), calls=%async_computation.1 | async-start | bytes 3145728 | tf_op jit(solution)/shard_map/all_to_all | solution.py:559
  145.6 33.3 %collective-permute-start.1 = (bf16[352,2048]{1,0:T(8,128)(2,1)}, bf16[352,2048]{1,0:T(8,128)(2,1)}, u32[]{:S(2)}, u32[]{:S(2)}) collective-permute-start(bf16[352,2048]{1,0:T(8,128)(2,1)} %get-tuple-element.206), channel_id=1, source_target_pairs={{0,16},{1,17},{2,18},{3,19},{4,20},{5,21},{6,22},{7,23},{8,24},{9,... | collective-permute-start | bytes 4325384 | tf_op jit(solution)/shard_map/ppermute | solution.py:982
  183.4 45.0 %all-to-all-start.3 = ((bf16[8,104,1024]{2,1,0:T(8,128)(2,1)}), bf16[8,104,1024]{2,1,0:T(8,128)(2,1)}, u32[]{:S(2)}, u32[]{:S(2)}) async-start(bf16[8,104,1024]{2,1,0:T(8,128)(2,1)} %bitcast.236), calls=%async_computation.3 | async-start | bytes 3407872 | tf_op jit(solution)/shard_map/all_to_all | solution.py:559
  187.7 30.4 %collective-permute-start.2 = (bf16[320,2048]{1,0:T(8,128)(2,1)}, bf16[320,2048]{1,0:T(8,128)(2,1)}, u32[]{:S(2)}, u32[]{:S(2)}) collective-permute-start(bf16[320,2048]{1,0:T(8,128)(2,1)} %pad_maximum_fusion.2), channel_id=1, source_target_pairs={{0,16},{1,17},{2,18},{3,19},{4,20},{5,21},{6,22},{7,23},{8,24},{9,... | collective-permute-start | bytes 3932168 | tf_op jit(solution)/shard_map/ppermute | solution.py:987
  190.1 280.0 %copy-start.89 = (s32[640]{0:T(1024)}, s32[640]{0:T(1024)S(1)}, u32[]{:S(2)}) copy-start(s32[640]{0:T(1024)S(1)} %get-tuple-element.448) | copy-start | bytes 7684
  190.2 283.1 %copy-start.63 = (s32[640]{0:T(1024)}, s32[640]{0:T(1024)S(1)}, u32[]{:S(2)}) copy-start(s32[640]{0:T(1024)S(1)} %get-tuple-element.449) | copy-start | bytes 7684
  238.4 29.7 %collective-permute-start.3 = (bf16[640,1024]{1,0:T(8,128)(2,1)S(1)}, bf16[640,1024]{1,0:T(8,128)(2,1)S(1)}, u32[]{:S(2)}, u32[]{:S(2)}) collective-permute-start(bf16[640,1024]{1,0:T(8,128)(2,1)S(1)} %multiply_convert_fusion.3), channel_id=1, source_target_pairs={{0,16},{1,17},{2,18},{3,19},{4,20},{5,21},{6,22},{7,23},{8,24},{9,... | collective-permute-start | bytes 3932168 | tf_op jit(solution)/shard_map/ppermute | solution.py:996
  284.1 197.2 %copy-start.61 = (f32[640]{0:T(1024)}, f32[640]{0:T(1024)S(1)}, u32[]{:S(2)}) copy-start(f32[640]{0:T(1024)S(1)} %add_rsqrt_fusion) | copy-start | bytes 7684
  286.8 42.1 %all-to-all-start.4 = ((bf16[8,96,1024]{2,1,0:T(8,128)(2,1)}), bf16[8,96,1024]{2,1,0:T(8,128)(2,1)}, u32[]{:S(2)}, u32[]{:S(2)}) async-start(bf16[8,96,1024]{2,1,0:T(8,128)(2,1)} %bitcast.243), calls=%async_computation.4 | async-start | bytes 3145728 | tf_op jit(solution)/shard_map/all_to_all | solution.py:559
  328.9 44.9 %all-to-all-start.6 = ((bf16[8,104,1024]{2,1,0:T(8,128)(2,1)}), bf16[8,104,1024]{2,1,0:T(8,128)(2,1)}, u32[]{:S(2)}, u32[]{:S(2)}) async-start(bf16[8,104,1024]{2,1,0:T(8,128)(2,1)} %bitcast.238), calls=%async_computation.6 | async-start | bytes 3407872 | tf_op jit(solution)/shard_map/all_to_all | solution.py:559
  373.8 42.9 %all-to-all-start.5 = ((bf16[8,96,1024]{2,1,0:T(8,128)(2,1)}), bf16[8,96,1024]{2,1,0:T(8,128)(2,1)}, u32[]{:S(2)}, u32[]{:S(2)}) async-start(bf16[8,96,1024]{2,1,0:T(8,128)(2,1)} %bitcast.241), calls=%async_computation.5 | async-start | bytes 3145728 | tf_op jit(solution)/shard_map/all_to_all | solution.py:559
  416.8 53.4 %all-to-all-start.7 = ((bf16[8,104,1024]{2,1,0:T(8,128)(2,1)}), bf16[8,104,1024]{2,1,0:T(8,128)(2,1)}, u32[]{:S(2)}, u32[]{:S(2)}) async-start(bf16[8,104,1024]{2,1,0:T(8,128)(2,1)} %bitcast.234), calls=%async_computation.7 | async-start | bytes 3407872 | tf_op jit(solution)/shard_map/all_to_all | solution.py:559
  426.0 50.4 %copy-start.71 = (f32[640]{0:T(1024)}, f32[640]{0:T(1024)S(1)}, u32[]{:S(2)}) copy-start(f32[640]{0:T(1024)S(1)} %get-tuple-element.479) | copy-start | bytes 7684
  426.1 50.4 %copy-start.73 = (f32[640]{0:T(1024)}, f32[640]{0:T(1024)S(1)}, u32[]{:S(2)}) copy-start(f32[640]{0:T(1024)S(1)} %get-tuple-element.480) | copy-start | bytes 7684
  433.8 36.4 %copy-start.98 = (s32[832]{0:T(1024)S(1)}, s32[832]{0:T(1024)}, u32[]{:S(2)}) copy-start(s32[832]{0:T(1024)} %constant.106) | copy-start | bytes 9988
  502.2 33.4 %collective-permute-start.4 = (bf16[640,1024]{1,0:T(8,128)(2,1)S(1)}, bf16[640,1024]{1,0:T(8,128)(2,1)S(1)}, u32[]{:S(2)}, u32[]{:S(2)}) collective-permute-start(bf16[640,1024]{1,0:T(8,128)(2,1)S(1)} %add_convert_fusion.2), channel_id=1, source_target_pairs={{16,0},{17,1},{18,2},{19,3},{20,4},{21,5},{22,6},{23,7},{24,8},{25... | collective-permute-start | bytes 3932168 | tf_op jit(solution)/shard_map/ppermute | solution.py:1085
  510.1 26.9 %copy-start.15 = (f32[640,1024]{1,0:T(8,128)S(1)}, f32[640,1024]{1,0:T(8,128)}, u32[]{:S(2)}) copy-start(f32[640,1024]{1,0:T(8,128)} %get-tuple-element.485) | copy-start | bytes 7864324
  542.8 46.4 %all-to-all-start.9 = ((bf16[8,96,1024]{2,1,0:T(8,128)(2,1)}), bf16[8,96,1024]{2,1,0:T(8,128)(2,1)}, u32[]{:S(2)}, u32[]{:S(2)}) async-start(bf16[8,96,1024]{2,1,0:T(8,128)(2,1)} %bitcast.231), calls=%async_computation.9 | async-start | bytes 3145728 | tf_op jit(solution)/shard_map/all_to_all | solution.py:559
  552.6 33.1 %collective-permute-start.5 = (bf16[640,1024]{1,0:T(8,128)(2,1)}, bf16[640,1024]{1,0:T(8,128)(2,1)S(1)}, u32[]{:S(2)}, u32[]{:S(2)}) collective-permute-start(bf16[640,1024]{1,0:T(8,128)(2,1)} %get-tuple-element.235), channel_id=1, source_target_pairs={{16,0},{17,1},{18,2},{19,3},{20,4},{21,5},{22,6},{23,7},{24,8},{25... | collective-permute-start | bytes 3932168 | tf_op jit(solution)/shard_map/ppermute | solution.py:1090
  589.1 48.6 %all-to-all-start.8 = ((bf16[8,104,1024]{2,1,0:T(8,128)(2,1)}), bf16[8,104,1024]{2,1,0:T(8,128)(2,1)}, u32[]{:S(2)}, u32[]{:S(2)}) async-start(bf16[8,104,1024]{2,1,0:T(8,128)(2,1)} %bitcast.230), calls=%async_computation.8 | async-start | bytes 3407872 | tf_op jit(solution)/shard_map/all_to_all | solution.py:559
  593.9 144.7 %copy-start.80 = (f32[640]{0:T(1024)}, f32[640]{0:T(1024)S(1)}, u32[]{:S(2)}) copy-start(f32[640]{0:T(1024)S(1)} %subtract_multiply_fusion) | copy-start | bytes 7684
  594.9 42.8 %collective-permute-start.7 = (bf16[512,1024]{1,0:T(8,128)(2,1)}, bf16[512,1024]{1,0:T(8,128)(2,1)}, u32[]{:S(2)}, u32[]{:S(2)}) collective-permute-start(bf16[512,1024]{1,0:T(8,128)(2,1)} %get-tuple-element.246), channel_id=1, source_target_pairs={{0,1},{1,0},{2,3},{3,2},{4,5},{5,4},{6,7},{7,6},{8,9},{9,8},{10,11... | collective-permute-start | bytes 3145736 | tf_op jit(solution)/shard_map/ppermute | solution.py:1120
  596.4 41.3 %collective-permute-start.6 = (bf16[640,1024]{1,0:T(8,128)(2,1)}, bf16[640,1024]{1,0:T(8,128)(2,1)}, u32[]{:S(2)}, u32[]{:S(2)}) collective-permute-start(bf16[640,1024]{1,0:T(8,128)(2,1)} %get-tuple-element.244), channel_id=1, source_target_pairs={{16,0},{17,1},{18,2},{19,3},{20,4},{21,5},{22,6},{23,7},{24,8},{25... | collective-permute-start | bytes 3932168 | tf_op jit(solution)/shard_map/ppermute | solution.py:1108
  637.7 52.6 %all-to-all-start.10 = ((bf16[8,96,1024]{2,1,0:T(8,128)(2,1)}), bf16[8,96,1024]{2,1,0:T(8,128)(2,1)}, u32[]{:S(2)}, u32[]{:S(2)}) async-start(bf16[8,96,1024]{2,1,0:T(8,128)(2,1)} %bitcast.239), calls=%async_computation.10 | async-start | bytes 3145728 | tf_op jit(solution)/shard_map/all_to_all | solution.py:559
  648.3 41.9 %collective-permute-start.8 = (bf16[512,1024]{1,0:T(8,128)(2,1)S(1)}, bf16[512,1024]{1,0:T(8,128)(2,1)}, u32[]{:S(2)}, u32[]{:S(2)}) collective-permute-start(bf16[512,1024]{1,0:T(8,128)(2,1)S(1)} %get-tuple-element.467), channel_id=1, source_target_pairs={{0,1},{1,0},{2,3},{3,2},{4,5},{5,4},{6,7},{7,6},{8,9},{9,8},{10,11... | collective-permute-start | bytes 3145736 | tf_op jit(solution)/shard_map/ppermute | solution.py:791
  690.3 48.1 %all-to-all-start.11 = ((bf16[8,104,1024]{2,1,0:T(8,128)(2,1)}), bf16[8,104,1024]{2,1,0:T(8,128)(2,1)}, u32[]{:S(2)}, u32[]{:S(2)}) async-start(bf16[8,104,1024]{2,1,0:T(8,128)(2,1)} %bitcast.235), calls=%async_computation.11 | async-start | bytes 3407872 | tf_op jit(solution)/shard_map/all_to_all | solution.py:559
  695.6 84.8 %reduce-scatter.4.cloned.1.call-start = ((), (), s32[]{:S(2)}) async-start(), calls=%async_computation.15 | async-start | bytes 2359296 | tf_op jit(solution)/shard_map/reduce_scatter | solution.py:806
  704.1 34.3 %collective-permute-start.9 = (bf16[256,2816]{1,0:T(8,128)(2,1)}, bf16[256,2816]{1,0:T(8,128)(2,1)}, u32[]{:S(2)}, u32[]{:S(2)}) collective-permute-start(bf16[256,2816]{1,0:T(8,128)(2,1)} %convolution_convert_fusion.1), channel_id=1, source_target_pairs={{0,1},{1,0},{2,3},{3,2},{4,5},{5,4},{6,7},{7,6},{8,9},{9,8},{10,11... | collective-permute-start | bytes 4325384 | tf_op jit(solution)/shard_map/ppermute | solution.py:1168
  738.4 71.3 %all-gather.5.cloned.1.call-start = ((), (), s32[]{:S(2)}) async-start(), calls=%async_computation.16 | async-start | bytes 2359296 | tf_op jit(solution)/shard_map/all_gather | solution.py:810
  744.4 36.0 %collective-permute-start.10 = (bf16[256,2816]{1,0:T(8,128)(2,1)S(1)}, bf16[256,2816]{1,0:T(8,128)(2,1)}, u32[]{:S(2)}, u32[]{:S(2)}) collective-permute-start(bf16[256,2816]{1,0:T(8,128)(2,1)S(1)} %slice.211), channel_id=1, source_target_pairs={{0,1},{1,0},{2,3},{3,2},{4,5},{5,4},{6,7},{7,6},{8,9},{9,8},{10,11... | collective-permute-start | bytes 4325384 | tf_op jit(solution)/shard_map/ppermute | solution.py:1168
  780.4 92.7 %reduce-scatter.8.cloned.1.call-start = ((), (), s32[]{:S(2)}) async-start(), calls=%async_computation.18 | async-start | bytes 3538944 | tf_op jit(solution)/shard_map/reduce_scatter | solution.py:806
  780.5 18.0 %collective-permute-start.11 = (bf16[128,2816]{1,0:T(8,128)(2,1)}, bf16[128,2816]{1,0:T(8,128)(2,1)}, u32[]{:S(2)}, u32[]{:S(2)}) collective-permute-start(bf16[128,2816]{1,0:T(8,128)(2,1)} %get-tuple-element.294), channel_id=1, source_target_pairs={{0,1},{1,0},{2,3},{3,2},{4,5},{5,4},{6,7},{7,6},{8,9},{9,8},{10,11... | collective-permute-start | bytes 2162696 | tf_op jit(solution)/shard_map/ppermute | solution.py:1168
  809.7 124.6 %reduce-scatter.6.cloned.1.call-start = ((), (), s32[]{:S(2)}) async-start(), calls=%async_computation.17 | async-start | bytes 6193152 | tf_op jit(solution)/shard_map/reduce_scatter | solution.py:806
  814.5 20.8 %collective-permute-start.12 = (bf16[128,2816]{1,0:T(8,128)(2,1)}, bf16[128,2816]{1,0:T(8,128)(2,1)}, u32[]{:S(2)}, u32[]{:S(2)}) collective-permute-start(bf16[128,2816]{1,0:T(8,128)(2,1)} %get-tuple-element.320), channel_id=1, source_target_pairs={{0,1},{1,0},{2,3},{3,2},{4,5},{5,4},{6,7},{7,6},{8,9},{9,8},{10,11... | collective-permute-start | bytes 2162696 | tf_op jit(solution)/shard_map/ppermute | solution.py:1168
  836.2 18.3 %collective-permute-start.13 = (bf16[128,2816]{1,0:T(8,128)(2,1)}, bf16[128,2816]{1,0:T(8,128)(2,1)}, u32[]{:S(2)}, u32[]{:S(2)}) collective-permute-start(bf16[128,2816]{1,0:T(8,128)(2,1)} %get-tuple-element.330), channel_id=1, source_target_pairs={{0,1},{1,0},{2,3},{3,2},{4,5},{5,4},{6,7},{7,6},{8,9},{9,8},{10,11... | collective-permute-start | bytes 2162696 | tf_op jit(solution)/shard_map/ppermute | solution.py:1168
  854.5 110.2 %all-gather.9.cloned.1.call-start = ((), (), s32[]{:S(2)}) async-start(), calls=%async_computation.20 | async-start | bytes 1769472 | tf_op jit(solution)/shard_map/all_gather | solution.py:810
  854.6 18.5 %collective-permute-start.14 = (bf16[128,2816]{1,0:T(8,128)(2,1)}, bf16[128,2816]{1,0:T(8,128)(2,1)}, u32[]{:S(2)}, u32[]{:S(2)}) collective-permute-start(bf16[128,2816]{1,0:T(8,128)(2,1)} %get-tuple-element.339), channel_id=1, source_target_pairs={{0,1},{1,0},{2,3},{3,2},{4,5},{5,4},{6,7},{7,6},{8,9},{9,8},{10,11... | collective-permute-start | bytes 2162696 | tf_op jit(solution)/shard_map/ppermute | solution.py:1168
  886.2 13.8 %collective-permute-start.15 = (bf16[64,1536]{1,0:T(8,128)(2,1)}, bf16[64,1536]{1,0:T(8,128)(2,1)}, u32[]{:S(2)}, u32[]{:S(2)}) collective-permute-start(bf16[64,1536]{1,0:T(8,128)(2,1)} %constant_dynamic-slice_fusion.1), channel_id=1, source_target_pairs={{0,1},{1,0},{2,3},{3,2},{4,5},{5,4},{6,7},{7,6},{8,9},{9,8},{10,11... | collective-permute-start | bytes 589832 | tf_op jit(solution)/shard_map/ppermute | solution.py:791
  901.7 16.9 %collective-permute-start.16 = (bf16[352,1024]{1,0:T(8,128)(2,1)}, bf16[352,1024]{1,0:T(8,128)(2,1)}, u32[]{:S(2)}, u32[]{:S(2)}) collective-permute-start(bf16[352,1024]{1,0:T(8,128)(2,1)} %get-tuple-element.367), channel_id=1, source_target_pairs={{0,1},{1,0},{2,3},{3,2},{4,5},{5,4},{6,7},{7,6},{8,9},{9,8},{10,11... | collective-permute-start | bytes 2162696 | tf_op jit(solution)/shard_map/ppermute | solution.py:1168
  902.3 88.1 %all-gather.7.cloned.1.call-start = ((), (), s32[]{:S(2)}) async-start(), calls=%async_computation.19 | async-start | bytes 3096576 | tf_op jit(solution)/shard_map/all_gather | solution.py:810
  918.6 15.7 %collective-permute-start.17 = (bf16[352,1024]{1,0:T(8,128)(2,1)S(1)}, bf16[352,1024]{1,0:T(8,128)(2,1)}, u32[]{:S(2)}, u32[]{:S(2)}) collective-permute-start(bf16[352,1024]{1,0:T(8,128)(2,1)S(1)} %copy-done.48), channel_id=1, source_target_pairs={{0,1},{1,0},{2,3},{3,2},{4,5},{5,4},{6,7},{7,6},{8,9},{9,8},{10,11... | collective-permute-start | bytes 2162696 | tf_op jit(solution)/shard_map/ppermute | solution.py:1168
  935.3 7.3 collective-permute-start.18
  950.5 29.6 %collective-permute-start.19 = (bf16[704,1024]{1,0:T(8,128)(2,1)}, bf16[704,1024]{1,0:T(8,128)(2,1)S(1)}, u32[]{:S(2)}, u32[]{:S(2)}) collective-permute-start(bf16[704,1024]{1,0:T(8,128)(2,1)} %slice.218), channel_id=1, source_target_pairs={{0,1},{1,0},{2,3},{3,2},{4,5},{5,4},{6,7},{7,6},{8,9},{9,8},{10,11... | collective-permute-start | bytes 4325384 | tf_op jit(solution)/shard_map/ppermute | solution.py:1168
  (107 other events, 640.5 us)
Sparse Core Ops, SparseCore 0:
  738.5 38.6 reduce-scatter.3
  780.5 29.0 all-gather.4
  812.0 39.8 reduce-scatter.7
  854.7 61.3 reduce-scatter.5
  918.1 23.4 all-gather.8
  944.6 34.0 all-gather.6

commit v7 on v6

--- a/solution.py
+++ b/solution.py
@@ -1249,17 +1249,16 @@
     out_sends, gots, late_first, kept = together(out_sends, gots, late_first, kept)
     late_first = group_swap(late_first, group)
     grad_expert_in = add_pieces(keep_in, [part[0] for part in gots], BLOCK)
-    grad_expert_in, late_first, out_sends, kept = together(
-        grad_expert_in, late_first, out_sends, kept
+    grad_expert_in, late_first, out_sends, kept, first_got = together(
+        grad_expert_in, late_first, out_sends, kept, swapped(out_sends[0])
     )
     late_first = expert_gather(late_first)
-    out_gots = [swapped(out_sends[0])]
+    out_gots = [first_got, swapped(out_sends[1])]
     actives, expert_grad_rows = kept
     keep_out = dot_tn(
         jnp.where(first_group, actives[:, :half_ff], actives[:, half_ff:]), expert_grad_rows
     )
     keep_out, out_gots, out_sends = together(keep_out, out_gots, out_sends)
-    out_gots.append(swapped(out_sends[1]))
     late_second, out_gots, out_sends, arrived_three = together(
         late_second, out_gots, out_sends, arrived_three
     )

time: 1020 us -> 1010 us (level)
    ppermute x9, waiting for transfers between devices: 58.5 us -> 42.4 us  [swapped(): return [lax.ppermute(part, 'group', SWAP) for part in parts]]
  transfers between devices with their start and end apart: 38 -> 38, of which waited for: 19 -> 19; matrix products, arithmetic and copies ran while one was open for 23% -> 23% of each run, Pallas kernels for 25% -> 26%
where the time goes in v7:
time: 1010 us; the launch traced here: 999 us
  Pallas kernels  296 us (29%)
  waiting for transfers between devices  252 us (25%)
  matrix products  228 us (23%)
  starting transfers between devices  85.9 us (9%)
  other arithmetic  52.2 us (5%)
  local copies, waits for them, and re-layouts  37.9 us (4%)
  blocking collectives  30.6 us (3%)
  between operations  16.6 us (2%)
    dot_general x32, matrix products, dot(): return jnp.dot(a, b, preferred_element_type=F32)  113 us
    all_to_all x12, waiting for transfers between devices, exchange(): lax.all_to_all(parts, 'expert', split_axis=0, concat_axis=0, tiled=True)  90.3 us
    pallas_call x2, Pallas kernels, expert_back(): pl.pallas_call(partial(expert_back_kernel, count=rows), grid_spec=pltpu.P...  80.4 us
    pallas_call x2, Pallas kernels, expert_both(): pl.pallas_call(expert_both_kernel, grid=(tiles,), in_specs=[whole, whole]...  74.4 us
    dot_general x10, matrix products, dot_tn(): lax.dot_general(a, b, (((0,), (0,)), ((), ())), preferred_element_type=F32)  73.8 us
    pallas_call x5, Pallas kernels, pair_call(): pl.pallas_call(kernel, grid_spec=pltpu.PrefetchScalarGridSpec(num_scalar_...  71.4 us
    all_to_all x12, starting transfers between devices, exchange(): lax.all_to_all(parts, 'expert', split_axis=0, concat_axis=0, tiled=True)  57.4 us
    pallas_call x2, Pallas kernels, expert_forward(): pl.pallas_call(expert_forward_kernel, grid=(tiles,), in_specs=[whole] + w...  43.3 us
  transfers between devices with their start and end apart: 38, of which 19 were waited for; matrix products, arithmetic and copies ran while one was open for 23% of the time, Pallas kernels for 26%

profile of v7, /device:TPU:0, one launch (start us, length us, event | category | flops | bytes accessed | tf_op | source)
XLA Modules:
  0.0 998.7 jit_solution(13392738589938989268)
XLA Ops:
  15.2 8.8 fusion.4.q_ref.k_ref.v_ref
  24.0 18.7 %self_attend_kernel.1 = (bf16[640,1024]{1,0:T(8,128)(2,1)}, f32[8,2,640]{2,1,0:T(2,128)}) custom-call(s32[2]{0:T(128)} %get-tuple-element.490.place_ref, bf16[640,3072]{1,0:T(8,128)(2,1)} %fusion.4.q_ref.k_ref.v_ref, bf16[640,3072]{1,0:T(8,128)(2,1)} %fusion.4.q_ref.k_ref.v_ref, bf16[640,3072]{1,0:T(8,128)(2,1)} %fusion.4.q_ref.k_ref.v_ref, ...), custom_call_target="tpu_custom_call" | custom-call | flops 1677721600 | bytes 10485760 | tf_op jit(solution)/shard_map/self_attend_kernel/pallas_call | solution.py:483
  51.8 6.5 all-to-all-start
  62.3 33.9 %all-to-all-done = bf16[8,96,1024]{2,1,0:T(8,128)(2,1)} async-done(((bf16[8,96,1024]{2,1,0:T(8,128)(2,1)}), bf16[8,96,1024]{2,1,0:T(8,128)(2,1)}, u32[]{:S(2)}, u32[]{:S(2)}) %all-to-all-start) | async-done | bytes 1572896 | tf_op jit(solution)/shard_map/all_to_all | solution.py:559
  106.6 21.3 %expert_forward.2 = bf16[768,1024]{1,0:T(8,128)(2,1)} custom-call(bf16[768,1024]{1,0:T(8,128)(2,1)} %bitcast.15.x_ref.g_ref.refs_0_, bf16[1024,5632]{1,0:T(8,128)(2,1)} %bitcast.273, bf16[1024,5632]{1,0:T(8,128)(2,1)} %bitcast.274, bf16[2816,1024]{1,0:T(8,128)(2,1)} %bitcast.285), custom_call_target="tpu_custom_call" | custom-call | flops 13287555072 | bytes 17301504 | tf_op jit(solution)/shard_map/expert_forward/pallas_call | solution.py:703
  128.0 9.5 collective-permute-done
  150.4 22.0 %expert_forward.3 = bf16[832,1024]{1,0:T(8,128)(2,1)} custom-call(bf16[832,1024]{1,0:T(8,128)(2,1)} %bitcast.22.x_ref.g_ref.refs_0_, bf16[1024,5632]{1,0:T(8,128)(2,1)} %bitcast.275, bf16[1024,5632]{1,0:T(8,128)(2,1)} %bitcast.276, bf16[2816,1024]{1,0:T(8,128)(2,1)} %bitcast.286), custom_call_target="tpu_custom_call" | custom-call | flops 14394851328 | bytes 17301504 | tf_op jit(solution)/shard_map/expert_forward/pallas_call | solution.py:703
  172.4 6.4 collective-permute-done.1
  198.4 19.7 %collective-permute-done.2 = bf16[320,2048]{1,0:T(8,128)(2,1)} collective-permute-done((bf16[320,2048]{1,0:T(8,128)(2,1)}, bf16[320,2048]{1,0:T(8,128)(2,1)}, u32[]{:S(2)}, u32[]{:S(2)}) %collective-permute-start.2) | collective-permute-done | bytes 1310752 | tf_op jit(solution)/shard_map/ppermute | solution.py:987
  218.1 10.2 %all-to-all-done.3 = bf16[8,104,1024]{2,1,0:T(8,128)(2,1)} async-done(((bf16[8,104,1024]{2,1,0:T(8,128)(2,1)}), bf16[8,104,1024]{2,1,0:T(8,128)(2,1)}, u32[]{:S(2)}, u32[]{:S(2)}) %all-to-all-start.3) | async-done | bytes 1703968 | tf_op jit(solution)/shard_map/all_to_all | solution.py:559
  232.3 5.7 multiply_reduce_fusion.9
  248.4 19.5 %collective-permute-done.3 = bf16[640,1024]{1,0:T(8,128)(2,1)S(1)} collective-permute-done((bf16[640,1024]{1,0:T(8,128)(2,1)S(1)}, bf16[640,1024]{1,0:T(8,128)(2,1)S(1)}, u32[]{:S(2)}, u32[]{:S(2)}) %collective-permute-start.3) | collective-permute-done | bytes 1310752 | tf_op jit(solution)/shard_map/ppermute | solution.py:996
  272.2 7.5 cross_attend_kernel.1
  295.6 33.3 %all-to-all-done.4 = bf16[8,96,1024]{2,1,0:T(8,128)(2,1)} async-done(((bf16[8,96,1024]{2,1,0:T(8,128)(2,1)}), bf16[8,96,1024]{2,1,0:T(8,128)(2,1)}, u32[]{:S(2)}, u32[]{:S(2)}) %all-to-all-start.4) | async-done | bytes 1572896 | tf_op jit(solution)/shard_map/all_to_all | solution.py:559
  333.2 36.0 %expert_both.2 = (bf16[768,1024]{1,0:T(8,128)(2,1)}, bf16[768,2816]{1,0:T(8,128)(2,1)}, f32[768,1]{1,0:T(8,128)}) custom-call(bf16[768,1024]{1,0:T(8,128)(2,1)} %bitcast.27.x_ref.refs_1_, bf16[768,1024]{1,0:T(8,128)(2,1)} %bitcast.15.x_ref.g_ref.refs_0_, bf16[1024,5632]{1,0:T(8,128)(2,1)} %bitcast.277, bf16[1024,5632]{1,0:T(8,128)(2,1)} %bitcast.278, ...), custom_call_target="tpu_custom_call" | custom-call | flops 22145925120 | bytes 17301504 | tf_op jit(solution)/shard_map/expert_both/pallas_call | solution.py:721
  369.2 4.7 all-to-all-done.6
  378.3 38.4 %expert_both.3 = (bf16[832,1024]{1,0:T(8,128)(2,1)}, bf16[832,2816]{1,0:T(8,128)(2,1)}, f32[832,1]{1,0:T(8,128)}) custom-call(bf16[832,1024]{1,0:T(8,128)(2,1)} %bitcast.31.x_ref.refs_1_, bf16[832,1024]{1,0:T(8,128)(2,1)} %bitcast.22.x_ref.g_ref.refs_0_, bf16[1024,5632]{1,0:T(8,128)(2,1)} %bitcast.279, bf16[1024,5632]{1,0:T(8,128)(2,1)} %bitcast.280, ...), custom_call_target="tpu_custom_call" | custom-call | flops 23991418880 | bytes 17301504 | tf_op jit(solution)/shard_map/expert_both/pallas_call | solution.py:721
  416.7 5.1 all-to-all-start.7
  438.2 30.6 %all-gather = f32[64,400]{1,0:T(8,128)S(1)} all-gather(f32[8,400]{1,0:T(8,128)S(1)} %pad_maximum_fusion.7), channel_id=2, replica_groups=mesh['half'=2,'expert'=8,'group'=2] {'expert'}, dimensions={0}, use_global_device_ids=true | all-gather | bytes 115200 | tf_op jit(solution)/shard_map/all_gather | solution.py:1022
  485.5 10.7 %cross_attend_back_kernel.1 = (bf16[640,1024]{1,0:T(8,128)(2,1)}, bf16[640,1024]{1,0:T(8,128)(2,1)}, bf16[640,1024]{1,0:T(8,128)(2,1)}) custom-call(s32[2]{0:T(128)} %get-tuple-element.490.place_ref, bf16[640,1024]{1,0:T(8,128)(2,1)} %convolution_convert_fusion.15.q_ref, bf16[640,2048]{1,0:T(8,128)(2,1)} %convolution_convert_fusion.4.k_ref.v_ref, ...), custom_call_target="tpu_custom_call" | custom-call | flops 4194304000 | bytes 10485760 | tf_op jit(solution)/shard_map/cross_attend_back_kernel/pallas_call | solution.py:483
  503.8 6.3 convolution_convert_fusion.8
  510.1 4.6 convolution_convert_fusion.13
  514.8 20.7 %collective-permute-done.4 = bf16[640,1024]{1,0:T(8,128)(2,1)S(1)} collective-permute-done((bf16[640,1024]{1,0:T(8,128)(2,1)S(1)}, bf16[640,1024]{1,0:T(8,128)(2,1)S(1)}, u32[]{:S(2)}, u32[]{:S(2)}) %collective-permute-start.4) | collective-permute-done | bytes 1310752 | tf_op jit(solution)/shard_map/ppermute | solution.py:1085
  560.6 25.0 %collective-permute-done.5 = bf16[640,1024]{1,0:T(8,128)(2,1)S(1)} collective-permute-done((bf16[640,1024]{1,0:T(8,128)(2,1)}, bf16[640,1024]{1,0:T(8,128)(2,1)S(1)}, u32[]{:S(2)}, u32[]{:S(2)}) %collective-permute-start.5) | collective-permute-done | bytes 1310752 | tf_op jit(solution)/shard_map/ppermute | solution.py:1090
  589.1 4.8 all-to-all-start.8
  598.6 39.0 %expert_back.2 = (bf16[768,1024]{1,0:T(8,128)(2,1)}, bf16[2,832,1024]{2,1,0:T(8,128)(2,1)}, bf16[2,832,1024]{2,1,0:T(8,128)(2,1)}, bf16[2,832,2816]{2,1,0:T(8,12...) custom-call(s32[2]{0:T(128)} %get-tuple-element.239.flags_ref, ...), custom_call_target="tpu_custom_call" | custom-call | flops 22145925120 | bytes 17301504 | tf_op jit(solution)/shard_map/expert_back/pallas_call | solution.py:757
  637.6 5.4 all-to-all-start.10
  648.7 41.4 %expert_back.3 = (bf16[832,1024]{1,0:T(8,128)(2,1)}, bf16[2,832,1024]{2,1,0:T(8,128)(2,1)}, bf16[2,832,1024]{2,1,0:T(8,128)(2,1)}, bf16[2,832,2816]{2,1,0:T(8,12...) custom-call(s32[2]{0:T(128)} %get-tuple-element.239.flags_ref, ...), custom_call_target="tpu_custom_call", output_to_operand_aliasing={{1}: (8, {}), {2}: (9, {}), {3}: (10, {}), {4}: (11, {}), {... | custom-call | flops 23991418880 | bytes 17301504 | tf_op jit(solution)/shard_map/expert_back/pallas_call | solution.py:757
  690.2 5.3 all-to-all-start.11
  696.0 8.0 convolution_convert_fusion.1
  705.5 8.4 convolution_convert_fusion
  724.4 13.9 %collective-permute-done.9.refs_0_ = bf16[256,2816]{1,0:T(8,128)(2,1)} collective-permute-done((bf16[256,2816]{1,0:T(8,128)(2,1)}, bf16[256,2816]{1,0:T(8,128)(2,1)}, u32[]{:S(2)}, u32[]{:S(2)}) %collective-permute-start.9) | collective-permute-done | bytes 1441824 | tf_op jit(solution)/shard_map/ppermute | solution.py:1168
  763.2 17.1 %self_attend_back_kernel.2 = (bf16[640,512]{1,0:T(8,128)(2,1)}, bf16[640,512]{1,0:T(8,128)(2,1)}, bf16[640,512]{1,0:T(8,128)(2,1)}, f32[4,2,1024]{2,1,0:T(2,128)}) custom-call(s32[2]{0:T(128)} %get-tuple-element.490.place_ref, bf16[640,3072]{1,0:T(8,128)(2,1)} %fusion.4.q_ref.k_ref.v_ref, bf16[640,3072]{1,0:T(8,128)(2,1)} %fusion.4.q_ref.k_ref.v_ref, ...), custom_call_target="tpu_custom_call" | custom-call | flops 2097152000 | bytes 10485760 | tf_op jit(solution)/shard_map/self_attend_back_kernel/pallas_call | solution.py:483
  781.0 17.4 %self_attend_back_kernel.3 = (bf16[640,512]{1,0:T(8,128)(2,1)}, bf16[640,512]{1,0:T(8,128)(2,1)}, bf16[640,512]{1,0:T(8,128)(2,1)}, f32[4,2,1024]{2,1,0:T(2,128)}) custom-call(s32[2]{0:T(128)} %get-tuple-element.490.place_ref, bf16[640,3072]{1,0:T(8,128)(2,1)} %fusion.4.q_ref.k_ref.v_ref, bf16[640,3072]{1,0:T(8,128)(2,1)} %fusion.4.q_ref.k_ref.v_ref, ...), custom_call_target="tpu_custom_call" | custom-call | flops 2097152000 | bytes 10485760 | tf_op jit(solution)/shard_map/self_attend_back_kernel/pallas_call | solution.py:483
  798.4 5.6 convolution_convert_fusion.3
  804.0 5.5 all-gather.5.cloned.1.call-done
  809.7 4.6 fusion.169
  819.6 6.9 fusion
  838.6 5.8 pad_maximum_fusion
  844.4 10.0 %collective-permute-done.13.refs_4_ = bf16[128,2816]{1,0:T(8,128)(2,1)} collective-permute-done((bf16[128,2816]{1,0:T(8,128)(2,1)}, bf16[128,2816]{1,0:T(8,128)(2,1)}, u32[]{:S(2)}, u32[]{:S(2)}) %collective-permute-start.13) | collective-permute-done | bytes 720928 | tf_op jit(solution)/shard_map/ppermute | solution.py:1168
  855.1 17.8 %convolution_bitcast_fusion.kept_ref = f32[1024,2816]{1,0:T(8,128)} fusion(bf16[2,832,1024]{2,1,0:T(8,128)(2,1)} %get-tuple-element.267, bf16[2,832,2816]{2,1,0:T(8,128)(2,1)} %get-tuple-element.333), kind=kOutput, calls=%fused_computation | convolution fusion | flops 9596567552 | bytes 24313856 | tf_op jit(solution)/shard_map/dot_general | solution.py:94
  873.0 10.0 %fusion.33 = bf16[1408,1024]{1,0:T(8,128)(2,1)S(1)} fusion(bf16[1664,1024]{1,0:T(8,128)(2,1)} %bitcast.295, bf16[1664,2816]{1,0:T(8,128)(2,1)} %bitcast.293, pred[]{:T(512)S(6)} %eq.594), kind=kOutput, calls=%fused_computation.44 | convolution fusion | flops 4802068480 | bytes 15663105 | tf_op jit(solution)/shard_map/dot_general | solution.py:94
  888.1 12.4 %add_pieces.2 = f32[1024,2816]{1,0:T(8,128)} custom-call(f32[1024,2816]{1,0:T(8,128)} %convolution_bitcast_fusion.kept_ref, bf16[256,2816]{1,0:T(8,128)(2,1)} %collective-permute-done.9.refs_0_, bf16[256,2816]{1,0:T(8,128)(2,1)} %collective-permute-done.10.refs_1_, bf16[128,2816]{1,0:T(8,128)(2,1)} %collective-permute-done.11.refs_2_, ...), custom_call_target="tpu_custom_call" | custom-call | flops 2883584 | bytes 28835840 | tf_op jit(solution)/shard_map/add_pieces/pallas_call | solution.py:859
  900.5 6.3 collective-permute-done.15
  909.9 11.9 %fusion.7.kept_ref = f32[1408,1024]{1,0:T(8,128)} fusion(bf16[1664,1024]{1,0:T(8,128)(2,1)} %bitcast.296, bf16[1664,2816]{1,0:T(8,128)(2,1)} %bitcast.294, pred[]{:T(512)S(6)} %eq.594), kind=kOutput, calls=%fused_computation.12 | convolution fusion | flops 4800626688 | bytes 18546688 | tf_op jit(solution)/shard_map/dot_general | solution.py:94
  927.2 6.1 collective-permute-done.18
  955.9 15.3 %collective-permute-done.19.refs_2_ = bf16[704,1024]{1,0:T(8,128)(2,1)S(1)} collective-permute-done((bf16[704,1024]{1,0:T(8,128)(2,1)}, bf16[704,1024]{1,0:T(8,128)(2,1)S(1)}, u32[]{:S(2)}, u32[]{:S(2)}) %collective-permute-start.19) | collective-permute-done | bytes 1441824 | tf_op jit(solution)/shard_map/ppermute | solution.py:1168
  975.3 6.4 add_pieces.3
  (462 shorter events, 291.8 us)
Async XLA Ops:
  7.2 35.5 %copy-start = (bf16[1,1024,1024]{2,1,0:T(8,128)(2,1)S(1)}, bf16[1,1024,1024]{2,1,0:T(8,128)(2,1)}, u32[]{:S(2)}) copy-start(bf16[1,1024,1024]{2,1,0:T(8,128)(2,1)} %param.55) | copy-start | bytes 6291460
  12.3 34.3 %copy-start.64 = (f32[1,1,1024]{2,0,1:T(1,128)}, f32[1,1,1024]{2,0,1:T(1,128)S(1)}, u32[]{:S(2)}) copy-start(f32[1,1,1024]{2,0,1:T(1,128)S(1)} %get-tuple-element.478) | copy-start | bytes 12292
  51.8 44.4 %all-to-all-start = ((bf16[8,96,1024]{2,1,0:T(8,128)(2,1)}), bf16[8,96,1024]{2,1,0:T(8,128)(2,1)}, u32[]{:S(2)}, u32[]{:S(2)}) async-start(bf16[8,96,1024]{2,1,0:T(8,128)(2,1)} %bitcast.242), calls=%async_computation | async-start | bytes 3145728 | tf_op jit(solution)/shard_map/all_to_all | solution.py:559
  96.2 45.0 %all-to-all-start.2 = ((bf16[8,104,1024]{2,1,0:T(8,128)(2,1)}), bf16[8,104,1024]{2,1,0:T(8,128)(2,1)}, u32[]{:S(2)}, u32[]{:S(2)}) async-start(bf16[8,104,1024]{2,1,0:T(8,128)(2,1)} %bitcast.237), calls=%async_computation.2 | async-start | bytes 3407872 | tf_op jit(solution)/shard_map/all_to_all | solution.py:559
  104.2 33.2 %collective-permute-start = (bf16[352,2048]{1,0:T(8,128)(2,1)}, bf16[352,2048]{1,0:T(8,128)(2,1)}, u32[]{:S(2)}, u32[]{:S(2)}) collective-permute-start(bf16[352,2048]{1,0:T(8,128)(2,1)} %get-tuple-element.203), channel_id=1, source_target_pairs={{0,16},{1,17},{2,18},{3,19},{4,20},{5,21},{6,22},{7,23},{8,24},{9,... | collective-permute-start | bytes 4325384 | tf_op jit(solution)/shard_map/ppermute | solution.py:982
  141.2 42.1 %all-to-all-start.1 = ((bf16[8,96,1024]{2,1,0:T(8,128)(2,1)}), bf16[8,96,1024]{2,1,0:T(8,128)(2,1)}, u32[]{:S(2)}, u32[]{:S(2)}) async-start(bf16[8,96,1024]{2,1,0:T(8,128)(2,1)} %bitcast.240), calls=%async_computation.1 | async-start | bytes 3145728 | tf_op jit(solution)/shard_map/all_to_all | solution.py:559
  145.5 33.3 %collective-permute-start.1 = (bf16[352,2048]{1,0:T(8,128)(2,1)}, bf16[352,2048]{1,0:T(8,128)(2,1)}, u32[]{:S(2)}, u32[]{:S(2)}) collective-permute-start(bf16[352,2048]{1,0:T(8,128)(2,1)} %get-tuple-element.206), channel_id=1, source_target_pairs={{0,16},{1,17},{2,18},{3,19},{4,20},{5,21},{6,22},{7,23},{8,24},{9,... | collective-permute-start | bytes 4325384 | tf_op jit(solution)/shard_map/ppermute | solution.py:982
  183.3 45.0 %all-to-all-start.3 = ((bf16[8,104,1024]{2,1,0:T(8,128)(2,1)}), bf16[8,104,1024]{2,1,0:T(8,128)(2,1)}, u32[]{:S(2)}, u32[]{:S(2)}) async-start(bf16[8,104,1024]{2,1,0:T(8,128)(2,1)} %bitcast.236), calls=%async_computation.3 | async-start | bytes 3407872 | tf_op jit(solution)/shard_map/all_to_all | solution.py:559
  187.6 30.4 %collective-permute-start.2 = (bf16[320,2048]{1,0:T(8,128)(2,1)}, bf16[320,2048]{1,0:T(8,128)(2,1)}, u32[]{:S(2)}, u32[]{:S(2)}) collective-permute-start(bf16[320,2048]{1,0:T(8,128)(2,1)} %pad_maximum_fusion.2), channel_id=1, source_target_pairs={{0,16},{1,17},{2,18},{3,19},{4,20},{5,21},{6,22},{7,23},{8,24},{9,... | collective-permute-start | bytes 3932168 | tf_op jit(solution)/shard_map/ppermute | solution.py:987
  190.1 280.1 %copy-start.88 = (s32[640]{0:T(1024)}, s32[640]{0:T(1024)S(1)}, u32[]{:S(2)}) copy-start(s32[640]{0:T(1024)S(1)} %get-tuple-element.448) | copy-start | bytes 7684
  190.1 283.1 %copy-start.62 = (s32[640]{0:T(1024)}, s32[640]{0:T(1024)S(1)}, u32[]{:S(2)}) copy-start(s32[640]{0:T(1024)S(1)} %get-tuple-element.449) | copy-start | bytes 7684
  238.3 29.7 %collective-permute-start.3 = (bf16[640,1024]{1,0:T(8,128)(2,1)S(1)}, bf16[640,1024]{1,0:T(8,128)(2,1)S(1)}, u32[]{:S(2)}, u32[]{:S(2)}) collective-permute-start(bf16[640,1024]{1,0:T(8,128)(2,1)S(1)} %multiply_convert_fusion.3), channel_id=1, source_target_pairs={{0,16},{1,17},{2,18},{3,19},{4,20},{5,21},{6,22},{7,23},{8,24},{9,... | collective-permute-start | bytes 3932168 | tf_op jit(solution)/shard_map/ppermute | solution.py:996
  284.0 197.2 %copy-start.60 = (f32[640]{0:T(1024)}, f32[640]{0:T(1024)S(1)}, u32[]{:S(2)}) copy-start(f32[640]{0:T(1024)S(1)} %add_rsqrt_fusion) | copy-start | bytes 7684
  286.7 42.1 %all-to-all-start.4 = ((bf16[8,96,1024]{2,1,0:T(8,128)(2,1)}), bf16[8,96,1024]{2,1,0:T(8,128)(2,1)}, u32[]{:S(2)}, u32[]{:S(2)}) async-start(bf16[8,96,1024]{2,1,0:T(8,128)(2,1)} %bitcast.243), calls=%async_computation.4 | async-start | bytes 3145728 | tf_op jit(solution)/shard_map/all_to_all | solution.py:559
  328.9 45.0 %all-to-all-start.6 = ((bf16[8,104,1024]{2,1,0:T(8,128)(2,1)}), bf16[8,104,1024]{2,1,0:T(8,128)(2,1)}, u32[]{:S(2)}, u32[]{:S(2)}) async-start(bf16[8,104,1024]{2,1,0:T(8,128)(2,1)} %bitcast.238), calls=%async_computation.6 | async-start | bytes 3407872 | tf_op jit(solution)/shard_map/all_to_all | solution.py:559
  373.8 42.9 %all-to-all-start.5 = ((bf16[8,96,1024]{2,1,0:T(8,128)(2,1)}), bf16[8,96,1024]{2,1,0:T(8,128)(2,1)}, u32[]{:S(2)}, u32[]{:S(2)}) async-start(bf16[8,96,1024]{2,1,0:T(8,128)(2,1)} %bitcast.241), calls=%async_computation.5 | async-start | bytes 3145728 | tf_op jit(solution)/shard_map/all_to_all | solution.py:559
  416.7 53.4 %all-to-all-start.7 = ((bf16[8,104,1024]{2,1,0:T(8,128)(2,1)}), bf16[8,104,1024]{2,1,0:T(8,128)(2,1)}, u32[]{:S(2)}, u32[]{:S(2)}) async-start(bf16[8,104,1024]{2,1,0:T(8,128)(2,1)} %bitcast.234), calls=%async_computation.7 | async-start | bytes 3407872 | tf_op jit(solution)/shard_map/all_to_all | solution.py:559
  426.1 50.4 %copy-start.70 = (f32[640]{0:T(1024)}, f32[640]{0:T(1024)S(1)}, u32[]{:S(2)}) copy-start(f32[640]{0:T(1024)S(1)} %get-tuple-element.479) | copy-start | bytes 7684
  426.1 50.4 %copy-start.72 = (f32[640]{0:T(1024)}, f32[640]{0:T(1024)S(1)}, u32[]{:S(2)}) copy-start(f32[640]{0:T(1024)S(1)} %get-tuple-element.480) | copy-start | bytes 7684
  433.8 36.4 %copy-start.97 = (s32[832]{0:T(1024)S(1)}, s32[832]{0:T(1024)}, u32[]{:S(2)}) copy-start(s32[832]{0:T(1024)} %constant.106) | copy-start | bytes 9988
  502.2 33.3 %collective-permute-start.4 = (bf16[640,1024]{1,0:T(8,128)(2,1)S(1)}, bf16[640,1024]{1,0:T(8,128)(2,1)S(1)}, u32[]{:S(2)}, u32[]{:S(2)}) collective-permute-start(bf16[640,1024]{1,0:T(8,128)(2,1)S(1)} %add_convert_fusion.2), channel_id=1, source_target_pairs={{16,0},{17,1},{18,2},{19,3},{20,4},{21,5},{22,6},{23,7},{24,8},{25... | collective-permute-start | bytes 3932168 | tf_op jit(solution)/shard_map/ppermute | solution.py:1085
  510.1 26.8 %copy-start.15 = (f32[640,1024]{1,0:T(8,128)S(1)}, f32[640,1024]{1,0:T(8,128)}, u32[]{:S(2)}) copy-start(f32[640,1024]{1,0:T(8,128)} %get-tuple-element.485) | copy-start | bytes 7864324
  542.7 46.4 %all-to-all-start.9 = ((bf16[8,96,1024]{2,1,0:T(8,128)(2,1)}), bf16[8,96,1024]{2,1,0:T(8,128)(2,1)}, u32[]{:S(2)}, u32[]{:S(2)}) async-start(bf16[8,96,1024]{2,1,0:T(8,128)(2,1)} %bitcast.231), calls=%async_computation.9 | async-start | bytes 3145728 | tf_op jit(solution)/shard_map/all_to_all | solution.py:559
  552.5 33.1 %collective-permute-start.5 = (bf16[640,1024]{1,0:T(8,128)(2,1)}, bf16[640,1024]{1,0:T(8,128)(2,1)S(1)}, u32[]{:S(2)}, u32[]{:S(2)}) collective-permute-start(bf16[640,1024]{1,0:T(8,128)(2,1)} %get-tuple-element.235), channel_id=1, source_target_pairs={{16,0},{17,1},{18,2},{19,3},{20,4},{21,5},{22,6},{23,7},{24,8},{25... | collective-permute-start | bytes 3932168 | tf_op jit(solution)/shard_map/ppermute | solution.py:1090
  589.1 48.6 %all-to-all-start.8 = ((bf16[8,104,1024]{2,1,0:T(8,128)(2,1)}), bf16[8,104,1024]{2,1,0:T(8,128)(2,1)}, u32[]{:S(2)}, u32[]{:S(2)}) async-start(bf16[8,104,1024]{2,1,0:T(8,128)(2,1)} %bitcast.230), calls=%async_computation.8 | async-start | bytes 3407872 | tf_op jit(solution)/shard_map/all_to_all | solution.py:559
  593.8 144.7 %copy-start.79 = (f32[640]{0:T(1024)}, f32[640]{0:T(1024)S(1)}, u32[]{:S(2)}) copy-start(f32[640]{0:T(1024)S(1)} %subtract_multiply_fusion) | copy-start | bytes 7684
  594.8 42.8 %collective-permute-start.7 = (bf16[512,1024]{1,0:T(8,128)(2,1)}, bf16[512,1024]{1,0:T(8,128)(2,1)}, u32[]{:S(2)}, u32[]{:S(2)}) collective-permute-start(bf16[512,1024]{1,0:T(8,128)(2,1)} %get-tuple-element.246), channel_id=1, source_target_pairs={{0,1},{1,0},{2,3},{3,2},{4,5},{5,4},{6,7},{7,6},{8,9},{9,8},{10,11... | collective-permute-start | bytes 3145736 | tf_op jit(solution)/shard_map/ppermute | solution.py:1120
  596.3 41.3 %collective-permute-start.6 = (bf16[640,1024]{1,0:T(8,128)(2,1)}, bf16[640,1024]{1,0:T(8,128)(2,1)}, u32[]{:S(2)}, u32[]{:S(2)}) collective-permute-start(bf16[640,1024]{1,0:T(8,128)(2,1)} %get-tuple-element.244), channel_id=1, source_target_pairs={{16,0},{17,1},{18,2},{19,3},{20,4},{21,5},{22,6},{23,7},{24,8},{25... | collective-permute-start | bytes 3932168 | tf_op jit(solution)/shard_map/ppermute | solution.py:1108
  637.6 52.5 %all-to-all-start.10 = ((bf16[8,96,1024]{2,1,0:T(8,128)(2,1)}), bf16[8,96,1024]{2,1,0:T(8,128)(2,1)}, u32[]{:S(2)}, u32[]{:S(2)}) async-start(bf16[8,96,1024]{2,1,0:T(8,128)(2,1)} %bitcast.239), calls=%async_computation.10 | async-start | bytes 3145728 | tf_op jit(solution)/shard_map/all_to_all | solution.py:559
  648.2 41.9 %collective-permute-start.8 = (bf16[512,1024]{1,0:T(8,128)(2,1)S(1)}, bf16[512,1024]{1,0:T(8,128)(2,1)}, u32[]{:S(2)}, u32[]{:S(2)}) collective-permute-start(bf16[512,1024]{1,0:T(8,128)(2,1)S(1)} %get-tuple-element.467), channel_id=1, source_target_pairs={{0,1},{1,0},{2,3},{3,2},{4,5},{5,4},{6,7},{7,6},{8,9},{9,8},{10,11... | collective-permute-start | bytes 3145736 | tf_op jit(solution)/shard_map/ppermute | solution.py:791
  690.2 48.1 %all-to-all-start.11 = ((bf16[8,104,1024]{2,1,0:T(8,128)(2,1)}), bf16[8,104,1024]{2,1,0:T(8,128)(2,1)}, u32[]{:S(2)}, u32[]{:S(2)}) async-start(bf16[8,104,1024]{2,1,0:T(8,128)(2,1)} %bitcast.235), calls=%async_computation.11 | async-start | bytes 3407872 | tf_op jit(solution)/shard_map/all_to_all | solution.py:559
  695.5 84.9 %reduce-scatter.4.cloned.1.call-start = ((), (), s32[]{:S(2)}) async-start(), calls=%async_computation.15 | async-start | bytes 2359296 | tf_op jit(solution)/shard_map/reduce_scatter | solution.py:806
  704.0 34.3 %collective-permute-start.9 = (bf16[256,2816]{1,0:T(8,128)(2,1)}, bf16[256,2816]{1,0:T(8,128)(2,1)}, u32[]{:S(2)}, u32[]{:S(2)}) collective-permute-start(bf16[256,2816]{1,0:T(8,128)(2,1)} %convolution_convert_fusion.1), channel_id=1, source_target_pairs={{0,1},{1,0},{2,3},{3,2},{4,5},{5,4},{6,7},{7,6},{8,9},{9,8},{10,11... | collective-permute-start | bytes 4325384 | tf_op jit(solution)/shard_map/ppermute | solution.py:1168
  738.3 71.2 %all-gather.5.cloned.1.call-start = ((), (), s32[]{:S(2)}) async-start(), calls=%async_computation.16 | async-start | bytes 2359296 | tf_op jit(solution)/shard_map/all_gather | solution.py:810
  744.3 36.0 %collective-permute-start.10 = (bf16[256,2816]{1,0:T(8,128)(2,1)S(1)}, bf16[256,2816]{1,0:T(8,128)(2,1)}, u32[]{:S(2)}, u32[]{:S(2)}) collective-permute-start(bf16[256,2816]{1,0:T(8,128)(2,1)S(1)} %slice.211), channel_id=1, source_target_pairs={{0,1},{1,0},{2,3},{3,2},{4,5},{5,4},{6,7},{7,6},{8,9},{9,8},{10,11... | collective-permute-start | bytes 4325384 | tf_op jit(solution)/shard_map/ppermute | solution.py:1168
  780.4 92.6 %reduce-scatter.8.cloned.1.call-start = ((), (), s32[]{:S(2)}) async-start(), calls=%async_computation.18 | async-start | bytes 3538944 | tf_op jit(solution)/shard_map/reduce_scatter | solution.py:806
  780.4 18.0 %collective-permute-start.11 = (bf16[128,2816]{1,0:T(8,128)(2,1)}, bf16[128,2816]{1,0:T(8,128)(2,1)}, u32[]{:S(2)}, u32[]{:S(2)}) collective-permute-start(bf16[128,2816]{1,0:T(8,128)(2,1)} %get-tuple-element.294), channel_id=1, source_target_pairs={{0,1},{1,0},{2,3},{3,2},{4,5},{5,4},{6,7},{7,6},{8,9},{9,8},{10,11... | collective-permute-start | bytes 2162696 | tf_op jit(solution)/shard_map/ppermute | solution.py:1168
  809.5 115.5 %reduce-scatter.6.cloned.1.call-start = ((), (), s32[]{:S(2)}) async-start(), calls=%async_computation.17 | async-start | bytes 6193152 | tf_op jit(solution)/shard_map/reduce_scatter | solution.py:806
  814.4 20.8 %collective-permute-start.12 = (bf16[128,2816]{1,0:T(8,128)(2,1)}, bf16[128,2816]{1,0:T(8,128)(2,1)}, u32[]{:S(2)}, u32[]{:S(2)}) collective-permute-start(bf16[128,2816]{1,0:T(8,128)(2,1)} %get-tuple-element.320), channel_id=1, source_target_pairs={{0,1},{1,0},{2,3},{3,2},{4,5},{5,4},{6,7},{7,6},{8,9},{9,8},{10,11... | collective-permute-start | bytes 2162696 | tf_op jit(solution)/shard_map/ppermute | solution.py:1168
  836.1 18.3 %collective-permute-start.13 = (bf16[128,2816]{1,0:T(8,128)(2,1)}, bf16[128,2816]{1,0:T(8,128)(2,1)}, u32[]{:S(2)}, u32[]{:S(2)}) collective-permute-start(bf16[128,2816]{1,0:T(8,128)(2,1)} %get-tuple-element.330), channel_id=1, source_target_pairs={{0,1},{1,0},{2,3},{3,2},{4,5},{5,4},{6,7},{7,6},{8,9},{9,8},{10,11... | collective-permute-start | bytes 2162696 | tf_op jit(solution)/shard_map/ppermute | solution.py:1168
  854.4 101.5 %all-gather.9.cloned.1.call-start = ((), (), s32[]{:S(2)}) async-start(), calls=%async_computation.20 | async-start | bytes 1769472 | tf_op jit(solution)/shard_map/all_gather | solution.py:810
  854.5 18.5 %collective-permute-start.14 = (bf16[128,2816]{1,0:T(8,128)(2,1)}, bf16[128,2816]{1,0:T(8,128)(2,1)}, u32[]{:S(2)}, u32[]{:S(2)}) collective-permute-start(bf16[128,2816]{1,0:T(8,128)(2,1)} %get-tuple-element.339), channel_id=1, source_target_pairs={{0,1},{1,0},{2,3},{3,2},{4,5},{5,4},{6,7},{7,6},{8,9},{9,8},{10,11... | collective-permute-start | bytes 2162696 | tf_op jit(solution)/shard_map/ppermute | solution.py:1168
  885.4 23.1 %collective-permute-start.16 = (bf16[352,1024]{1,0:T(8,128)(2,1)}, bf16[352,1024]{1,0:T(8,128)(2,1)}, u32[]{:S(2)}, u32[]{:S(2)}) collective-permute-start(bf16[352,1024]{1,0:T(8,128)(2,1)} %get-tuple-element.360), channel_id=1, source_target_pairs={{0,1},{1,0},{2,3},{3,2},{4,5},{5,4},{6,7},{7,6},{8,9},{9,8},{10,11... | collective-permute-start | bytes 2162696 | tf_op jit(solution)/shard_map/ppermute | solution.py:1168
  887.5 19.4 %collective-permute-start.15 = (bf16[64,1536]{1,0:T(8,128)(2,1)}, bf16[64,1536]{1,0:T(8,128)(2,1)}, u32[]{:S(2)}, u32[]{:S(2)}) collective-permute-start(bf16[64,1536]{1,0:T(8,128)(2,1)} %constant_dynamic-slice_fusion.1), channel_id=1, source_target_pairs={{0,1},{1,0},{2,3},{3,2},{4,5},{5,4},{6,7},{7,6},{8,9},{9,8},{10,11... | collective-permute-start | bytes 589832 | tf_op jit(solution)/shard_map/ppermute | solution.py:791
  908.5 73.1 %all-gather.7.cloned.1.call-start = ((), (), s32[]{:S(2)}) async-start(), calls=%async_computation.19 | async-start | bytes 3096576 | tf_op jit(solution)/shard_map/all_gather | solution.py:810
  908.6 16.4 %collective-permute-start.17 = (bf16[352,1024]{1,0:T(8,128)(2,1)}, bf16[352,1024]{1,0:T(8,128)(2,1)}, u32[]{:S(2)}, u32[]{:S(2)}) collective-permute-start(bf16[352,1024]{1,0:T(8,128)(2,1)} %get-tuple-element.368), channel_id=1, source_target_pairs={{0,1},{1,0},{2,3},{3,2},{4,5},{5,4},{6,7},{7,6},{8,9},{9,8},{10,11... | collective-permute-start | bytes 2162696 | tf_op jit(solution)/shard_map/ppermute | solution.py:1168
  926.0 7.3 collective-permute-start.18
  941.2 30.0 %collective-permute-start.19 = (bf16[704,1024]{1,0:T(8,128)(2,1)}, bf16[704,1024]{1,0:T(8,128)(2,1)S(1)}, u32[]{:S(2)}, u32[]{:S(2)}) collective-permute-start(bf16[704,1024]{1,0:T(8,128)(2,1)} %slice.218), channel_id=1, source_target_pairs={{0,1},{1,0},{2,3},{3,2},{4,5},{5,4},{6,7},{7,6},{8,9},{9,8},{10,11... | collective-permute-start | bytes 4325384 | tf_op jit(solution)/shard_map/ppermute | solution.py:1168
  (106 other events, 632.9 us)
Sparse Core Ops, SparseCore 0:
  738.4 38.6 reduce-scatter.3
  780.5 28.9 all-gather.4
  811.8 39.8 reduce-scatter.7
  854.5 61.3 reduce-scatter.5
  918.0 23.3 all-gather.8
  942.9 34.5 all-gather.6
